TPU v7x, 512 devices: a whole 4x4x16 slice. The times are simulated.
512 devices in a mesh: section: 4 (over z_hi), dp: 16 (over y, z_lo), expert: 8 (over x, core).
Axes of the slice: x: 4, y: 4, z: 16 (z_hi: 4, z_lo: 4; z = z_hi * 4 + z_lo), core: 2. Of those that a mesh axis runs over, the one named last changes fastest.
Arguments:
- normed: bfloat16 [4, 2048, 3584], P('section', 'dp'), may hold values from -6 to 6
- residual: bfloat16 [4, 2048, 3584], P('section', 'dp', 'expert'), may hold values from -6 to 6
- expert_index: int32 [4, 2048, 2], P('section', 'dp'), may hold values from 0 to 7, all different within a row; in each aligned block of 128 rows (0 to 127, 128 to 255, ..., all dimensions but the last counted through in order) at most 36 rows name the same one
- pick_weight: float32 [4, 2048, 2], P('section', 'dp'), may hold values from 0.25 to 1
- dense_gate: bfloat16 [4, 3584, 3072], P('section', 'dp', 'expert'), may hold values from -0.09375 to 0.09375
- dense_up: bfloat16 [4, 3584, 3072], P('section', 'dp', 'expert'), may hold values from -0.09375 to 0.09375
- dense_down: bfloat16 [4, 3584, 3072], P('section', 'dp', 'expert'), may hold values from -0.109375 to 0.109375
- expert_gate: bfloat16 [4, 8, 3584, 2432], P('section', 'expert', None, 'dp'), may hold values from -0.09375 to 0.09375
- expert_up: bfloat16 [4, 8, 3584, 2432], P('section', 'expert', None, 'dp'), may hold values from -0.09375 to 0.09375
- expert_down: bfloat16 [4, 8, 2432, 3584], P('section', 'expert', 'dp'), may hold values from -0.125 to 0.125
Outputs:
- layer_out: bfloat16 [4, 2048, 3584], P('section', 'dp', 'expert')
Inputs may be any that keep to these rules, and one draw needn't show every extreme that they name: `expert_index`: each row names 2 different experts. Among the 128 tokens of one block no expert is named by more than 36 of them, and in every draw some expert is named by exactly 36 tokens of some block.
All inputs are finite; a program needn't handle non-finite values.
Results may differ from a plain program's by a relative error of at most 0.0051.
Values may be sent and summed in bfloat16 or wider, within the bound.
No kernel may reach another device: no remote copies, remote signals or barrier semaphores. Data moves between devices by JAX's collectives and lax.ppermute only.
A program may use at most 64 MiB of HBM per device.

v0:
```python
import jax
import jax.numpy as jnp
from jax import lax
from jax.sharding import PartitionSpec as P


def shifted(x, axis, by):
    peers = lax.axis_size(axis)
    return lax.ppermute(x, axis, [(i, (i + by) % peers) for i in range(peers)])


def swiglu(first, second):
    return (jax.nn.silu(first) * second).astype(jnp.bfloat16)


def body(
    normed,
    residual,
    expert_index,
    pick_weight,
    dense_gate,
    dense_up,
    dense_down,
    expert_gate,
    expert_up,
    expert_down,
):
    tokens = normed[0]
    picks = expert_index[0]
    weights = pick_weight[0]
    tok_rows, model_width = tokens.shape
    n_expert = lax.axis_size("expert")
    n_data = lax.axis_size("dp")
    capacity = min(tok_rows, 9 * tok_rows // (4 * n_expert))
    mine = lax.axis_index("expert")
    labels = jnp.arange(n_expert, dtype=jnp.int32)
    named = (picks[:, :, None] == labels[None, None, :]).astype(jnp.int32)
    per_token = jnp.sum(named, axis=1, dtype=jnp.int32)
    earlier = jnp.cumsum(per_token, axis=0, dtype=jnp.int32) - per_token
    slot = jnp.take_along_axis(earlier, picks, axis=1)
    is_mine = picks == mine
    my_slot = jnp.sum(jnp.where(is_mine, slot, 0), axis=1, dtype=jnp.int32)
    chosen = jnp.any(is_mine, axis=1)
    positions = jnp.arange(capacity, dtype=jnp.int32)
    select = ((positions[:, None] == my_slot[None, :]) & chosen[None, :]).astype(jnp.bfloat16)
    routed = jnp.dot(select, tokens, preferred_element_type=jnp.float32).astype(jnp.bfloat16)
    own_gate = expert_gate[0, 0]
    own_up = expert_up[0, 0]
    own_down = expert_down[0, 0]
    gathered_rows = lax.all_gather(routed, "dp", axis=0, tiled=True)
    expert_hidden = swiglu(
        jnp.dot(gathered_rows, own_gate, preferred_element_type=jnp.float32),
        jnp.dot(gathered_rows, own_up, preferred_element_type=jnp.float32),
    )
    partials = jnp.dot(expert_hidden, own_down, preferred_element_type=jnp.float32).astype(
        jnp.bfloat16
    )
    contract = (((1,), (1,)), ((), ()))
    gate_full, up_full, down_full = (
        lax.all_gather(dense_gate[0], "dp", axis=0, tiled=True),
        lax.all_gather(dense_up[0], "dp", axis=0, tiled=True),
        lax.all_gather(dense_down[0], "dp", axis=0, tiled=True),
    )
    dense_hidden = swiglu(
        jnp.dot(tokens, gate_full, preferred_element_type=jnp.float32),
        jnp.dot(tokens, up_full, preferred_element_type=jnp.float32),
    )
    dense_part = lax.dot_general(
        dense_hidden, down_full, contract, preferred_element_type=jnp.float32
    ).astype(jnp.bfloat16)
    returned = lax.all_to_all(
        partials.reshape(n_data, capacity, model_width),
        "dp",
        split_axis=0,
        concat_axis=0,
        tiled=True,
    )
    expert_out = jnp.sum(returned, axis=0, dtype=jnp.float32).astype(jnp.bfloat16)
    from_experts, from_dense = (
        lax.all_to_all(expert_out, "expert", split_axis=1, concat_axis=0, tiled=True),
        lax.all_to_all(dense_part, "expert", split_axis=1, concat_axis=0, tiled=True),
    )
    dense_total = jnp.sum(from_dense.reshape(n_expert, tok_rows, -1), axis=0, dtype=jnp.float32)
    lookup = (picks * capacity + slot).reshape(-1)
    picked = (
        jnp.take(from_experts, lookup, axis=0)
        .reshape(tok_rows, picks.shape[1], -1)
        .astype(jnp.float32)
    )
    mixed = (
        residual[0].astype(jnp.float32)
        + dense_total
        + jnp.sum(weights[:, :, None] * picked, axis=1)
    )
    moved = shifted(mixed.astype(jnp.bfloat16), "section", 1)
    return moved[None]


def solution(mesh):
    placed = (
        P("section", "dp", None),
        P("section", "dp", "expert"),
        P("section", "dp", None),
        P("section", "dp", None),
        P("section", "dp", "expert"),
        P("section", "dp", "expert"),
        P("section", "dp", "expert"),
        P("section", "expert", None, "dp"),
        P("section", "expert", None, "dp"),
        P("section", "expert", "dp", None),
    )
    return jax.shard_map(
        body, mesh=mesh, in_specs=placed, out_specs=P("section", "dp", "expert"), check_vma=False
    )
```

profile of v0, /device:TPU:24, one launch (start us, length us, event | category | flops | bytes accessed | tf_op | source)
XLA Modules:
  0.0 540.6 jit_solution(5372944657459863311)
XLA Ops:
  6.5 0.8 fusion.44
  7.3 0.7 convert_reduce_fusion.1
  8.1 0.2 reduce_window_sum.11
  8.6 1.9 gather_fusion.1
  10.8 1.0 fusion
  11.8 0.7 all-gather.9.cloned.1.call-update
  12.5 116.6 %all-gather.15.cloned.1.call-done = bf16[16,36,3584]{2,1,0:T(8,128)(2,1)} async-done(((bf16[1,36,3584]{2,1,0:T(8,128)(2,1)}), bf16[16,36,3584]{2,1,0:T(8,128)(2,1)}) %all-gather.15.cloned.1.call-update) | async-done | bytes 4128784 | tf_op jit(solution)/shard_map/all_gather | solution.py:50
  129.2 7.0 %reshape.164 = bf16[576,3584]{1,0:T(8,128)(2,1)} reshape(bf16[16,36,3584]{2,1,0:T(8,128)(2,1)} %all-gather.15.cloned.1.call-done) | data formatting | bytes 8257536
  136.2 3.8 fusion.18
  139.9 7.9 %convolution_convert_fusion = bf16[576,3584]{1,0:T(8,128)(2,1)} fusion(bf16[576,3584]{1,0:T(8,128)(2,1)} %reshape.164, bf16[1,1,152,3584]{3,2,1,0:T(8,128)(2,1)S(1)} %copy-done, bf16[1,1,3584,152]{2,3,1,0:T(8,128)(2,1)} %param.18, f32[576,152]{0,1:T(8,128)S(1)} %fusion.18), kind=kOutput, calls=%fused_computation.2 | convolution fusion | flops 1257735168 | bytes 10786816 | tf_op jit(solution)/shard_map/dot_general | solution.py:55
  147.8 6.9 %reshape.143 = bf16[16,36,3584]{2,1,0:T(8,128)(2,1)} reshape(bf16[576,3584]{1,0:T(8,128)(2,1)} %convolution_convert_fusion) | data formatting | bytes 8257536 | tf_op jit(solution)/shard_map/reshape | solution.py:72
  154.7 6.8 %all-to-all-start.1 = ((bf16[16,36,3584]{2,1,0:T(8,128)(2,1)}), bf16[16,36,3584]{2,1,0:T(8,128)(2,1)}, u32[]{:S(2)}, u32[]{:S(2)}) async-start(bf16[16,36,3584]{2,1,0:T(8,128)(2,1)} %reshape.143), calls=%async_computation.1 | async-start | bytes 9175040 | tf_op jit(solution)/shard_map/all_to_all | solution.py:71
  161.5 0.7 all-gather.11.cloned.1.call-update
  162.2 0.5 all-gather.13.cloned.1.call-update
  162.8 126.4 %all-gather.9.cloned.1.call-done = bf16[1,3584,384]{2,1,0:T(8,128)(2,1)} async-done(((bf16[1,224,384]{2,1,0:T(8,128)(2,1)}), bf16[1,3584,384]{2,1,0:T(8,128)(2,1)}) %all-gather.9.cloned.1.call-update) | async-done | bytes 2752528 | tf_op jit(solution)/shard_map/all_gather | solution.py:60
  289.1 2.5 fusion.4
  291.6 90.2 %all-gather.11.cloned.1.call-done = bf16[1,3584,384]{2,1,0:T(8,128)(2,1)} async-done(((bf16[1,224,384]{2,1,0:T(8,128)(2,1)}), bf16[1,3584,384]{2,1,0:T(8,128)(2,1)}) %all-gather.11.cloned.1.call-update) | async-done | bytes 2752528 | tf_op jit(solution)/shard_map/all_gather | solution.py:61
  381.9 95.6 %all-gather.13.cloned.1.call-done = bf16[1,3584,384]{2,1,0:T(8,128)(2,1)} async-done(((bf16[1,224,384]{2,1,0:T(8,128)(2,1)}), bf16[1,3584,384]{2,1,0:T(8,128)(2,1)}) %all-gather.13.cloned.1.call-update) | async-done | bytes 2752528 | tf_op jit(solution)/shard_map/all_gather | solution.py:62
  477.4 4.2 convolution_convert_fusion.1
  481.6 1.3 copy.45
  482.9 4.3 all-to-all-start
  487.8 3.1 reduce_sum.51
  490.9 0.4 all_to_all.30
  491.2 0.8 copy.52
  492.1 9.7 %all-to-all-done = bf16[128,8,448]{0,2,1:T(8,128)(2,1)S(1)} async-done(((bf16[128,8,448]{0,2,1:T(8,128)(2,1)}), bf16[128,8,448]{0,2,1:T(8,128)(2,1)S(1)}, u32[]{:S(2)}, u32[]{:S(2)}) %all-to-all-start) | async-done | bytes 917536 | tf_op jit(solution)/shard_map/all_to_all | solution.py:81
  501.8 3.4 all-to-all-start.2
  505.4 8.0 %all-to-all-done.2 = bf16[36,8,448]{2,0,1:T(8,128)(2,1)S(1)} async-done(((bf16[36,8,448]{2,0,1:T(8,128)(2,1)}), bf16[36,8,448]{2,0,1:T(8,128)(2,1)S(1)}, u32[]{:S(2)}, u32[]{:S(2)}) %all-to-all-start.2) | async-done | bytes 258080 | tf_op jit(solution)/shard_map/all_to_all | solution.py:80
  513.5 1.2 gather_fusion
  514.8 0.9 multiply_reduce_fusion
  515.8 7.9 %collective-permute-start = (bf16[128,448]{0,1:T(8,128)(2,1)S(1)}, bf16[128,448]{0,1:T(8,128)(2,1)S(1)}, u32[]{:S(2)}, u32[]{:S(2)}) collective-permute-start(bf16[128,448]{0,1:T(8,128)(2,1)S(1)} %fusion.30), channel_id=1, source_target_pairs={{0,128},{128,256},{256,384},{384,0},{1,129},{129,257},{257,385},{3... | collective-permute-start | bytes 344072 | tf_op jit(solution)/shard_map/ppermute | solution.py:9
  523.8 9.7 %collective-permute-done = bf16[128,448]{0,1:T(8,128)(2,1)S(1)} collective-permute-done((bf16[128,448]{0,1:T(8,128)(2,1)S(1)}, bf16[128,448]{0,1:T(8,128)(2,1)S(1)}, u32[]{:S(2)}, u32[]{:S(2)}) %collective-permute-start) | collective-permute-done | bytes 114720 | tf_op jit(solution)/shard_map/ppermute | solution.py:9
  533.5 0.6 copy.56
  (37 shorter events, 1.8 us)
Async XLA Ops:
  6.5 133.4 %copy-start = (bf16[1,1,152,3584]{3,2,1,0:T(8,128)(2,1)S(1)}, bf16[1,1,152,3584]{3,2,1,0:T(8,128)(2,1)}, u32[]{:S(2)}) copy-start(bf16[1,1,152,3584]{3,2,1,0:T(8,128)(2,1)} %param.19) | copy-start | bytes 3268612
  6.5 122.7 %all-gather.15.cloned.1.call-start = ((), (), s32[]{:S(2)}) async-start(), calls=%async_computation.6 | async-start | bytes 4874240 | tf_op jit(solution)/shard_map/all_gather | solution.py:50
  8.5 2.2 copy-start.3
  8.6 2.2 copy-start.1
  11.8 277.4 %all-gather.9.cloned.1.call-start = ((), (), s32[]{:S(2)}) async-start(), calls=%async_computation.3 | async-start | bytes 2924544 | tf_op jit(solution)/shard_map/all_gather | solution.py:60
  12.5 123.6 %copy-start.5 = (bf16[1,1,3584,152]{2,3,1,0:T(8,128)(2,1)S(1)}, bf16[1,1,3584,152]{2,3,1,0:T(8,128)(2,1)}, u32[]{:S(2)}) copy-start(bf16[1,1,3584,152]{2,3,1,0:T(8,128)(2,1)} %param.17) | copy-start | bytes 3268612
  154.7 328.2 %all-to-all-start.1 = ((bf16[16,36,3584]{2,1,0:T(8,128)(2,1)}), bf16[16,36,3584]{2,1,0:T(8,128)(2,1)}, u32[]{:S(2)}, u32[]{:S(2)}) async-start(bf16[16,36,3584]{2,1,0:T(8,128)(2,1)} %reshape.143), calls=%async_computation.1 | async-start | bytes 9175040 | tf_op jit(solution)/shard_map/all_to_all | solution.py:71
  161.5 220.4 %all-gather.11.cloned.1.call-start = ((), (), s32[]{:S(2)}) async-start(), calls=%async_computation.4 | async-start | bytes 2924544 | tf_op jit(solution)/shard_map/all_gather | solution.py:61
  162.2 315.2 %all-gather.13.cloned.1.call-start = ((), (), s32[]{:S(2)}) async-start(), calls=%async_computation.5 | async-start | bytes 2924544 | tf_op jit(solution)/shard_map/all_gather | solution.py:62
  481.6 6.0 %copy-start.4 = (f32[1,128,2]{1,2,0:T(2,128)S(1)}, f32[1,128,2]{1,2,0:T(2,128)}, u32[]{:S(2)}) copy-start(f32[1,128,2]{1,2,0:T(2,128)} %param.13) | copy-start | bytes 3076
  482.9 18.9 %all-to-all-start = ((bf16[128,8,448]{0,2,1:T(8,128)(2,1)}), bf16[128,8,448]{0,2,1:T(8,128)(2,1)S(1)}, u32[]{:S(2)}, u32[]{:S(2)}) async-start(bf16[128,8,448]{0,2,1:T(8,128)(2,1)} %bitcast.5), calls=%async_computation | async-start | bytes 1835008 | tf_op jit(solution)/shard_map/all_to_all | solution.py:81
  501.8 11.6 %all-to-all-start.2 = ((bf16[36,8,448]{2,0,1:T(8,128)(2,1)}), bf16[36,8,448]{2,0,1:T(8,128)(2,1)S(1)}, u32[]{:S(2)}, u32[]{:S(2)}) async-start(bf16[36,8,448]{2,0,1:T(8,128)(2,1)} %copy.52), calls=%async_computation.2 | async-start | bytes 655360 | tf_op jit(solution)/shard_map/all_to_all | solution.py:80
  505.2 10.5 %copy-start.2 = (bf16[1,128,448]{1,2,0:T(8,128)(2,1)S(1)}, bf16[1,128,448]{1,2,0:T(8,128)(2,1)}, u32[]{:S(2)}) copy-start(bf16[1,128,448]{1,2,0:T(8,128)(2,1)} %param.11) | copy-start | bytes 344068
  515.8 17.6 %collective-permute-start = (bf16[128,448]{0,1:T(8,128)(2,1)S(1)}, bf16[128,448]{0,1:T(8,128)(2,1)S(1)}, u32[]{:S(2)}, u32[]{:S(2)}) collective-permute-start(bf16[128,448]{0,1:T(8,128)(2,1)S(1)} %fusion.30), channel_id=1, source_target_pairs={{0,128},{128,256},{256,384},{384,0},{1,129},{129,257},{257,385},{3... | collective-permute-start | bytes 344072 | tf_op jit(solution)/shard_map/ppermute | solution.py:9
Sparse Core Ops, SparseCore 0:
  11.9 117.2 all-gather.14
  131.3 157.8 all-gather.8
  291.2 90.5 all-gather.10
  383.8 93.5 all-gather.12
where the time goes:
time: 545 us; the launch traced here: 541 us
  waiting for transfers between devices  458 us (84%)
  starting transfers between devices  22.6 us (4%)
  local copies, waits for them, and re-layouts  21.5 us (4%)
  matrix products  19.2 us (4%)
  between operations  13.3 us (2%)
  other arithmetic  5.85 us (1%)
    all_gather x1, waiting for transfers between devices, body(): lax.all_gather(dense_gate[0], 'dp', axis=0, tiled=True)  126 us
    all_gather x1, waiting for transfers between devices, body(): gathered_rows = lax.all_gather(routed, 'dp', axis=0, tiled=True)  117 us
    all_gather x1, waiting for transfers between devices, body(): lax.all_gather(dense_down[0], 'dp', axis=0, tiled=True)  95.6 us
    all_gather x1, waiting for transfers between devices, body(): lax.all_gather(dense_up[0], 'dp', axis=0, tiled=True)  90.2 us
  transfers between devices with their start and end apart: 8, of which 7 were waited for; matrix products, arithmetic and copies ran while one was open for 7% of the time, Pallas kernels for 0%

commit v1 on v0

v1 whole, which is shorter than its diff:
```python
import jax
import jax.numpy as jnp
from jax import lax
from jax.sharding import Mesh, PartitionSpec as P

AXES = ("section", "y", "z", "x", "core")
GRID = (4, 4, 4, 4, 2)
EXPERT_AXES = ("x", "core")


def shifted(x, axis, by):
    peers = lax.axis_size(axis)
    return lax.ppermute(x, axis, [(i, (i + by) % peers) for i in range(peers)])


def exchanged(x, axes):
    return lax.all_to_all(x, axes, split_axis=0, concat_axis=0, tiled=True)


def swiglu(first, second):
    return (jax.nn.silu(first) * second).astype(jnp.bfloat16)


def dot(a, b):
    return jnp.dot(a, b, preferred_element_type=jnp.float32)


def slots_of(picks, n_expert):
    labels = jnp.arange(n_expert, dtype=jnp.int32)
    named = (picks[:, :, None] == labels[None, None, :]).astype(jnp.int32)
    per_token = jnp.sum(named, axis=1, dtype=jnp.int32)
    earlier = jnp.cumsum(per_token, axis=0, dtype=jnp.int32) - per_token
    return jnp.sum(named * earlier[:, None, :], axis=2, dtype=jnp.int32)


def gathered_line(x, axis):
    mine = lax.axis_index(axis)
    parts = [x] + [shifted(x, axis, by) for by in (1, 2, 3)]
    stacked = jnp.stack(parts)
    order = (mine - jnp.arange(4, dtype=jnp.int32)) % 4
    return jnp.take(stacked, order, axis=0)


def body(
    normed,
    residual,
    expert_index,
    pick_weight,
    dense_gate,
    dense_up,
    dense_down,
    expert_gate,
    expert_up,
    expert_down,
):
    bf16, f32 = jnp.bfloat16, jnp.float32
    tokens = normed[0]
    picks = expert_index[0]
    weights = pick_weight[0]
    tok_rows, width = tokens.shape
    n_expert = 8
    capacity = min(tok_rows, 9 * tok_rows // (4 * n_expert))
    core = lax.axis_index("core")
    mine = lax.axis_index("x") * 2 + core
    hidden = dense_gate.shape[2]
    slab = width // 4
    step = dense_gate.shape[1]
    piece = width // n_expert

    stacked = jnp.concatenate([dense_gate[0], dense_up[0], dense_down[0]], axis=0)
    slabs = lax.all_gather(stacked, "y", axis=0, tiled=True).reshape(4, 3, step, hidden)
    gate_slab, up_slab, down_slab = (slabs[:, i].reshape(slab, hidden) for i in range(3))

    slot = slots_of(picks, n_expert)
    is_mine = picks == mine
    positions = jnp.arange(capacity, dtype=jnp.int32)
    select = jnp.any(
        (positions[:, None, None] == slot[None, :, :]) & is_mine[None, :, :], axis=2
    ).astype(bf16)
    routed = dot(select, tokens).astype(bf16)
    group = gathered_line(routed, "z").reshape(4 * capacity, width)

    packed = jnp.concatenate([picks * 128 + slot, jnp.zeros_like(picks)], axis=1)
    line_picks = lax.all_gather(packed[:, :2], "z", axis=0, tiled=True)
    line_weights = lax.all_gather(weights, "z", axis=0, tiled=True)

    gate_up = jnp.concatenate([expert_gate[0, 0], expert_up[0, 0]], axis=1)
    down = expert_down[0, 0]
    inner = down.shape[0]

    def ffn(rows):
        both = dot(rows, gate_up)
        return dot(swiglu(both[:, :inner], both[:, inner:]), down)

    half = 2 * capacity
    from_prev, from_next = shifted(group, "y", 1), shifted(group, "y", -1)
    far_low, far_high = shifted(from_prev[:half], "y", 1), shifted(from_next[half:], "y", -1)
    own_part = ffn(group)
    prev_part = ffn(from_prev)
    next_part = ffn(from_next)
    far_part = ffn(jnp.concatenate([far_low, far_high], axis=0)).astype(bf16)
    relay_next = shifted(far_part[:half], "y", 1)
    relay_prev = shifted(far_part[half:], "y", -1)
    to_next = jnp.concatenate(
        [next_part[:half] + relay_next.astype(f32), next_part[half:]], axis=0
    ).astype(bf16)
    to_prev = jnp.concatenate(
        [prev_part[:half], prev_part[half:] + relay_prev.astype(f32)], axis=0
    ).astype(bf16)
    back_a, back_b = shifted(to_next, "y", 1), shifted(to_prev, "y", -1)
    summed = (own_part + back_a.astype(f32) + back_b.astype(f32)).astype(bf16)

    half_tokens = tok_rows // 2
    by_line = tokens.reshape(tok_rows, 4, 4, step).transpose(2, 0, 1, 3).reshape(4, tok_rows, slab)
    own_half = lax.dynamic_slice_in_dim(by_line, core * half_tokens, half_tokens, axis=1)
    half_in = exchanged(own_half, "z")
    other_half = shifted(half_in, "core", 1)
    low = jnp.where(core == 0, half_in, other_half)
    high = jnp.where(core == 0, other_half, half_in)
    line_tokens = jnp.concatenate([low, high], axis=1).reshape(4 * tok_rows, slab)
    pre = jnp.concatenate([dot(line_tokens, gate_slab), dot(line_tokens, up_slab)], axis=1)
    pre = exchanged(pre.astype(bf16).reshape(4, tok_rows, 2 * hidden), "z")
    pre = jnp.sum(pre.astype(f32), axis=0)
    act = swiglu(pre[:, :hidden], pre[:, hidden:])
    line_act = gathered_line(act, "z").reshape(4 * tok_rows, hidden)
    contract = (((1,), (1,)), ((), ()))
    dense_out = lax.dot_general(line_act, down_slab, contract, preferred_element_type=f32)
    dense_in = exchanged(dense_out.astype(bf16).reshape(4, tok_rows, slab), "z")
    by_owner = (
        dense_in.reshape(2, 2, tok_rows, 4, step)
        .transpose(3, 0, 2, 1, 4)
        .reshape(n_expert, tok_rows, piece)
    )
    dense_total = jnp.sum(exchanged(by_owner, EXPERT_AXES).astype(f32), axis=0)
    base = residual[0].astype(f32) + dense_total

    by_feature = summed.reshape(4 * capacity, n_expert, piece).transpose(1, 0, 2)
    returned = exchanged(by_feature, EXPERT_AXES).reshape(n_expert * 4 * capacity, piece)
    line_expert, line_slot = line_picks // 128, line_picks % 128
    block = (jnp.arange(4 * tok_rows, dtype=jnp.int32) // tok_rows)[:, None]
    target = line_expert * (4 * capacity) + block * capacity + line_slot
    columns = jnp.arange(n_expert * 4 * capacity, dtype=jnp.int32)
    combine = jnp.sum(
        jnp.where(columns[None, None, :] == target[:, :, None], line_weights[:, :, None], 0.0),
        axis=1,
    )
    coarse = combine.astype(bf16)
    fine = (combine - coarse.astype(f32)).astype(bf16)
    mixed_part = (dot(coarse, returned) + dot(fine, returned)).astype(bf16)
    arrived = exchanged(mixed_part.reshape(4, tok_rows, piece), "z")
    mixed = (base + jnp.sum(arrived.astype(f32), axis=0)).astype(bf16)
    return shifted(mixed, "section", 1)[None]


def solution(mesh):
    fine_mesh = Mesh(mesh.devices.reshape(GRID), AXES)
    data = ("y", "z")
    placed = (
        P("section", data, None),
        P("section", data, EXPERT_AXES),
        P("section", data, None),
        P("section", data, None),
        P("section", data, EXPERT_AXES),
        P("section", data, EXPERT_AXES),
        P("section", data, EXPERT_AXES),
        P("section", EXPERT_AXES, None, data),
        P("section", EXPERT_AXES, None, data),
        P("section", EXPERT_AXES, data, None),
    )
    return jax.shard_map(
        body,
        mesh=fine_mesh,
        in_specs=placed,
        out_specs=P("section", data, EXPERT_AXES),
        check_vma=False,
    )
```

time: 545 us -> 296 us (0.54)
  waiting for transfers between devices: 458 us -> 104 us
  starting transfers between devices: 22.6 us -> 89.1 us
  blocking collectives: 0 us -> 33.4 us
  other arithmetic: 5.85 us -> 13.6 us
    all_gather x4 -> x1, waiting for transfers between devices: 429 us -> 0.02 us  [body(): lax.all_gather(stacked, 'y', axis=0, tiled=True).reshape(4, 3, step, hidden)]
    ppermute x1 -> x16, waiting for transfers between devices: 9.69 us -> 82.3 us  [shifted(): return lax.ppermute(x, axis, [(i, (i + by) % peers) for i in range(peers)])]
    ppermute x1 -> x16, starting transfers between devices: 7.94 us -> 58.2 us  [shifted(): return lax.ppermute(x, axis, [(i, (i + by) % peers) for i in range(peers)])]
    all_gather x0 -> x2, blocking collectives: none -> 33.4 us  [the longest x1 20.2 us: body(): line_weights = lax.all_gather(weights, 'z', axis=0, tiled=True)]
    all_to_all x3 -> x6, starting transfers between devices: 14.5 us -> 30.9 us  [exchanged(): return lax.all_to_all(x, axes, split_axis=0, concat_axis=0, tiled=True)]
    slice x0 -> x6, local copies, waits for them, and re-layouts: none -> 9.07 us  [the longest x1 2.66 us: body(): slabs[:, i].reshape(slab, hidden)]
    all_to_all x3 -> x6, waiting for transfers between devices: 17.7 us -> 22.1 us  [exchanged(): return lax.all_to_all(x, axes, split_axis=0, concat_axis=0, tiled=True)]
    dot_general x5 -> x14, matrix products: 19.2 us -> 18.9 us  [the longest x13 17.1 us: dot(): return jnp.dot(a, b, preferred_element_type=jnp.float32)]
  transfers between devices with their start and end apart: 8 -> 23, of which waited for: 7 -> 13; matrix products, arithmetic and copies ran while one was open for 7% -> 15% of each run, Pallas kernels for 0% -> 0%
where the time goes in v1:
time: 296 us; the launch traced here: 295 us
  waiting for transfers between devices  104 us (35%)
  starting transfers between devices  89.1 us (30%)
  blocking collectives  33.4 us (11%)
  local copies, waits for them, and re-layouts  21.4 us (7%)
  matrix products  18.9 us (6%)
  between operations  14 us (5%)
  other arithmetic  13.6 us (5%)
    ppermute x16, waiting for transfers between devices, shifted(): return lax.ppermute(x, axis, [(i, (i + by) % peers) for i in range(peers)])  82.3 us
    ppermute x16, starting transfers between devices, shifted(): return lax.ppermute(x, axis, [(i, (i + by) % peers) for i in range(peers)])  58.2 us
    all_to_all x6, starting transfers between devices, exchanged(): return lax.all_to_all(x, axes, split_axis=0, concat_axis=0, tiled=True)  30.9 us
    all_to_all x6, waiting for transfers between devices, exchanged(): return lax.all_to_all(x, axes, split_axis=0, concat_axis=0, tiled=True)  22.1 us
    all_gather x1, blocking collectives, body(): line_weights = lax.all_gather(weights, 'z', axis=0, tiled=True)  20.2 us
    dot_general x13, matrix products, dot(): return jnp.dot(a, b, preferred_element_type=jnp.float32)  17.1 us
    all_gather x1, blocking collectives, body(): line_picks = lax.all_gather(packed[:, :2], 'z', axis=0, tiled=True)  13.2 us
  transfers between devices with their start and end apart: 23, of which 13 were waited for; matrix products, arithmetic and copies ran while one was open for 15% of the time, Pallas kernels for 0%

profile of v1, /device:TPU:24, one launch (start us, length us, event | category | flops | bytes accessed | tf_op | source)
XLA Modules:
  0.0 294.9 jit_solution(1422220086396531194)
XLA Ops:
  10.6 6.5 %collective-permute-start.6 = (bf16[36,3584]{1,0:T(8,128)(2,1)S(1)}, bf16[36,3584]{1,0:T(8,128)(2,1)S(1)}, u32[]{:S(2)}, u32[]{:S(2)}) collective-permute-start(bf16[36,3584]{1,0:T(8,128)(2,1)S(1)} %convolution_convert_fusion.1), channel_id=1, source_target_pairs={{0,24},{8,0},{16,8},{24,16},{1,25},{9,1},{17,9},{25,17},{2,26},{10... | collective-permute-start | bytes 774152 | tf_op jit(solution)/shard_map/ppermute | solution.py:13
  19.0 2.6 collective-permute-start.4
  21.8 2.5 collective-permute-done.6
  24.4 16.6 %collective-permute-done.5 = bf16[36,3584]{1,0:T(8,128)(2,1)S(1)} collective-permute-done((bf16[36,3584]{1,0:T(8,128)(2,1)S(1)}, bf16[36,3584]{1,0:T(8,128)(2,1)S(1)}, u32[]{:S(2)}, u32[]{:S(2)}) %collective-permute-start.5) | collective-permute-done | bytes 258080 | tf_op jit(solution)/shard_map/ppermute | solution.py:13
  45.4 3.7 %collective-permute-start.7 = (bf16[144,3584]{1,0:T(8,128)(2,1)}, bf16[144,3584]{1,0:T(8,128)(2,1)}, u32[]{:S(2)}, u32[]{:S(2)}) collective-permute-start(bf16[144,3584]{1,0:T(8,128)(2,1)} %broadcast_select_fusion), channel_id=1, source_target_pairs={{0,96},{32,0},{64,32},{96,64},{1,97},{33,1},{65,33},{97,65},{2,98}... | collective-permute-start | bytes 3096584 | tf_op jit(solution)/shard_map/ppermute | solution.py:13
  51.3 5.2 %all-to-all-start = ((bf16[4,64,896]{2,1,0:T(8,128)(2,1)}), bf16[4,64,896]{2,1,0:T(8,128)(2,1)}, u32[]{:S(2)}, u32[]{:S(2)}) async-start(bf16[4,64,896]{2,1,0:T(8,128)(2,1)} %copy.60), calls=%async_computation | async-start | bytes 917504 | tf_op jit(solution)/shard_map/all_to_all | solution.py:17
  57.4 12.1 %collective-permute-done.8 = bf16[144,3584]{1,0:T(8,128)(2,1)} collective-permute-done((bf16[144,3584]{1,0:T(8,128)(2,1)}, bf16[144,3584]{1,0:T(8,128)(2,1)}, u32[]{:S(2)}, u32[]{:S(2)}) %collective-permute-start.8) | collective-permute-done | bytes 1032224 | tf_op jit(solution)/shard_map/ppermute | solution.py:13
  71.5 3.4 %collective-permute-start.9 = (bf16[72,3584]{1,0:T(8,128)(2,1)}, bf16[72,3584]{1,0:T(8,128)(2,1)}, u32[]{:S(2)}, u32[]{:S(2)}) collective-permute-start(bf16[72,3584]{1,0:T(8,128)(2,1)} %slice.100), channel_id=1, source_target_pairs={{0,32},{32,64},{64,96},{96,0},{1,33},{33,65},{65,97},{97,1},{2,34}... | collective-permute-start | bytes 1548296 | tf_op jit(solution)/shard_map/ppermute | solution.py:13
  76.8 2.4 collective-permute-start.10
  79.2 2.2 fusion.52
  87.3 5.2 %collective-permute-done.9 = bf16[72,3584]{1,0:T(8,128)(2,1)} collective-permute-done((bf16[72,3584]{1,0:T(8,128)(2,1)}, bf16[72,3584]{1,0:T(8,128)(2,1)}, u32[]{:S(2)}, u32[]{:S(2)}) %collective-permute-start.9) | collective-permute-done | bytes 516128 | tf_op jit(solution)/shard_map/ppermute | solution.py:13
  92.6 11.8 %collective-permute-done.10 = bf16[72,3584]{1,0:T(8,128)(2,1)} collective-permute-done((bf16[72,3584]{1,0:T(8,128)(2,1)}, bf16[72,3584]{1,0:T(8,128)(2,1)}, u32[]{:S(2)}, u32[]{:S(2)}) %collective-permute-start.10) | collective-permute-done | bytes 516128 | tf_op jit(solution)/shard_map/ppermute | solution.py:13
  104.4 2.9 fusion.13
  113.2 4.0 %collective-permute-start.13 = (bf16[72,3584]{1,0:T(8,128)(2,1)}, bf16[72,3584]{1,0:T(8,128)(2,1)}, u32[]{:S(2)}, u32[]{:S(2)}) collective-permute-start(bf16[72,3584]{1,0:T(8,128)(2,1)} %get-tuple-element.9), channel_id=1, source_target_pairs={{0,96},{32,0},{64,32},{96,64},{1,97},{33,1},{65,33},{97,65},{2,98}... | collective-permute-start | bytes 1548296 | tf_op jit(solution)/shard_map/ppermute | solution.py:13
  122.0 3.4 %collective-permute-start.12 = (bf16[144,3584]{1,0:T(8,128)(2,1)}, bf16[144,3584]{1,0:T(8,128)(2,1)}, u32[]{:S(2)}, u32[]{:S(2)}) collective-permute-start(bf16[144,3584]{1,0:T(8,128)(2,1)} %pad_maximum_fusion.2), channel_id=1, source_target_pairs={{0,32},{32,64},{64,96},{96,0},{1,33},{33,65},{65,97},{97,1},{2,34}... | collective-permute-start | bytes 3096584 | tf_op jit(solution)/shard_map/ppermute | solution.py:13
  125.4 2.7 fusion.54
  130.4 8.1 %all-to-all-start.1 = ((bf16[4,128,768]{2,1,0:T(8,128)(2,1)}), bf16[4,128,768]{2,1,0:T(8,128)(2,1)}, u32[]{:S(2)}, u32[]{:S(2)}) async-start(bf16[4,128,768]{2,1,0:T(8,128)(2,1)} %pad_maximum_fusion.5), calls=%async_computation.1 | async-start | bytes 1572864 | tf_op jit(solution)/shard_map/all_to_all | solution.py:17
  139.9 2.4 collective-permute-start.14
  144.6 20.0 %collective-permute-done.14 = bf16[144,3584]{1,0:T(8,128)(2,1)S(1)} collective-permute-done((bf16[144,3584]{1,0:T(8,128)(2,1)S(1)}, bf16[144,3584]{1,0:T(8,128)(2,1)S(1)}, u32[]{:S(2)}, u32[]{:S(2)}) %collective-permute-start.14) | collective-permute-done | bytes 1032224 | tf_op jit(solution)/shard_map/ppermute | solution.py:13
  169.4 4.3 %all-to-all-start.4 = ((bf16[8,144,448]{2,1,0:T(8,128)(2,1)}), bf16[8,144,448]{2,1,0:T(8,128)(2,1)S(1)}, u32[]{:S(2)}, u32[]{:S(2)}) async-start(bf16[8,144,448]{2,1,0:T(8,128)(2,1)} %bitcast.78), calls=%async_computation.4 | async-start | bytes 2359296 | tf_op jit(solution)/shard_map/all_to_all | solution.py:17
  175.0 5.1 %collective-permute-start.2 = (bf16[128,384]{1,0:T(8,128)(2,1)S(1)}, bf16[128,384]{1,0:T(8,128)(2,1)S(1)}, u32[]{:S(2)}, u32[]{:S(2)}) collective-permute-start(bf16[128,384]{1,0:T(8,128)(2,1)S(1)} %fusion.23), channel_id=1, source_target_pairs={{0,16},{8,24},{16,0},{24,8},{1,17},{9,25},{17,1},{25,9},{2,18},{10... | collective-permute-start | bytes 294920 | tf_op jit(solution)/shard_map/ppermute | solution.py:13
  180.2 2.8 collective-permute-start.1
  183.0 5.0 %collective-permute-start.3 = (bf16[128,384]{1,0:T(8,128)(2,1)S(1)}, bf16[128,384]{1,0:T(8,128)(2,1)S(1)}, u32[]{:S(2)}, u32[]{:S(2)}) collective-permute-start(bf16[128,384]{1,0:T(8,128)(2,1)S(1)} %fusion.23), channel_id=1, source_target_pairs={{0,24},{8,0},{16,8},{24,16},{1,25},{9,1},{17,9},{25,17},{2,26},{10... | collective-permute-start | bytes 294920 | tf_op jit(solution)/shard_map/ppermute | solution.py:13
  194.9 4.6 %all-to-all-start.2 = ((bf16[4,128,896]{1,2,0:T(8,128)(2,1)}), bf16[4,128,896]{1,2,0:T(8,128)(2,1)S(1)}, u32[]{:S(2)}, u32[]{:S(2)}) async-start(bf16[4,128,896]{1,2,0:T(8,128)(2,1)} %copy.51), calls=%async_computation.2 | async-start | bytes 1835008 | tf_op jit(solution)/shard_map/all_to_all | solution.py:17
  199.5 20.2 %all-gather = f32[1,512,2]{1,2,0:T(2,128)S(1)} all-gather(f32[1,128,2]{1,2,0:T(2,128)S(1)} %copy-done.13), channel_id=2, replica_groups=mesh['section'=4,'y'=4,'z'=4,'x'=4,'core'=2] {'z'}, dimensions={1}, use_global_device_ids=true | all-gather | bytes 5120 | tf_op jit(solution)/shard_map/all_gather | solution.py:85
  219.6 13.2 %all_gather.10 = s32[512,2]{0,1:T(2,128)S(1)} all-gather(s32[128,2]{0,1:T(2,128)S(1)} %multiply_add_fusion), channel_id=1, replica_groups=mesh['section'=4,'y'=4,'z'=4,'x'=4,'core'=2] {'z'}, dimensions={0}, use_global_device_ids=true | all-gather | bytes 5120 | tf_op jit(solution)/shard_map/all_gather | solution.py:84
  235.9 4.1 %all-to-all-start.5 = ((bf16[4,128,448]{1,2,0:T(8,128)(2,1)}), bf16[4,128,448]{1,2,0:T(8,128)(2,1)}, u32[]{:S(2)}, u32[]{:S(2)}) async-start(bf16[4,128,448]{1,2,0:T(8,128)(2,1)} %bitcast.79), calls=%async_computation.5 | async-start | bytes 917504 | tf_op jit(solution)/shard_map/all_to_all | solution.py:17
  241.1 8.6 %all-to-all-done.5 = bf16[4,128,448]{1,2,0:T(8,128)(2,1)} async-done(((bf16[4,128,448]{1,2,0:T(8,128)(2,1)}), bf16[4,128,448]{1,2,0:T(8,128)(2,1)}, u32[]{:S(2)}, u32[]{:S(2)}) %all-to-all-start.5) | async-done | bytes 458784 | tf_op jit(solution)/shard_map/all_to_all | solution.py:17
  249.7 4.6 %all-to-all-start.3 = ((bf16[8,128,448]{1,2,0:T(8,128)(2,1)}), bf16[8,128,448]{1,2,0:T(8,128)(2,1)S(1)}, u32[]{:S(2)}, u32[]{:S(2)}) async-start(bf16[8,128,448]{1,2,0:T(8,128)(2,1)} %bitcast.22), calls=%async_computation.3 | async-start | bytes 1835008 | tf_op jit(solution)/shard_map/all_to_all | solution.py:17
  255.4 13.5 %all-to-all-done.3 = bf16[8,128,448]{1,2,0:T(8,128)(2,1)S(1)} async-done(((bf16[8,128,448]{1,2,0:T(8,128)(2,1)}), bf16[8,128,448]{1,2,0:T(8,128)(2,1)S(1)}, u32[]{:S(2)}, u32[]{:S(2)}) %all-to-all-start.3) | async-done | bytes 917536 | tf_op jit(solution)/shard_map/all_to_all | solution.py:17
  269.0 8.9 %collective-permute-start.15 = (bf16[128,448]{0,1:T(8,128)(2,1)S(1)}, bf16[128,448]{0,1:T(8,128)(2,1)S(1)}, u32[]{:S(2)}, u32[]{:S(2)}) collective-permute-start(bf16[128,448]{0,1:T(8,128)(2,1)S(1)} %fusion.22), channel_id=1, source_target_pairs={{0,128},{128,256},{256,384},{384,0},{1,129},{129,257},{257,385},{3... | collective-permute-start | bytes 344072 | tf_op jit(solution)/shard_map/ppermute | solution.py:13
  277.9 9.6 %collective-permute-done.15 = bf16[128,448]{0,1:T(8,128)(2,1)S(1)} collective-permute-done((bf16[128,448]{0,1:T(8,128)(2,1)S(1)}, bf16[128,448]{0,1:T(8,128)(2,1)S(1)}, u32[]{:S(2)}, u32[]{:S(2)}) %collective-permute-start.15) | collective-permute-done | bytes 114720 | tf_op jit(solution)/shard_map/ppermute | solution.py:13
  (124 shorter events, 58.5 us)
Async XLA Ops:
  6.5 74.9 %copy-start = (bf16[1,1,152,3584]{3,2,1,0:T(8,128)(2,1)S(1)}, bf16[1,1,152,3584]{3,2,1,0:T(8,128)(2,1)}, u32[]{:S(2)}) copy-start(bf16[1,1,152,3584]{3,2,1,0:T(8,128)(2,1)} %param.19) | copy-start | bytes 3268612
  10.6 13.8 %collective-permute-start.6 = (bf16[36,3584]{1,0:T(8,128)(2,1)S(1)}, bf16[36,3584]{1,0:T(8,128)(2,1)S(1)}, u32[]{:S(2)}, u32[]{:S(2)}) collective-permute-start(bf16[36,3584]{1,0:T(8,128)(2,1)S(1)} %convolution_convert_fusion.1), channel_id=1, source_target_pairs={{0,24},{8,0},{16,8},{24,16},{1,25},{9,1},{17,9},{25,17},{2,26},{10... | collective-permute-start | bytes 774152 | tf_op jit(solution)/shard_map/ppermute | solution.py:13
  17.1 23.9 %collective-permute-start.5 = (bf16[36,3584]{1,0:T(8,128)(2,1)S(1)}, bf16[36,3584]{1,0:T(8,128)(2,1)S(1)}, u32[]{:S(2)}, u32[]{:S(2)}) collective-permute-start(bf16[36,3584]{1,0:T(8,128)(2,1)S(1)} %convolution_convert_fusion.1), channel_id=1, source_target_pairs={{0,16},{8,24},{16,0},{24,8},{1,17},{9,25},{17,1},{25,9},{2,18},{10... | collective-permute-start | bytes 774152 | tf_op jit(solution)/shard_map/ppermute | solution.py:13
  19.0 22.0 %collective-permute-start.4 = (bf16[36,3584]{1,0:T(8,128)(2,1)S(1)}, bf16[36,3584]{1,0:T(8,128)(2,1)S(1)}, u32[]{:S(2)}, u32[]{:S(2)}) collective-permute-start(bf16[36,3584]{1,0:T(8,128)(2,1)S(1)} %convolution_convert_fusion.1), channel_id=1, source_target_pairs={{0,8},{8,16},{16,24},{24,0},{1,9},{9,17},{17,25},{25,1},{2,10},{10... | collective-permute-start | bytes 774152 | tf_op jit(solution)/shard_map/ppermute | solution.py:13
  42.1 7.0 %copy-start.3 = (bf16[1,128,3584]{2,1,0:T(8,128)(2,1)S(1)}, bf16[1,128,3584]{2,1,0:T(8,128)(2,1)}, u32[]{:S(2)}) copy-start(bf16[1,128,3584]{2,1,0:T(8,128)(2,1)} %param.10) | copy-start | bytes 2752516
  43.2 26.3 %collective-permute-start.8 = (bf16[144,3584]{1,0:T(8,128)(2,1)}, bf16[144,3584]{1,0:T(8,128)(2,1)}, u32[]{:S(2)}, u32[]{:S(2)}) collective-permute-start(bf16[144,3584]{1,0:T(8,128)(2,1)} %broadcast_select_fusion), channel_id=1, source_target_pairs={{0,32},{32,64},{64,96},{96,0},{1,33},{33,65},{65,97},{97,1},{2,34}... | collective-permute-start | bytes 3096584 | tf_op jit(solution)/shard_map/ppermute | solution.py:13
  45.4 29.5 %collective-permute-start.7 = (bf16[144,3584]{1,0:T(8,128)(2,1)}, bf16[144,3584]{1,0:T(8,128)(2,1)}, u32[]{:S(2)}, u32[]{:S(2)}) collective-permute-start(bf16[144,3584]{1,0:T(8,128)(2,1)} %broadcast_select_fusion), channel_id=1, source_target_pairs={{0,96},{32,0},{64,32},{96,64},{1,97},{33,1},{65,33},{97,65},{2,98}... | collective-permute-start | bytes 3096584 | tf_op jit(solution)/shard_map/ppermute | solution.py:13
  49.8 6.7 %copy-start.8 = (bf16[1,224,384]{2,1,0:T(8,128)(2,1)S(1)}, bf16[1,224,384]{2,1,0:T(8,128)(2,1)}, u32[]{:S(2)}) copy-start(bf16[1,224,384]{2,1,0:T(8,128)(2,1)} %param.16) | copy-start | bytes 516100
  51.3 34.1 %all-to-all-start = ((bf16[4,64,896]{2,1,0:T(8,128)(2,1)}), bf16[4,64,896]{2,1,0:T(8,128)(2,1)}, u32[]{:S(2)}, u32[]{:S(2)}) async-start(bf16[4,64,896]{2,1,0:T(8,128)(2,1)} %copy.60), calls=%async_computation | async-start | bytes 917504 | tf_op jit(solution)/shard_map/all_to_all | solution.py:17
  56.5 22.7 %copy-start.14 = (bf16[1,1,3584,152]{2,3,1,0:T(8,128)(2,1)S(1)}, bf16[1,1,3584,152]{2,3,1,0:T(8,128)(2,1)}, u32[]{:S(2)}) copy-start(bf16[1,1,3584,152]{2,3,1,0:T(8,128)(2,1)} %param.18) | copy-start | bytes 3268612
  56.5 68.9 %all-gather.3.cloned.1.call-start = ((), (), s32[]{:S(2)}) async-start(), calls=%async_computation.6 | async-start | bytes 2580480 | tf_op jit(solution)/shard_map/all_gather | solution.py:71
  57.4 21.8 %copy-start.17 = (bf16[1,1,3584,152]{2,3,1,0:T(8,128)(2,1)S(1)}, bf16[1,1,3584,152]{2,3,1,0:T(8,128)(2,1)}, u32[]{:S(2)}) copy-start(bf16[1,1,3584,152]{2,3,1,0:T(8,128)(2,1)} %param.17) | copy-start | bytes 3268612
  71.5 21.1 %collective-permute-start.9 = (bf16[72,3584]{1,0:T(8,128)(2,1)}, bf16[72,3584]{1,0:T(8,128)(2,1)}, u32[]{:S(2)}, u32[]{:S(2)}) collective-permute-start(bf16[72,3584]{1,0:T(8,128)(2,1)} %slice.100), channel_id=1, source_target_pairs={{0,32},{32,64},{64,96},{96,0},{1,33},{33,65},{65,97},{97,1},{2,34}... | collective-permute-start | bytes 1548296 | tf_op jit(solution)/shard_map/ppermute | solution.py:13
  76.8 27.6 %collective-permute-start.10 = (bf16[72,3584]{1,0:T(8,128)(2,1)}, bf16[72,3584]{1,0:T(8,128)(2,1)}, u32[]{:S(2)}, u32[]{:S(2)}) collective-permute-start(bf16[72,3584]{1,0:T(8,128)(2,1)} %slice.101), channel_id=1, source_target_pairs={{0,96},{32,0},{64,32},{96,64},{1,97},{33,1},{65,33},{97,65},{2,98}... | collective-permute-start | bytes 1548296 | tf_op jit(solution)/shard_map/ppermute | solution.py:13
  85.4 31.9 %collective-permute-start = (bf16[4,64,896]{2,1,0:T(8,128)(2,1)}, bf16[4,64,896]{2,1,0:T(8,128)(2,1)S(1)}, u32[]{:S(2)}, u32[]{:S(2)}) collective-permute-start(bf16[4,64,896]{2,1,0:T(8,128)(2,1)} %all-to-all-done), channel_id=1, source_target_pairs={{0,1},{1,0},{2,3},{3,2},{4,5},{5,4},{6,7},{7,6},{8,9},{9,8},{10,11... | collective-permute-start | bytes 1376264 | tf_op jit(solution)/shard_map/ppermute | solution.py:13
  108.6 12.2 %collective-permute-start.11 = (bf16[72,3584]{1,0:T(8,128)(2,1)S(1)}, bf16[72,3584]{1,0:T(8,128)(2,1)S(1)}, u32[]{:S(2)}, u32[]{:S(2)}) collective-permute-start(bf16[72,3584]{1,0:T(8,128)(2,1)S(1)} %get-tuple-element.8), channel_id=1, source_target_pairs={{0,32},{32,64},{64,96},{96,0},{1,33},{33,65},{65,97},{97,1},{2,34}... | collective-permute-start | bytes 1548296 | tf_op jit(solution)/shard_map/ppermute | solution.py:13
  113.2 7.7 %copy-start.5 = (bf16[72,3584]{1,0:T(8,128)(2,1)S(1)}, bf16[72,3584]{1,0:T(8,128)(2,1)}, u32[]{:S(2)}) copy-start(bf16[72,3584]{1,0:T(8,128)(2,1)} %slice.148) | copy-start | bytes 1548292
  113.2 25.3 %collective-permute-start.13 = (bf16[72,3584]{1,0:T(8,128)(2,1)}, bf16[72,3584]{1,0:T(8,128)(2,1)}, u32[]{:S(2)}, u32[]{:S(2)}) collective-permute-start(bf16[72,3584]{1,0:T(8,128)(2,1)} %get-tuple-element.9), channel_id=1, source_target_pairs={{0,96},{32,0},{64,32},{96,64},{1,97},{33,1},{65,33},{97,65},{2,98}... | collective-permute-start | bytes 1548296 | tf_op jit(solution)/shard_map/ppermute | solution.py:13
  122.0 22.6 %collective-permute-start.12 = (bf16[144,3584]{1,0:T(8,128)(2,1)}, bf16[144,3584]{1,0:T(8,128)(2,1)}, u32[]{:S(2)}, u32[]{:S(2)}) collective-permute-start(bf16[144,3584]{1,0:T(8,128)(2,1)} %pad_maximum_fusion.2), channel_id=1, source_target_pairs={{0,32},{32,64},{64,96},{96,0},{1,33},{33,65},{65,97},{97,1},{2,34}... | collective-permute-start | bytes 3096584 | tf_op jit(solution)/shard_map/ppermute | solution.py:13
  129.4 9.1 %copy-start.2 = (f32[144,3584]{1,0:T(8,128)S(1)}, f32[144,3584]{1,0:T(8,128)}, u32[]{:S(2)}) copy-start(f32[144,3584]{1,0:T(8,128)} %copy-done.1) | copy-start | bytes 6193156
  130.4 39.0 %all-to-all-start.1 = ((bf16[4,128,768]{2,1,0:T(8,128)(2,1)}), bf16[4,128,768]{2,1,0:T(8,128)(2,1)}, u32[]{:S(2)}, u32[]{:S(2)}) async-start(bf16[4,128,768]{2,1,0:T(8,128)(2,1)} %pad_maximum_fusion.5), calls=%async_computation.1 | async-start | bytes 1572864 | tf_op jit(solution)/shard_map/all_to_all | solution.py:17
  139.9 24.7 %collective-permute-start.14 = (bf16[144,3584]{1,0:T(8,128)(2,1)S(1)}, bf16[144,3584]{1,0:T(8,128)(2,1)S(1)}, u32[]{:S(2)}, u32[]{:S(2)}) collective-permute-start(bf16[144,3584]{1,0:T(8,128)(2,1)S(1)} %pad_maximum_fusion.3), channel_id=1, source_target_pairs={{0,96},{32,0},{64,32},{96,64},{1,97},{33,1},{65,33},{97,65},{2,98}... | collective-permute-start | bytes 3096584 | tf_op jit(solution)/shard_map/ppermute | solution.py:13
  169.4 25.5 %all-to-all-start.4 = ((bf16[8,144,448]{2,1,0:T(8,128)(2,1)}), bf16[8,144,448]{2,1,0:T(8,128)(2,1)S(1)}, u32[]{:S(2)}, u32[]{:S(2)}) async-start(bf16[8,144,448]{2,1,0:T(8,128)(2,1)} %bitcast.78), calls=%async_computation.4 | async-start | bytes 2359296 | tf_op jit(solution)/shard_map/all_to_all | solution.py:17
  175.0 13.1 %collective-permute-start.2 = (bf16[128,384]{1,0:T(8,128)(2,1)S(1)}, bf16[128,384]{1,0:T(8,128)(2,1)S(1)}, u32[]{:S(2)}, u32[]{:S(2)}) collective-permute-start(bf16[128,384]{1,0:T(8,128)(2,1)S(1)} %fusion.23), channel_id=1, source_target_pairs={{0,16},{8,24},{16,0},{24,8},{1,17},{9,25},{17,1},{25,9},{2,18},{10... | collective-permute-start | bytes 294920 | tf_op jit(solution)/shard_map/ppermute | solution.py:13
  180.2 8.8 %collective-permute-start.1 = (bf16[128,384]{1,0:T(8,128)(2,1)S(1)}, bf16[128,384]{1,0:T(8,128)(2,1)S(1)}, u32[]{:S(2)}, u32[]{:S(2)}) collective-permute-start(bf16[128,384]{1,0:T(8,128)(2,1)S(1)} %fusion.23), channel_id=1, source_target_pairs={{0,8},{8,16},{16,24},{24,0},{1,9},{9,17},{17,25},{25,1},{2,10},{10... | collective-permute-start | bytes 294920 | tf_op jit(solution)/shard_map/ppermute | solution.py:13
  183.0 8.0 %collective-permute-start.3 = (bf16[128,384]{1,0:T(8,128)(2,1)S(1)}, bf16[128,384]{1,0:T(8,128)(2,1)S(1)}, u32[]{:S(2)}, u32[]{:S(2)}) collective-permute-start(bf16[128,384]{1,0:T(8,128)(2,1)S(1)} %fusion.23), channel_id=1, source_target_pairs={{0,24},{8,0},{16,8},{24,16},{1,25},{9,1},{17,9},{25,17},{2,26},{10... | collective-permute-start | bytes 294920 | tf_op jit(solution)/shard_map/ppermute | solution.py:13
  193.5 26.1 %copy-start.12 = (s32[1,128,2]{1,2,0:T(2,128)S(1)}, s32[1,128,2]{1,2,0:T(2,128)}, u32[]{:S(2)}) copy-start(s32[1,128,2]{1,2,0:T(2,128)} %param.12) | copy-start | bytes 3076
  194.9 41.1 %all-to-all-start.2 = ((bf16[4,128,896]{1,2,0:T(8,128)(2,1)}), bf16[4,128,896]{1,2,0:T(8,128)(2,1)S(1)}, u32[]{:S(2)}, u32[]{:S(2)}) async-start(bf16[4,128,896]{1,2,0:T(8,128)(2,1)} %copy.51), calls=%async_computation.2 | async-start | bytes 1835008 | tf_op jit(solution)/shard_map/all_to_all | solution.py:17
  235.9 13.8 %all-to-all-start.5 = ((bf16[4,128,448]{1,2,0:T(8,128)(2,1)}), bf16[4,128,448]{1,2,0:T(8,128)(2,1)}, u32[]{:S(2)}, u32[]{:S(2)}) async-start(bf16[4,128,448]{1,2,0:T(8,128)(2,1)} %bitcast.79), calls=%async_computation.5 | async-start | bytes 917504 | tf_op jit(solution)/shard_map/all_to_all | solution.py:17
  249.7 19.3 %copy-start.11 = (bf16[1,128,448]{1,2,0:T(8,128)(2,1)S(1)}, bf16[1,128,448]{1,2,0:T(8,128)(2,1)}, u32[]{:S(2)}) copy-start(bf16[1,128,448]{1,2,0:T(8,128)(2,1)} %param.11) | copy-start | bytes 344068
  249.7 19.1 %all-to-all-start.3 = ((bf16[8,128,448]{1,2,0:T(8,128)(2,1)}), bf16[8,128,448]{1,2,0:T(8,128)(2,1)S(1)}, u32[]{:S(2)}, u32[]{:S(2)}) async-start(bf16[8,128,448]{1,2,0:T(8,128)(2,1)} %bitcast.22), calls=%async_computation.3 | async-start | bytes 1835008 | tf_op jit(solution)/shard_map/all_to_all | solution.py:17
  269.0 18.4 %collective-permute-start.15 = (bf16[128,448]{0,1:T(8,128)(2,1)S(1)}, bf16[128,448]{0,1:T(8,128)(2,1)S(1)}, u32[]{:S(2)}, u32[]{:S(2)}) collective-permute-start(bf16[128,448]{0,1:T(8,128)(2,1)S(1)} %fusion.22), channel_id=1, source_target_pairs={{0,128},{128,256},{256,384},{384,0},{1,129},{129,257},{257,385},{3... | collective-permute-start | bytes 344072 | tf_op jit(solution)/shard_map/ppermute | solution.py:13
  (11 other events, 38.3 us)
Sparse Core Ops, SparseCore 0:
  59.4 49.4 all-gather.2

commit v2 on v1

v2 whole, which is shorter than its diff:
```python
import jax
import jax.numpy as jnp
from jax import lax
from jax.sharding import Mesh, PartitionSpec as P

AXES = ("section", "y", "z", "x", "core")
GRID = (4, 4, 4, 4, 2)
EXPERT_AXES = ("x", "core")
BF16, F32 = jnp.bfloat16, jnp.float32


def shifted(x, axis, by):
    peers = lax.axis_size(axis)
    return lax.ppermute(x, axis, [(i, (i + by) % peers) for i in range(peers)])


def exchanged(x, axes):
    return lax.all_to_all(x, axes, split_axis=0, concat_axis=0, tiled=True)


def after(x, *others):
    return lax.optimization_barrier((x,) + others)[0]


def swiglu(first, second):
    return (jax.nn.silu(first) * second).astype(BF16)


def dot(a, b):
    return jnp.dot(a, b, preferred_element_type=F32)


def slots_of(picks, n_expert):
    labels = jnp.arange(n_expert, dtype=jnp.int32)
    named = (picks[:, :, None] == labels[None, None, :]).astype(jnp.int32)
    per_token = jnp.sum(named, axis=1, dtype=jnp.int32)
    earlier = jnp.cumsum(per_token, axis=0, dtype=jnp.int32) - per_token
    return jnp.sum(named * earlier[:, None, :], axis=2, dtype=jnp.int32)


def body(
    normed,
    residual,
    expert_index,
    pick_weight,
    dense_gate,
    dense_up,
    dense_down,
    expert_gate,
    expert_up,
    expert_down,
):
    tokens = normed[0]
    picks = expert_index[0]
    weights = pick_weight[0]
    tok_rows, width = tokens.shape
    n_expert = 8
    capacity = min(tok_rows, 9 * tok_rows // (4 * n_expert))
    core = lax.axis_index("core")
    mine = lax.axis_index("x") * 2 + core
    hidden = dense_gate.shape[2]
    slab = width // 4
    step = dense_gate.shape[1]
    piece = width // n_expert

    with jax.named_scope("dense_weights"):
        stacked = jnp.concatenate([dense_gate[0], dense_up[0], dense_down[0]], axis=0)
        slabs = lax.all_gather(stacked, "y", axis=0, tiled=True)

    with jax.named_scope("dispatch"):
        slot = slots_of(picks, n_expert)
        is_mine = picks == mine
        positions = jnp.arange(capacity, dtype=jnp.int32)
        select = jnp.any(
            (positions[:, None, None] == slot[None, :, :]) & is_mine[None, :, :], axis=2
        ).astype(BF16)
        routed = dot(select, tokens).astype(BF16)

    with jax.named_scope("rows_z"):
        lines = [routed] + [shifted(routed, "z", by) for by in (1, 3, 2)]
        low = jnp.concatenate([lines[0], lines[1]], axis=0)
        high = jnp.concatenate([lines[2], lines[3]], axis=0)

    gate_up = jnp.concatenate([expert_gate[0, 0], expert_up[0, 0]], axis=1)
    down = expert_down[0, 0]
    inner = down.shape[0]

    def ffn(rows):
        both = dot(rows, gate_up)
        return dot(swiglu(both[:, :inner], both[:, inner:]), down)

    half = 2 * capacity
    with jax.named_scope("rows_y"):
        prev_low, next_low = shifted(low, "y", 1), shifted(low, "y", -1)
        far_low = shifted(prev_low, "y", 1)
        next_high, prev_high = shifted(high, "y", -1), shifted(high, "y", 1)
        far_high = shifted(next_high, "y", -1)
    with jax.named_scope("experts"):
        near_part = ffn(jnp.concatenate([prev_low, prev_high, next_low, next_high], axis=0))
        far_part = ffn(jnp.concatenate([far_low, far_high], axis=0)).astype(BF16)
        own_part = ffn(after(jnp.concatenate([low, high], axis=0), far_part))
    prev_part, next_part = near_part[: 2 * half], near_part[2 * half :]
    with jax.named_scope("partials_y"):
        early_next = shifted(next_part[half:].astype(BF16), "y", 1)
        early_prev = shifted(prev_part[:half].astype(BF16), "y", -1)
        relay_next = shifted(far_part[:half], "y", 1)
        relay_prev = shifted(far_part[half:], "y", -1)
        late_next = shifted((next_part[:half] + relay_next.astype(F32)).astype(BF16), "y", 1)
        late_prev = shifted((prev_part[half:] + relay_prev.astype(F32)).astype(BF16), "y", -1)
        summed_low = own_part[:half] + late_next.astype(F32) + early_prev.astype(F32)
        summed_high = own_part[half:] + early_next.astype(F32) + late_prev.astype(F32)
        summed_low, summed_high = summed_low.astype(BF16), summed_high.astype(BF16)

    with jax.named_scope("dense_tokens"):
        half_tokens = tok_rows // 2
        by_line = (
            tokens.reshape(tok_rows, 4, 4, step).transpose(2, 0, 1, 3).reshape(4, tok_rows, slab)
        )
        own_half = lax.dynamic_slice_in_dim(by_line, core * half_tokens, half_tokens, axis=1)
        half_in = exchanged(after(own_half, lines[1]), "z")
        other_half = shifted(half_in, "core", 1)
        first = jnp.where(core == 0, half_in, other_half)
        second = jnp.where(core == 0, other_half, half_in)
        line_tokens = jnp.concatenate([first, second], axis=1).reshape(4 * tok_rows, slab)
    slabs = slabs.reshape(4, 3, step, hidden)
    gate_slab, up_slab, down_slab = (slabs[:, i].reshape(slab, hidden) for i in range(3))
    with jax.named_scope("dense_hidden"):
        pre = jnp.concatenate([dot(line_tokens, gate_slab), dot(line_tokens, up_slab)], axis=1)
        pre = pre.astype(BF16).reshape(4, tok_rows, 2 * hidden)
        pre = exchanged(pre, "z")
        pre = jnp.sum(pre.astype(F32), axis=0)
        act = swiglu(pre[:, :hidden], pre[:, hidden:])
        line_act = exchanged(jnp.broadcast_to(act[None], (4,) + act.shape), "z")
        line_act = line_act.reshape(4 * tok_rows, hidden)
    with jax.named_scope("dense_out"):
        contract = (((1,), (1,)), ((), ()))
        dense_out = lax.dot_general(line_act, down_slab, contract, preferred_element_type=F32)
        by_block = (
            dense_out.astype(BF16)
            .reshape(4, 2, half_tokens, 4, step)
            .transpose(3, 1, 0, 2, 4)
            .reshape(n_expert, 4 * half_tokens, step)
        )
        block_sum = jnp.sum(exchanged(by_block, EXPERT_AXES).astype(F32), axis=0).astype(BF16)
        blocks = exchanged(block_sum.reshape(4, half_tokens, step), "z")
        kept = lax.dynamic_slice_in_dim(blocks, 2 * core, 2, axis=0)
        given = lax.dynamic_slice_in_dim(blocks, 2 - 2 * core, 2, axis=0)
        taken = shifted(given, "core", 1)
        first = jnp.where(core == 0, kept, taken)
        second = jnp.where(core == 0, taken, kept)
        dense_total = jnp.concatenate([first, second], axis=1).transpose(1, 0, 2)
    base = residual[0].astype(F32) + dense_total.reshape(tok_rows, piece).astype(F32)

    with jax.named_scope("partials_z"):
        total = summed_low[:capacity].astype(F32)
        for k, (part, by) in enumerate(
            ((summed_low[capacity:], -1), (summed_high[:capacity], -3), (summed_high[capacity:], -2))
        ):
            total = total + shifted(part, "z", by).astype(F32)
        expert_out = total.astype(BF16)
    with jax.named_scope("combine"):
        by_feature = expert_out.reshape(capacity, n_expert, piece).transpose(1, 0, 2)
        returned = exchanged(by_feature, EXPERT_AXES).reshape(n_expert * capacity, piece)
        target = picks * capacity + slot
        columns = jnp.arange(n_expert * capacity, dtype=jnp.int32)
        chosen = jnp.where(columns[None, None, :] == target[:, :, None], weights[:, :, None], 0.0)
        combine = jnp.sum(chosen, axis=1)
        coarse = lax.reduce_precision(combine, 8, 7)
        fine = lax.reduce_precision(combine - coarse, 8, 7)
        spread = dot(coarse.astype(BF16), returned) + dot(fine.astype(BF16), returned)
        mixed = (base + spread).astype(BF16)
    with jax.named_scope("next_section"):
        return shifted(mixed, "section", 1)[None]


def solution(mesh):
    fine_mesh = Mesh(mesh.devices.reshape(GRID), AXES)
    data = ("y", "z")
    placed = (
        P("section", data, None),
        P("section", data, EXPERT_AXES),
        P("section", data, None),
        P("section", data, None),
        P("section", data, EXPERT_AXES),
        P("section", data, EXPERT_AXES),
        P("section", data, EXPERT_AXES),
        P("section", EXPERT_AXES, None, data),
        P("section", EXPERT_AXES, None, data),
        P("section", EXPERT_AXES, data, None),
    )
    return jax.shard_map(
        body,
        mesh=fine_mesh,
        in_specs=placed,
        out_specs=P("section", data, EXPERT_AXES),
        check_vma=False,
    )
```

time: 296 us -> 244 us (0.82)
  waiting for transfers between devices: 104 us -> 56.5 us
  blocking collectives: 33.4 us -> 0 us
  starting transfers between devices: 89.1 us -> 119 us
  other arithmetic: 13.6 us -> 19.7 us
  local copies, waits for them, and re-layouts: 21.4 us -> 15.9 us
    ppermute x16 -> x21, waiting for transfers between devices: 82.3 us -> 35.6 us  [shifted(): return lax.ppermute(x, axis, [(i, (i + by) % peers) for i in range(peers)])]
    all_gather x2 -> x0, blocking collectives: 33.4 us -> none  [the longest x1 20.2 us: body(): line_weights = lax.all_gather(weights, 'z', axis=0, tiled=True)]
    ppermute x16 -> x21, starting transfers between devices: 58.2 us -> 80.6 us  [shifted(): return lax.ppermute(x, axis, [(i, (i + by) % peers) for i in range(peers)])]
    all_to_all x6, starting transfers between devices: 30.9 us -> 38.5 us  [exchanged(): return lax.all_to_all(x, axes, split_axis=0, concat_axis=0, tiled=True)]
    convert_element_type x2 -> x5, other arithmetic: 0.1 us -> 5.62 us  [the longest x1 2.37 us: body(): (next_part[:half] + relay_next.astype(F32)).astype(BF16)]
    concatenate x2 -> x3, other arithmetic: 1.17 us -> 5.16 us  [the longest x1 2.31 us: body(): own_part = ffn(after(jnp.concatenate([low, high], axis=0), far_part))]
    dot_general x14 -> x12, matrix products: 18.9 us -> 16.1 us  [the longest x11 14.3 us: dot(): return jnp.dot(a, b, preferred_element_type=F32)]
  transfers between devices with their start and end apart: 23 -> 28, of which waited for: 13 -> 14; matrix products, arithmetic and copies ran while one was open for 15% -> 19% of each run, Pallas kernels for 0% -> 0%
where the time goes in v2:
time: 244 us; the launch traced here: 241 us
  starting transfers between devices  119 us (49%)
  waiting for transfers between devices  56.5 us (23%)
  other arithmetic  19.7 us (8%)
  matrix products  16.1 us (7%)
  local copies, waits for them, and re-layouts  15.9 us (7%)
  between operations  14 us (6%)
    ppermute x21, starting transfers between devices, shifted(): return lax.ppermute(x, axis, [(i, (i + by) % peers) for i in range(peers)])  80.6 us
    all_to_all x6, starting transfers between devices, exchanged(): return lax.all_to_all(x, axes, split_axis=0, concat_axis=0, tiled=True)  38.5 us
    ppermute x21, waiting for transfers between devices, shifted(): return lax.ppermute(x, axis, [(i, (i + by) % peers) for i in range(peers)])  35.6 us
    all_to_all x6, waiting for transfers between devices, exchanged(): return lax.all_to_all(x, axes, split_axis=0, concat_axis=0, tiled=True)  20.9 us
    dot_general x11, matrix products, dot(): return jnp.dot(a, b, preferred_element_type=F32)  14.3 us
  transfers between devices with their start and end apart: 28, of which 14 were waited for; matrix products, arithmetic and copies ran while one was open for 19% of the time, Pallas kernels for 0%

profile of v2, /device:TPU:24, one launch (start us, length us, event | category | flops | bytes accessed | tf_op | source)
XLA Modules:
  0.0 241.2 jit_solution(5707630590363892644)
XLA Ops:
  10.6 3.8 %collective-permute-start = (bf16[36,3584]{1,0:T(8,128)(2,1)S(1)}, bf16[36,3584]{1,0:T(8,128)(2,1)S(1)}, u32[]{:S(2)}, u32[]{:S(2)}) collective-permute-start(bf16[36,3584]{1,0:T(8,128)(2,1)S(1)} %convolution_convert_fusion.1), channel_id=1, source_target_pairs={{0,8},{8,16},{16,24},{24,0},{1,9},{9,17},{17,25},{25,1},{2,10},{10... | collective-permute-start | bytes 774152 | tf_op jit(solution)/shard_map/rows_z/ppermute | solution.py:14
  14.4 5.2 %collective-permute-start.4 = (bf16[36,3584]{1,0:T(8,128)(2,1)S(1)}, bf16[36,3584]{1,0:T(8,128)(2,1)}, u32[]{:S(2)}, u32[]{:S(2)}) collective-permute-start(bf16[36,3584]{1,0:T(8,128)(2,1)S(1)} %convolution_convert_fusion.1), channel_id=1, source_target_pairs={{0,16},{8,24},{16,0},{24,8},{1,17},{9,25},{17,1},{25,9},{2,18},{10... | collective-permute-start | bytes 774152 | tf_op jit(solution)/shard_map/rows_z/ppermute | solution.py:14
  19.6 2.9 %collective-permute-start.3 = (bf16[36,3584]{1,0:T(8,128)(2,1)S(1)}, bf16[36,3584]{1,0:T(8,128)(2,1)}, u32[]{:S(2)}, u32[]{:S(2)}) collective-permute-start(bf16[36,3584]{1,0:T(8,128)(2,1)S(1)} %convolution_convert_fusion.1), channel_id=1, source_target_pairs={{0,24},{8,0},{16,8},{24,16},{1,25},{9,1},{17,9},{25,17},{2,26},{10... | collective-permute-start | bytes 774152 | tf_op jit(solution)/shard_map/rows_z/ppermute | solution.py:14
  26.1 6.4 %collective-permute-start.5 = (bf16[72,3584]{1,0:T(8,128)(2,1)}, bf16[72,3584]{1,0:T(8,128)(2,1)}, u32[]{:S(2)}, u32[]{:S(2)}) collective-permute-start(bf16[72,3584]{1,0:T(8,128)(2,1)} %pad_maximum_fusion.10), channel_id=1, source_target_pairs={{0,32},{32,64},{64,96},{96,0},{1,33},{33,65},{65,97},{97,1},{2,34}... | collective-permute-start | bytes 1548296 | tf_op jit(solution)/shard_map/rows_y/ppermute | solution.py:14
  38.5 2.6 %collective-permute-start.7 = (bf16[72,3584]{1,0:T(8,128)(2,1)}, bf16[72,3584]{1,0:T(8,128)(2,1)}, u32[]{:S(2)}, u32[]{:S(2)}) collective-permute-start(bf16[72,3584]{1,0:T(8,128)(2,1)} %pad_maximum_fusion.11), channel_id=1, source_target_pairs={{0,96},{32,0},{64,32},{96,64},{1,97},{33,1},{65,33},{97,65},{2,98}... | collective-permute-start | bytes 1548296 | tf_op jit(solution)/shard_map/rows_y/ppermute | solution.py:14
  41.1 4.4 %collective-permute-start.9 = (bf16[72,3584]{1,0:T(8,128)(2,1)}, bf16[72,3584]{1,0:T(8,128)(2,1)}, u32[]{:S(2)}, u32[]{:S(2)}) collective-permute-start(bf16[72,3584]{1,0:T(8,128)(2,1)} %pad_maximum_fusion.11), channel_id=1, source_target_pairs={{0,32},{32,64},{64,96},{96,0},{1,33},{33,65},{65,97},{97,1},{2,34}... | collective-permute-start | bytes 1548296 | tf_op jit(solution)/shard_map/rows_y/ppermute | solution.py:14
  47.0 9.5 %all-to-all-start = ((bf16[4,64,896]{2,1,0:T(8,128)(2,1)}), bf16[4,64,896]{2,1,0:T(8,128)(2,1)}, u32[]{:S(2)}, u32[]{:S(2)}) async-start(bf16[4,64,896]{2,1,0:T(8,128)(2,1)} %copy.76), calls=%async_computation | async-start | bytes 917504 | tf_op jit(solution)/shard_map/dense_tokens/all_to_all | solution.py:18
  58.7 7.1 %collective-permute-done.7 = bf16[72,3584]{1,0:T(8,128)(2,1)} collective-permute-done((bf16[72,3584]{1,0:T(8,128)(2,1)}, bf16[72,3584]{1,0:T(8,128)(2,1)}, u32[]{:S(2)}, u32[]{:S(2)}) %collective-permute-start.7) | collective-permute-done | bytes 516128 | tf_op jit(solution)/shard_map/rows_y/ppermute | solution.py:14
  67.8 5.1 %collective-permute-start.6 = (bf16[72,3584]{1,0:T(8,128)(2,1)}, bf16[72,3584]{1,0:T(8,128)(2,1)S(1)}, u32[]{:S(2)}, u32[]{:S(2)}) collective-permute-start(bf16[72,3584]{1,0:T(8,128)(2,1)} %collective-permute-done.5), channel_id=1, source_target_pairs={{0,32},{32,64},{64,96},{96,0},{1,33},{33,65},{65,97},{97,1},{2,34}... | collective-permute-start | bytes 1548296 | tf_op jit(solution)/shard_map/rows_y/ppermute | solution.py:14
  73.0 2.7 %fusion = f32[288,304]{1,0:T(8,128)S(1)} fusion(bf16[72,3584]{1,0:T(8,128)(2,1)} %collective-permute-done.7, bf16[72,3584]{1,0:T(8,128)(2,1)} %collective-permute-done.10, bf16[72,3584]{1,0:T(8,128)(2,1)} %collective-permute-done.9, bf16[72,3584]{1,0:T(8,128)(2,1)} %collective-permute-done.5, bf16[3584,152]{0,1:T(8,128)(2,1)S(1)} %bitcast.78, ...), kind=kOutput, calls=%fused_computation.3 | convolution fusion | flops 640188416 | bytes 4593664 | tf_op jit(solution)/shard_map/experts/dot_general | solution.py:30
  75.7 2.7 %fusion.53 = (bf16[288,3584]{1,0:T(8,128)(2,1)S(1)}, f32[288,3584]{1,0:T(8,128)}) fusion(bf16[1,1,152,3584]{3,2,1,0:T(8,128)(2,1)S(1)} %copy-done, f32[288,304]{1,0:T(8,128)S(1)} %fusion), kind=kOutput, calls=%fused_computation.91 | convolution fusion | flops 315081216 | bytes 7872512 | tf_op jit(solution)/shard_map/experts/dot_general | solution.py:30
  78.5 5.2 %collective-permute-done.8 = bf16[72,3584]{1,0:T(8,128)(2,1)S(1)} collective-permute-done((bf16[72,3584]{1,0:T(8,128)(2,1)}, bf16[72,3584]{1,0:T(8,128)(2,1)S(1)}, u32[]{:S(2)}, u32[]{:S(2)}) %collective-permute-start.8) | collective-permute-done | bytes 516128 | tf_op jit(solution)/shard_map/rows_y/ppermute | solution.py:14
  90.7 5.3 %collective-permute-start.11 = (bf16[72,3584]{1,0:T(8,128)(2,1)}, bf16[72,3584]{1,0:T(8,128)(2,1)}, u32[]{:S(2)}, u32[]{:S(2)}) collective-permute-start(bf16[72,3584]{1,0:T(8,128)(2,1)} %get-tuple-element.18), channel_id=1, source_target_pairs={{0,32},{32,64},{64,96},{96,0},{1,33},{33,65},{65,97},{97,1},{2,34}... | collective-permute-start | bytes 1548296 | tf_op jit(solution)/shard_map/partials_y/ppermute | solution.py:14
  100.0 2.7 %fusion.49 = (bf16[4,1,224,384]{3,2,1,0:T(8,128)(2,1)}, bf16[4,1,224,384]{3,2,1,0:T(8,128)(2,1)S(1)}, bf16[4,1,224,384]{3,2,1,0:T(8,128)(2,1)S(1)}) fusion(bf16[4,3,224,384]{3,2,1,0:T(8,128)(2,1)} %bitcast.65), kind=kLoop, calls=%fused_computation.87 | loop fusion | bytes 4128768 | tf_op jit(solution)/shard_map/slice | solution.py:126
  105.0 13.9 %all-to-all-start.1 = ((bf16[4,128,768]{2,1,0:T(8,128)(2,1)}), bf16[4,128,768]{2,1,0:T(8,128)(2,1)}, u32[]{:S(2)}, u32[]{:S(2)}) async-start(bf16[4,128,768]{2,1,0:T(8,128)(2,1)} %pad_maximum_fusion.3), calls=%async_computation.1 | async-start | bytes 1572864 | tf_op jit(solution)/shard_map/dense_hidden/all_to_all | solution.py:18
  122.1 5.2 %collective-permute-start.15 = (bf16[72,3584]{1,0:T(8,128)(2,1)}, bf16[72,3584]{1,0:T(8,128)(2,1)}, u32[]{:S(2)}, u32[]{:S(2)}) collective-permute-start(bf16[72,3584]{1,0:T(8,128)(2,1)} %get-tuple-element.17), channel_id=1, source_target_pairs={{0,32},{32,64},{64,96},{96,0},{1,33},{33,65},{65,97},{97,1},{2,34}... | collective-permute-start | bytes 1548296 | tf_op jit(solution)/shard_map/partials_y/ppermute | solution.py:14
  132.2 3.9 %collective-permute-start.12 = (bf16[72,3584]{1,0:T(8,128)(2,1)}, bf16[72,3584]{1,0:T(8,128)(2,1)}, u32[]{:S(2)}, u32[]{:S(2)}) collective-permute-start(bf16[72,3584]{1,0:T(8,128)(2,1)} %get-tuple-element.9), channel_id=1, source_target_pairs={{0,32},{32,64},{64,96},{96,0},{1,33},{33,65},{65,97},{97,1},{2,34}... | collective-permute-start | bytes 1548296 | tf_op jit(solution)/shard_map/partials_y/ppermute | solution.py:14
  142.1 3.6 %all-to-all-start.2 = ((bf16[4,128,384]{2,1,0:T(8,128)(2,1)}), bf16[4,128,384]{2,1,0:T(8,128)(2,1)S(1)}, u32[]{:S(2)}, u32[]{:S(2)}) async-start(bf16[4,128,384]{2,1,0:T(8,128)(2,1)} %broadcast_in_dim.14), calls=%async_computation.2 | async-start | bytes 786432 | tf_op jit(solution)/shard_map/dense_hidden/all_to_all | solution.py:18
  145.8 3.6 %collective-permute-done.12 = bf16[72,3584]{1,0:T(8,128)(2,1)} collective-permute-done((bf16[72,3584]{1,0:T(8,128)(2,1)}, bf16[72,3584]{1,0:T(8,128)(2,1)}, u32[]{:S(2)}, u32[]{:S(2)}) %collective-permute-start.12) | collective-permute-done | bytes 516128 | tf_op jit(solution)/shard_map/partials_y/ppermute | solution.py:14
  149.4 2.6 %collective-permute-done.17 = bf16[72,3584]{1,0:T(8,128)(2,1)} collective-permute-done((bf16[72,3584]{1,0:T(8,128)(2,1)}, bf16[72,3584]{1,0:T(8,128)(2,1)}, u32[]{:S(2)}, u32[]{:S(2)}) %collective-permute-start.17) | collective-permute-done | bytes 516128 | tf_op jit(solution)/shard_map/partials_y/ppermute | solution.py:14
  154.8 5.1 %collective-permute-start.19 = (bf16[36,3584]{1,0:T(8,128)(2,1)}, bf16[36,3584]{1,0:T(8,128)(2,1)}, u32[]{:S(2)}, u32[]{:S(2)}) collective-permute-start(bf16[36,3584]{1,0:T(8,128)(2,1)} %get-tuple-element.23), channel_id=1, source_target_pairs={{0,16},{8,24},{16,0},{24,8},{1,17},{9,25},{17,1},{25,9},{2,18},{10... | collective-permute-start | bytes 774152 | tf_op jit(solution)/shard_map/partials_z/ppermute | solution.py:14
  160.0 2.8 %collective-permute-start.18 = (bf16[36,3584]{1,0:T(8,128)(2,1)}, bf16[36,3584]{1,0:T(8,128)(2,1)}, u32[]{:S(2)}, u32[]{:S(2)}) collective-permute-start(bf16[36,3584]{1,0:T(8,128)(2,1)} %get-tuple-element.22), channel_id=1, source_target_pairs={{0,8},{8,16},{16,24},{24,0},{1,9},{9,17},{17,25},{25,1},{2,10},{10... | collective-permute-start | bytes 774152 | tf_op jit(solution)/shard_map/partials_z/ppermute | solution.py:14
  163.6 4.8 %collective-permute-start.14 = (bf16[36,3584]{1,0:T(8,128)(2,1)}, bf16[36,3584]{1,0:T(8,128)(2,1)}, u32[]{:S(2)}, u32[]{:S(2)}) collective-permute-start(bf16[36,3584]{1,0:T(8,128)(2,1)} %slice.116), channel_id=1, source_target_pairs={{0,24},{8,0},{16,8},{24,16},{1,25},{9,1},{17,9},{25,17},{2,26},{10... | collective-permute-start | bytes 774152 | tf_op jit(solution)/shard_map/partials_z/ppermute | solution.py:14
  172.6 4.8 %all-to-all-start.3 = ((bf16[8,256,224]{1,2,0:T(8,128)(2,1)}), bf16[8,256,224]{1,2,0:T(8,128)(2,1)S(1)}, u32[]{:S(2)}, u32[]{:S(2)}) async-start(bf16[8,256,224]{1,2,0:T(8,128)(2,1)} %copy.71), calls=%async_computation.3 | async-start | bytes 1835008 | tf_op jit(solution)/shard_map/dense_out/all_to_all | solution.py:18
  177.9 5.1 %collective-permute-done.14 = bf16[36,3584]{1,0:T(8,128)(2,1)} collective-permute-done((bf16[36,3584]{1,0:T(8,128)(2,1)}, bf16[36,3584]{1,0:T(8,128)(2,1)}, u32[]{:S(2)}, u32[]{:S(2)}) %collective-permute-start.14) | collective-permute-done | bytes 258080 | tf_op jit(solution)/shard_map/partials_z/ppermute | solution.py:14
  185.5 6.3 %all-to-all-done.3 = bf16[8,256,224]{1,2,0:T(8,128)(2,1)S(1)} async-done(((bf16[8,256,224]{1,2,0:T(8,128)(2,1)}), bf16[8,256,224]{1,2,0:T(8,128)(2,1)S(1)}, u32[]{:S(2)}, u32[]{:S(2)}) %all-to-all-start.3) | async-done | bytes 917536 | tf_op jit(solution)/shard_map/dense_out/all_to_all | solution.py:18
  191.9 3.4 %all-to-all-start.5 = ((bf16[8,36,448]{2,1,0:T(8,128)(2,1)}), bf16[8,36,448]{2,1,0:T(8,128)(2,1)S(1)}, u32[]{:S(2)}, u32[]{:S(2)}) async-start(bf16[8,36,448]{2,1,0:T(8,128)(2,1)} %bitcast.60), calls=%async_computation.5 | async-start | bytes 655360 | tf_op jit(solution)/shard_map/combine/all_to_all | solution.py:18
  196.2 7.2 %all-to-all-done.5 = bf16[8,36,448]{2,1,0:T(8,128)(2,1)S(1)} async-done(((bf16[8,36,448]{2,1,0:T(8,128)(2,1)}), bf16[8,36,448]{2,1,0:T(8,128)(2,1)S(1)}, u32[]{:S(2)}, u32[]{:S(2)}) %all-to-all-start.5) | async-done | bytes 258080 | tf_op jit(solution)/shard_map/combine/all_to_all | solution.py:18
  203.5 3.3 %all-to-all-start.4 = ((bf16[4,64,224]{2,1,0:T(8,128)(2,1)}), bf16[4,64,224]{2,1,0:T(8,128)(2,1)S(1)}, u32[]{:S(2)}, u32[]{:S(2)}) async-start(bf16[4,64,224]{2,1,0:T(8,128)(2,1)} %bitcast.19), calls=%async_computation.4 | async-start | bytes 262144 | tf_op jit(solution)/shard_map/dense_out/all_to_all | solution.py:18
  207.0 5.9 %all-to-all-done.4 = bf16[4,64,224]{2,1,0:T(8,128)(2,1)S(1)} async-done(((bf16[4,64,224]{2,1,0:T(8,128)(2,1)}), bf16[4,64,224]{2,1,0:T(8,128)(2,1)S(1)}, u32[]{:S(2)}, u32[]{:S(2)}) %all-to-all-start.4) | async-done | bytes 114720 | tf_op jit(solution)/shard_map/dense_out/all_to_all | solution.py:18
  216.5 9.3 %collective-permute-start.20 = (bf16[128,448]{0,1:T(8,128)(2,1)S(1)}, bf16[128,448]{0,1:T(8,128)(2,1)S(1)}, u32[]{:S(2)}, u32[]{:S(2)}) collective-permute-start(bf16[128,448]{0,1:T(8,128)(2,1)S(1)} %fusion.9), channel_id=1, source_target_pairs={{0,128},{128,256},{256,384},{384,0},{1,129},{129,257},{257,385},{3... | collective-permute-start | bytes 344072 | tf_op jit(solution)/shard_map/next_section/ppermute | solution.py:14
  225.8 7.9 %collective-permute-done.20 = bf16[128,448]{0,1:T(8,128)(2,1)S(1)} collective-permute-done((bf16[128,448]{0,1:T(8,128)(2,1)S(1)}, bf16[128,448]{0,1:T(8,128)(2,1)S(1)}, u32[]{:S(2)}, u32[]{:S(2)}) %collective-permute-start.20) | collective-permute-done | bytes 114720 | tf_op jit(solution)/shard_map/next_section/ppermute | solution.py:14
  (109 shorter events, 62.8 us)
Async XLA Ops:
  6.5 69.2 %copy-start = (bf16[1,1,152,3584]{3,2,1,0:T(8,128)(2,1)S(1)}, bf16[1,1,152,3584]{3,2,1,0:T(8,128)(2,1)}, u32[]{:S(2)}) copy-start(bf16[1,1,152,3584]{3,2,1,0:T(8,128)(2,1)} %param.19) | copy-start | bytes 3268612
  6.5 93.5 %all-gather.2.cloned.1.call-start = ((), (), s32[]{:S(2)}) async-start(), calls=%async_computation.6 | async-start | bytes 2580480 | tf_op jit(solution)/shard_map/dense_weights/all_gather | solution.py:68
  10.6 14.6 %collective-permute-start = (bf16[36,3584]{1,0:T(8,128)(2,1)S(1)}, bf16[36,3584]{1,0:T(8,128)(2,1)S(1)}, u32[]{:S(2)}, u32[]{:S(2)}) collective-permute-start(bf16[36,3584]{1,0:T(8,128)(2,1)S(1)} %convolution_convert_fusion.1), channel_id=1, source_target_pairs={{0,8},{8,16},{16,24},{24,0},{1,9},{9,17},{17,25},{25,1},{2,10},{10... | collective-permute-start | bytes 774152 | tf_op jit(solution)/shard_map/rows_z/ppermute | solution.py:14
  14.4 22.0 %collective-permute-start.4 = (bf16[36,3584]{1,0:T(8,128)(2,1)S(1)}, bf16[36,3584]{1,0:T(8,128)(2,1)}, u32[]{:S(2)}, u32[]{:S(2)}) collective-permute-start(bf16[36,3584]{1,0:T(8,128)(2,1)S(1)} %convolution_convert_fusion.1), channel_id=1, source_target_pairs={{0,16},{8,24},{16,0},{24,8},{1,17},{9,25},{17,1},{25,9},{2,18},{10... | collective-permute-start | bytes 774152 | tf_op jit(solution)/shard_map/rows_z/ppermute | solution.py:14
  19.6 16.9 %collective-permute-start.3 = (bf16[36,3584]{1,0:T(8,128)(2,1)S(1)}, bf16[36,3584]{1,0:T(8,128)(2,1)}, u32[]{:S(2)}, u32[]{:S(2)}) collective-permute-start(bf16[36,3584]{1,0:T(8,128)(2,1)S(1)} %convolution_convert_fusion.1), channel_id=1, source_target_pairs={{0,24},{8,0},{16,8},{24,16},{1,25},{9,1},{17,9},{25,17},{2,26},{10... | collective-permute-start | bytes 774152 | tf_op jit(solution)/shard_map/rows_z/ppermute | solution.py:14
  26.1 41.7 %collective-permute-start.5 = (bf16[72,3584]{1,0:T(8,128)(2,1)}, bf16[72,3584]{1,0:T(8,128)(2,1)}, u32[]{:S(2)}, u32[]{:S(2)}) collective-permute-start(bf16[72,3584]{1,0:T(8,128)(2,1)} %pad_maximum_fusion.10), channel_id=1, source_target_pairs={{0,32},{32,64},{64,96},{96,0},{1,33},{33,65},{65,97},{97,1},{2,34}... | collective-permute-start | bytes 1548296 | tf_op jit(solution)/shard_map/rows_y/ppermute | solution.py:14
  32.5 40.4 %collective-permute-start.10 = (bf16[72,3584]{1,0:T(8,128)(2,1)}, bf16[72,3584]{1,0:T(8,128)(2,1)}, u32[]{:S(2)}, u32[]{:S(2)}) collective-permute-start(bf16[72,3584]{1,0:T(8,128)(2,1)} %pad_maximum_fusion.10), channel_id=1, source_target_pairs={{0,96},{32,0},{64,32},{96,64},{1,97},{33,1},{65,33},{97,65},{2,98}... | collective-permute-start | bytes 1548296 | tf_op jit(solution)/shard_map/rows_y/ppermute | solution.py:14
  38.5 27.4 %collective-permute-start.7 = (bf16[72,3584]{1,0:T(8,128)(2,1)}, bf16[72,3584]{1,0:T(8,128)(2,1)}, u32[]{:S(2)}, u32[]{:S(2)}) collective-permute-start(bf16[72,3584]{1,0:T(8,128)(2,1)} %pad_maximum_fusion.11), channel_id=1, source_target_pairs={{0,96},{32,0},{64,32},{96,64},{1,97},{33,1},{65,33},{97,65},{2,98}... | collective-permute-start | bytes 1548296 | tf_op jit(solution)/shard_map/rows_y/ppermute | solution.py:14
  41.1 31.8 %collective-permute-start.9 = (bf16[72,3584]{1,0:T(8,128)(2,1)}, bf16[72,3584]{1,0:T(8,128)(2,1)}, u32[]{:S(2)}, u32[]{:S(2)}) collective-permute-start(bf16[72,3584]{1,0:T(8,128)(2,1)} %pad_maximum_fusion.11), channel_id=1, source_target_pairs={{0,32},{32,64},{64,96},{96,0},{1,33},{33,65},{65,97},{97,1},{2,34}... | collective-permute-start | bytes 1548296 | tf_op jit(solution)/shard_map/rows_y/ppermute | solution.py:14
  47.0 26.0 %copy-start.11 = (bf16[1,1,3584,152]{2,3,1,0:T(8,128)(2,1)S(1)}, bf16[1,1,3584,152]{2,3,1,0:T(8,128)(2,1)}, u32[]{:S(2)}) copy-start(bf16[1,1,3584,152]{2,3,1,0:T(8,128)(2,1)} %param.18) | copy-start | bytes 3268612
  47.0 39.6 %all-to-all-start = ((bf16[4,64,896]{2,1,0:T(8,128)(2,1)}), bf16[4,64,896]{2,1,0:T(8,128)(2,1)}, u32[]{:S(2)}, u32[]{:S(2)}) async-start(bf16[4,64,896]{2,1,0:T(8,128)(2,1)} %copy.76), calls=%async_computation | async-start | bytes 917504 | tf_op jit(solution)/shard_map/dense_tokens/all_to_all | solution.py:18
  65.9 17.8 %collective-permute-start.8 = (bf16[72,3584]{1,0:T(8,128)(2,1)}, bf16[72,3584]{1,0:T(8,128)(2,1)S(1)}, u32[]{:S(2)}, u32[]{:S(2)}) collective-permute-start(bf16[72,3584]{1,0:T(8,128)(2,1)} %collective-permute-done.7), channel_id=1, source_target_pairs={{0,96},{32,0},{64,32},{96,64},{1,97},{33,1},{65,33},{97,65},{2,98}... | collective-permute-start | bytes 1548296 | tf_op jit(solution)/shard_map/rows_y/ppermute | solution.py:14
  67.8 16.4 %collective-permute-start.6 = (bf16[72,3584]{1,0:T(8,128)(2,1)}, bf16[72,3584]{1,0:T(8,128)(2,1)S(1)}, u32[]{:S(2)}, u32[]{:S(2)}) collective-permute-start(bf16[72,3584]{1,0:T(8,128)(2,1)} %collective-permute-done.5), channel_id=1, source_target_pairs={{0,32},{32,64},{64,96},{96,0},{1,33},{33,65},{65,97},{97,1},{2,34}... | collective-permute-start | bytes 1548296 | tf_op jit(solution)/shard_map/rows_y/ppermute | solution.py:14
  86.6 11.4 %collective-permute-start.1 = (bf16[4,64,896]{2,1,0:T(8,128)(2,1)}, bf16[4,64,896]{2,1,0:T(8,128)(2,1)S(1)}, u32[]{:S(2)}, u32[]{:S(2)}) collective-permute-start(bf16[4,64,896]{2,1,0:T(8,128)(2,1)} %all-to-all-done), channel_id=1, source_target_pairs={{0,1},{1,0},{2,3},{3,2},{4,5},{5,4},{6,7},{7,6},{8,9},{9,8},{10,11... | collective-permute-start | bytes 1376264 | tf_op jit(solution)/shard_map/dense_tokens/ppermute | solution.py:14
  90.7 39.1 %collective-permute-start.11 = (bf16[72,3584]{1,0:T(8,128)(2,1)}, bf16[72,3584]{1,0:T(8,128)(2,1)}, u32[]{:S(2)}, u32[]{:S(2)}) collective-permute-start(bf16[72,3584]{1,0:T(8,128)(2,1)} %get-tuple-element.18), channel_id=1, source_target_pairs={{0,32},{32,64},{64,96},{96,0},{1,33},{33,65},{65,97},{97,1},{2,34}... | collective-permute-start | bytes 1548296 | tf_op jit(solution)/shard_map/partials_y/ppermute | solution.py:14
  96.0 33.8 %collective-permute-start.16 = (bf16[72,3584]{1,0:T(8,128)(2,1)}, bf16[72,3584]{1,0:T(8,128)(2,1)}, u32[]{:S(2)}, u32[]{:S(2)}) collective-permute-start(bf16[72,3584]{1,0:T(8,128)(2,1)} %get-tuple-element.19), channel_id=1, source_target_pairs={{0,96},{32,0},{64,32},{96,64},{1,97},{33,1},{65,33},{97,65},{2,98}... | collective-permute-start | bytes 1548296 | tf_op jit(solution)/shard_map/partials_y/ppermute | solution.py:14
  105.0 35.0 %all-to-all-start.1 = ((bf16[4,128,768]{2,1,0:T(8,128)(2,1)}), bf16[4,128,768]{2,1,0:T(8,128)(2,1)}, u32[]{:S(2)}, u32[]{:S(2)}) async-start(bf16[4,128,768]{2,1,0:T(8,128)(2,1)} %pad_maximum_fusion.3), calls=%async_computation.1 | async-start | bytes 1572864 | tf_op jit(solution)/shard_map/dense_hidden/all_to_all | solution.py:18
  119.9 25.9 %collective-permute-start.13 = (bf16[72,3584]{1,0:T(8,128)(2,1)}, bf16[72,3584]{1,0:T(8,128)(2,1)}, u32[]{:S(2)}, u32[]{:S(2)}) collective-permute-start(bf16[72,3584]{1,0:T(8,128)(2,1)} %get-tuple-element.16), channel_id=1, source_target_pairs={{0,96},{32,0},{64,32},{96,64},{1,97},{33,1},{65,33},{97,65},{2,98}... | collective-permute-start | bytes 1548296 | tf_op jit(solution)/shard_map/partials_y/ppermute | solution.py:14
  122.1 23.7 %collective-permute-start.15 = (bf16[72,3584]{1,0:T(8,128)(2,1)}, bf16[72,3584]{1,0:T(8,128)(2,1)}, u32[]{:S(2)}, u32[]{:S(2)}) collective-permute-start(bf16[72,3584]{1,0:T(8,128)(2,1)} %get-tuple-element.17), channel_id=1, source_target_pairs={{0,32},{32,64},{64,96},{96,0},{1,33},{33,65},{65,97},{97,1},{2,34}... | collective-permute-start | bytes 1548296 | tf_op jit(solution)/shard_map/partials_y/ppermute | solution.py:14
  132.2 17.2 %collective-permute-start.12 = (bf16[72,3584]{1,0:T(8,128)(2,1)}, bf16[72,3584]{1,0:T(8,128)(2,1)}, u32[]{:S(2)}, u32[]{:S(2)}) collective-permute-start(bf16[72,3584]{1,0:T(8,128)(2,1)} %get-tuple-element.9), channel_id=1, source_target_pairs={{0,32},{32,64},{64,96},{96,0},{1,33},{33,65},{65,97},{97,1},{2,34}... | collective-permute-start | bytes 1548296 | tf_op jit(solution)/shard_map/partials_y/ppermute | solution.py:14
  136.1 15.9 %collective-permute-start.17 = (bf16[72,3584]{1,0:T(8,128)(2,1)}, bf16[72,3584]{1,0:T(8,128)(2,1)}, u32[]{:S(2)}, u32[]{:S(2)}) collective-permute-start(bf16[72,3584]{1,0:T(8,128)(2,1)} %get-tuple-element.10), channel_id=1, source_target_pairs={{0,96},{32,0},{64,32},{96,64},{1,97},{33,1},{65,33},{97,65},{2,98}... | collective-permute-start | bytes 1548296 | tf_op jit(solution)/shard_map/partials_y/ppermute | solution.py:14
  142.1 26.2 %all-to-all-start.2 = ((bf16[4,128,384]{2,1,0:T(8,128)(2,1)}), bf16[4,128,384]{2,1,0:T(8,128)(2,1)S(1)}, u32[]{:S(2)}, u32[]{:S(2)}) async-start(bf16[4,128,384]{2,1,0:T(8,128)(2,1)} %broadcast_in_dim.14), calls=%async_computation.2 | async-start | bytes 786432 | tf_op jit(solution)/shard_map/dense_hidden/all_to_all | solution.py:18
  154.8 23.0 %collective-permute-start.19 = (bf16[36,3584]{1,0:T(8,128)(2,1)}, bf16[36,3584]{1,0:T(8,128)(2,1)}, u32[]{:S(2)}, u32[]{:S(2)}) collective-permute-start(bf16[36,3584]{1,0:T(8,128)(2,1)} %get-tuple-element.23), channel_id=1, source_target_pairs={{0,16},{8,24},{16,0},{24,8},{1,17},{9,25},{17,1},{25,9},{2,18},{10... | collective-permute-start | bytes 774152 | tf_op jit(solution)/shard_map/partials_z/ppermute | solution.py:14
  160.0 17.9 %collective-permute-start.18 = (bf16[36,3584]{1,0:T(8,128)(2,1)}, bf16[36,3584]{1,0:T(8,128)(2,1)}, u32[]{:S(2)}, u32[]{:S(2)}) collective-permute-start(bf16[36,3584]{1,0:T(8,128)(2,1)} %get-tuple-element.22), channel_id=1, source_target_pairs={{0,8},{8,16},{16,24},{24,0},{1,9},{9,17},{17,25},{25,1},{2,10},{10... | collective-permute-start | bytes 774152 | tf_op jit(solution)/shard_map/partials_z/ppermute | solution.py:14
  163.6 19.5 %collective-permute-start.14 = (bf16[36,3584]{1,0:T(8,128)(2,1)}, bf16[36,3584]{1,0:T(8,128)(2,1)}, u32[]{:S(2)}, u32[]{:S(2)}) collective-permute-start(bf16[36,3584]{1,0:T(8,128)(2,1)} %slice.116), channel_id=1, source_target_pairs={{0,24},{8,0},{16,8},{24,16},{1,25},{9,1},{17,9},{25,17},{2,26},{10... | collective-permute-start | bytes 774152 | tf_op jit(solution)/shard_map/partials_z/ppermute | solution.py:14
  172.6 19.3 %all-to-all-start.3 = ((bf16[8,256,224]{1,2,0:T(8,128)(2,1)}), bf16[8,256,224]{1,2,0:T(8,128)(2,1)S(1)}, u32[]{:S(2)}, u32[]{:S(2)}) async-start(bf16[8,256,224]{1,2,0:T(8,128)(2,1)} %copy.71), calls=%async_computation.3 | async-start | bytes 1835008 | tf_op jit(solution)/shard_map/dense_out/all_to_all | solution.py:18
  184.3 22.5 %copy-start.9 = (s32[1,128,2]{1,2,0:T(2,128)S(1)}, s32[1,128,2]{1,2,0:T(2,128)}, u32[]{:S(2)}) copy-start(s32[1,128,2]{1,2,0:T(2,128)} %param.12) | copy-start | bytes 3076
  184.3 22.5 %copy-start.10 = (f32[1,128,2]{1,2,0:T(2,128)S(1)}, f32[1,128,2]{1,2,0:T(2,128)}, u32[]{:S(2)}) copy-start(f32[1,128,2]{1,2,0:T(2,128)} %param.13) | copy-start | bytes 3076
  191.9 11.6 %all-to-all-start.5 = ((bf16[8,36,448]{2,1,0:T(8,128)(2,1)}), bf16[8,36,448]{2,1,0:T(8,128)(2,1)S(1)}, u32[]{:S(2)}, u32[]{:S(2)}) async-start(bf16[8,36,448]{2,1,0:T(8,128)(2,1)} %bitcast.60), calls=%async_computation.5 | async-start | bytes 655360 | tf_op jit(solution)/shard_map/combine/all_to_all | solution.py:18
  203.5 9.4 %all-to-all-start.4 = ((bf16[4,64,224]{2,1,0:T(8,128)(2,1)}), bf16[4,64,224]{2,1,0:T(8,128)(2,1)S(1)}, u32[]{:S(2)}, u32[]{:S(2)}) async-start(bf16[4,64,224]{2,1,0:T(8,128)(2,1)} %bitcast.19), calls=%async_computation.4 | async-start | bytes 262144 | tf_op jit(solution)/shard_map/dense_out/all_to_all | solution.py:18
  212.9 3.1 %collective-permute-start.2 = (bf16[2,64,224]{2,1,0:T(8,128)(2,1)S(1)}, bf16[2,64,224]{2,1,0:T(8,128)(2,1)S(1)}, u32[]{:S(2)}, u32[]{:S(2)}) collective-permute-start(bf16[2,64,224]{2,1,0:T(8,128)(2,1)S(1)} %constant_dynamic-slice_fusion), channel_id=1, source_target_pairs={{0,1},{1,0},{2,3},{3,2},{4,5},{5,4},{6,7},{7,6},{8,9},{9,8},{10,11... | collective-permute-start | bytes 172040 | tf_op jit(solution)/shard_map/dense_out/ppermute | solution.py:14
  216.5 17.2 %collective-permute-start.20 = (bf16[128,448]{0,1:T(8,128)(2,1)S(1)}, bf16[128,448]{0,1:T(8,128)(2,1)S(1)}, u32[]{:S(2)}, u32[]{:S(2)}) collective-permute-start(bf16[128,448]{0,1:T(8,128)(2,1)S(1)} %fusion.9), channel_id=1, source_target_pairs={{0,128},{128,256},{256,384},{384,0},{1,129},{129,257},{257,385},{3... | collective-permute-start | bytes 344072 | tf_op jit(solution)/shard_map/next_section/ppermute | solution.py:14
  (10 other events, 105.9 us)
Sparse Core Ops, SparseCore 0:
  24.6 50.4 all-gather.1

commit v3 on v2

--- a/solution.py
+++ b/solution.py
@@ -64,8 +64,9 @@
     piece = width // n_expert
 
     with jax.named_scope("dense_weights"):
-        stacked = jnp.concatenate([dense_gate[0], dense_up[0], dense_down[0]], axis=0)
+        stacked = jnp.concatenate([dense_gate[0], dense_up[0], dense_down[0]], axis=1)
         slabs = lax.all_gather(stacked, "y", axis=0, tiled=True)
+        picks = after(picks, stacked)
 
     with jax.named_scope("dispatch"):
         slot = slots_of(picks, n_expert)
@@ -80,36 +81,6 @@
         lines = [routed] + [shifted(routed, "z", by) for by in (1, 3, 2)]
         low = jnp.concatenate([lines[0], lines[1]], axis=0)
         high = jnp.concatenate([lines[2], lines[3]], axis=0)
-
-    gate_up = jnp.concatenate([expert_gate[0, 0], expert_up[0, 0]], axis=1)
-    down = expert_down[0, 0]
-    inner = down.shape[0]
-
-    def ffn(rows):
-        both = dot(rows, gate_up)
-        return dot(swiglu(both[:, :inner], both[:, inner:]), down)
-
-    half = 2 * capacity
-    with jax.named_scope("rows_y"):
-        prev_low, next_low = shifted(low, "y", 1), shifted(low, "y", -1)
-        far_low = shifted(prev_low, "y", 1)
-        next_high, prev_high = shifted(high, "y", -1), shifted(high, "y", 1)
-        far_high = shifted(next_high, "y", -1)
-    with jax.named_scope("experts"):
-        near_part = ffn(jnp.concatenate([prev_low, prev_high, next_low, next_high], axis=0))
-        far_part = ffn(jnp.concatenate([far_low, far_high], axis=0)).astype(BF16)
-        own_part = ffn(after(jnp.concatenate([low, high], axis=0), far_part))
-    prev_part, next_part = near_part[: 2 * half], near_part[2 * half :]
-    with jax.named_scope("partials_y"):
-        early_next = shifted(next_part[half:].astype(BF16), "y", 1)
-        early_prev = shifted(prev_part[:half].astype(BF16), "y", -1)
-        relay_next = shifted(far_part[:half], "y", 1)
-        relay_prev = shifted(far_part[half:], "y", -1)
-        late_next = shifted((next_part[:half] + relay_next.astype(F32)).astype(BF16), "y", 1)
-        late_prev = shifted((prev_part[half:] + relay_prev.astype(F32)).astype(BF16), "y", -1)
-        summed_low = own_part[:half] + late_next.astype(F32) + early_prev.astype(F32)
-        summed_high = own_part[half:] + early_next.astype(F32) + late_prev.astype(F32)
-        summed_low, summed_high = summed_low.astype(BF16), summed_high.astype(BF16)
 
     with jax.named_scope("dense_tokens"):
         half_tokens = tok_rows // 2
@@ -122,11 +93,47 @@
         first = jnp.where(core == 0, half_in, other_half)
         second = jnp.where(core == 0, other_half, half_in)
         line_tokens = jnp.concatenate([first, second], axis=1).reshape(4 * tok_rows, slab)
-    slabs = slabs.reshape(4, 3, step, hidden)
-    gate_slab, up_slab, down_slab = (slabs[:, i].reshape(slab, hidden) for i in range(3))
+        pre = dot(line_tokens, slabs[:, : 2 * hidden]).astype(BF16)
+        pre = pre.reshape(4, tok_rows, 2 * hidden)
+
+    gate_up = jnp.concatenate([expert_gate[0, 0], expert_up[0, 0]], axis=1)
+    down = expert_down[0, 0]
+    inner = down.shape[0]
+
+    def activate(rows):
+        both = dot(rows, gate_up)
+        return swiglu(both[:, :inner], both[:, inner:])
+
+    half = 2 * capacity
+    with jax.named_scope("rows_y"):
+        prev_low, next_low = shifted(low, "y", 1), shifted(low, "y", -1)
+        far_low = shifted(prev_low, "y", 1)
+        next_high, prev_high = shifted(high, "y", -1), shifted(high, "y", 1)
+        far_high = shifted(next_high, "y", -1)
+    with jax.named_scope("experts"):
+        far_act = activate(after(jnp.concatenate([far_low, far_high], axis=0), pre))
+        relay_next = dot(far_act[:half], down).astype(BF16)
+        relay_prev = dot(far_act[half:], down).astype(BF16)
+        near = jnp.concatenate([next_high, prev_low, next_low, prev_high], axis=0)
+        near_act = activate(after(near, relay_next, relay_prev))
+        early_next = dot(near_act[:half], down).astype(BF16)
+        early_prev = dot(near_act[half : 2 * half], down).astype(BF16)
+        own_low, own_high = after((low, high), early_next, early_prev)
+        own_low, own_high = activate(own_low), activate(own_high)
+    with jax.named_scope("partials_y"):
+        relay_next, relay_prev = shifted(relay_next, "y", 1), shifted(relay_prev, "y", -1)
+        early_next, early_prev = shifted(early_next, "y", 1), shifted(early_prev, "y", -1)
+        late_next = dot(near_act[2 * half : 3 * half], down) + relay_next.astype(F32)
+        late_prev = dot(near_act[3 * half :], down) + relay_prev.astype(F32)
+        late_next = shifted(late_next.astype(BF16), "y", 1)
+        late_prev = shifted(late_prev.astype(BF16), "y", -1)
+        total = [
+            dot(act[rows], down) + one[rows].astype(F32) + two[rows].astype(F32)
+            for act, one, two in ((own_low, late_next, early_prev), (own_high, early_next, late_prev))
+            for rows in (slice(0, capacity), slice(capacity, half))
+        ]
+
     with jax.named_scope("dense_hidden"):
-        pre = jnp.concatenate([dot(line_tokens, gate_slab), dot(line_tokens, up_slab)], axis=1)
-        pre = pre.astype(BF16).reshape(4, tok_rows, 2 * hidden)
         pre = exchanged(pre, "z")
         pre = jnp.sum(pre.astype(F32), axis=0)
         act = swiglu(pre[:, :hidden], pre[:, hidden:])
@@ -134,7 +141,9 @@
         line_act = line_act.reshape(4 * tok_rows, hidden)
     with jax.named_scope("dense_out"):
         contract = (((1,), (1,)), ((), ()))
-        dense_out = lax.dot_general(line_act, down_slab, contract, preferred_element_type=F32)
+        dense_out = lax.dot_general(
+            line_act, slabs[:, 2 * hidden :], contract, preferred_element_type=F32
+        )
         by_block = (
             dense_out.astype(BF16)
             .reshape(4, 2, half_tokens, 4, step)
@@ -152,12 +161,10 @@
     base = residual[0].astype(F32) + dense_total.reshape(tok_rows, piece).astype(F32)
 
     with jax.named_scope("partials_z"):
-        total = summed_low[:capacity].astype(F32)
-        for k, (part, by) in enumerate(
-            ((summed_low[capacity:], -1), (summed_high[:capacity], -3), (summed_high[capacity:], -2))
-        ):
-            total = total + shifted(part, "z", by).astype(F32)
-        expert_out = total.astype(BF16)
+        expert_out = total[0]
+        for part, by in zip(total[1:], (-1, -3, -2)):
+            expert_out = expert_out + shifted(part.astype(BF16), "z", by).astype(F32)
+        expert_out = expert_out.astype(BF16)
     with jax.named_scope("combine"):
         by_feature = expert_out.reshape(capacity, n_expert, piece).transpose(1, 0, 2)
         returned = exchanged(by_feature, EXPERT_AXES).reshape(n_expert * capacity, piece)

time: 244 us -> 245 us (level)
  the two profiles are of different devices: /device:TPU:24 before, /device:TPU:96 now
where the time goes in v3:
time: 245 us; the launch traced here: 243 us
  starting transfers between devices  109 us (44%)
  waiting for transfers between devices  72.3 us (30%)
  matrix products  24 us (10%)
  other arithmetic  14 us (6%)
  between operations  14 us (6%)
  local copies, waits for them, and re-layouts  9.69 us (4%)
    ppermute x21, starting transfers between devices, shifted(): return lax.ppermute(x, axis, [(i, (i + by) % peers) for i in range(peers)])  79.7 us
    ppermute x21, waiting for transfers between devices, shifted(): return lax.ppermute(x, axis, [(i, (i + by) % peers) for i in range(peers)])  54.6 us
    all_to_all x6, starting transfers between devices, exchanged(): return lax.all_to_all(x, axes, split_axis=0, concat_axis=0, tiled=True)  29.6 us
    dot_general x18, matrix products, dot(): return jnp.dot(a, b, preferred_element_type=F32)  22.1 us
    all_to_all x6, waiting for transfers between devices, exchanged(): return lax.all_to_all(x, axes, split_axis=0, concat_axis=0, tiled=True)  17.7 us
  transfers between devices with their start and end apart: 28, of which 13 were waited for; matrix products, arithmetic and copies ran while one was open for 15% of the time, Pallas kernels for 0%

profile of v3, /device:TPU:96, one launch (start us, length us, event | category | flops | bytes accessed | tf_op | source)
XLA Modules:
  0.0 243.4 jit_solution(2541914648045079948)
XLA Ops:
  11.4 6.5 %collective-permute-start = (bf16[36,3584]{1,0:T(8,128)(2,1)S(1)}, bf16[36,3584]{1,0:T(8,128)(2,1)}, u32[]{:S(2)}, u32[]{:S(2)}) collective-permute-start(bf16[36,3584]{1,0:T(8,128)(2,1)S(1)} %convolution_convert_fusion.4), channel_id=1, source_target_pairs={{0,8},{8,16},{16,24},{24,0},{1,9},{9,17},{17,25},{25,1},{2,10},{10... | collective-permute-start | bytes 774152 | tf_op jit(solution)/shard_map/rows_z/ppermute | solution.py:14
  19.8 2.5 %collective-permute-start.4 = (bf16[36,3584]{1,0:T(8,128)(2,1)S(1)}, bf16[36,3584]{1,0:T(8,128)(2,1)}, u32[]{:S(2)}, u32[]{:S(2)}) collective-permute-start(bf16[36,3584]{1,0:T(8,128)(2,1)S(1)} %convolution_convert_fusion.4), channel_id=1, source_target_pairs={{0,16},{8,24},{16,0},{24,8},{1,17},{9,25},{17,1},{25,9},{2,18},{10... | collective-permute-start | bytes 774152 | tf_op jit(solution)/shard_map/rows_z/ppermute | solution.py:14
  23.3 3.4 %collective-permute-done = bf16[36,3584]{1,0:T(8,128)(2,1)} collective-permute-done((bf16[36,3584]{1,0:T(8,128)(2,1)S(1)}, bf16[36,3584]{1,0:T(8,128)(2,1)}, u32[]{:S(2)}, u32[]{:S(2)}) %collective-permute-start) | collective-permute-done | bytes 258080 | tf_op jit(solution)/shard_map/rows_z/ppermute | solution.py:14
  27.8 6.3 %all-to-all-start = ((bf16[4,64,896]{2,1,0:T(8,128)(2,1)}), bf16[4,64,896]{2,1,0:T(8,128)(2,1)S(1)}, u32[]{:S(2)}, u32[]{:S(2)}) async-start(bf16[4,64,896]{2,1,0:T(8,128)(2,1)} %copy.68), calls=%async_computation | async-start | bytes 917504 | tf_op jit(solution)/shard_map/dense_tokens/all_to_all | solution.py:18
  35.2 8.6 %collective-permute-start.6 = (bf16[72,3584]{1,0:T(8,128)(2,1)S(1)}, bf16[72,3584]{1,0:T(8,128)(2,1)}, u32[]{:S(2)}, u32[]{:S(2)}) collective-permute-start(bf16[72,3584]{1,0:T(8,128)(2,1)S(1)} %pad_maximum_fusion.5), channel_id=1, source_target_pairs={{0,32},{32,64},{64,96},{96,0},{1,33},{33,65},{65,97},{97,1},{2,34}... | collective-permute-start | bytes 1548296 | tf_op jit(solution)/shard_map/rows_y/ppermute | solution.py:14
  47.2 4.1 %collective-permute-start.5 = (bf16[72,3584]{1,0:T(8,128)(2,1)S(1)}, bf16[72,3584]{1,0:T(8,128)(2,1)S(1)}, u32[]{:S(2)}, u32[]{:S(2)}) collective-permute-start(bf16[72,3584]{1,0:T(8,128)(2,1)S(1)} %pad_maximum_fusion.6), channel_id=1, source_target_pairs={{0,96},{32,0},{64,32},{96,64},{1,97},{33,1},{65,33},{97,65},{2,98}... | collective-permute-start | bytes 1548296 | tf_op jit(solution)/shard_map/rows_y/ppermute | solution.py:14
  51.4 2.7 %collective-permute-start.7 = (bf16[72,3584]{1,0:T(8,128)(2,1)S(1)}, bf16[72,3584]{1,0:T(8,128)(2,1)}, u32[]{:S(2)}, u32[]{:S(2)}) collective-permute-start(bf16[72,3584]{1,0:T(8,128)(2,1)S(1)} %pad_maximum_fusion.5), channel_id=1, source_target_pairs={{0,96},{32,0},{64,32},{96,64},{1,97},{33,1},{65,33},{97,65},{2,98}... | collective-permute-start | bytes 1548296 | tf_op jit(solution)/shard_map/rows_y/ppermute | solution.py:14
  54.0 3.2 %collective-permute-start.8 = (bf16[72,3584]{1,0:T(8,128)(2,1)S(1)}, bf16[72,3584]{1,0:T(8,128)(2,1)}, u32[]{:S(2)}, u32[]{:S(2)}) collective-permute-start(bf16[72,3584]{1,0:T(8,128)(2,1)S(1)} %pad_maximum_fusion.6), channel_id=1, source_target_pairs={{0,32},{32,64},{64,96},{96,0},{1,33},{33,65},{65,97},{97,1},{2,34}... | collective-permute-start | bytes 1548296 | tf_op jit(solution)/shard_map/rows_y/ppermute | solution.py:14
  57.2 7.5 %collective-permute-done.6 = bf16[72,3584]{1,0:T(8,128)(2,1)} collective-permute-done((bf16[72,3584]{1,0:T(8,128)(2,1)S(1)}, bf16[72,3584]{1,0:T(8,128)(2,1)}, u32[]{:S(2)}, u32[]{:S(2)}) %collective-permute-start.6) | collective-permute-done | bytes 516128 | tf_op jit(solution)/shard_map/rows_y/ppermute | solution.py:14
  67.0 4.8 %collective-permute-start.10 = (bf16[72,3584]{1,0:T(8,128)(2,1)S(1)}, bf16[72,3584]{1,0:T(8,128)(2,1)}, u32[]{:S(2)}, u32[]{:S(2)}) collective-permute-start(bf16[72,3584]{1,0:T(8,128)(2,1)S(1)} %collective-permute-done.5), channel_id=1, source_target_pairs={{0,96},{32,0},{64,32},{96,64},{1,97},{33,1},{65,33},{97,65},{2,98}... | collective-permute-start | bytes 1548296 | tf_op jit(solution)/shard_map/rows_y/ppermute | solution.py:14
  71.8 6.3 %collective-permute-done.7 = bf16[72,3584]{1,0:T(8,128)(2,1)} collective-permute-done((bf16[72,3584]{1,0:T(8,128)(2,1)S(1)}, bf16[72,3584]{1,0:T(8,128)(2,1)}, u32[]{:S(2)}, u32[]{:S(2)}) %collective-permute-start.7) | collective-permute-done | bytes 516128 | tf_op jit(solution)/shard_map/rows_y/ppermute | solution.py:14
  78.1 2.8 %pad_maximum_fusion.1 = bf16[288,3584]{1,0:T(8,128)(2,1)} fusion(bf16[72,3584]{1,0:T(8,128)(2,1)} %collective-permute-done.8, bf16[72,3584]{1,0:T(8,128)(2,1)} %collective-permute-done.7, bf16[72,3584]{1,0:T(8,128)(2,1)} %collective-permute-done.6, bf16[72,3584]{1,0:T(8,128)(2,1)S(1)} %collective-permute-done.5), kind=kLoop, calls=%fused_computation.6 | loop fusion | flops 8257536 | bytes 4128768 | tf_op jit(solution)/shard_map/experts/concatenate | solution.py:117
  84.4 3.7 %collective-permute-done.10 = bf16[72,3584]{1,0:T(8,128)(2,1)} collective-permute-done((bf16[72,3584]{1,0:T(8,128)(2,1)S(1)}, bf16[72,3584]{1,0:T(8,128)(2,1)}, u32[]{:S(2)}, u32[]{:S(2)}) %collective-permute-start.10) | collective-permute-done | bytes 516128 | tf_op jit(solution)/shard_map/rows_y/ppermute | solution.py:14
  90.5 3.5 %convolution_convert_fusion.6 = bf16[512,768]{1,0:T(8,128)(2,1)} fusion(bf16[512,896]{1,0:T(8,128)(2,1)} %bitcast.74, bf16[896,1152]{1,0:T(8,128)(2,1)} %all-gather.2.cloned.1.call-done), kind=kOutput, calls=%fused_computation.9 | convolution fusion | flops 705036288 | bytes 3080192 | tf_op jit(solution)/shard_map/dense_tokens/dot_general | solution.py:30
  94.0 5.1 %all-to-all-start.1 = ((bf16[4,128,768]{2,1,0:T(8,128)(2,1)}), bf16[4,128,768]{2,1,0:T(8,128)(2,1)S(1)}, u32[]{:S(2)}, u32[]{:S(2)}) async-start(bf16[4,128,768]{2,1,0:T(8,128)(2,1)} %bitcast.76), calls=%async_computation.1 | async-start | bytes 1572864 | tf_op jit(solution)/shard_map/dense_hidden/all_to_all | solution.py:18
  99.1 2.6 %fusion.63 = f32[144,304]{1,0:T(8,128)S(1)} fusion(bf16[144,3584]{1,0:T(8,128)(2,1)S(1)} %pad_maximum_fusion.2, bf16[3584,152]{0,1:T(8,128)(2,1)} %bitcast.87, bf16[3584,152]{0,1:T(8,128)(2,1)} %bitcast.91), kind=kOutput, calls=%fused_computation.88 | convolution fusion | flops 318144512 | bytes 3386368 | tf_op jit(solution)/shard_map/experts/dot_general | solution.py:30
  102.4 3.5 %collective-permute-start.11 = (bf16[72,3584]{1,0:T(8,128)(2,1)S(1)}, bf16[72,3584]{1,0:T(8,128)(2,1)S(1)}, u32[]{:S(2)}, u32[]{:S(2)}) collective-permute-start(bf16[72,3584]{1,0:T(8,128)(2,1)S(1)} %convolution_convert_fusion.3), channel_id=1, source_target_pairs={{0,32},{32,64},{64,96},{96,0},{1,33},{33,65},{65,97},{97,1},{2,34}... | collective-permute-start | bytes 1548296 | tf_op jit(solution)/shard_map/partials_y/ppermute | solution.py:14
  107.7 3.7 %collective-permute-start.13 = (bf16[72,3584]{1,0:T(8,128)(2,1)S(1)}, bf16[72,3584]{1,0:T(8,128)(2,1)}, u32[]{:S(2)}, u32[]{:S(2)}) collective-permute-start(bf16[72,3584]{1,0:T(8,128)(2,1)S(1)} %convolution_convert_fusion), channel_id=1, source_target_pairs={{0,96},{32,0},{64,32},{96,64},{1,97},{33,1},{65,33},{97,65},{2,98}... | collective-permute-start | bytes 1548296 | tf_op jit(solution)/shard_map/partials_y/ppermute | solution.py:14
  113.9 4.9 %collective-permute-start.16 = (bf16[72,3584]{1,0:T(8,128)(2,1)S(1)}, bf16[72,3584]{1,0:T(8,128)(2,1)S(1)}, u32[]{:S(2)}, u32[]{:S(2)}) collective-permute-start(bf16[72,3584]{1,0:T(8,128)(2,1)S(1)} %convolution_convert_fusion.2), channel_id=1, source_target_pairs={{0,96},{32,0},{64,32},{96,64},{1,97},{33,1},{65,33},{97,65},{2,98}... | collective-permute-start | bytes 1548296 | tf_op jit(solution)/shard_map/partials_y/ppermute | solution.py:14
  123.8 8.4 %collective-permute-done.16 = bf16[72,3584]{1,0:T(8,128)(2,1)S(1)} collective-permute-done((bf16[72,3584]{1,0:T(8,128)(2,1)S(1)}, bf16[72,3584]{1,0:T(8,128)(2,1)S(1)}, u32[]{:S(2)}, u32[]{:S(2)}) %collective-permute-start.16) | collective-permute-done | bytes 516128 | tf_op jit(solution)/shard_map/partials_y/ppermute | solution.py:14
  133.3 5.2 %collective-permute-start.17 = (bf16[72,3584]{1,0:T(8,128)(2,1)}, bf16[72,3584]{1,0:T(8,128)(2,1)}, u32[]{:S(2)}, u32[]{:S(2)}) collective-permute-start(bf16[72,3584]{1,0:T(8,128)(2,1)} %add_convert_fusion), channel_id=1, source_target_pairs={{0,96},{32,0},{64,32},{96,64},{1,97},{33,1},{65,33},{97,65},{2,98}... | collective-permute-start | bytes 1548296 | tf_op jit(solution)/shard_map/partials_y/ppermute | solution.py:14
  139.4 5.1 %all-to-all-start.2 = ((bf16[4,128,384]{2,1,0:T(8,128)(2,1)}), bf16[4,128,384]{2,1,0:T(8,128)(2,1)S(1)}, u32[]{:S(2)}, u32[]{:S(2)}) async-start(bf16[4,128,384]{2,1,0:T(8,128)(2,1)} %broadcast_in_dim.14), calls=%async_computation.2 | async-start | bytes 786432 | tf_op jit(solution)/shard_map/dense_hidden/all_to_all | solution.py:18
  153.7 5.2 %collective-permute-start.18 = (bf16[36,3584]{1,0:T(8,128)(2,1)}, bf16[36,3584]{1,0:T(8,128)(2,1)}, u32[]{:S(2)}, u32[]{:S(2)}) collective-permute-start(bf16[36,3584]{1,0:T(8,128)(2,1)} %add_convert_fusion.4), channel_id=1, source_target_pairs={{0,8},{8,16},{16,24},{24,0},{1,9},{9,17},{17,25},{25,1},{2,10},{10... | collective-permute-start | bytes 774152 | tf_op jit(solution)/shard_map/partials_z/ppermute | solution.py:14
  167.9 4.0 %all-to-all-start.3 = ((bf16[8,256,224]{1,2,0:T(8,128)(2,1)}), bf16[8,256,224]{1,2,0:T(8,128)(2,1)S(1)}, u32[]{:S(2)}, u32[]{:S(2)}) async-start(bf16[8,256,224]{1,2,0:T(8,128)(2,1)} %copy.70), calls=%async_computation.3 | async-start | bytes 1835008 | tf_op jit(solution)/shard_map/dense_out/all_to_all | solution.py:18
  171.9 4.8 %collective-permute-done.19 = bf16[36,3584]{1,0:T(8,128)(2,1)} collective-permute-done((bf16[36,3584]{1,0:T(8,128)(2,1)}, bf16[36,3584]{1,0:T(8,128)(2,1)}, u32[]{:S(2)}, u32[]{:S(2)}) %collective-permute-start.19) | collective-permute-done | bytes 258080 | tf_op jit(solution)/shard_map/partials_z/ppermute | solution.py:14
  179.3 7.1 %all-to-all-done.3 = bf16[8,256,224]{1,2,0:T(8,128)(2,1)S(1)} async-done(((bf16[8,256,224]{1,2,0:T(8,128)(2,1)}), bf16[8,256,224]{1,2,0:T(8,128)(2,1)S(1)}, u32[]{:S(2)}, u32[]{:S(2)}) %all-to-all-start.3) | async-done | bytes 917536 | tf_op jit(solution)/shard_map/dense_out/all_to_all | solution.py:18
  186.4 3.4 %all-to-all-start.5 = ((bf16[8,36,448]{2,1,0:T(8,128)(2,1)}), bf16[8,36,448]{2,1,0:T(8,128)(2,1)S(1)}, u32[]{:S(2)}, u32[]{:S(2)}) async-start(bf16[8,36,448]{2,1,0:T(8,128)(2,1)} %bitcast.70), calls=%async_computation.5 | async-start | bytes 655360 | tf_op jit(solution)/shard_map/combine/all_to_all | solution.py:18
  190.7 7.3 %all-to-all-done.5 = bf16[8,36,448]{2,1,0:T(8,128)(2,1)S(1)} async-done(((bf16[8,36,448]{2,1,0:T(8,128)(2,1)}), bf16[8,36,448]{2,1,0:T(8,128)(2,1)S(1)}, u32[]{:S(2)}, u32[]{:S(2)}) %all-to-all-start.5) | async-done | bytes 258080 | tf_op jit(solution)/shard_map/combine/all_to_all | solution.py:18
  198.0 5.6 %all-to-all-start.4 = ((bf16[4,64,224]{2,1,0:T(8,128)(2,1)}), bf16[4,64,224]{2,1,0:T(8,128)(2,1)S(1)}, u32[]{:S(2)}, u32[]{:S(2)}) async-start(bf16[4,64,224]{2,1,0:T(8,128)(2,1)} %bitcast.14), calls=%async_computation.4 | async-start | bytes 262144 | tf_op jit(solution)/shard_map/dense_out/all_to_all | solution.py:18
  203.8 3.4 %all-to-all-done.4 = bf16[4,64,224]{2,1,0:T(8,128)(2,1)S(1)} async-done(((bf16[4,64,224]{2,1,0:T(8,128)(2,1)}), bf16[4,64,224]{2,1,0:T(8,128)(2,1)S(1)}, u32[]{:S(2)}, u32[]{:S(2)}) %all-to-all-start.4) | async-done | bytes 114720 | tf_op jit(solution)/shard_map/dense_out/all_to_all | solution.py:18
  210.8 8.6 %collective-permute-start.20 = (bf16[128,448]{0,1:T(8,128)(2,1)S(1)}, bf16[128,448]{0,1:T(8,128)(2,1)S(1)}, u32[]{:S(2)}, u32[]{:S(2)}) collective-permute-start(bf16[128,448]{0,1:T(8,128)(2,1)S(1)} %fusion.2), channel_id=1, source_target_pairs={{0,128},{128,256},{256,384},{384,0},{1,129},{129,257},{257,385},{3... | collective-permute-start | bytes 344072 | tf_op jit(solution)/shard_map/next_section/ppermute | solution.py:14
  219.4 16.5 %collective-permute-done.20 = bf16[128,448]{0,1:T(8,128)(2,1)S(1)} collective-permute-done((bf16[128,448]{0,1:T(8,128)(2,1)S(1)}, bf16[128,448]{0,1:T(8,128)(2,1)S(1)}, u32[]{:S(2)}, u32[]{:S(2)}) %collective-permute-start.20) | collective-permute-done | bytes 114720 | tf_op jit(solution)/shard_map/next_section/ppermute | solution.py:14
  (112 shorter events, 59.3 us)
Async XLA Ops:
  6.5 95.3 %copy-start = (bf16[1,1,152,3584]{3,2,1,0:T(8,128)(2,1)S(1)}, bf16[1,1,152,3584]{3,2,1,0:T(8,128)(2,1)}, u32[]{:S(2)}) copy-start(bf16[1,1,152,3584]{3,2,1,0:T(8,128)(2,1)} %param.19) | copy-start | bytes 3268612
  6.5 83.9 %all-gather.2.cloned.1.call-start = ((), (), s32[]{:S(2)}) async-start(), calls=%async_computation.6 | async-start | bytes 2580480 | tf_op jit(solution)/shard_map/dense_weights/all_gather | solution.py:68
  11.4 15.3 %collective-permute-start = (bf16[36,3584]{1,0:T(8,128)(2,1)S(1)}, bf16[36,3584]{1,0:T(8,128)(2,1)}, u32[]{:S(2)}, u32[]{:S(2)}) collective-permute-start(bf16[36,3584]{1,0:T(8,128)(2,1)S(1)} %convolution_convert_fusion.4), channel_id=1, source_target_pairs={{0,8},{8,16},{16,24},{24,0},{1,9},{9,17},{17,25},{25,1},{2,10},{10... | collective-permute-start | bytes 774152 | tf_op jit(solution)/shard_map/rows_z/ppermute | solution.py:14
  17.9 25.9 %collective-permute-start.3 = (bf16[36,3584]{1,0:T(8,128)(2,1)S(1)}, bf16[36,3584]{1,0:T(8,128)(2,1)S(1)}, u32[]{:S(2)}, u32[]{:S(2)}) collective-permute-start(bf16[36,3584]{1,0:T(8,128)(2,1)S(1)} %convolution_convert_fusion.4), channel_id=1, source_target_pairs={{0,24},{8,0},{16,8},{24,16},{1,25},{9,1},{17,9},{25,17},{2,26},{10... | collective-permute-start | bytes 774152 | tf_op jit(solution)/shard_map/rows_z/ppermute | solution.py:14
  19.8 26.3 %collective-permute-start.4 = (bf16[36,3584]{1,0:T(8,128)(2,1)S(1)}, bf16[36,3584]{1,0:T(8,128)(2,1)}, u32[]{:S(2)}, u32[]{:S(2)}) collective-permute-start(bf16[36,3584]{1,0:T(8,128)(2,1)S(1)} %convolution_convert_fusion.4), channel_id=1, source_target_pairs={{0,16},{8,24},{16,0},{24,8},{1,17},{9,25},{17,1},{25,9},{2,18},{10... | collective-permute-start | bytes 774152 | tf_op jit(solution)/shard_map/rows_z/ppermute | solution.py:14
  27.8 53.2 %all-to-all-start = ((bf16[4,64,896]{2,1,0:T(8,128)(2,1)}), bf16[4,64,896]{2,1,0:T(8,128)(2,1)S(1)}, u32[]{:S(2)}, u32[]{:S(2)}) async-start(bf16[4,64,896]{2,1,0:T(8,128)(2,1)} %copy.68), calls=%async_computation | async-start | bytes 917504 | tf_op jit(solution)/shard_map/dense_tokens/all_to_all | solution.py:18
  35.2 45.8 %copy-start.4 = (bf16[72,3584]{1,0:T(8,128)(2,1)}, bf16[72,3584]{1,0:T(8,128)(2,1)S(1)}, u32[]{:S(2)}) copy-start(bf16[72,3584]{1,0:T(8,128)(2,1)S(1)} %pad_maximum_fusion.5) | copy-start | bytes 1548292
  35.2 29.5 %collective-permute-start.6 = (bf16[72,3584]{1,0:T(8,128)(2,1)S(1)}, bf16[72,3584]{1,0:T(8,128)(2,1)}, u32[]{:S(2)}, u32[]{:S(2)}) collective-permute-start(bf16[72,3584]{1,0:T(8,128)(2,1)S(1)} %pad_maximum_fusion.5), channel_id=1, source_target_pairs={{0,32},{32,64},{64,96},{96,0},{1,33},{33,65},{65,97},{97,1},{2,34}... | collective-permute-start | bytes 1548296 | tf_op jit(solution)/shard_map/rows_y/ppermute | solution.py:14
  47.2 19.8 %collective-permute-start.5 = (bf16[72,3584]{1,0:T(8,128)(2,1)S(1)}, bf16[72,3584]{1,0:T(8,128)(2,1)S(1)}, u32[]{:S(2)}, u32[]{:S(2)}) collective-permute-start(bf16[72,3584]{1,0:T(8,128)(2,1)S(1)} %pad_maximum_fusion.6), channel_id=1, source_target_pairs={{0,96},{32,0},{64,32},{96,64},{1,97},{33,1},{65,33},{97,65},{2,98}... | collective-permute-start | bytes 1548296 | tf_op jit(solution)/shard_map/rows_y/ppermute | solution.py:14
  51.4 26.8 %collective-permute-start.7 = (bf16[72,3584]{1,0:T(8,128)(2,1)S(1)}, bf16[72,3584]{1,0:T(8,128)(2,1)}, u32[]{:S(2)}, u32[]{:S(2)}) collective-permute-start(bf16[72,3584]{1,0:T(8,128)(2,1)S(1)} %pad_maximum_fusion.5), channel_id=1, source_target_pairs={{0,96},{32,0},{64,32},{96,64},{1,97},{33,1},{65,33},{97,65},{2,98}... | collective-permute-start | bytes 1548296 | tf_op jit(solution)/shard_map/rows_y/ppermute | solution.py:14
  54.0 24.1 %collective-permute-start.8 = (bf16[72,3584]{1,0:T(8,128)(2,1)S(1)}, bf16[72,3584]{1,0:T(8,128)(2,1)}, u32[]{:S(2)}, u32[]{:S(2)}) collective-permute-start(bf16[72,3584]{1,0:T(8,128)(2,1)S(1)} %pad_maximum_fusion.6), channel_id=1, source_target_pairs={{0,32},{32,64},{64,96},{96,0},{1,33},{33,65},{65,97},{97,1},{2,34}... | collective-permute-start | bytes 1548296 | tf_op jit(solution)/shard_map/rows_y/ppermute | solution.py:14
  64.7 19.6 %collective-permute-start.9 = (bf16[72,3584]{1,0:T(8,128)(2,1)}, bf16[72,3584]{1,0:T(8,128)(2,1)}, u32[]{:S(2)}, u32[]{:S(2)}) collective-permute-start(bf16[72,3584]{1,0:T(8,128)(2,1)} %collective-permute-done.6), channel_id=1, source_target_pairs={{0,32},{32,64},{64,96},{96,0},{1,33},{33,65},{65,97},{97,1},{2,34}... | collective-permute-start | bytes 1548296 | tf_op jit(solution)/shard_map/rows_y/ppermute | solution.py:14
  67.0 21.1 %collective-permute-start.10 = (bf16[72,3584]{1,0:T(8,128)(2,1)S(1)}, bf16[72,3584]{1,0:T(8,128)(2,1)}, u32[]{:S(2)}, u32[]{:S(2)}) collective-permute-start(bf16[72,3584]{1,0:T(8,128)(2,1)S(1)} %collective-permute-done.5), channel_id=1, source_target_pairs={{0,96},{32,0},{64,32},{96,64},{1,97},{33,1},{65,33},{97,65},{2,98}... | collective-permute-start | bytes 1548296 | tf_op jit(solution)/shard_map/rows_y/ppermute | solution.py:14
  81.0 8.4 %collective-permute-start.1 = (bf16[4,64,896]{2,1,0:T(8,128)(2,1)S(1)}, bf16[4,64,896]{2,1,0:T(8,128)(2,1)S(1)}, u32[]{:S(2)}, u32[]{:S(2)}) collective-permute-start(bf16[4,64,896]{2,1,0:T(8,128)(2,1)S(1)} %all-to-all-done), channel_id=1, source_target_pairs={{0,1},{1,0},{2,3},{3,2},{4,5},{5,4},{6,7},{7,6},{8,9},{9,8},{10,11... | collective-permute-start | bytes 1376264 | tf_op jit(solution)/shard_map/dense_tokens/ppermute | solution.py:14
  94.0 44.5 %all-to-all-start.1 = ((bf16[4,128,768]{2,1,0:T(8,128)(2,1)}), bf16[4,128,768]{2,1,0:T(8,128)(2,1)S(1)}, u32[]{:S(2)}, u32[]{:S(2)}) async-start(bf16[4,128,768]{2,1,0:T(8,128)(2,1)} %bitcast.76), calls=%async_computation.1 | async-start | bytes 1572864 | tf_op jit(solution)/shard_map/dense_hidden/all_to_all | solution.py:18
  102.4 18.3 %collective-permute-start.11 = (bf16[72,3584]{1,0:T(8,128)(2,1)S(1)}, bf16[72,3584]{1,0:T(8,128)(2,1)S(1)}, u32[]{:S(2)}, u32[]{:S(2)}) collective-permute-start(bf16[72,3584]{1,0:T(8,128)(2,1)S(1)} %convolution_convert_fusion.3), channel_id=1, source_target_pairs={{0,32},{32,64},{64,96},{96,0},{1,33},{33,65},{65,97},{97,1},{2,34}... | collective-permute-start | bytes 1548296 | tf_op jit(solution)/shard_map/partials_y/ppermute | solution.py:14
  107.7 39.3 %collective-permute-start.13 = (bf16[72,3584]{1,0:T(8,128)(2,1)S(1)}, bf16[72,3584]{1,0:T(8,128)(2,1)}, u32[]{:S(2)}, u32[]{:S(2)}) collective-permute-start(bf16[72,3584]{1,0:T(8,128)(2,1)S(1)} %convolution_convert_fusion), channel_id=1, source_target_pairs={{0,96},{32,0},{64,32},{96,64},{1,97},{33,1},{65,33},{97,65},{2,98}... | collective-permute-start | bytes 1548296 | tf_op jit(solution)/shard_map/partials_y/ppermute | solution.py:14
  111.7 39.9 %collective-permute-start.15 = (bf16[72,3584]{1,0:T(8,128)(2,1)S(1)}, bf16[72,3584]{1,0:T(8,128)(2,1)}, u32[]{:S(2)}, u32[]{:S(2)}) collective-permute-start(bf16[72,3584]{1,0:T(8,128)(2,1)S(1)} %convolution_convert_fusion.1), channel_id=1, source_target_pairs={{0,32},{32,64},{64,96},{96,0},{1,33},{33,65},{65,97},{97,1},{2,34}... | collective-permute-start | bytes 1548296 | tf_op jit(solution)/shard_map/partials_y/ppermute | solution.py:14
  113.9 18.3 %collective-permute-start.16 = (bf16[72,3584]{1,0:T(8,128)(2,1)S(1)}, bf16[72,3584]{1,0:T(8,128)(2,1)S(1)}, u32[]{:S(2)}, u32[]{:S(2)}) collective-permute-start(bf16[72,3584]{1,0:T(8,128)(2,1)S(1)} %convolution_convert_fusion.2), channel_id=1, source_target_pairs={{0,96},{32,0},{64,32},{96,64},{1,97},{33,1},{65,33},{97,65},{2,98}... | collective-permute-start | bytes 1548296 | tf_op jit(solution)/shard_map/partials_y/ppermute | solution.py:14
  121.9 25.2 %collective-permute-start.12 = (bf16[72,3584]{1,0:T(8,128)(2,1)}, bf16[72,3584]{1,0:T(8,128)(2,1)}, u32[]{:S(2)}, u32[]{:S(2)}) collective-permute-start(bf16[72,3584]{1,0:T(8,128)(2,1)} %add_convert_fusion.1), channel_id=1, source_target_pairs={{0,32},{32,64},{64,96},{96,0},{1,33},{33,65},{65,97},{97,1},{2,34}... | collective-permute-start | bytes 1548296 | tf_op jit(solution)/shard_map/partials_y/ppermute | solution.py:14
  133.3 18.3 %collective-permute-start.17 = (bf16[72,3584]{1,0:T(8,128)(2,1)}, bf16[72,3584]{1,0:T(8,128)(2,1)}, u32[]{:S(2)}, u32[]{:S(2)}) collective-permute-start(bf16[72,3584]{1,0:T(8,128)(2,1)} %add_convert_fusion), channel_id=1, source_target_pairs={{0,96},{32,0},{64,32},{96,64},{1,97},{33,1},{65,33},{97,65},{2,98}... | collective-permute-start | bytes 1548296 | tf_op jit(solution)/shard_map/partials_y/ppermute | solution.py:14
  139.4 23.4 %all-to-all-start.2 = ((bf16[4,128,384]{2,1,0:T(8,128)(2,1)}), bf16[4,128,384]{2,1,0:T(8,128)(2,1)S(1)}, u32[]{:S(2)}, u32[]{:S(2)}) async-start(bf16[4,128,384]{2,1,0:T(8,128)(2,1)} %broadcast_in_dim.14), calls=%async_computation.2 | async-start | bytes 786432 | tf_op jit(solution)/shard_map/dense_hidden/all_to_all | solution.py:18
  149.1 22.7 %collective-permute-start.14 = (bf16[36,3584]{1,0:T(8,128)(2,1)}, bf16[36,3584]{1,0:T(8,128)(2,1)S(1)}, u32[]{:S(2)}, u32[]{:S(2)}) collective-permute-start(bf16[36,3584]{1,0:T(8,128)(2,1)} %add_convert_fusion.5), channel_id=1, source_target_pairs={{0,24},{8,0},{16,8},{24,16},{1,25},{9,1},{17,9},{25,17},{2,26},{10... | collective-permute-start | bytes 774152 | tf_op jit(solution)/shard_map/partials_z/ppermute | solution.py:14
  153.7 18.2 %collective-permute-start.18 = (bf16[36,3584]{1,0:T(8,128)(2,1)}, bf16[36,3584]{1,0:T(8,128)(2,1)}, u32[]{:S(2)}, u32[]{:S(2)}) collective-permute-start(bf16[36,3584]{1,0:T(8,128)(2,1)} %add_convert_fusion.4), channel_id=1, source_target_pairs={{0,8},{8,16},{16,24},{24,0},{1,9},{9,17},{17,25},{25,1},{2,10},{10... | collective-permute-start | bytes 774152 | tf_op jit(solution)/shard_map/partials_z/ppermute | solution.py:14
  160.9 15.8 %collective-permute-start.19 = (bf16[36,3584]{1,0:T(8,128)(2,1)}, bf16[36,3584]{1,0:T(8,128)(2,1)}, u32[]{:S(2)}, u32[]{:S(2)}) collective-permute-start(bf16[36,3584]{1,0:T(8,128)(2,1)} %add_convert_fusion.3), channel_id=1, source_target_pairs={{0,16},{8,24},{16,0},{24,8},{1,17},{9,25},{17,1},{25,9},{2,18},{10... | collective-permute-start | bytes 774152 | tf_op jit(solution)/shard_map/partials_z/ppermute | solution.py:14
  167.9 18.5 %all-to-all-start.3 = ((bf16[8,256,224]{1,2,0:T(8,128)(2,1)}), bf16[8,256,224]{1,2,0:T(8,128)(2,1)S(1)}, u32[]{:S(2)}, u32[]{:S(2)}) async-start(bf16[8,256,224]{1,2,0:T(8,128)(2,1)} %copy.70), calls=%async_computation.3 | async-start | bytes 1835008 | tf_op jit(solution)/shard_map/dense_out/all_to_all | solution.py:18
  178.1 25.5 %copy-start.9 = (s32[1,128,2]{1,2,0:T(2,128)S(1)}, s32[1,128,2]{1,2,0:T(2,128)}, u32[]{:S(2)}) copy-start(s32[1,128,2]{1,2,0:T(2,128)} %param.12) | copy-start | bytes 3076
  178.1 25.5 %copy-start.10 = (f32[1,128,2]{1,2,0:T(2,128)S(1)}, f32[1,128,2]{1,2,0:T(2,128)}, u32[]{:S(2)}) copy-start(f32[1,128,2]{1,2,0:T(2,128)} %param.13) | copy-start | bytes 3076
  186.4 11.6 %all-to-all-start.5 = ((bf16[8,36,448]{2,1,0:T(8,128)(2,1)}), bf16[8,36,448]{2,1,0:T(8,128)(2,1)S(1)}, u32[]{:S(2)}, u32[]{:S(2)}) async-start(bf16[8,36,448]{2,1,0:T(8,128)(2,1)} %bitcast.70), calls=%async_computation.5 | async-start | bytes 655360 | tf_op jit(solution)/shard_map/combine/all_to_all | solution.py:18
  198.0 9.1 %all-to-all-start.4 = ((bf16[4,64,224]{2,1,0:T(8,128)(2,1)}), bf16[4,64,224]{2,1,0:T(8,128)(2,1)S(1)}, u32[]{:S(2)}, u32[]{:S(2)}) async-start(bf16[4,64,224]{2,1,0:T(8,128)(2,1)} %bitcast.14), calls=%async_computation.4 | async-start | bytes 262144 | tf_op jit(solution)/shard_map/dense_out/all_to_all | solution.py:18
  207.2 3.1 %collective-permute-start.2 = (bf16[2,64,224]{2,1,0:T(8,128)(2,1)S(1)}, bf16[2,64,224]{2,1,0:T(8,128)(2,1)S(1)}, u32[]{:S(2)}, u32[]{:S(2)}) collective-permute-start(bf16[2,64,224]{2,1,0:T(8,128)(2,1)S(1)} %constant_dynamic-slice_fusion), channel_id=1, source_target_pairs={{0,1},{1,0},{2,3},{3,2},{4,5},{5,4},{6,7},{7,6},{8,9},{9,8},{10,11... | collective-permute-start | bytes 172040 | tf_op jit(solution)/shard_map/dense_out/ppermute | solution.py:14
  210.8 25.2 %collective-permute-start.20 = (bf16[128,448]{0,1:T(8,128)(2,1)S(1)}, bf16[128,448]{0,1:T(8,128)(2,1)S(1)}, u32[]{:S(2)}, u32[]{:S(2)}) collective-permute-start(bf16[128,448]{0,1:T(8,128)(2,1)S(1)} %fusion.2), channel_id=1, source_target_pairs={{0,128},{128,256},{256,384},{384,0},{1,129},{129,257},{257,385},{3... | collective-permute-start | bytes 344072 | tf_op jit(solution)/shard_map/next_section/ppermute | solution.py:14
  (9 other events, 63.7 us)
Sparse Core Ops, SparseCore 0:
  18.0 45.7 all-gather.1

commit v4 on v3

--- a/solution.py
+++ b/solution.py
@@ -88,7 +88,7 @@
             tokens.reshape(tok_rows, 4, 4, step).transpose(2, 0, 1, 3).reshape(4, tok_rows, slab)
         )
         own_half = lax.dynamic_slice_in_dim(by_line, core * half_tokens, half_tokens, axis=1)
-        half_in = exchanged(after(own_half, lines[1]), "z")
+        half_in = exchanged(after(own_half, lines[1], lines[2]), "z")
         other_half = shifted(half_in, "core", 1)
         first = jnp.where(core == 0, half_in, other_half)
         second = jnp.where(core == 0, other_half, half_in)
@@ -111,20 +111,20 @@
         next_high, prev_high = shifted(high, "y", -1), shifted(high, "y", 1)
         far_high = shifted(next_high, "y", -1)
     with jax.named_scope("experts"):
-        far_act = activate(after(jnp.concatenate([far_low, far_high], axis=0), pre))
-        relay_next = dot(far_act[:half], down).astype(BF16)
-        relay_prev = dot(far_act[half:], down).astype(BF16)
-        near = jnp.concatenate([next_high, prev_low, next_low, prev_high], axis=0)
-        near_act = activate(after(near, relay_next, relay_prev))
-        early_next = dot(near_act[:half], down).astype(BF16)
-        early_prev = dot(near_act[half : 2 * half], down).astype(BF16)
-        own_low, own_high = after((low, high), early_next, early_prev)
+        next_high, prev_low = after((next_high, prev_low), pre)
+        early_next = dot(activate(next_high), down).astype(BF16)
+        early_prev = dot(activate(prev_low), down).astype(BF16)
+        next_act, prev_act = activate(next_low), activate(prev_high)
+        far_low, far_high = after((far_low, far_high), early_next, early_prev)
+        relay_next = dot(activate(far_low), down).astype(BF16)
+        relay_prev = dot(activate(far_high), down).astype(BF16)
+        own_low, own_high = after((low, high), relay_next, relay_prev)
         own_low, own_high = activate(own_low), activate(own_high)
     with jax.named_scope("partials_y"):
         relay_next, relay_prev = shifted(relay_next, "y", 1), shifted(relay_prev, "y", -1)
         early_next, early_prev = shifted(early_next, "y", 1), shifted(early_prev, "y", -1)
-        late_next = dot(near_act[2 * half : 3 * half], down) + relay_next.astype(F32)
-        late_prev = dot(near_act[3 * half :], down) + relay_prev.astype(F32)
+        late_next = dot(next_act, down) + relay_next.astype(F32)
+        late_prev = dot(prev_act, down) + relay_prev.astype(F32)
         late_next = shifted(late_next.astype(BF16), "y", 1)
         late_prev = shifted(late_prev.astype(BF16), "y", -1)
         total = [

time: 245 us -> 234 us (0.955)
  matrix products: 24 us -> 33.5 us
  starting transfers between devices: 109 us -> 101 us
  other arithmetic: 14 us -> 6.71 us
  waiting for transfers between devices: 72.3 us -> 68.3 us
    dot_general x18 -> x22, matrix products: 22.1 us -> 31.7 us  [dot(): return jnp.dot(a, b, preferred_element_type=F32)]
    ppermute x21, starting transfers between devices: 79.7 us -> 72.1 us  [shifted(): return lax.ppermute(x, axis, [(i, (i + by) % peers) for i in range(peers)])]
    concatenate x2 -> x0, other arithmetic: 4.09 us -> none  [the longest x1 2.83 us: body(): near = jnp.concatenate([next_high, prev_low, next_low, prev_high], axis=0)]
  transfers between devices with their start and end apart: 28 -> 28, of which waited for: 13 -> 15; matrix products, arithmetic and copies ran while one was open for 15% -> 19% of each run, Pallas kernels for 0% -> 0%
where the time goes in v4:
time: 234 us; the launch traced here: 232 us
  starting transfers between devices  101 us (43%)
  waiting for transfers between devices  68.3 us (29%)
  matrix products  33.5 us (14%)
  between operations  14.1 us (6%)
  local copies, waits for them, and re-layouts  9.1 us (4%)
  other arithmetic  6.71 us (3%)
    ppermute x21, starting transfers between devices, shifted(): return lax.ppermute(x, axis, [(i, (i + by) % peers) for i in range(peers)])  72.1 us
    ppermute x21, waiting for transfers between devices, shifted(): return lax.ppermute(x, axis, [(i, (i + by) % peers) for i in range(peers)])  52.3 us
    dot_general x22, matrix products, dot(): return jnp.dot(a, b, preferred_element_type=F32)  31.7 us
    all_to_all x6, starting transfers between devices, exchanged(): return lax.all_to_all(x, axes, split_axis=0, concat_axis=0, tiled=True)  28.6 us
    all_to_all x6, waiting for transfers between devices, exchanged(): return lax.all_to_all(x, axes, split_axis=0, concat_axis=0, tiled=True)  15.9 us
  transfers between devices with their start and end apart: 28, of which 15 were waited for; matrix products, arithmetic and copies ran while one was open for 19% of the time, Pallas kernels for 0%

profile of v4, /device:TPU:96, one launch (start us, length us, event | category | flops | bytes accessed | tf_op | source)
XLA Modules:
  0.0 232.4 jit_solution(8764042390846151233)
XLA Ops:
  9.4 6.5 %collective-permute-start = (bf16[36,3584]{1,0:T(8,128)(2,1)S(1)}, bf16[36,3584]{1,0:T(8,128)(2,1)S(1)}, u32[]{:S(2)}, u32[]{:S(2)}) collective-permute-start(bf16[36,3584]{1,0:T(8,128)(2,1)S(1)} %convolution_convert_fusion.4), channel_id=1, source_target_pairs={{0,8},{8,16},{16,24},{24,0},{1,9},{9,17},{17,25},{25,1},{2,10},{10... | collective-permute-start | bytes 774152 | tf_op jit(solution)/shard_map/rows_z/ppermute | solution.py:14
  17.8 2.5 %collective-permute-start.4 = (bf16[36,3584]{1,0:T(8,128)(2,1)S(1)}, bf16[36,3584]{1,0:T(8,128)(2,1)}, u32[]{:S(2)}, u32[]{:S(2)}) collective-permute-start(bf16[36,3584]{1,0:T(8,128)(2,1)S(1)} %convolution_convert_fusion.4), channel_id=1, source_target_pairs={{0,16},{8,24},{16,0},{24,8},{1,17},{9,25},{17,1},{25,9},{2,18},{10... | collective-permute-start | bytes 774152 | tf_op jit(solution)/shard_map/rows_z/ppermute | solution.py:14
  21.3 3.3 %collective-permute-done = bf16[36,3584]{1,0:T(8,128)(2,1)S(1)} collective-permute-done((bf16[36,3584]{1,0:T(8,128)(2,1)S(1)}, bf16[36,3584]{1,0:T(8,128)(2,1)S(1)}, u32[]{:S(2)}, u32[]{:S(2)}) %collective-permute-start) | collective-permute-done | bytes 258080 | tf_op jit(solution)/shard_map/rows_z/ppermute | solution.py:14
  24.6 5.3 %collective-permute-done.1 = bf16[36,3584]{1,0:T(8,128)(2,1)} collective-permute-done((bf16[36,3584]{1,0:T(8,128)(2,1)S(1)}, bf16[36,3584]{1,0:T(8,128)(2,1)}, u32[]{:S(2)}, u32[]{:S(2)}) %collective-permute-start.1) | collective-permute-done | bytes 258080 | tf_op jit(solution)/shard_map/rows_z/ppermute | solution.py:14
  31.0 5.1 %all-to-all-start = ((bf16[4,64,896]{2,1,0:T(8,128)(2,1)}), bf16[4,64,896]{2,1,0:T(8,128)(2,1)S(1)}, u32[]{:S(2)}, u32[]{:S(2)}) async-start(bf16[4,64,896]{2,1,0:T(8,128)(2,1)} %copy.68), calls=%async_computation | async-start | bytes 917504 | tf_op jit(solution)/shard_map/dense_tokens/all_to_all | solution.py:18
  36.1 8.1 %collective-permute-done.4 = bf16[36,3584]{1,0:T(8,128)(2,1)} collective-permute-done((bf16[36,3584]{1,0:T(8,128)(2,1)S(1)}, bf16[36,3584]{1,0:T(8,128)(2,1)}, u32[]{:S(2)}, u32[]{:S(2)}) %collective-permute-start.4) | collective-permute-done | bytes 258080 | tf_op jit(solution)/shard_map/rows_z/ppermute | solution.py:14
  45.3 4.2 %collective-permute-start.7 = (bf16[72,3584]{1,0:T(8,128)(2,1)S(1)}, bf16[72,3584]{1,0:T(8,128)(2,1)}, u32[]{:S(2)}, u32[]{:S(2)}) collective-permute-start(bf16[72,3584]{1,0:T(8,128)(2,1)S(1)} %pad_maximum_fusion.4), channel_id=1, source_target_pairs={{0,96},{32,0},{64,32},{96,64},{1,97},{33,1},{65,33},{97,65},{2,98}... | collective-permute-start | bytes 1548296 | tf_op jit(solution)/shard_map/rows_y/ppermute | solution.py:14
  52.5 5.1 %collective-permute-start.9 = (bf16[72,3584]{1,0:T(8,128)(2,1)S(1)}, bf16[72,3584]{1,0:T(8,128)(2,1)}, u32[]{:S(2)}, u32[]{:S(2)}) collective-permute-start(bf16[72,3584]{1,0:T(8,128)(2,1)S(1)} %pad_maximum_fusion.3), channel_id=1, source_target_pairs={{0,96},{32,0},{64,32},{96,64},{1,97},{33,1},{65,33},{97,65},{2,98}... | collective-permute-start | bytes 1548296 | tf_op jit(solution)/shard_map/rows_y/ppermute | solution.py:14
  59.5 3.1 %collective-permute-done.7 = bf16[72,3584]{1,0:T(8,128)(2,1)} collective-permute-done((bf16[72,3584]{1,0:T(8,128)(2,1)S(1)}, bf16[72,3584]{1,0:T(8,128)(2,1)}, u32[]{:S(2)}, u32[]{:S(2)}) %collective-permute-start.7) | collective-permute-done | bytes 516128 | tf_op jit(solution)/shard_map/rows_y/ppermute | solution.py:14
  62.7 4.7 %collective-permute-start.8 = (bf16[72,3584]{1,0:T(8,128)(2,1)}, bf16[72,3584]{1,0:T(8,128)(2,1)}, u32[]{:S(2)}, u32[]{:S(2)}) collective-permute-start(bf16[72,3584]{1,0:T(8,128)(2,1)} %collective-permute-done.7), channel_id=1, source_target_pairs={{0,96},{32,0},{64,32},{96,64},{1,97},{33,1},{65,33},{97,65},{2,98}... | collective-permute-start | bytes 1548296 | tf_op jit(solution)/shard_map/rows_y/ppermute | solution.py:14
  73.8 3.3 %fusion.78 = f32[72,304]{1,0:T(8,128)} fusion(bf16[72,3584]{1,0:T(8,128)(2,1)} %collective-permute-done.9, bf16[3584,152]{0,1:T(8,128)(2,1)} %bitcast.90, bf16[3584,152]{0,1:T(8,128)(2,1)} %bitcast.98), kind=kOutput, calls=%fused_computation.99 | convolution fusion | flops 161251328 | bytes 2782720 | tf_op jit(solution)/shard_map/experts/dot_general | solution.py:30
  81.4 3.2 %convolution_convert_fusion.6 = bf16[512,768]{1,0:T(8,128)(2,1)} fusion(bf16[512,896]{1,0:T(8,128)(2,1)S(1)} %bitcast.78, bf16[896,1152]{1,0:T(8,128)(2,1)} %all-gather.2.cloned.1.call-done), kind=kOutput, calls=%fused_computation.8 | convolution fusion | flops 705036288 | bytes 3080192 | tf_op jit(solution)/shard_map/dense_tokens/dot_general | solution.py:30
  84.7 5.1 %all-to-all-start.1 = ((bf16[4,128,768]{2,1,0:T(8,128)(2,1)}), bf16[4,128,768]{2,1,0:T(8,128)(2,1)S(1)}, u32[]{:S(2)}, u32[]{:S(2)}) async-start(bf16[4,128,768]{2,1,0:T(8,128)(2,1)} %bitcast.10), calls=%async_computation.1 | async-start | bytes 1572864 | tf_op jit(solution)/shard_map/dense_hidden/all_to_all | solution.py:18
  89.8 2.6 %fusion.82 = f32[72,304]{1,0:T(8,128)S(1)} fusion(bf16[72,3584]{1,0:T(8,128)(2,1)} %collective-permute-done.5, bf16[3584,152]{0,1:T(8,128)(2,1)} %bitcast.91, bf16[3584,152]{0,1:T(8,128)(2,1)} %bitcast.99), kind=kOutput, calls=%fused_computation.103 | convolution fusion | flops 161251328 | bytes 2782720 | tf_op jit(solution)/shard_map/experts/dot_general | solution.py:30
  95.8 2.4 %collective-permute-start.12 = (bf16[72,3584]{1,0:T(8,128)(2,1)S(1)}, bf16[72,3584]{1,0:T(8,128)(2,1)}, u32[]{:S(2)}, u32[]{:S(2)}) collective-permute-start(bf16[72,3584]{1,0:T(8,128)(2,1)S(1)} %convolution_convert_fusion.2), channel_id=1, source_target_pairs={{0,96},{32,0},{64,32},{96,64},{1,97},{33,1},{65,33},{97,65},{2,98}... | collective-permute-start | bytes 1548296 | tf_op jit(solution)/shard_map/partials_y/ppermute | solution.py:14
  100.5 3.4 %collective-permute-start.10 = (bf16[72,3584]{1,0:T(8,128)(2,1)S(1)}, bf16[72,3584]{1,0:T(8,128)(2,1)S(1)}, u32[]{:S(2)}, u32[]{:S(2)}) collective-permute-start(bf16[72,3584]{1,0:T(8,128)(2,1)S(1)} %convolution_convert_fusion.1), channel_id=1, source_target_pairs={{0,32},{32,64},{64,96},{96,0},{1,33},{33,65},{65,97},{97,1},{2,34}... | collective-permute-start | bytes 1548296 | tf_op jit(solution)/shard_map/partials_y/ppermute | solution.py:14
  106.2 3.6 %collective-permute-start.16 = (bf16[72,3584]{1,0:T(8,128)(2,1)S(1)}, bf16[72,3584]{1,0:T(8,128)(2,1)S(1)}, u32[]{:S(2)}, u32[]{:S(2)}) collective-permute-start(bf16[72,3584]{1,0:T(8,128)(2,1)S(1)} %convolution_convert_fusion), channel_id=1, source_target_pairs={{0,96},{32,0},{64,32},{96,64},{1,97},{33,1},{65,33},{97,65},{2,98}... | collective-permute-start | bytes 1548296 | tf_op jit(solution)/shard_map/partials_y/ppermute | solution.py:14
  114.1 4.0 %collective-permute-done.10 = bf16[72,3584]{1,0:T(8,128)(2,1)S(1)} collective-permute-done((bf16[72,3584]{1,0:T(8,128)(2,1)S(1)}, bf16[72,3584]{1,0:T(8,128)(2,1)S(1)}, u32[]{:S(2)}, u32[]{:S(2)}) %collective-permute-start.10) | collective-permute-done | bytes 516128 | tf_op jit(solution)/shard_map/partials_y/ppermute | solution.py:14
  122.3 5.3 %collective-permute-start.17 = (bf16[72,3584]{1,0:T(8,128)(2,1)}, bf16[72,3584]{1,0:T(8,128)(2,1)}, u32[]{:S(2)}, u32[]{:S(2)}) collective-permute-start(bf16[72,3584]{1,0:T(8,128)(2,1)} %add_convert_fusion), channel_id=1, source_target_pairs={{0,96},{32,0},{64,32},{96,64},{1,97},{33,1},{65,33},{97,65},{2,98}... | collective-permute-start | bytes 1548296 | tf_op jit(solution)/shard_map/partials_y/ppermute | solution.py:14
  128.6 5.1 %all-to-all-start.2 = ((bf16[4,128,384]{2,1,0:T(8,128)(2,1)}), bf16[4,128,384]{2,1,0:T(8,128)(2,1)S(1)}, u32[]{:S(2)}, u32[]{:S(2)}) async-start(bf16[4,128,384]{2,1,0:T(8,128)(2,1)} %broadcast_in_dim.14), calls=%async_computation.2 | async-start | bytes 786432 | tf_op jit(solution)/shard_map/dense_hidden/all_to_all | solution.py:18
  133.7 2.4 %fusion.77 = f32[72,304]{1,0:T(8,128)S(1)} fusion(bf16[72,3584]{1,0:T(8,128)(2,1)S(1)} %copy-done.4, bf16[3584,152]{0,1:T(8,128)(2,1)} %bitcast.92, bf16[3584,152]{0,1:T(8,128)(2,1)} %bitcast.100), kind=kOutput, calls=%fused_computation.98 | convolution fusion | flops 161251328 | bytes 2782720 | tf_op jit(solution)/shard_map/experts/dot_general | solution.py:30
  140.1 2.5 %collective-permute-start.13 = (bf16[36,3584]{1,0:T(8,128)(2,1)}, bf16[36,3584]{1,0:T(8,128)(2,1)S(1)}, u32[]{:S(2)}, u32[]{:S(2)}) collective-permute-start(bf16[36,3584]{1,0:T(8,128)(2,1)} %add_convert_fusion.5), channel_id=1, source_target_pairs={{0,24},{8,0},{16,8},{24,16},{1,25},{9,1},{17,9},{25,17},{2,26},{10... | collective-permute-start | bytes 774152 | tf_op jit(solution)/shard_map/partials_z/ppermute | solution.py:14
  144.7 5.2 %collective-permute-start.18 = (bf16[36,3584]{1,0:T(8,128)(2,1)}, bf16[36,3584]{1,0:T(8,128)(2,1)}, u32[]{:S(2)}, u32[]{:S(2)}) collective-permute-start(bf16[36,3584]{1,0:T(8,128)(2,1)} %add_convert_fusion.4), channel_id=1, source_target_pairs={{0,8},{8,16},{16,24},{24,0},{1,9},{9,17},{17,25},{25,1},{2,10},{10... | collective-permute-start | bytes 774152 | tf_op jit(solution)/shard_map/partials_z/ppermute | solution.py:14
  158.3 4.3 %all-to-all-start.3 = ((bf16[8,256,224]{1,2,0:T(8,128)(2,1)}), bf16[8,256,224]{1,2,0:T(8,128)(2,1)S(1)}, u32[]{:S(2)}, u32[]{:S(2)}) async-start(bf16[8,256,224]{1,2,0:T(8,128)(2,1)} %copy.70), calls=%async_computation.3 | async-start | bytes 1835008 | tf_op jit(solution)/shard_map/dense_out/all_to_all | solution.py:18
  162.6 6.6 %collective-permute-done.19 = bf16[36,3584]{1,0:T(8,128)(2,1)} collective-permute-done((bf16[36,3584]{1,0:T(8,128)(2,1)}, bf16[36,3584]{1,0:T(8,128)(2,1)}, u32[]{:S(2)}, u32[]{:S(2)}) %collective-permute-start.19) | collective-permute-done | bytes 258080 | tf_op jit(solution)/shard_map/partials_z/ppermute | solution.py:14
  171.8 5.3 %all-to-all-done.3 = bf16[8,256,224]{1,2,0:T(8,128)(2,1)S(1)} async-done(((bf16[8,256,224]{1,2,0:T(8,128)(2,1)}), bf16[8,256,224]{1,2,0:T(8,128)(2,1)S(1)}, u32[]{:S(2)}, u32[]{:S(2)}) %all-to-all-start.3) | async-done | bytes 917536 | tf_op jit(solution)/shard_map/dense_out/all_to_all | solution.py:18
  177.1 3.4 %all-to-all-start.5 = ((bf16[8,36,448]{2,1,0:T(8,128)(2,1)}), bf16[8,36,448]{2,1,0:T(8,128)(2,1)S(1)}, u32[]{:S(2)}, u32[]{:S(2)}) async-start(bf16[8,36,448]{2,1,0:T(8,128)(2,1)} %bitcast.74), calls=%async_computation.5 | async-start | bytes 655360 | tf_op jit(solution)/shard_map/combine/all_to_all | solution.py:18
  181.5 7.3 %all-to-all-done.5 = bf16[8,36,448]{2,1,0:T(8,128)(2,1)S(1)} async-done(((bf16[8,36,448]{2,1,0:T(8,128)(2,1)}), bf16[8,36,448]{2,1,0:T(8,128)(2,1)S(1)}, u32[]{:S(2)}, u32[]{:S(2)}) %all-to-all-start.5) | async-done | bytes 258080 | tf_op jit(solution)/shard_map/combine/all_to_all | solution.py:18
  188.7 5.6 %all-to-all-start.4 = ((bf16[4,64,224]{2,1,0:T(8,128)(2,1)}), bf16[4,64,224]{2,1,0:T(8,128)(2,1)S(1)}, u32[]{:S(2)}, u32[]{:S(2)}) async-start(bf16[4,64,224]{2,1,0:T(8,128)(2,1)} %bitcast.14), calls=%async_computation.4 | async-start | bytes 262144 | tf_op jit(solution)/shard_map/dense_out/all_to_all | solution.py:18
  194.5 3.4 %all-to-all-done.4 = bf16[4,64,224]{2,1,0:T(8,128)(2,1)S(1)} async-done(((bf16[4,64,224]{2,1,0:T(8,128)(2,1)}), bf16[4,64,224]{2,1,0:T(8,128)(2,1)S(1)}, u32[]{:S(2)}, u32[]{:S(2)}) %all-to-all-start.4) | async-done | bytes 114720 | tf_op jit(solution)/shard_map/dense_out/all_to_all | solution.py:18
  201.5 9.1 %collective-permute-start.20 = (bf16[128,448]{0,1:T(8,128)(2,1)S(1)}, bf16[128,448]{0,1:T(8,128)(2,1)S(1)}, u32[]{:S(2)}, u32[]{:S(2)}) collective-permute-start(bf16[128,448]{0,1:T(8,128)(2,1)S(1)} %fusion.2), channel_id=1, source_target_pairs={{0,128},{128,256},{256,384},{384,0},{1,129},{129,257},{257,385},{3... | collective-permute-start | bytes 344072 | tf_op jit(solution)/shard_map/next_section/ppermute | solution.py:14
  210.6 14.3 %collective-permute-done.20 = bf16[128,448]{0,1:T(8,128)(2,1)S(1)} collective-permute-done((bf16[128,448]{0,1:T(8,128)(2,1)S(1)}, bf16[128,448]{0,1:T(8,128)(2,1)S(1)}, u32[]{:S(2)}, u32[]{:S(2)}) %collective-permute-start.20) | collective-permute-done | bytes 114720 | tf_op jit(solution)/shard_map/next_section/ppermute | solution.py:14
  (118 shorter events, 63.2 us)
Async XLA Ops:
  6.5 85.8 %copy-start = (bf16[1,1,152,3584]{3,2,1,0:T(8,128)(2,1)S(1)}, bf16[1,1,152,3584]{3,2,1,0:T(8,128)(2,1)}, u32[]{:S(2)}) copy-start(bf16[1,1,152,3584]{3,2,1,0:T(8,128)(2,1)} %param.19) | copy-start | bytes 3268612
  6.5 74.9 %all-gather.2.cloned.1.call-start = ((), (), s32[]{:S(2)}) async-start(), calls=%async_computation.6 | async-start | bytes 2580480 | tf_op jit(solution)/shard_map/dense_weights/all_gather | solution.py:68
  9.4 15.2 %collective-permute-start = (bf16[36,3584]{1,0:T(8,128)(2,1)S(1)}, bf16[36,3584]{1,0:T(8,128)(2,1)S(1)}, u32[]{:S(2)}, u32[]{:S(2)}) collective-permute-start(bf16[36,3584]{1,0:T(8,128)(2,1)S(1)} %convolution_convert_fusion.4), channel_id=1, source_target_pairs={{0,8},{8,16},{16,24},{24,0},{1,9},{9,17},{17,25},{25,1},{2,10},{10... | collective-permute-start | bytes 774152 | tf_op jit(solution)/shard_map/rows_z/ppermute | solution.py:14
  15.9 14.0 %collective-permute-start.1 = (bf16[36,3584]{1,0:T(8,128)(2,1)S(1)}, bf16[36,3584]{1,0:T(8,128)(2,1)}, u32[]{:S(2)}, u32[]{:S(2)}) collective-permute-start(bf16[36,3584]{1,0:T(8,128)(2,1)S(1)} %convolution_convert_fusion.4), channel_id=1, source_target_pairs={{0,24},{8,0},{16,8},{24,16},{1,25},{9,1},{17,9},{25,17},{2,26},{10... | collective-permute-start | bytes 774152 | tf_op jit(solution)/shard_map/rows_z/ppermute | solution.py:14
  17.8 26.3 %collective-permute-start.4 = (bf16[36,3584]{1,0:T(8,128)(2,1)S(1)}, bf16[36,3584]{1,0:T(8,128)(2,1)}, u32[]{:S(2)}, u32[]{:S(2)}) collective-permute-start(bf16[36,3584]{1,0:T(8,128)(2,1)S(1)} %convolution_convert_fusion.4), channel_id=1, source_target_pairs={{0,16},{8,24},{16,0},{24,8},{1,17},{9,25},{17,1},{25,9},{2,18},{10... | collective-permute-start | bytes 774152 | tf_op jit(solution)/shard_map/rows_z/ppermute | solution.py:14
  31.0 39.3 %all-to-all-start = ((bf16[4,64,896]{2,1,0:T(8,128)(2,1)}), bf16[4,64,896]{2,1,0:T(8,128)(2,1)S(1)}, u32[]{:S(2)}, u32[]{:S(2)}) async-start(bf16[4,64,896]{2,1,0:T(8,128)(2,1)} %copy.68), calls=%async_computation | async-start | bytes 917504 | tf_op jit(solution)/shard_map/dense_tokens/all_to_all | solution.py:18
  45.3 31.8 %copy-start.3 = (bf16[72,3584]{1,0:T(8,128)(2,1)}, bf16[72,3584]{1,0:T(8,128)(2,1)S(1)}, u32[]{:S(2)}) copy-start(bf16[72,3584]{1,0:T(8,128)(2,1)S(1)} %pad_maximum_fusion.4) | copy-start | bytes 1548292
  45.3 17.4 %collective-permute-start.7 = (bf16[72,3584]{1,0:T(8,128)(2,1)S(1)}, bf16[72,3584]{1,0:T(8,128)(2,1)}, u32[]{:S(2)}, u32[]{:S(2)}) collective-permute-start(bf16[72,3584]{1,0:T(8,128)(2,1)S(1)} %pad_maximum_fusion.4), channel_id=1, source_target_pairs={{0,96},{32,0},{64,32},{96,64},{1,97},{33,1},{65,33},{97,65},{2,98}... | collective-permute-start | bytes 1548296 | tf_op jit(solution)/shard_map/rows_y/ppermute | solution.py:14
  50.5 26.5 %copy-start.5 = (bf16[72,3584]{1,0:T(8,128)(2,1)}, bf16[72,3584]{1,0:T(8,128)(2,1)S(1)}, u32[]{:S(2)}) copy-start(bf16[72,3584]{1,0:T(8,128)(2,1)S(1)} %pad_maximum_fusion.3) | copy-start | bytes 1548292
  50.5 17.8 %collective-permute-start.5 = (bf16[72,3584]{1,0:T(8,128)(2,1)S(1)}, bf16[72,3584]{1,0:T(8,128)(2,1)}, u32[]{:S(2)}, u32[]{:S(2)}) collective-permute-start(bf16[72,3584]{1,0:T(8,128)(2,1)S(1)} %pad_maximum_fusion.3), channel_id=1, source_target_pairs={{0,32},{32,64},{64,96},{96,0},{1,33},{33,65},{65,97},{97,1},{2,34}... | collective-permute-start | bytes 1548296 | tf_op jit(solution)/shard_map/rows_y/ppermute | solution.py:14
  52.5 21.3 %collective-permute-start.9 = (bf16[72,3584]{1,0:T(8,128)(2,1)S(1)}, bf16[72,3584]{1,0:T(8,128)(2,1)}, u32[]{:S(2)}, u32[]{:S(2)}) collective-permute-start(bf16[72,3584]{1,0:T(8,128)(2,1)S(1)} %pad_maximum_fusion.3), channel_id=1, source_target_pairs={{0,96},{32,0},{64,32},{96,64},{1,97},{33,1},{65,33},{97,65},{2,98}... | collective-permute-start | bytes 1548296 | tf_op jit(solution)/shard_map/rows_y/ppermute | solution.py:14
  57.6 21.8 %collective-permute-start.15 = (bf16[72,3584]{1,0:T(8,128)(2,1)S(1)}, bf16[72,3584]{1,0:T(8,128)(2,1)}, u32[]{:S(2)}, u32[]{:S(2)}) collective-permute-start(bf16[72,3584]{1,0:T(8,128)(2,1)S(1)} %pad_maximum_fusion.4), channel_id=1, source_target_pairs={{0,32},{32,64},{64,96},{96,0},{1,33},{33,65},{65,97},{97,1},{2,34}... | collective-permute-start | bytes 1548296 | tf_op jit(solution)/shard_map/rows_y/ppermute | solution.py:14
  62.7 35.6 %collective-permute-start.8 = (bf16[72,3584]{1,0:T(8,128)(2,1)}, bf16[72,3584]{1,0:T(8,128)(2,1)}, u32[]{:S(2)}, u32[]{:S(2)}) collective-permute-start(bf16[72,3584]{1,0:T(8,128)(2,1)} %collective-permute-done.7), channel_id=1, source_target_pairs={{0,96},{32,0},{64,32},{96,64},{1,97},{33,1},{65,33},{97,65},{2,98}... | collective-permute-start | bytes 1548296 | tf_op jit(solution)/shard_map/rows_y/ppermute | solution.py:14
  68.3 30.0 %collective-permute-start.6 = (bf16[72,3584]{1,0:T(8,128)(2,1)}, bf16[72,3584]{1,0:T(8,128)(2,1)}, u32[]{:S(2)}, u32[]{:S(2)}) collective-permute-start(bf16[72,3584]{1,0:T(8,128)(2,1)} %collective-permute-done.5), channel_id=1, source_target_pairs={{0,32},{32,64},{64,96},{96,0},{1,33},{33,65},{65,97},{97,1},{2,34}... | collective-permute-start | bytes 1548296 | tf_op jit(solution)/shard_map/rows_y/ppermute | solution.py:14
  70.2 11.0 %collective-permute-start.2 = (bf16[4,64,896]{2,1,0:T(8,128)(2,1)S(1)}, bf16[4,64,896]{2,1,0:T(8,128)(2,1)S(1)}, u32[]{:S(2)}, u32[]{:S(2)}) collective-permute-start(bf16[4,64,896]{2,1,0:T(8,128)(2,1)S(1)} %all-to-all-done), channel_id=1, source_target_pairs={{0,1},{1,0},{2,3},{3,2},{4,5},{5,4},{6,7},{7,6},{8,9},{9,8},{10,11... | collective-permute-start | bytes 1376264 | tf_op jit(solution)/shard_map/dense_tokens/ppermute | solution.py:14
  84.7 42.9 %all-to-all-start.1 = ((bf16[4,128,768]{2,1,0:T(8,128)(2,1)}), bf16[4,128,768]{2,1,0:T(8,128)(2,1)S(1)}, u32[]{:S(2)}, u32[]{:S(2)}) async-start(bf16[4,128,768]{2,1,0:T(8,128)(2,1)} %bitcast.10), calls=%async_computation.1 | async-start | bytes 1572864 | tf_op jit(solution)/shard_map/dense_hidden/all_to_all | solution.py:18
  95.8 40.3 %collective-permute-start.12 = (bf16[72,3584]{1,0:T(8,128)(2,1)S(1)}, bf16[72,3584]{1,0:T(8,128)(2,1)}, u32[]{:S(2)}, u32[]{:S(2)}) collective-permute-start(bf16[72,3584]{1,0:T(8,128)(2,1)S(1)} %convolution_convert_fusion.2), channel_id=1, source_target_pairs={{0,96},{32,0},{64,32},{96,64},{1,97},{33,1},{65,33},{97,65},{2,98}... | collective-permute-start | bytes 1548296 | tf_op jit(solution)/shard_map/partials_y/ppermute | solution.py:14
  100.5 17.6 %collective-permute-start.10 = (bf16[72,3584]{1,0:T(8,128)(2,1)S(1)}, bf16[72,3584]{1,0:T(8,128)(2,1)S(1)}, u32[]{:S(2)}, u32[]{:S(2)}) collective-permute-start(bf16[72,3584]{1,0:T(8,128)(2,1)S(1)} %convolution_convert_fusion.1), channel_id=1, source_target_pairs={{0,32},{32,64},{64,96},{96,0},{1,33},{33,65},{65,97},{97,1},{2,34}... | collective-permute-start | bytes 1548296 | tf_op jit(solution)/shard_map/partials_y/ppermute | solution.py:14
  106.2 15.0 %collective-permute-start.16 = (bf16[72,3584]{1,0:T(8,128)(2,1)S(1)}, bf16[72,3584]{1,0:T(8,128)(2,1)S(1)}, u32[]{:S(2)}, u32[]{:S(2)}) collective-permute-start(bf16[72,3584]{1,0:T(8,128)(2,1)S(1)} %convolution_convert_fusion), channel_id=1, source_target_pairs={{0,96},{32,0},{64,32},{96,64},{1,97},{33,1},{65,33},{97,65},{2,98}... | collective-permute-start | bytes 1548296 | tf_op jit(solution)/shard_map/partials_y/ppermute | solution.py:14
  109.8 32.8 %collective-permute-start.14 = (bf16[72,3584]{1,0:T(8,128)(2,1)S(1)}, bf16[72,3584]{1,0:T(8,128)(2,1)}, u32[]{:S(2)}, u32[]{:S(2)}) collective-permute-start(bf16[72,3584]{1,0:T(8,128)(2,1)S(1)} %convolution_convert_fusion.3), channel_id=1, source_target_pairs={{0,32},{32,64},{64,96},{96,0},{1,33},{33,65},{65,97},{97,1},{2,34}... | collective-permute-start | bytes 1548296 | tf_op jit(solution)/shard_map/partials_y/ppermute | solution.py:14
  119.2 18.8 %collective-permute-start.11 = (bf16[72,3584]{1,0:T(8,128)(2,1)}, bf16[72,3584]{1,0:T(8,128)(2,1)}, u32[]{:S(2)}, u32[]{:S(2)}) collective-permute-start(bf16[72,3584]{1,0:T(8,128)(2,1)} %add_convert_fusion.1), channel_id=1, source_target_pairs={{0,32},{32,64},{64,96},{96,0},{1,33},{33,65},{65,97},{97,1},{2,34}... | collective-permute-start | bytes 1548296 | tf_op jit(solution)/shard_map/partials_y/ppermute | solution.py:14
  122.3 20.3 %collective-permute-start.17 = (bf16[72,3584]{1,0:T(8,128)(2,1)}, bf16[72,3584]{1,0:T(8,128)(2,1)}, u32[]{:S(2)}, u32[]{:S(2)}) collective-permute-start(bf16[72,3584]{1,0:T(8,128)(2,1)} %add_convert_fusion), channel_id=1, source_target_pairs={{0,96},{32,0},{64,32},{96,64},{1,97},{33,1},{65,33},{97,65},{2,98}... | collective-permute-start | bytes 1548296 | tf_op jit(solution)/shard_map/partials_y/ppermute | solution.py:14
  128.6 25.5 %all-to-all-start.2 = ((bf16[4,128,384]{2,1,0:T(8,128)(2,1)}), bf16[4,128,384]{2,1,0:T(8,128)(2,1)S(1)}, u32[]{:S(2)}, u32[]{:S(2)}) async-start(bf16[4,128,384]{2,1,0:T(8,128)(2,1)} %broadcast_in_dim.14), calls=%async_computation.2 | async-start | bytes 786432 | tf_op jit(solution)/shard_map/dense_hidden/all_to_all | solution.py:18
  140.1 22.4 %collective-permute-start.13 = (bf16[36,3584]{1,0:T(8,128)(2,1)}, bf16[36,3584]{1,0:T(8,128)(2,1)S(1)}, u32[]{:S(2)}, u32[]{:S(2)}) collective-permute-start(bf16[36,3584]{1,0:T(8,128)(2,1)} %add_convert_fusion.5), channel_id=1, source_target_pairs={{0,24},{8,0},{16,8},{24,16},{1,25},{9,1},{17,9},{25,17},{2,26},{10... | collective-permute-start | bytes 774152 | tf_op jit(solution)/shard_map/partials_z/ppermute | solution.py:14
  144.7 17.8 %collective-permute-start.18 = (bf16[36,3584]{1,0:T(8,128)(2,1)}, bf16[36,3584]{1,0:T(8,128)(2,1)}, u32[]{:S(2)}, u32[]{:S(2)}) collective-permute-start(bf16[36,3584]{1,0:T(8,128)(2,1)} %add_convert_fusion.4), channel_id=1, source_target_pairs={{0,8},{8,16},{16,24},{24,0},{1,9},{9,17},{17,25},{25,1},{2,10},{10... | collective-permute-start | bytes 774152 | tf_op jit(solution)/shard_map/partials_z/ppermute | solution.py:14
  152.0 17.2 %collective-permute-start.19 = (bf16[36,3584]{1,0:T(8,128)(2,1)}, bf16[36,3584]{1,0:T(8,128)(2,1)}, u32[]{:S(2)}, u32[]{:S(2)}) collective-permute-start(bf16[36,3584]{1,0:T(8,128)(2,1)} %add_convert_fusion.3), channel_id=1, source_target_pairs={{0,16},{8,24},{16,0},{24,8},{1,17},{9,25},{17,1},{25,9},{2,18},{10... | collective-permute-start | bytes 774152 | tf_op jit(solution)/shard_map/partials_z/ppermute | solution.py:14
  158.3 18.9 %all-to-all-start.3 = ((bf16[8,256,224]{1,2,0:T(8,128)(2,1)}), bf16[8,256,224]{1,2,0:T(8,128)(2,1)S(1)}, u32[]{:S(2)}, u32[]{:S(2)}) async-start(bf16[8,256,224]{1,2,0:T(8,128)(2,1)} %copy.70), calls=%async_computation.3 | async-start | bytes 1835008 | tf_op jit(solution)/shard_map/dense_out/all_to_all | solution.py:18
  170.6 23.8 %copy-start.11 = (f32[1,128,2]{1,2,0:T(2,128)S(1)}, f32[1,128,2]{1,2,0:T(2,128)}, u32[]{:S(2)}) copy-start(f32[1,128,2]{1,2,0:T(2,128)} %param.13) | copy-start | bytes 3076
  177.1 11.6 %all-to-all-start.5 = ((bf16[8,36,448]{2,1,0:T(8,128)(2,1)}), bf16[8,36,448]{2,1,0:T(8,128)(2,1)S(1)}, u32[]{:S(2)}, u32[]{:S(2)}) async-start(bf16[8,36,448]{2,1,0:T(8,128)(2,1)} %bitcast.74), calls=%async_computation.5 | async-start | bytes 655360 | tf_op jit(solution)/shard_map/combine/all_to_all | solution.py:18
  188.7 9.1 %all-to-all-start.4 = ((bf16[4,64,224]{2,1,0:T(8,128)(2,1)}), bf16[4,64,224]{2,1,0:T(8,128)(2,1)S(1)}, u32[]{:S(2)}, u32[]{:S(2)}) async-start(bf16[4,64,224]{2,1,0:T(8,128)(2,1)} %bitcast.14), calls=%async_computation.4 | async-start | bytes 262144 | tf_op jit(solution)/shard_map/dense_out/all_to_all | solution.py:18
  197.9 3.1 %collective-permute-start.3 = (bf16[2,64,224]{2,1,0:T(8,128)(2,1)S(1)}, bf16[2,64,224]{2,1,0:T(8,128)(2,1)S(1)}, u32[]{:S(2)}, u32[]{:S(2)}) collective-permute-start(bf16[2,64,224]{2,1,0:T(8,128)(2,1)S(1)} %constant_dynamic-slice_fusion), channel_id=1, source_target_pairs={{0,1},{1,0},{2,3},{3,2},{4,5},{5,4},{6,7},{7,6},{8,9},{9,8},{10,11... | collective-permute-start | bytes 172040 | tf_op jit(solution)/shard_map/dense_out/ppermute | solution.py:14
  201.5 23.4 %collective-permute-start.20 = (bf16[128,448]{0,1:T(8,128)(2,1)S(1)}, bf16[128,448]{0,1:T(8,128)(2,1)S(1)}, u32[]{:S(2)}, u32[]{:S(2)}) collective-permute-start(bf16[128,448]{0,1:T(8,128)(2,1)S(1)} %fusion.2), channel_id=1, source_target_pairs={{0,128},{128,256},{256,384},{384,0},{1,129},{129,257},{257,385},{3... | collective-permute-start | bytes 344072 | tf_op jit(solution)/shard_map/next_section/ppermute | solution.py:14
  (12 other events, 96.4 us)
Sparse Core Ops, SparseCore 0:
  9.5 43.4 all-gather.1

commit v5 on v2

v5 whole, which is shorter than its diff:
```python
import jax
import jax.numpy as jnp
from jax import lax
from jax.sharding import Mesh, PartitionSpec as P

AXES = ("section", "y", "z", "x", "core")
GRID = (4, 4, 4, 4, 2)
EXPERT_AXES = ("x", "core")
BF16, F32 = jnp.bfloat16, jnp.float32


def shifted(x, axis, by):
    peers = lax.axis_size(axis)
    return lax.ppermute(x, axis, [(i, (i + by) % peers) for i in range(peers)])


def exchanged(x, axes):
    return lax.all_to_all(x, axes, split_axis=0, concat_axis=0, tiled=True)


def after(x, *others):
    return lax.optimization_barrier((x,) + others)[0]


def swiglu(first, second):
    return (jax.nn.silu(first) * second).astype(BF16)


def dot(a, b):
    return jnp.dot(a, b, preferred_element_type=F32)


def slots_of(picks, n_expert):
    labels = jnp.arange(n_expert, dtype=jnp.int32)
    named = (picks[:, :, None] == labels[None, None, :]).astype(jnp.int32)
    per_token = jnp.sum(named, axis=1, dtype=jnp.int32)
    earlier = jnp.cumsum(per_token, axis=0, dtype=jnp.int32) - per_token
    return jnp.sum(named * earlier[:, None, :], axis=2, dtype=jnp.int32)


def body(
    normed,
    residual,
    expert_index,
    pick_weight,
    dense_gate,
    dense_up,
    dense_down,
    expert_gate,
    expert_up,
    expert_down,
):
    tokens = normed[0]
    picks = expert_index[0]
    weights = pick_weight[0]
    tok_rows, width = tokens.shape
    n_expert = 8
    capacity = min(tok_rows, 9 * tok_rows // (4 * n_expert))
    core = lax.axis_index("core")
    mine = lax.axis_index("x") * 2 + core
    hidden = dense_gate.shape[2]
    slab = width // 4
    step = dense_gate.shape[1]
    piece = width // n_expert

    with jax.named_scope("dispatch"):
        slot = slots_of(picks, n_expert)
        is_mine = picks == mine
        positions = jnp.arange(capacity, dtype=jnp.int32)
        select = jnp.any(
            (positions[:, None, None] == slot[None, :, :]) & is_mine[None, :, :], axis=2
        ).astype(BF16)
        routed = dot(select, tokens).astype(BF16)

    with jax.named_scope("dense_weights"):
        stacked = jnp.concatenate([dense_gate[0], dense_up[0], dense_down[0]], axis=1)
        stacked = jnp.broadcast_to(after(stacked, routed)[None], (4,) + stacked.shape)
        slabs = exchanged(stacked, "y").reshape(slab, 3 * hidden)

    with jax.named_scope("combine"):
        target = picks * capacity + slot
        columns = jnp.arange(n_expert * capacity, dtype=jnp.int32)
        chosen = jnp.where(columns[None, None, :] == target[:, :, None], weights[:, :, None], 0.0)
        combine = jnp.sum(chosen, axis=1)
        coarse = lax.reduce_precision(combine, 8, 7)
        fine = lax.reduce_precision(combine - coarse, 8, 7)
        coarse, fine = coarse.astype(BF16), fine.astype(BF16)

    gate_up = jnp.concatenate([expert_gate[0, 0], expert_up[0, 0]], axis=1)
    down = expert_down[0, 0]
    inner = down.shape[0]

    with jax.named_scope("rows_z"):
        lines = [routed] + [shifted(routed, "z", by) for by in (1, 3, 2)]
        low = jnp.concatenate([lines[0], lines[1]], axis=0)
        high = jnp.concatenate([lines[2], lines[3]], axis=0)
        gate_up, coarse, fine = after((gate_up, coarse, fine), routed)
        low = after(low, gate_up, coarse, fine)

    half = 2 * capacity
    with jax.named_scope("rows_y"):
        prev_low, next_low = shifted(low, "y", 1), shifted(low, "y", -1)
        far_low = shifted(prev_low, "y", 1)
        next_high, prev_high = shifted(high, "y", -1), shifted(high, "y", 1)
        far_high = shifted(next_high, "y", -1)

    with jax.named_scope("dense_tokens"):
        half_tokens = tok_rows // 2
        by_line = (
            tokens.reshape(tok_rows, 4, 4, step).transpose(2, 0, 1, 3).reshape(4, tok_rows, slab)
        )
        own_half = lax.dynamic_slice_in_dim(by_line, core * half_tokens, half_tokens, axis=1)
        half_in = exchanged(after(own_half, slabs, low, high), "z")
        half_in = after(half_in, prev_low, next_low, prev_high, next_high)
        other_half = shifted(half_in, "core", 1)
        first = jnp.where(core == 0, half_in, other_half)
        second = jnp.where(core == 0, other_half, half_in)
        line_tokens = jnp.concatenate([first, second], axis=1).reshape(4 * tok_rows, slab)
        pre = dot(line_tokens, slabs[:, : 2 * hidden]).astype(BF16)
        pre = pre.reshape(4, tok_rows, 2 * hidden)

    def activate(rows, *first):
        both = dot(rows, after(gate_up, *first))
        return swiglu(both[:, :inner], both[:, inner:])

    with jax.named_scope("experts"):
        early_next = dot(activate(next_high, pre), down).astype(BF16)
        early_prev = dot(activate(prev_low, pre), down).astype(BF16)
        next_act, prev_act = activate(next_low, pre), activate(prev_high, pre)
        done = (early_next, early_prev, next_act, prev_act)
        relay_next = dot(activate(far_low, *done), down).astype(BF16)
        relay_prev = dot(activate(far_high, *done), down).astype(BF16)

    with jax.named_scope("dense_hidden"):
        pre = exchanged(pre, "z")
        pre = jnp.sum(pre.astype(F32), axis=0)
        act = swiglu(pre[:, :hidden], pre[:, hidden:])
        line_act = jnp.broadcast_to(act[None], (4,) + act.shape)
    with jax.named_scope("dense_out"):
        every_act = exchanged(line_act, "z").reshape(4 * tok_rows, hidden)
        contract = (((1,), (1,)), ((), ()))
        dense_out = lax.dot_general(
            every_act, slabs[:, 2 * hidden :], contract, preferred_element_type=F32
        )
        by_block = (
            dense_out.astype(BF16)
            .reshape(4, 2, half_tokens, 4, step)
            .transpose(3, 1, 0, 2, 4)
            .reshape(n_expert, 4 * half_tokens, step)
        )

    with jax.named_scope("partials_y"):
        relay_next, relay_prev = shifted(relay_next, "y", 1), shifted(relay_prev, "y", -1)
        relay_next, relay_prev = after((relay_next, relay_prev), line_act)
        early_next, early_prev = shifted(early_next, "y", 1), shifted(early_prev, "y", -1)
        late_next = dot(next_act, down) + relay_next.astype(F32)
        late_prev = dot(prev_act, down) + relay_prev.astype(F32)
        late_next, late_prev = late_next.astype(BF16), late_prev.astype(BF16)
        done = (late_next, late_prev)
        own_low, own_high = activate(low, *done), activate(high, *done)
        late_next, late_prev = shifted(late_next, "y", 1), shifted(late_prev, "y", -1)
        total = [
            dot(act[rows], down) + one[rows].astype(F32) + two[rows].astype(F32)
            for act, one, two in ((own_low, late_next, early_prev), (own_high, early_next, late_prev))
            for rows in (slice(0, capacity), slice(capacity, half))
        ]

    with jax.named_scope("partials_z"):
        recv = [shifted(part.astype(BF16), "z", by) for part, by in zip(total[1:], (-1, -3, -2))]
        expert_out = total[0] + sum(part.astype(F32) for part in recv)
        expert_out = expert_out.astype(BF16)

    with jax.named_scope("dense_out"):
        block_sum = jnp.sum(exchanged(by_block, EXPERT_AXES).astype(F32), axis=0).astype(BF16)
        block_sum = after(block_sum, recv[0])
        blocks = exchanged(block_sum.reshape(4, half_tokens, step), "z")
        kept = lax.dynamic_slice_in_dim(blocks, 2 * core, 2, axis=0)
        given = lax.dynamic_slice_in_dim(blocks, 2 - 2 * core, 2, axis=0)
        taken = shifted(given, "core", 1)
        first = jnp.where(core == 0, kept, taken)
        second = jnp.where(core == 0, taken, kept)
        dense_total = jnp.concatenate([first, second], axis=1).transpose(1, 0, 2)
    base = residual[0].astype(F32) + dense_total.reshape(tok_rows, piece).astype(F32)

    with jax.named_scope("combine"):
        by_feature = expert_out.reshape(capacity, n_expert, piece).transpose(1, 0, 2)
        by_feature = after(by_feature, blocks)
        returned = exchanged(by_feature, EXPERT_AXES).reshape(n_expert * capacity, piece)
        spread = dot(coarse, returned) + dot(fine, returned)
        mixed = (base + spread).astype(BF16)
    with jax.named_scope("next_section"):
        return shifted(mixed, "section", 1)[None]


def solution(mesh):
    fine_mesh = Mesh(mesh.devices.reshape(GRID), AXES)
    data = ("y", "z")
    placed = (
        P("section", data, None),
        P("section", data, EXPERT_AXES),
        P("section", data, None),
        P("section", data, None),
        P("section", data, EXPERT_AXES),
        P("section", data, EXPERT_AXES),
        P("section", data, EXPERT_AXES),
        P("section", EXPERT_AXES, None, data),
        P("section", EXPERT_AXES, None, data),
        P("section", EXPERT_AXES, data, None),
    )
    return jax.shard_map(
        body,
        mesh=fine_mesh,
        in_specs=placed,
        out_specs=P("section", data, EXPERT_AXES),
        check_vma=False,
    )
```

time: 244 us -> 237 us (0.971)
  matrix products: 16.1 us -> 31.5 us
  between operations: 14 us -> 0.7 us
  waiting for transfers between devices: 56.5 us -> 50.8 us
    dot_general x11 -> x22, matrix products: 14.3 us -> 29.6 us  [dot(): return jnp.dot(a, b, preferred_element_type=F32)]
    slice x5 -> x0, local copies, waits for them, and re-layouts: 7.66 us -> none  [the longest x1 2.66 us: body(): slabs[:, i].reshape(slab, hidden)]
    ppermute x21, starting transfers between devices: 80.6 us -> 76.5 us  [shifted(): return lax.ppermute(x, axis, [(i, (i + by) % peers) for i in range(peers)])]
    ppermute x21, waiting for transfers between devices: 35.6 us -> 31.6 us  [shifted(): return lax.ppermute(x, axis, [(i, (i + by) % peers) for i in range(peers)])]
    concatenate x3, other arithmetic: 5.22 us -> 1.87 us  [the longest x1 1.75 us: body(): gate_up = jnp.concatenate([expert_gate[0, 0], expert_up[0, 0]], axis=1)]
    all_to_all x6 -> x7, starting transfers between devices: 38.5 us -> 41 us  [exchanged(): return lax.all_to_all(x, axes, split_axis=0, concat_axis=0, tiled=True)]
    all_to_all x6 -> x7, waiting for transfers between devices: 20.9 us -> 19.1 us  [exchanged(): return lax.all_to_all(x, axes, split_axis=0, concat_axis=0, tiled=True)]
    convert_element_type x3 -> x4, other arithmetic: 5.54 us -> 6.27 us  [the longest x2 4.31 us: body(): late_next, late_prev = (late_next.astype(BF16), late_prev.astype(BF16))]
  transfers between devices with their start and end apart: 28 -> 28, of which waited for: 14 -> 9; matrix products, arithmetic and copies ran while one was open for 19% -> 24% of each run, Pallas kernels for 0% -> 0%
where the time goes in v5:
time: 237 us; the launch traced here: 234 us
  starting transfers between devices  117 us (49%)
  waiting for transfers between devices  50.8 us (21%)
  matrix products  31.5 us (13%)
  other arithmetic  17.5 us (7%)
  local copies, waits for them, and re-layouts  15.7 us (7%)
    ppermute x21, starting transfers between devices, shifted(): return lax.ppermute(x, axis, [(i, (i + by) % peers) for i in range(peers)])  76.5 us
    all_to_all x7, starting transfers between devices, exchanged(): return lax.all_to_all(x, axes, split_axis=0, concat_axis=0, tiled=True)  41 us
    ppermute x21, waiting for transfers between devices, shifted(): return lax.ppermute(x, axis, [(i, (i + by) % peers) for i in range(peers)])  31.6 us
    dot_general x22, matrix products, dot(): return jnp.dot(a, b, preferred_element_type=F32)  29.6 us
    all_to_all x7, waiting for transfers between devices, exchanged(): return lax.all_to_all(x, axes, split_axis=0, concat_axis=0, tiled=True)  19.1 us
  transfers between devices with their start and end apart: 28, of which 9 were waited for; matrix products, arithmetic and copies ran while one was open for 24% of the time, Pallas kernels for 0%

profile of v5, /device:TPU:24, one launch (start us, length us, event | category | flops | bytes accessed | tf_op | source)
XLA Modules:
  0.0 233.6 jit_solution(3762443805251800548)
XLA Ops:
  4.1 3.8 %collective-permute-start = (bf16[36,3584]{1,0:T(8,128)(2,1)S(1)}, bf16[36,3584]{1,0:T(8,128)(2,1)}, u32[]{:S(2)}, u32[]{:S(2)}) collective-permute-start(bf16[36,3584]{1,0:T(8,128)(2,1)S(1)} %convolution_convert_fusion.4), channel_id=1, source_target_pairs={{0,8},{8,16},{16,24},{24,0},{1,9},{9,17},{17,25},{25,1},{2,10},{10... | collective-permute-start | bytes 774152 | tf_op jit(solution)/shard_map/rows_z/ppermute | solution.py:14
  7.9 4.6 %collective-permute-start.1 = (bf16[36,3584]{1,0:T(8,128)(2,1)S(1)}, bf16[36,3584]{1,0:T(8,128)(2,1)}, u32[]{:S(2)}, u32[]{:S(2)}) collective-permute-start(bf16[36,3584]{1,0:T(8,128)(2,1)S(1)} %convolution_convert_fusion.4), channel_id=1, source_target_pairs={{0,24},{8,0},{16,8},{24,16},{1,25},{9,1},{17,9},{25,17},{2,26},{10... | collective-permute-start | bytes 774152 | tf_op jit(solution)/shard_map/rows_z/ppermute | solution.py:14
  12.6 2.6 %collective-permute-start.2 = (bf16[36,3584]{1,0:T(8,128)(2,1)S(1)}, bf16[36,3584]{1,0:T(8,128)(2,1)}, u32[]{:S(2)}, u32[]{:S(2)}) collective-permute-start(bf16[36,3584]{1,0:T(8,128)(2,1)S(1)} %convolution_convert_fusion.4), channel_id=1, source_target_pairs={{0,16},{8,24},{16,0},{24,8},{1,17},{9,25},{17,1},{25,9},{2,18},{10... | collective-permute-start | bytes 774152 | tf_op jit(solution)/shard_map/rows_z/ppermute | solution.py:14
  16.7 8.7 %all-to-all-start = ((bf16[4,224,1152]{2,1,0:T(8,128)(2,1)}), bf16[4,224,1152]{2,1,0:T(8,128)(2,1)}, u32[]{:S(2)}, u32[]{:S(2)}) async-start(bf16[4,224,1152]{2,1,0:T(8,128)(2,1)} %broadcast_in_dim.20), calls=%async_computation | async-start | bytes 4128768 | tf_op jit(solution)/shard_map/dense_weights/all_to_all | solution.py:18
  29.1 2.2 copy.63
  31.3 2.4 %constant_dynamic-slice_fusion.1 = bf16[4,64,896]{1,2,0:T(8,128)(2,1)} fusion(bf16[4,128,896]{1,2,0:T(8,128)(2,1)} %bitcast.89, s32[]{:T(128)S(6)} %select_n.39), kind=kLoop, calls=%fused_computation.87 | loop fusion | bytes 917508 | tf_op jit(solution)/shard_map/dense_tokens/dynamic_slice | solution.py:112
  37.9 7.1 %all-to-all-done = bf16[4,224,1152]{2,1,0:T(8,128)(2,1)} async-done(((bf16[4,224,1152]{2,1,0:T(8,128)(2,1)}), bf16[4,224,1152]{2,1,0:T(8,128)(2,1)}, u32[]{:S(2)}, u32[]{:S(2)}) %all-to-all-start) | async-done | bytes 2064416 | tf_op jit(solution)/shard_map/dense_weights/all_to_all | solution.py:18
  45.1 2.2 copy.68
  47.3 4.1 %all-to-all-start.1 = ((bf16[4,64,896]{2,1,0:T(8,128)(2,1)}), bf16[4,64,896]{2,1,0:T(8,128)(2,1)}, u32[]{:S(2)}, u32[]{:S(2)}) async-start(bf16[4,64,896]{2,1,0:T(8,128)(2,1)} %copy.68), calls=%async_computation.1 | async-start | bytes 917504 | tf_op jit(solution)/shard_map/dense_tokens/all_to_all | solution.py:18
  51.4 4.0 %collective-permute-start.3 = (bf16[72,3584]{1,0:T(8,128)(2,1)}, bf16[72,3584]{1,0:T(8,128)(2,1)}, u32[]{:S(2)}, u32[]{:S(2)}) collective-permute-start(bf16[72,3584]{1,0:T(8,128)(2,1)} %pad_maximum_fusion.3), channel_id=1, source_target_pairs={{0,32},{32,64},{64,96},{96,0},{1,33},{33,65},{65,97},{97,1},{2,34}... | collective-permute-start | bytes 1548296 | tf_op jit(solution)/shard_map/rows_y/ppermute | solution.py:14
  59.3 5.1 %collective-permute-start.5 = (bf16[72,3584]{1,0:T(8,128)(2,1)}, bf16[72,3584]{1,0:T(8,128)(2,1)}, u32[]{:S(2)}, u32[]{:S(2)}) collective-permute-start(bf16[72,3584]{1,0:T(8,128)(2,1)} %pad_maximum_fusion.4), channel_id=1, source_target_pairs={{0,32},{32,64},{64,96},{96,0},{1,33},{33,65},{65,97},{97,1},{2,34}... | collective-permute-start | bytes 1548296 | tf_op jit(solution)/shard_map/rows_y/ppermute | solution.py:14
  64.4 3.2 %collective-permute-done.3 = bf16[72,3584]{1,0:T(8,128)(2,1)} collective-permute-done((bf16[72,3584]{1,0:T(8,128)(2,1)}, bf16[72,3584]{1,0:T(8,128)(2,1)}, u32[]{:S(2)}, u32[]{:S(2)}) %collective-permute-start.3) | collective-permute-done | bytes 516128 | tf_op jit(solution)/shard_map/rows_y/ppermute | solution.py:14
  67.6 4.2 %collective-permute-done.4 = bf16[72,3584]{1,0:T(8,128)(2,1)} collective-permute-done((bf16[72,3584]{1,0:T(8,128)(2,1)}, bf16[72,3584]{1,0:T(8,128)(2,1)}, u32[]{:S(2)}, u32[]{:S(2)}) %collective-permute-start.4) | collective-permute-done | bytes 516128 | tf_op jit(solution)/shard_map/rows_y/ppermute | solution.py:14
  71.8 5.5 %collective-permute-done.6 = bf16[72,3584]{1,0:T(8,128)(2,1)} collective-permute-done((bf16[72,3584]{1,0:T(8,128)(2,1)}, bf16[72,3584]{1,0:T(8,128)(2,1)}, u32[]{:S(2)}, u32[]{:S(2)}) %collective-permute-start.6) | collective-permute-done | bytes 516128 | tf_op jit(solution)/shard_map/rows_y/ppermute | solution.py:14
  81.2 5.1 %collective-permute-start.8 = (bf16[72,3584]{1,0:T(8,128)(2,1)}, bf16[72,3584]{1,0:T(8,128)(2,1)}, u32[]{:S(2)}, u32[]{:S(2)}) collective-permute-start(bf16[72,3584]{1,0:T(8,128)(2,1)} %collective-permute-done.3), channel_id=1, source_target_pairs={{0,32},{32,64},{64,96},{96,0},{1,33},{33,65},{65,97},{97,1},{2,34}... | collective-permute-start | bytes 1548296 | tf_op jit(solution)/shard_map/rows_y/ppermute | solution.py:14
  87.7 3.3 %convolution_convert_fusion.6 = bf16[512,768]{1,0:T(8,128)(2,1)} fusion(bf16[512,896]{1,0:T(8,128)(2,1)S(1)} %bitcast.92, bf16[896,1152]{1,0:T(8,128)(2,1)} %bitcast.10), kind=kOutput, calls=%fused_computation.8 | convolution fusion | flops 705036288 | bytes 3080192 | tf_op jit(solution)/shard_map/dense_tokens/dot_general | solution.py:30
  91.0 4.8 %all-to-all-start.2 = ((bf16[4,128,768]{2,1,0:T(8,128)(2,1)}), bf16[4,128,768]{2,1,0:T(8,128)(2,1)}, u32[]{:S(2)}, u32[]{:S(2)}) async-start(bf16[4,128,768]{2,1,0:T(8,128)(2,1)} %bitcast.94), calls=%async_computation.2 | async-start | bytes 1572864 | tf_op jit(solution)/shard_map/dense_hidden/all_to_all | solution.py:18
  113.6 5.1 %collective-permute-start.9 = (bf16[72,3584]{1,0:T(8,128)(2,1)}, bf16[72,3584]{1,0:T(8,128)(2,1)}, u32[]{:S(2)}, u32[]{:S(2)}) collective-permute-start(bf16[72,3584]{1,0:T(8,128)(2,1)} %convolution_convert_fusion.1), channel_id=1, source_target_pairs={{0,32},{32,64},{64,96},{96,0},{1,33},{33,65},{65,97},{97,1},{2,34}... | collective-permute-start | bytes 1548296 | tf_op jit(solution)/shard_map/partials_y/ppermute | solution.py:14
  123.2 5.1 %collective-permute-start.16 = (bf16[72,3584]{1,0:T(8,128)(2,1)}, bf16[72,3584]{1,0:T(8,128)(2,1)}, u32[]{:S(2)}, u32[]{:S(2)}) collective-permute-start(bf16[72,3584]{1,0:T(8,128)(2,1)} %convolution_convert_fusion.3), channel_id=1, source_target_pairs={{0,32},{32,64},{64,96},{96,0},{1,33},{33,65},{65,97},{97,1},{2,34}... | collective-permute-start | bytes 1548296 | tf_op jit(solution)/shard_map/partials_y/ppermute | solution.py:14
  130.5 5.1 %all-to-all-start.3 = ((bf16[4,128,384]{2,1,0:T(8,128)(2,1)}), bf16[4,128,384]{2,1,0:T(8,128)(2,1)}, u32[]{:S(2)}, u32[]{:S(2)}) async-start(bf16[4,128,384]{2,1,0:T(8,128)(2,1)} %broadcast_in_dim.40), calls=%async_computation.3 | async-start | bytes 786432 | tf_op jit(solution)/shard_map/dense_out/all_to_all | solution.py:18
  135.6 2.4 %add_convert_fusion.1 = bf16[72,3584]{1,0:T(8,128)(2,1)} fusion(f32[72,3584]{1,0:T(8,128)} %fusion.17, bf16[72,3584]{1,0:T(8,128)(2,1)} %collective-permute-done.9), kind=kLoop, calls=%fused_computation.30 | loop fusion | flops 774144 | bytes 2064384 | tf_op jit(solution)/shard_map/partials_y/convert_element_type | solution.py:158
  141.8 4.0 %collective-permute-start.17 = (bf16[72,3584]{1,0:T(8,128)(2,1)}, bf16[72,3584]{1,0:T(8,128)(2,1)}, u32[]{:S(2)}, u32[]{:S(2)}) collective-permute-start(bf16[72,3584]{1,0:T(8,128)(2,1)} %add_convert_fusion), channel_id=1, source_target_pairs={{0,96},{32,0},{64,32},{96,64},{1,97},{33,1},{65,33},{97,65},{2,98}... | collective-permute-start | bytes 1548296 | tf_op jit(solution)/shard_map/partials_y/ppermute | solution.py:14
  151.8 8.3 %all-to-all-start.4 = ((bf16[8,256,224]{1,2,0:T(8,128)(2,1)}), bf16[8,256,224]{1,2,0:T(8,128)(2,1)S(1)}, u32[]{:S(2)}, u32[]{:S(2)}) async-start(bf16[8,256,224]{1,2,0:T(8,128)(2,1)} %copy.70), calls=%async_computation.4 | async-start | bytes 1835008 | tf_op jit(solution)/shard_map/dense_out/all_to_all | solution.py:18
  161.7 5.7 %collective-permute-start.14 = (bf16[36,3584]{1,0:T(8,128)(2,1)S(1)}, bf16[36,3584]{1,0:T(8,128)(2,1)S(1)}, u32[]{:S(2)}, u32[]{:S(2)}) collective-permute-start(bf16[36,3584]{1,0:T(8,128)(2,1)S(1)} %add_convert_fusion.5), channel_id=1, source_target_pairs={{0,24},{8,0},{16,8},{24,16},{1,25},{9,1},{17,9},{25,17},{2,26},{10... | collective-permute-start | bytes 774152 | tf_op jit(solution)/shard_map/partials_z/ppermute | solution.py:14
  170.8 3.9 %all-to-all-done.4 = bf16[8,256,224]{1,2,0:T(8,128)(2,1)S(1)} async-done(((bf16[8,256,224]{1,2,0:T(8,128)(2,1)}), bf16[8,256,224]{1,2,0:T(8,128)(2,1)S(1)}, u32[]{:S(2)}, u32[]{:S(2)}) %all-to-all-start.4) | async-done | bytes 917536 | tf_op jit(solution)/shard_map/dense_out/all_to_all | solution.py:18
  175.6 5.3 %all-to-all-start.5 = ((bf16[4,64,224]{2,1,0:T(8,128)(2,1)}), bf16[4,64,224]{2,1,0:T(8,128)(2,1)S(1)}, u32[]{:S(2)}, u32[]{:S(2)}) async-start(bf16[4,64,224]{2,1,0:T(8,128)(2,1)} %bitcast.20), calls=%async_computation.5 | async-start | bytes 262144 | tf_op jit(solution)/shard_map/dense_out/all_to_all | solution.py:18
  182.3 4.8 %collective-permute-start.19 = (bf16[36,3584]{1,0:T(8,128)(2,1)S(1)}, bf16[36,3584]{1,0:T(8,128)(2,1)S(1)}, u32[]{:S(2)}, u32[]{:S(2)}) collective-permute-start(bf16[36,3584]{1,0:T(8,128)(2,1)S(1)} %add_convert_fusion.3), channel_id=1, source_target_pairs={{0,16},{8,24},{16,0},{24,8},{1,17},{9,25},{17,1},{25,9},{2,18},{10... | collective-permute-start | bytes 774152 | tf_op jit(solution)/shard_map/partials_z/ppermute | solution.py:14
  189.4 10.1 %collective-permute-done.19 = bf16[36,3584]{1,0:T(8,128)(2,1)S(1)} collective-permute-done((bf16[36,3584]{1,0:T(8,128)(2,1)S(1)}, bf16[36,3584]{1,0:T(8,128)(2,1)S(1)}, u32[]{:S(2)}, u32[]{:S(2)}) %collective-permute-start.19) | collective-permute-done | bytes 258080 | tf_op jit(solution)/shard_map/partials_z/ppermute | solution.py:14
  202.0 4.7 %all-to-all-start.6 = ((bf16[8,36,448]{2,1,0:T(8,128)(2,1)}), bf16[8,36,448]{2,1,0:T(8,128)(2,1)S(1)}, u32[]{:S(2)}, u32[]{:S(2)}) async-start(bf16[8,36,448]{2,1,0:T(8,128)(2,1)} %bitcast.86), calls=%async_computation.6 | async-start | bytes 655360 | tf_op jit(solution)/shard_map/combine/all_to_all | solution.py:18
  206.9 8.1 %all-to-all-done.6 = bf16[8,36,448]{2,1,0:T(8,128)(2,1)S(1)} async-done(((bf16[8,36,448]{2,1,0:T(8,128)(2,1)}), bf16[8,36,448]{2,1,0:T(8,128)(2,1)S(1)}, u32[]{:S(2)}, u32[]{:S(2)}) %all-to-all-start.6) | async-done | bytes 258080 | tf_op jit(solution)/shard_map/combine/all_to_all | solution.py:18
  215.7 9.1 %collective-permute-start.20 = (bf16[128,448]{0,1:T(8,128)(2,1)S(1)}, bf16[128,448]{0,1:T(8,128)(2,1)S(1)}, u32[]{:S(2)}, u32[]{:S(2)}) collective-permute-start(bf16[128,448]{0,1:T(8,128)(2,1)S(1)} %fusion.2), channel_id=1, source_target_pairs={{0,128},{128,256},{256,384},{384,0},{1,129},{129,257},{257,385},{3... | collective-permute-start | bytes 344072 | tf_op jit(solution)/shard_map/next_section/ppermute | solution.py:14
  224.8 8.2 %collective-permute-done.20 = bf16[128,448]{0,1:T(8,128)(2,1)S(1)} collective-permute-done((bf16[128,448]{0,1:T(8,128)(2,1)S(1)}, bf16[128,448]{0,1:T(8,128)(2,1)S(1)}, u32[]{:S(2)}, u32[]{:S(2)}) %collective-permute-start.20) | collective-permute-done | bytes 114720 | tf_op jit(solution)/shard_map/next_section/ppermute | solution.py:14
  (121 shorter events, 69.9 us)
Async XLA Ops:
  0.0 103.3 %copy-start = (bf16[1,1,152,3584]{3,2,1,0:T(8,128)(2,1)S(1)}, bf16[1,1,152,3584]{3,2,1,0:T(8,128)(2,1)}, u32[]{:S(2)}) copy-start(bf16[1,1,152,3584]{3,2,1,0:T(8,128)(2,1)} %param.19) | copy-start | bytes 3268612
  0.0 15.1 %copy-start.9 = (bf16[1,224,384]{2,1,0:T(8,128)(2,1)S(1)}, bf16[1,224,384]{2,1,0:T(8,128)(2,1)}, u32[]{:S(2)}) copy-start(bf16[1,224,384]{2,1,0:T(8,128)(2,1)} %param.14) | copy-start | bytes 516100
  0.0 15.1 %copy-start.8 = (bf16[1,224,384]{2,1,0:T(8,128)(2,1)S(1)}, bf16[1,224,384]{2,1,0:T(8,128)(2,1)}, u32[]{:S(2)}) copy-start(bf16[1,224,384]{2,1,0:T(8,128)(2,1)} %param.15) | copy-start | bytes 516100
  0.0 15.1 %copy-start.7 = (bf16[1,224,384]{2,1,0:T(8,128)(2,1)S(1)}, bf16[1,224,384]{2,1,0:T(8,128)(2,1)}, u32[]{:S(2)}) copy-start(bf16[1,224,384]{2,1,0:T(8,128)(2,1)} %param.16) | copy-start | bytes 516100
  4.1 29.6 %collective-permute-start = (bf16[36,3584]{1,0:T(8,128)(2,1)S(1)}, bf16[36,3584]{1,0:T(8,128)(2,1)}, u32[]{:S(2)}, u32[]{:S(2)}) collective-permute-start(bf16[36,3584]{1,0:T(8,128)(2,1)S(1)} %convolution_convert_fusion.4), channel_id=1, source_target_pairs={{0,8},{8,16},{16,24},{24,0},{1,9},{9,17},{17,25},{25,1},{2,10},{10... | collective-permute-start | bytes 774152 | tf_op jit(solution)/shard_map/rows_z/ppermute | solution.py:14
  7.9 27.7 %collective-permute-start.1 = (bf16[36,3584]{1,0:T(8,128)(2,1)S(1)}, bf16[36,3584]{1,0:T(8,128)(2,1)}, u32[]{:S(2)}, u32[]{:S(2)}) collective-permute-start(bf16[36,3584]{1,0:T(8,128)(2,1)S(1)} %convolution_convert_fusion.4), channel_id=1, source_target_pairs={{0,24},{8,0},{16,8},{24,16},{1,25},{9,1},{17,9},{25,17},{2,26},{10... | collective-permute-start | bytes 774152 | tf_op jit(solution)/shard_map/rows_z/ppermute | solution.py:14
  12.6 23.4 %collective-permute-start.2 = (bf16[36,3584]{1,0:T(8,128)(2,1)S(1)}, bf16[36,3584]{1,0:T(8,128)(2,1)}, u32[]{:S(2)}, u32[]{:S(2)}) collective-permute-start(bf16[36,3584]{1,0:T(8,128)(2,1)S(1)} %convolution_convert_fusion.4), channel_id=1, source_target_pairs={{0,16},{8,24},{16,0},{24,8},{1,17},{9,25},{17,1},{25,9},{2,18},{10... | collective-permute-start | bytes 774152 | tf_op jit(solution)/shard_map/rows_z/ppermute | solution.py:14
  16.7 28.4 %all-to-all-start = ((bf16[4,224,1152]{2,1,0:T(8,128)(2,1)}), bf16[4,224,1152]{2,1,0:T(8,128)(2,1)}, u32[]{:S(2)}, u32[]{:S(2)}) async-start(bf16[4,224,1152]{2,1,0:T(8,128)(2,1)} %broadcast_in_dim.20), calls=%async_computation | async-start | bytes 4128768 | tf_op jit(solution)/shard_map/dense_weights/all_to_all | solution.py:18
  47.3 30.1 %all-to-all-start.1 = ((bf16[4,64,896]{2,1,0:T(8,128)(2,1)}), bf16[4,64,896]{2,1,0:T(8,128)(2,1)}, u32[]{:S(2)}, u32[]{:S(2)}) async-start(bf16[4,64,896]{2,1,0:T(8,128)(2,1)} %copy.68), calls=%async_computation.1 | async-start | bytes 917504 | tf_op jit(solution)/shard_map/dense_tokens/all_to_all | solution.py:18
  51.4 16.2 %collective-permute-start.3 = (bf16[72,3584]{1,0:T(8,128)(2,1)}, bf16[72,3584]{1,0:T(8,128)(2,1)}, u32[]{:S(2)}, u32[]{:S(2)}) collective-permute-start(bf16[72,3584]{1,0:T(8,128)(2,1)} %pad_maximum_fusion.3), channel_id=1, source_target_pairs={{0,32},{32,64},{64,96},{96,0},{1,33},{33,65},{65,97},{97,1},{2,34}... | collective-permute-start | bytes 1548296 | tf_op jit(solution)/shard_map/rows_y/ppermute | solution.py:14
  55.4 16.4 %collective-permute-start.4 = (bf16[72,3584]{1,0:T(8,128)(2,1)}, bf16[72,3584]{1,0:T(8,128)(2,1)}, u32[]{:S(2)}, u32[]{:S(2)}) collective-permute-start(bf16[72,3584]{1,0:T(8,128)(2,1)} %pad_maximum_fusion.3), channel_id=1, source_target_pairs={{0,96},{32,0},{64,32},{96,64},{1,97},{33,1},{65,33},{97,65},{2,98}... | collective-permute-start | bytes 1548296 | tf_op jit(solution)/shard_map/rows_y/ppermute | solution.py:14
  57.3 20.0 %collective-permute-start.6 = (bf16[72,3584]{1,0:T(8,128)(2,1)}, bf16[72,3584]{1,0:T(8,128)(2,1)}, u32[]{:S(2)}, u32[]{:S(2)}) collective-permute-start(bf16[72,3584]{1,0:T(8,128)(2,1)} %pad_maximum_fusion.4), channel_id=1, source_target_pairs={{0,96},{32,0},{64,32},{96,64},{1,97},{33,1},{65,33},{97,65},{2,98}... | collective-permute-start | bytes 1548296 | tf_op jit(solution)/shard_map/rows_y/ppermute | solution.py:14
  59.3 18.1 %collective-permute-start.5 = (bf16[72,3584]{1,0:T(8,128)(2,1)}, bf16[72,3584]{1,0:T(8,128)(2,1)}, u32[]{:S(2)}, u32[]{:S(2)}) collective-permute-start(bf16[72,3584]{1,0:T(8,128)(2,1)} %pad_maximum_fusion.4), channel_id=1, source_target_pairs={{0,32},{32,64},{64,96},{96,0},{1,33},{33,65},{65,97},{97,1},{2,34}... | collective-permute-start | bytes 1548296 | tf_op jit(solution)/shard_map/rows_y/ppermute | solution.py:14
  77.4 9.0 %collective-permute-start.7 = (bf16[4,64,896]{2,1,0:T(8,128)(2,1)}, bf16[4,64,896]{2,1,0:T(8,128)(2,1)}, u32[]{:S(2)}, u32[]{:S(2)}) collective-permute-start(bf16[4,64,896]{2,1,0:T(8,128)(2,1)} %all-to-all-done.1), channel_id=1, source_target_pairs={{0,1},{1,0},{2,3},{3,2},{4,5},{5,4},{6,7},{7,6},{8,9},{9,8},{10,11... | collective-permute-start | bytes 1376264 | tf_op jit(solution)/shard_map/dense_tokens/ppermute | solution.py:14
  79.3 26.3 %collective-permute-start.10 = (bf16[72,3584]{1,0:T(8,128)(2,1)}, bf16[72,3584]{1,0:T(8,128)(2,1)}, u32[]{:S(2)}, u32[]{:S(2)}) collective-permute-start(bf16[72,3584]{1,0:T(8,128)(2,1)} %collective-permute-done.6), channel_id=1, source_target_pairs={{0,96},{32,0},{64,32},{96,64},{1,97},{33,1},{65,33},{97,65},{2,98}... | collective-permute-start | bytes 1548296 | tf_op jit(solution)/shard_map/rows_y/ppermute | solution.py:14
  81.2 29.3 %collective-permute-start.8 = (bf16[72,3584]{1,0:T(8,128)(2,1)}, bf16[72,3584]{1,0:T(8,128)(2,1)}, u32[]{:S(2)}, u32[]{:S(2)}) collective-permute-start(bf16[72,3584]{1,0:T(8,128)(2,1)} %collective-permute-done.3), channel_id=1, source_target_pairs={{0,32},{32,64},{64,96},{96,0},{1,33},{33,65},{65,97},{97,1},{2,34}... | collective-permute-start | bytes 1548296 | tf_op jit(solution)/shard_map/rows_y/ppermute | solution.py:14
  91.0 37.3 %all-to-all-start.2 = ((bf16[4,128,768]{2,1,0:T(8,128)(2,1)}), bf16[4,128,768]{2,1,0:T(8,128)(2,1)}, u32[]{:S(2)}, u32[]{:S(2)}) async-start(bf16[4,128,768]{2,1,0:T(8,128)(2,1)} %bitcast.94), calls=%async_computation.2 | async-start | bytes 1572864 | tf_op jit(solution)/shard_map/dense_hidden/all_to_all | solution.py:18
  108.6 26.9 %collective-permute-start.11 = (bf16[72,3584]{1,0:T(8,128)(2,1)}, bf16[72,3584]{1,0:T(8,128)(2,1)}, u32[]{:S(2)}, u32[]{:S(2)}) collective-permute-start(bf16[72,3584]{1,0:T(8,128)(2,1)} %convolution_convert_fusion), channel_id=1, source_target_pairs={{0,96},{32,0},{64,32},{96,64},{1,97},{33,1},{65,33},{97,65},{2,98}... | collective-permute-start | bytes 1548296 | tf_op jit(solution)/shard_map/partials_y/ppermute | solution.py:14
  113.6 22.0 %collective-permute-start.9 = (bf16[72,3584]{1,0:T(8,128)(2,1)}, bf16[72,3584]{1,0:T(8,128)(2,1)}, u32[]{:S(2)}, u32[]{:S(2)}) collective-permute-start(bf16[72,3584]{1,0:T(8,128)(2,1)} %convolution_convert_fusion.1), channel_id=1, source_target_pairs={{0,32},{32,64},{64,96},{96,0},{1,33},{33,65},{65,97},{97,1},{2,34}... | collective-permute-start | bytes 1548296 | tf_op jit(solution)/shard_map/partials_y/ppermute | solution.py:14
  121.3 39.1 %collective-permute-start.13 = (bf16[72,3584]{1,0:T(8,128)(2,1)}, bf16[72,3584]{1,0:T(8,128)(2,1)}, u32[]{:S(2)}, u32[]{:S(2)}) collective-permute-start(bf16[72,3584]{1,0:T(8,128)(2,1)} %convolution_convert_fusion.2), channel_id=1, source_target_pairs={{0,96},{32,0},{64,32},{96,64},{1,97},{33,1},{65,33},{97,65},{2,98}... | collective-permute-start | bytes 1548296 | tf_op jit(solution)/shard_map/partials_y/ppermute | solution.py:14
  123.2 44.3 %collective-permute-start.16 = (bf16[72,3584]{1,0:T(8,128)(2,1)}, bf16[72,3584]{1,0:T(8,128)(2,1)}, u32[]{:S(2)}, u32[]{:S(2)}) collective-permute-start(bf16[72,3584]{1,0:T(8,128)(2,1)} %convolution_convert_fusion.3), channel_id=1, source_target_pairs={{0,32},{32,64},{64,96},{96,0},{1,33},{33,65},{65,97},{97,1},{2,34}... | collective-permute-start | bytes 1548296 | tf_op jit(solution)/shard_map/partials_y/ppermute | solution.py:14
  130.5 17.1 %all-to-all-start.3 = ((bf16[4,128,384]{2,1,0:T(8,128)(2,1)}), bf16[4,128,384]{2,1,0:T(8,128)(2,1)}, u32[]{:S(2)}, u32[]{:S(2)}) async-start(bf16[4,128,384]{2,1,0:T(8,128)(2,1)} %broadcast_in_dim.40), calls=%async_computation.3 | async-start | bytes 786432 | tf_op jit(solution)/shard_map/dense_out/all_to_all | solution.py:18
  137.9 22.4 %collective-permute-start.12 = (bf16[72,3584]{1,0:T(8,128)(2,1)}, bf16[72,3584]{1,0:T(8,128)(2,1)}, u32[]{:S(2)}, u32[]{:S(2)}) collective-permute-start(bf16[72,3584]{1,0:T(8,128)(2,1)} %add_convert_fusion.1), channel_id=1, source_target_pairs={{0,32},{32,64},{64,96},{96,0},{1,33},{33,65},{65,97},{97,1},{2,34}... | collective-permute-start | bytes 1548296 | tf_op jit(solution)/shard_map/partials_y/ppermute | solution.py:14
  141.8 25.7 %collective-permute-start.17 = (bf16[72,3584]{1,0:T(8,128)(2,1)}, bf16[72,3584]{1,0:T(8,128)(2,1)}, u32[]{:S(2)}, u32[]{:S(2)}) collective-permute-start(bf16[72,3584]{1,0:T(8,128)(2,1)} %add_convert_fusion), channel_id=1, source_target_pairs={{0,96},{32,0},{64,32},{96,64},{1,97},{33,1},{65,33},{97,65},{2,98}... | collective-permute-start | bytes 1548296 | tf_op jit(solution)/shard_map/partials_y/ppermute | solution.py:14
  151.8 22.9 %all-to-all-start.4 = ((bf16[8,256,224]{1,2,0:T(8,128)(2,1)}), bf16[8,256,224]{1,2,0:T(8,128)(2,1)S(1)}, u32[]{:S(2)}, u32[]{:S(2)}) async-start(bf16[8,256,224]{1,2,0:T(8,128)(2,1)} %copy.70), calls=%async_computation.4 | async-start | bytes 1835008 | tf_op jit(solution)/shard_map/dense_out/all_to_all | solution.py:18
  161.7 13.1 %collective-permute-start.14 = (bf16[36,3584]{1,0:T(8,128)(2,1)S(1)}, bf16[36,3584]{1,0:T(8,128)(2,1)S(1)}, u32[]{:S(2)}, u32[]{:S(2)}) collective-permute-start(bf16[36,3584]{1,0:T(8,128)(2,1)S(1)} %add_convert_fusion.5), channel_id=1, source_target_pairs={{0,24},{8,0},{16,8},{24,16},{1,25},{9,1},{17,9},{25,17},{2,26},{10... | collective-permute-start | bytes 774152 | tf_op jit(solution)/shard_map/partials_z/ppermute | solution.py:14
  168.9 20.6 %collective-permute-start.18 = (bf16[36,3584]{1,0:T(8,128)(2,1)S(1)}, bf16[36,3584]{1,0:T(8,128)(2,1)S(1)}, u32[]{:S(2)}, u32[]{:S(2)}) collective-permute-start(bf16[36,3584]{1,0:T(8,128)(2,1)S(1)} %add_convert_fusion.4), channel_id=1, source_target_pairs={{0,8},{8,16},{16,24},{24,0},{1,9},{9,17},{17,25},{25,1},{2,10},{10... | collective-permute-start | bytes 774152 | tf_op jit(solution)/shard_map/partials_z/ppermute | solution.py:14
  175.6 11.9 %all-to-all-start.5 = ((bf16[4,64,224]{2,1,0:T(8,128)(2,1)}), bf16[4,64,224]{2,1,0:T(8,128)(2,1)S(1)}, u32[]{:S(2)}, u32[]{:S(2)}) async-start(bf16[4,64,224]{2,1,0:T(8,128)(2,1)} %bitcast.20), calls=%async_computation.5 | async-start | bytes 262144 | tf_op jit(solution)/shard_map/dense_out/all_to_all | solution.py:18
  182.3 17.2 %collective-permute-start.19 = (bf16[36,3584]{1,0:T(8,128)(2,1)S(1)}, bf16[36,3584]{1,0:T(8,128)(2,1)S(1)}, u32[]{:S(2)}, u32[]{:S(2)}) collective-permute-start(bf16[36,3584]{1,0:T(8,128)(2,1)S(1)} %add_convert_fusion.3), channel_id=1, source_target_pairs={{0,16},{8,24},{16,0},{24,8},{1,17},{9,25},{17,1},{25,9},{2,18},{10... | collective-permute-start | bytes 774152 | tf_op jit(solution)/shard_map/partials_z/ppermute | solution.py:14
  187.5 19.2 %collective-permute-start.15 = (bf16[2,64,224]{2,1,0:T(8,128)(2,1)S(1)}, bf16[2,64,224]{2,1,0:T(8,128)(2,1)S(1)}, u32[]{:S(2)}, u32[]{:S(2)}) collective-permute-start(bf16[2,64,224]{2,1,0:T(8,128)(2,1)S(1)} %constant_dynamic-slice_fusion), channel_id=1, source_target_pairs={{0,1},{1,0},{2,3},{3,2},{4,5},{5,4},{6,7},{7,6},{8,9},{9,8},{10,11... | collective-permute-start | bytes 172040 | tf_op jit(solution)/shard_map/dense_out/ppermute | solution.py:14
  202.0 12.9 %all-to-all-start.6 = ((bf16[8,36,448]{2,1,0:T(8,128)(2,1)}), bf16[8,36,448]{2,1,0:T(8,128)(2,1)S(1)}, u32[]{:S(2)}, u32[]{:S(2)}) async-start(bf16[8,36,448]{2,1,0:T(8,128)(2,1)} %bitcast.86), calls=%async_computation.6 | async-start | bytes 655360 | tf_op jit(solution)/shard_map/combine/all_to_all | solution.py:18
  215.7 17.3 %collective-permute-start.20 = (bf16[128,448]{0,1:T(8,128)(2,1)S(1)}, bf16[128,448]{0,1:T(8,128)(2,1)S(1)}, u32[]{:S(2)}, u32[]{:S(2)}) collective-permute-start(bf16[128,448]{0,1:T(8,128)(2,1)S(1)} %fusion.2), channel_id=1, source_target_pairs={{0,128},{128,256},{256,384},{384,0},{1,129},{129,257},{257,385},{3... | collective-permute-start | bytes 344072 | tf_op jit(solution)/shard_map/next_section/ppermute | solution.py:14
  (11 other events, 89.3 us)

commit v6 on v5

v6 whole, which is shorter than its diff:
```python
import functools

import jax
import jax.numpy as jnp
from jax import lax
from jax.experimental import pallas as pl
from jax.experimental.pallas import tpu as pltpu
from jax.sharding import Mesh, PartitionSpec as P

AXES = ("section", "y", "z", "x", "core")
GRID = (4, 4, 4, 4, 2)
EXPERT_AXES = ("x", "core")
BF16, F32 = jnp.bfloat16, jnp.float32


def shifted(x, axis, by):
    peers = lax.axis_size(axis)
    return lax.ppermute(x, axis, [(i, (i + by) % peers) for i in range(peers)])


def exchanged(x, axes):
    return lax.all_to_all(x, axes, split_axis=0, concat_axis=0, tiled=True)


def repeated(x, times):
    return jnp.broadcast_to(x[None], (times,) + x.shape)


def after(x, *others):
    return lax.optimization_barrier((x,) + others)[0]


def swiglu(first, second):
    return (jax.nn.silu(first) * second).astype(BF16)


def dot(a, b):
    return jnp.dot(a, b, preferred_element_type=F32)


def slots_of(picks, n_expert):
    labels = jnp.arange(n_expert, dtype=jnp.int32)
    named = (picks[:, :, None] == labels[None, None, :]).astype(jnp.int32)
    per_token = jnp.sum(named, axis=1, dtype=jnp.int32)
    earlier = jnp.cumsum(per_token, axis=0, dtype=jnp.int32) - per_token
    return jnp.sum(named * earlier[:, None, :], axis=2, dtype=jnp.int32)


def local_call(kernel, out_shape, **kwargs):
    return pl.pallas_call(
        kernel,
        out_shape=out_shape,
        compiler_params=pltpu.CompilerParams(vmem_limit_bytes=52 * 1024 * 1024),
        cost_estimate=pl.CostEstimate(
            flops=2 * 1024**3, bytes_accessed=4 * 1024**2, transcendentals=0
        ),
        **kwargs,
    )


def expert_rows(parts, gate_up, down):
    inner = down.shape[0]
    rows = jnp.concatenate([part[...].astype(F32) for part in parts], axis=0).astype(BF16)
    both = dot(rows, gate_up[...])
    start = both.shape[1] // 2
    first, second = both[:, :inner], both[:, start : start + inner]
    return dot((first / (1.0 + jnp.exp(-first)) * second).astype(BF16), down[...])


def rows_kernel(gate_up, down, *refs):
    parts, outs = refs[: len(refs) // 2], refs[len(refs) // 2 :]
    result = expert_rows(parts, gate_up, down)
    size = parts[0].shape[0]
    for k, out in enumerate(outs):
        out[...] = result[k * size : (k + 1) * size].astype(out.dtype)


def rows_and_dense_kernel(columns, place, own, other, *refs):
    weights, pre = refs[:4], refs[-1]
    joined = jnp.concatenate([part[:, :columns] for part in weights], axis=0)
    for z in range(4):
        shares = [side[k, z] for side in (own, other) for k in range(4)]
        size = shares[0].shape[0]
        result = dot(jnp.concatenate(shares, axis=0), joined).astype(BF16)
        for i in range(len(shares)):
            start = pl.multiple_of(place[i] * size, size)
            pre[z, pl.ds(start, size)] = result[i * size : (i + 1) * size]
    rows_kernel(*refs[4:-1])


def late_kernel(part, relay, out):
    out[...] = (part[...] + relay[...].astype(F32)).astype(BF16)


def total_kernel(capacity, place, low, high, *refs):
    sums, outs, whole = refs[:4], refs[4:8], refs[8]
    half = 2 * capacity
    whole[:half] = low[...] + sums[0][...].astype(F32) + sums[1][...].astype(F32)
    whole[half:] = high[...] + sums[2][...].astype(F32) + sums[3][...].astype(F32)
    for k, out in enumerate(outs):
        for j in range(4):

            @pl.when(place[k] == j)
            def _(out=out, j=j):
                out[...] = whole[j * capacity : (j + 1) * capacity].astype(out.dtype)


def in_line_order(parts, axis):
    order = (lax.axis_index(axis) - jnp.arange(4, dtype=jnp.int32)) % 4
    return jnp.stack(parts).at[order].get(mode="promise_in_bounds")


def dense_out_kernel(columns, place, act, *refs):
    weights, out = refs[:4], refs[4]
    contract = (((1,), (1,)), ((), ()))
    for k in range(4):
        part = lax.dot_general(
            act[...], weights[k][:, columns:], contract, preferred_element_type=F32
        ).astype(BF16)
        half = part.shape[0] // 8
        for side in range(2):
            pieces = [part[(2 * j + side) * half : (2 * j + side + 1) * half] for j in range(4)]
            out[2 * place[k] + side] = jnp.concatenate(pieces, axis=0)


def body(
    normed,
    residual,
    expert_index,
    pick_weight,
    dense_gate,
    dense_up,
    dense_down,
    expert_gate,
    expert_up,
    expert_down,
):
    tokens = normed[0]
    picks = expert_index[0]
    weights = pick_weight[0]
    tok_rows, width = tokens.shape
    n_expert = 8
    capacity = min(tok_rows, 9 * tok_rows // (4 * n_expert))
    core = lax.axis_index("core")
    mine = lax.axis_index("x") * 2 + core
    hidden = dense_gate.shape[2]
    slab = width // 4
    step = dense_gate.shape[1]
    piece = width // n_expert

    with jax.named_scope("dispatch"):
        slot = slots_of(picks, n_expert)
        is_mine = picks == mine
        positions = jnp.arange(capacity, dtype=jnp.int32)
        select = jnp.any(
            (positions[:, None, None] == slot[None, :, :]) & is_mine[None, :, :], axis=2
        ).astype(BF16)
        routed = dot(select, tokens).astype(BF16)

    with jax.named_scope("dense_weights"):
        stacked = jnp.concatenate([dense_gate[0], dense_up[0], dense_down[0]], axis=1)
        stacked = after(stacked, routed)
        slabs = [stacked] + [shifted(stacked, "y", by) for by in (1, 2, 3)]
        steps_back = jnp.arange(4, dtype=jnp.int32)
        place_y, place_z = ((lax.axis_index(axis) - steps_back) % 4 for axis in ("y", "z"))

    with jax.named_scope("combine"):
        target = picks * capacity + slot
        columns = jnp.arange(n_expert * capacity, dtype=jnp.int32)
        chosen = jnp.where(columns[None, None, :] == target[:, :, None], weights[:, :, None], 0.0)
        combine = jnp.sum(chosen, axis=1)
        coarse = lax.reduce_precision(combine, 8, 7)
        fine = lax.reduce_precision(combine - coarse, 8, 7)
        coarse, fine = coarse.astype(BF16), fine.astype(BF16)

    down = expert_down[0, 0]
    blank = jnp.zeros((width, -down.shape[0] % 256), BF16)
    gate_up = jnp.concatenate([expert_gate[0, 0], blank, expert_up[0, 0], blank], axis=1)

    half = 2 * capacity
    with jax.named_scope("rows_z"):
        share = tok_rows // n_expert
        own_share = lax.dynamic_slice_in_dim(tokens, mine * share, share, axis=0)
        own_share = own_share.reshape(share, 4, 4, step)
        own_share = own_share.at[:, place_y].get(mode="promise_in_bounds").transpose(2, 0, 1, 3)
        sent = [repeated(routed, 4), own_share.reshape(4, share // 4, width)]
        arrived = exchanged(jnp.concatenate(sent, axis=1), "z")
        line_share = arrived[:, capacity:].reshape(4, share, slab)
        coarse, fine, gate_up = after((coarse, fine, gate_up), routed)
        group = after(arrived, coarse, fine, gate_up, *slabs[1:])[:, :capacity]
        low, high = (block.reshape(half, width) for block in (group[:2], group[2:]))

    with jax.named_scope("rows_y"):
        prev_low, next_low = shifted(low, "y", 1), shifted(low, "y", -1)
        far_low = shifted(prev_low, "y", 1)
        next_high, prev_high = shifted(high, "y", -1), shifted(high, "y", 1)
        far_high = shifted(next_high, "y", -1)

    with jax.named_scope("dense_tokens"):
        own_shares = jnp.stack([line_share] + [shifted(line_share, "x", by) for by in (1, 2, 3)])
        other_shares = shifted(own_shares, "core", 1)
        place_x = (lax.axis_index("x") - steps_back) % 4
        place_share = jnp.concatenate([2 * place_x + core, 2 * place_x + 1 - core])

    half_bf16, half_f32 = (jax.ShapeDtypeStruct(low.shape, dtype) for dtype in (BF16, F32))
    in_smem, in_vmem = (pl.BlockSpec(memory_space=space) for space in (pltpu.SMEM, pltpu.VMEM))
    with jax.named_scope("experts"):
        relay_next, relay_prev, early_next, early_prev, next_part, prev_part, pre = local_call(
            functools.partial(rows_and_dense_kernel, 2 * hidden),
            [half_bf16] * 4
            + [half_f32] * 2
            + [jax.ShapeDtypeStruct((4, tok_rows, 2 * hidden), BF16)],
            in_specs=[in_smem] + [in_vmem] * 14,
        )(
            place_share,
            own_shares,
            other_shares,
            *slabs,
            gate_up,
            down,
            *(far_low, far_high, next_high, prev_low, next_low, prev_high),
        )

    with jax.named_scope("dense_hidden"):
        pre = exchanged(pre, "z")
        pre = jnp.sum(pre.astype(F32), axis=0)
        act = swiglu(pre[:, :hidden], pre[:, hidden:])
        line_act = jnp.broadcast_to(act[None], (4,) + act.shape)
    with jax.named_scope("dense_out"):
        half_tokens = tok_rows // 2
        every_act = exchanged(line_act, "z").reshape(4 * tok_rows, hidden)
        by_block = local_call(
            functools.partial(dense_out_kernel, 2 * hidden),
            jax.ShapeDtypeStruct((n_expert, 4 * half_tokens, step), BF16),
            in_specs=[in_smem] + [in_vmem] * 5,
        )(place_y, every_act, *slabs)

    with jax.named_scope("partials_y"):
        relay_next, relay_prev = shifted(relay_next, "y", 1), shifted(relay_prev, "y", -1)
        early_next, early_prev = shifted(early_next, "y", 1), shifted(early_prev, "y", -1)
        late_next = local_call(late_kernel, half_bf16)(next_part, relay_next)
        late_prev = local_call(late_kernel, half_bf16)(prev_part, relay_prev)
        own_low, own_high = local_call(rows_kernel, [half_f32] * 2)(
            after(gate_up, late_next, late_prev), down, low, high
        )
        late_next, late_prev = shifted(late_next, "y", 1), shifted(late_prev, "y", -1)

    with jax.named_scope("partials_z"):
        rows_f32, rows_bf16 = (jax.ShapeDtypeStruct(routed.shape, dtype) for dtype in (F32, BF16))
        kept_rows, *sent = local_call(
            functools.partial(total_kernel, capacity),
            [rows_f32] + [rows_bf16] * 3,
            in_specs=[in_smem] + [in_vmem] * 6,
            scratch_shapes=[pltpu.VMEM((4 * capacity, width), F32)],
        )(place_z, own_low, own_high, late_next, early_prev, early_next, late_prev)
        recv = [shifted(part, "z", by) for part, by in zip(sent, (-1, -2, -3))]
        expert_out = (kept_rows + sum(part.astype(F32) for part in recv)).astype(BF16)

    with jax.named_scope("dense_out"):
        block_sum = jnp.sum(exchanged(by_block, EXPERT_AXES).astype(F32), axis=0).astype(BF16)
        block_sum = block_sum.reshape(4, half_tokens, step)
        blocks = []
        for by in range(4):
            there = (lax.axis_index("z") + by) % 4
            block = lax.dynamic_index_in_dim(block_sum, there, 0, keepdims=False)
            blocks.append(shifted(block, "z", by) if by else block)
        blocks = in_line_order(blocks, "z")
        kept = lax.dynamic_slice_in_dim(blocks, 2 * core, 2, axis=0)
        given = lax.dynamic_slice_in_dim(blocks, 2 - 2 * core, 2, axis=0)
        taken = shifted(given, "core", 1)
        first = jnp.where(core == 0, kept, taken)
        second = jnp.where(core == 0, taken, kept)
        dense_total = jnp.concatenate([first, second], axis=1).transpose(1, 0, 2)
    base = residual[0].astype(F32) + dense_total.reshape(tok_rows, piece).astype(F32)

    with jax.named_scope("combine"):
        by_feature = expert_out.reshape(capacity, n_expert, piece).transpose(1, 0, 2)
        returned = exchanged(by_feature, EXPERT_AXES).reshape(n_expert * capacity, piece)
        spread = dot(coarse, returned) + dot(fine, returned)
        mixed = (base + spread).astype(BF16)
    with jax.named_scope("next_section"):
        return shifted(mixed, "section", 1)[None]


def solution(mesh):
    fine_mesh = Mesh(mesh.devices.reshape(GRID), AXES)
    data = ("y", "z")
    placed = (
        P("section", data, None),
        P("section", data, EXPERT_AXES),
        P("section", data, None),
        P("section", data, None),
        P("section", data, EXPERT_AXES),
        P("section", data, EXPERT_AXES),
        P("section", data, EXPERT_AXES),
        P("section", EXPERT_AXES, None, data),
        P("section", EXPERT_AXES, None, data),
        P("section", EXPERT_AXES, data, None),
    )
    return jax.shard_map(
        body,
        mesh=fine_mesh,
        in_specs=placed,
        out_specs=P("section", data, EXPERT_AXES),
        check_vma=False,
    )
```

time: 237 us -> 239 us (level)
  the two profiles are of different devices: /device:TPU:24 before, /device:TPU:99 now
where the time goes in v6:
time: 239 us; the launch traced here: 237 us
  starting transfers between devices  121 us (51%)
  waiting for transfers between devices  57 us (24%)
  Pallas kernels  24 us (10%)
  local copies, waits for them, and re-layouts  21.9 us (9%)
  other arithmetic  12.4 us (5%)
    ppermute x27, starting transfers between devices, shifted(): return lax.ppermute(x, axis, [(i, (i + by) % peers) for i in range(peers)])  91.8 us
    ppermute x27, waiting for transfers between devices, shifted(): return lax.ppermute(x, axis, [(i, (i + by) % peers) for i in range(peers)])  43.2 us
    all_to_all x5, starting transfers between devices, exchanged(): return lax.all_to_all(x, axes, split_axis=0, concat_axis=0, tiled=True)  28.7 us
    all_to_all x5, waiting for transfers between devices, exchanged(): return lax.all_to_all(x, axes, split_axis=0, concat_axis=0, tiled=True)  13.8 us
    unnamed x49, local copies, waits for them, and re-layouts  10.6 us
    pallas_call x1, Pallas kernels, body(): local_call(functools.partial(rows_and_dense_kernel, 2 * hidden), [half_bf...  9.05 us
    concatenate x1, other arithmetic, body(): jnp.concatenate([expert_gate[0, 0], blank, expert_up[0, 0], blank], axis=1)  5.07 us
    pallas_call x1, Pallas kernels, body(): local_call(rows_kernel, [half_f32] * 2)  4.81 us
  transfers between devices with their start and end apart: 32, of which 13 were waited for; matrix products, arithmetic and copies ran while one was open for 9% of the time, Pallas kernels for 6%

profile of v6, /device:TPU:99, one launch (start us, length us, event | category | flops | bytes accessed | tf_op | source)
XLA Modules:
  0.0 237.5 jit_solution(14249008316767046417)
XLA Ops:
  6.5 4.5 %all-to-all-start = ((bf16[4,40,3584]{2,1,0:T(8,128)(2,1)}), bf16[4,40,3584]{2,1,0:T(8,128)(2,1)}, u32[]{:S(2)}, u32[]{:S(2)}) async-start(bf16[4,40,3584]{2,1,0:T(8,128)(2,1)} %pad_maximum_fusion.1), calls=%async_computation | async-start | bytes 2293760 | tf_op jit(solution)/shard_map/rows_z/all_to_all | solution.py:22
  11.1 3.3 %collective-permute-start.4 = (bf16[224,1152]{1,0:T(8,128)(2,1)S(1)}, bf16[224,1152]{1,0:T(8,128)(2,1)S(1)}, u32[]{:S(2)}, u32[]{:S(2)}) collective-permute-start(bf16[224,1152]{1,0:T(8,128)(2,1)S(1)} %pad_maximum_fusion.2.refs_0_), channel_id=1, source_target_pairs={{0,32},{32,64},{64,96},{96,0},{1,33},{33,65},{65,97},{97,1},{2,34}... | collective-permute-start | bytes 1548296 | tf_op jit(solution)/shard_map/dense_weights/ppermute | solution.py:18
  14.5 4.5 %collective-permute-start.5 = (bf16[224,1152]{1,0:T(8,128)(2,1)S(1)}, bf16[224,1152]{1,0:T(8,128)(2,1)S(1)}, u32[]{:S(2)}, u32[]{:S(2)}) collective-permute-start(bf16[224,1152]{1,0:T(8,128)(2,1)S(1)} %pad_maximum_fusion.2.refs_0_), channel_id=1, source_target_pairs={{0,64},{32,96},{64,0},{96,32},{1,65},{33,97},{65,1},{97,33},{2,66}... | collective-permute-start | bytes 1548296 | tf_op jit(solution)/shard_map/dense_weights/ppermute | solution.py:18
  19.0 3.0 %collective-permute-start.6 = (bf16[224,1152]{1,0:T(8,128)(2,1)S(1)}, bf16[224,1152]{1,0:T(8,128)(2,1)S(1)}, u32[]{:S(2)}, u32[]{:S(2)}) collective-permute-start(bf16[224,1152]{1,0:T(8,128)(2,1)S(1)} %pad_maximum_fusion.2.refs_0_), channel_id=1, source_target_pairs={{0,96},{32,0},{64,32},{96,64},{1,97},{33,1},{65,33},{97,65},{2,98}... | collective-permute-start | bytes 1548296 | tf_op jit(solution)/shard_map/dense_weights/ppermute | solution.py:18
  28.1 5.1 %pad_maximum_fusion.refs_4_.gate_up = bf16[3584,512]{1,0:T(8,128)(2,1)} fusion(bf16[3584,104]{1,0:T(8,128)(2,1)S(1)} %broadcast_in_dim.26, bf16[3584,152]{1,0:T(8,128)(2,1)} %bitcast.50, bf16[3584,152]{1,0:T(8,128)(2,1)} %bitcast.49), kind=kLoop, calls=%fused_computation.3 | loop fusion | flops 14680064 | bytes 6594560 | tf_op jit(solution)/shard_map/concatenate | solution.py:178
  33.2 5.5 %collective-permute-done.5.refs_2_ = bf16[224,1152]{1,0:T(8,128)(2,1)S(1)} collective-permute-done((bf16[224,1152]{1,0:T(8,128)(2,1)S(1)}, bf16[224,1152]{1,0:T(8,128)(2,1)S(1)}, u32[]{:S(2)}, u32[]{:S(2)}) %collective-permute-start.5) | collective-permute-done | bytes 516128 | tf_op jit(solution)/shard_map/dense_weights/ppermute | solution.py:18
  44.8 5.3 %collective-permute-start.9 = (bf16[72,3584]{1,0:T(8,128)(2,1)S(1)}, bf16[72,3584]{1,0:T(8,128)(2,1)}, u32[]{:S(2)}, u32[]{:S(2)}) collective-permute-start(bf16[72,3584]{1,0:T(8,128)(2,1)S(1)} %reshape.162.refs_1_), channel_id=1, source_target_pairs={{0,96},{32,0},{64,32},{96,64},{1,97},{33,1},{65,33},{97,65},{2,98}... | collective-permute-start | bytes 1548296 | tf_op jit(solution)/shard_map/rows_y/ppermute | solution.py:18
  53.2 3.1 %collective-permute-start = (bf16[4,16,896]{2,1,0:T(8,128)(2,1)S(1)}, bf16[4,16,896]{2,1,0:T(8,128)(2,1)S(1)}, u32[]{:S(2)}, u32[]{:S(2)}) collective-permute-start(bf16[4,16,896]{2,1,0:T(8,128)(2,1)S(1)} %reshape.160), channel_id=1, source_target_pairs={{0,2},{2,4},{4,6},{6,0},{1,3},{3,5},{5,7},{7,1},{8,10},{10,12},{12... | collective-permute-start | bytes 344072 | tf_op jit(solution)/shard_map/dense_tokens/ppermute | solution.py:18
  59.0 3.9 %collective-permute-start.2 = (bf16[4,16,896]{2,1,0:T(8,128)(2,1)S(1)}, bf16[4,16,896]{2,1,0:T(8,128)(2,1)S(1)}, u32[]{:S(2)}, u32[]{:S(2)}) collective-permute-start(bf16[4,16,896]{2,1,0:T(8,128)(2,1)S(1)} %reshape.160), channel_id=1, source_target_pairs={{0,6},{2,0},{4,2},{6,4},{1,7},{3,1},{5,3},{7,5},{8,14},{10,8},{12,... | collective-permute-start | bytes 344072 | tf_op jit(solution)/shard_map/dense_tokens/ppermute | solution.py:18
  63.0 4.6 %collective-permute-start.11 = (bf16[72,3584]{1,0:T(8,128)(2,1)S(1)}, bf16[72,3584]{1,0:T(8,128)(2,1)S(1)}, u32[]{:S(2)}, u32[]{:S(2)}) collective-permute-start(bf16[72,3584]{1,0:T(8,128)(2,1)S(1)} %reshape.161.refs_0_), channel_id=1, source_target_pairs={{0,96},{32,0},{64,32},{96,64},{1,97},{33,1},{65,33},{97,65},{2,98}... | collective-permute-start | bytes 1548296 | tf_op jit(solution)/shard_map/rows_y/ppermute | solution.py:18
  69.5 4.6 %collective-permute-start.10 = (bf16[72,3584]{1,0:T(8,128)(2,1)}, bf16[72,3584]{1,0:T(8,128)(2,1)S(1)}, u32[]{:S(2)}, u32[]{:S(2)}) collective-permute-start(bf16[72,3584]{1,0:T(8,128)(2,1)} %collective-permute-done.9.refs_8_), channel_id=1, source_target_pairs={{0,96},{32,0},{64,32},{96,64},{1,97},{33,1},{65,33},{97,65},{2,98}... | collective-permute-start | bytes 1548296 | tf_op jit(solution)/shard_map/rows_y/ppermute | solution.py:18
  76.1 4.6 %collective-permute-start.3 = (bf16[4,4,16,896]{3,2,1,0:T(8,128)(2,1)S(1)}, bf16[4,4,16,896]{3,2,1,0:T(8,128)(2,1)S(1)}, u32[]{:S(2)}, u32[]{:S(2)}) collective-permute-start(bf16[4,4,16,896]{3,2,1,0:T(8,128)(2,1)S(1)} %pad_maximum_fusion.3.own), channel_id=1, source_target_pairs={{0,1},{1,0},{2,3},{3,2},{4,5},{5,4},{6,7},{7,6},{8,9},{9,8},{10,11... | collective-permute-start | bytes 1376264 | tf_op jit(solution)/shard_map/dense_tokens/ppermute | solution.py:18
  82.2 5.7 %collective-permute-done.10.refs_7_ = bf16[72,3584]{1,0:T(8,128)(2,1)S(1)} collective-permute-done((bf16[72,3584]{1,0:T(8,128)(2,1)}, bf16[72,3584]{1,0:T(8,128)(2,1)S(1)}, u32[]{:S(2)}, u32[]{:S(2)}) %collective-permute-start.10) | collective-permute-done | bytes 516128 | tf_op jit(solution)/shard_map/rows_y/ppermute | solution.py:18
  87.9 4.9 %collective-permute-done.8.refs_6_ = bf16[72,3584]{1,0:T(8,128)(2,1)S(1)} collective-permute-done((bf16[72,3584]{1,0:T(8,128)(2,1)}, bf16[72,3584]{1,0:T(8,128)(2,1)S(1)}, u32[]{:S(2)}, u32[]{:S(2)}) %collective-permute-start.8) | collective-permute-done | bytes 516128 | tf_op jit(solution)/shard_map/rows_y/ppermute | solution.py:18
  93.6 9.0 %experts.1 = (bf16[72,3584]{1,0:T(8,128)(2,1)}, bf16[72,3584]{1,0:T(8,128)(2,1)S(1)}, bf16[72,3584]{1,0:T(8,128)(2,1)}, bf16[72,3584]{1,0:T(8,128)(2,1)}, f32[72...) custom-call(s32[8]{0:T(128)S(1)} %pad_add_fusion.place, ...), custom_call_target="tpu_custom_call" | custom-call | flops 2147483648 | bytes 4194304 | tf_op jit(solution)/shard_map/experts/pallas_call | solution.py:208
  102.7 4.5 %all-to-all-start.1 = ((bf16[4,128,768]{2,1,0:T(8,128)(2,1)}), bf16[4,128,768]{2,1,0:T(8,128)(2,1)}, u32[]{:S(2)}, u32[]{:S(2)}) async-start(bf16[4,128,768]{2,1,0:T(8,128)(2,1)} %get-tuple-element.29), calls=%async_computation.1 | async-start | bytes 1572864 | tf_op jit(solution)/shard_map/dense_hidden/all_to_all | solution.py:22
  109.1 3.4 %collective-permute-start.17 = (bf16[72,3584]{1,0:T(8,128)(2,1)}, bf16[72,3584]{1,0:T(8,128)(2,1)}, u32[]{:S(2)}, u32[]{:S(2)}) collective-permute-start(bf16[72,3584]{1,0:T(8,128)(2,1)} %get-tuple-element.31), channel_id=1, source_target_pairs={{0,32},{32,64},{64,96},{96,0},{1,33},{33,65},{65,97},{97,1},{2,34}... | collective-permute-start | bytes 1548296 | tf_op jit(solution)/shard_map/partials_y/ppermute | solution.py:18
  112.5 3.1 %collective-permute-start.20 = (bf16[72,3584]{1,0:T(8,128)(2,1)}, bf16[72,3584]{1,0:T(8,128)(2,1)S(1)}, u32[]{:S(2)}, u32[]{:S(2)}) collective-permute-start(bf16[72,3584]{1,0:T(8,128)(2,1)} %get-tuple-element.37), channel_id=1, source_target_pairs={{0,96},{32,0},{64,32},{96,64},{1,97},{33,1},{65,33},{97,65},{2,98}... | collective-permute-start | bytes 1548296 | tf_op jit(solution)/shard_map/partials_y/ppermute | solution.py:18
  117.8 5.9 %all-to-all-done.1 = bf16[4,128,768]{2,1,0:T(8,128)(2,1)} async-done(((bf16[4,128,768]{2,1,0:T(8,128)(2,1)}), bf16[4,128,768]{2,1,0:T(8,128)(2,1)}, u32[]{:S(2)}, u32[]{:S(2)}) %all-to-all-start.1) | async-done | bytes 786464 | tf_op jit(solution)/shard_map/dense_hidden/all_to_all | solution.py:22
  125.9 5.9 %all-to-all-start.2 = ((bf16[4,128,384]{2,1,0:T(8,128)(2,1)}), bf16[4,128,384]{2,1,0:T(8,128)(2,1)S(1)}, u32[]{:S(2)}, u32[]{:S(2)}) async-start(bf16[4,128,384]{2,1,0:T(8,128)(2,1)} %broadcast_in_dim.46), calls=%async_computation.2 | async-start | bytes 786432 | tf_op jit(solution)/shard_map/dense_out/all_to_all | solution.py:22
  137.4 3.4 %collective-permute-start.19 = (bf16[72,3584]{1,0:T(8,128)(2,1)}, bf16[72,3584]{1,0:T(8,128)(2,1)}, u32[]{:S(2)}, u32[]{:S(2)}) collective-permute-start(bf16[72,3584]{1,0:T(8,128)(2,1)} %partials_y.3), channel_id=1, source_target_pairs={{0,32},{32,64},{64,96},{96,0},{1,33},{33,65},{65,97},{97,1},{2,34}... | collective-permute-start | bytes 1548296 | tf_op jit(solution)/shard_map/partials_y/ppermute | solution.py:18
  140.9 4.8 %partials_y.5 = (f32[72,3584]{1,0:T(8,128)}, f32[72,3584]{1,0:T(8,128)}) custom-call(bf16[3584,512]{1,0:T(8,128)(2,1)} %pad_maximum_fusion.refs_4_.gate_up, bf16[152,3584]{1,0:T(8,128)(2,1)} %bitcast.52, bf16[72,3584]{1,0:T(8,128)(2,1)S(1)} %reshape.161.refs_0_, bf16[72,3584]{1,0:T(8,128)(2,1)S(1)} %reshape.162.refs_1_), custom_call_target="tpu_custom_call" | custom-call | flops 2147483648 | bytes 4194304 | tf_op jit(solution)/shard_map/partials_y/pallas_call | solution.py:243
  146.5 5.1 %collective-permute-done.19.refs_0_ = bf16[72,3584]{1,0:T(8,128)(2,1)} collective-permute-done((bf16[72,3584]{1,0:T(8,128)(2,1)}, bf16[72,3584]{1,0:T(8,128)(2,1)}, u32[]{:S(2)}, u32[]{:S(2)}) %collective-permute-start.19) | collective-permute-done | bytes 516128 | tf_op jit(solution)/shard_map/partials_y/ppermute | solution.py:18
  152.6 3.6 %partials_z.1 = (f32[36,3584]{1,0:T(8,128)}, bf16[36,3584]{1,0:T(8,128)(2,1)}, bf16[36,3584]{1,0:T(8,128)(2,1)}, bf16[36,3584]{1,0:T(8,128)(2,1)S(1)}) custom-call(s32[4]{0:T(128)S(1)} %and_select_fusion.place, f32[72,3584]{1,0:T(8,128)} %get-tuple-element.35.low, f32[72,3584]{1,0:T(8,128)} %get-tuple-element.36.high, ...), custom_call_target="tpu_custom_call" | custom-call | flops 2147483648 | bytes 4194304 | tf_op jit(solution)/shard_map/partials_z/pallas_call | solution.py:250
  160.7 4.8 %collective-permute-start.25 = (bf16[36,3584]{1,0:T(8,128)(2,1)S(1)}, bf16[36,3584]{1,0:T(8,128)(2,1)}, u32[]{:S(2)}, u32[]{:S(2)}) collective-permute-start(bf16[36,3584]{1,0:T(8,128)(2,1)S(1)} %get-tuple-element.42), channel_id=1, source_target_pairs={{0,8},{8,16},{16,24},{24,0},{1,9},{9,17},{17,25},{25,1},{2,10},{10... | collective-permute-start | bytes 774152 | tf_op jit(solution)/shard_map/partials_z/ppermute | solution.py:18
  170.7 8.5 %all-to-all-start.3 = ((bf16[8,256,224]{1,2,0:T(8,128)(2,1)}), bf16[8,256,224]{1,2,0:T(8,128)(2,1)S(1)}, u32[]{:S(2)}, u32[]{:S(2)}) async-start(bf16[8,256,224]{1,2,0:T(8,128)(2,1)} %copy.71), calls=%async_computation.3 | async-start | bytes 1835008 | tf_op jit(solution)/shard_map/dense_out/all_to_all | solution.py:22
  183.9 7.8 %all-to-all-done.3 = bf16[8,256,224]{1,2,0:T(8,128)(2,1)S(1)} async-done(((bf16[8,256,224]{1,2,0:T(8,128)(2,1)}), bf16[8,256,224]{1,2,0:T(8,128)(2,1)S(1)}, u32[]{:S(2)}, u32[]{:S(2)}) %all-to-all-start.3) | async-done | bytes 917536 | tf_op jit(solution)/shard_map/dense_out/all_to_all | solution.py:22
  191.7 5.3 %all-to-all-start.4 = ((bf16[8,36,448]{2,1,0:T(8,128)(2,1)}), bf16[8,36,448]{2,1,0:T(8,128)(2,1)S(1)}, u32[]{:S(2)}, u32[]{:S(2)}) async-start(bf16[8,36,448]{2,1,0:T(8,128)(2,1)} %bitcast.47), calls=%async_computation.4 | async-start | bytes 655360 | tf_op jit(solution)/shard_map/combine/all_to_all | solution.py:22
  202.9 3.4 %collective-permute-start.15 = (bf16[64,224]{1,0:T(8,128)(2,1)S(1)}, bf16[64,224]{1,0:T(8,128)(2,1)S(1)}, u32[]{:S(2)}, u32[]{:S(2)}) collective-permute-start(bf16[64,224]{1,0:T(8,128)(2,1)S(1)} %get-tuple-element.50), channel_id=1, source_target_pairs={{0,24},{8,0},{16,8},{24,16},{1,25},{9,1},{17,9},{25,17},{2,26},{10... | collective-permute-start | bytes 86024 | tf_op jit(solution)/shard_map/dense_out/ppermute | solution.py:18
  210.0 3.7 %collective-permute-start.16 = (bf16[2,64,224]{2,1,0:T(8,128)(2,1)S(1)}, bf16[2,64,224]{2,1,0:T(8,128)(2,1)S(1)}, u32[]{:S(2)}, u32[]{:S(2)}) collective-permute-start(bf16[2,64,224]{2,1,0:T(8,128)(2,1)S(1)} %constant_dynamic-slice_fusion), channel_id=1, source_target_pairs={{0,1},{1,0},{2,3},{3,2},{4,5},{5,4},{6,7},{7,6},{8,9},{9,8},{10,11... | collective-permute-start | bytes 172040 | tf_op jit(solution)/shard_map/dense_out/ppermute | solution.py:18
  215.1 8.8 %collective-permute-start.26 = (bf16[128,448]{0,1:T(8,128)(2,1)S(1)}, bf16[128,448]{0,1:T(8,128)(2,1)S(1)}, u32[]{:S(2)}, u32[]{:S(2)}) collective-permute-start(bf16[128,448]{0,1:T(8,128)(2,1)S(1)} %fusion.1), channel_id=1, source_target_pairs={{0,128},{128,256},{256,384},{384,0},{1,129},{129,257},{257,385},{3... | collective-permute-start | bytes 344072 | tf_op jit(solution)/shard_map/next_section/ppermute | solution.py:18
  223.9 12.9 %collective-permute-done.26 = bf16[128,448]{0,1:T(8,128)(2,1)S(1)} collective-permute-done((bf16[128,448]{0,1:T(8,128)(2,1)S(1)}, bf16[128,448]{0,1:T(8,128)(2,1)S(1)}, u32[]{:S(2)}, u32[]{:S(2)}) %collective-permute-start.26) | collective-permute-done | bytes 114720 | tf_op jit(solution)/shard_map/next_section/ppermute | solution.py:18
  (144 shorter events, 70.0 us)
Async XLA Ops:
  6.5 35.0 %all-to-all-start = ((bf16[4,40,3584]{2,1,0:T(8,128)(2,1)}), bf16[4,40,3584]{2,1,0:T(8,128)(2,1)}, u32[]{:S(2)}, u32[]{:S(2)}) async-start(bf16[4,40,3584]{2,1,0:T(8,128)(2,1)} %pad_maximum_fusion.1), calls=%async_computation | async-start | bytes 2293760 | tf_op jit(solution)/shard_map/rows_z/all_to_all | solution.py:22
  11.1 22.1 %collective-permute-start.4 = (bf16[224,1152]{1,0:T(8,128)(2,1)S(1)}, bf16[224,1152]{1,0:T(8,128)(2,1)S(1)}, u32[]{:S(2)}, u32[]{:S(2)}) collective-permute-start(bf16[224,1152]{1,0:T(8,128)(2,1)S(1)} %pad_maximum_fusion.2.refs_0_), channel_id=1, source_target_pairs={{0,32},{32,64},{64,96},{96,0},{1,33},{33,65},{65,97},{97,1},{2,34}... | collective-permute-start | bytes 1548296 | tf_op jit(solution)/shard_map/dense_weights/ppermute | solution.py:18
  14.5 24.2 %collective-permute-start.5 = (bf16[224,1152]{1,0:T(8,128)(2,1)S(1)}, bf16[224,1152]{1,0:T(8,128)(2,1)S(1)}, u32[]{:S(2)}, u32[]{:S(2)}) collective-permute-start(bf16[224,1152]{1,0:T(8,128)(2,1)S(1)} %pad_maximum_fusion.2.refs_0_), channel_id=1, source_target_pairs={{0,64},{32,96},{64,0},{96,32},{1,65},{33,97},{65,1},{97,33},{2,66}... | collective-permute-start | bytes 1548296 | tf_op jit(solution)/shard_map/dense_weights/ppermute | solution.py:18
  19.0 21.6 %collective-permute-start.6 = (bf16[224,1152]{1,0:T(8,128)(2,1)S(1)}, bf16[224,1152]{1,0:T(8,128)(2,1)S(1)}, u32[]{:S(2)}, u32[]{:S(2)}) collective-permute-start(bf16[224,1152]{1,0:T(8,128)(2,1)S(1)} %pad_maximum_fusion.2.refs_0_), channel_id=1, source_target_pairs={{0,96},{32,0},{64,32},{96,64},{1,97},{33,1},{65,33},{97,65},{2,98}... | collective-permute-start | bytes 1548296 | tf_op jit(solution)/shard_map/dense_weights/ppermute | solution.py:18
  44.8 24.8 %collective-permute-start.9 = (bf16[72,3584]{1,0:T(8,128)(2,1)S(1)}, bf16[72,3584]{1,0:T(8,128)(2,1)}, u32[]{:S(2)}, u32[]{:S(2)}) collective-permute-start(bf16[72,3584]{1,0:T(8,128)(2,1)S(1)} %reshape.162.refs_1_), channel_id=1, source_target_pairs={{0,96},{32,0},{64,32},{96,64},{1,97},{33,1},{65,33},{97,65},{2,98}... | collective-permute-start | bytes 1548296 | tf_op jit(solution)/shard_map/rows_y/ppermute | solution.py:18
  50.2 23.9 %collective-permute-start.7 = (bf16[72,3584]{1,0:T(8,128)(2,1)S(1)}, bf16[72,3584]{1,0:T(8,128)(2,1)}, u32[]{:S(2)}, u32[]{:S(2)}) collective-permute-start(bf16[72,3584]{1,0:T(8,128)(2,1)S(1)} %reshape.161.refs_0_), channel_id=1, source_target_pairs={{0,32},{32,64},{64,96},{96,0},{1,33},{33,65},{65,97},{97,1},{2,34}... | collective-permute-start | bytes 1548296 | tf_op jit(solution)/shard_map/rows_y/ppermute | solution.py:18
  53.2 9.8 %collective-permute-start = (bf16[4,16,896]{2,1,0:T(8,128)(2,1)S(1)}, bf16[4,16,896]{2,1,0:T(8,128)(2,1)S(1)}, u32[]{:S(2)}, u32[]{:S(2)}) collective-permute-start(bf16[4,16,896]{2,1,0:T(8,128)(2,1)S(1)} %reshape.160), channel_id=1, source_target_pairs={{0,2},{2,4},{4,6},{6,0},{1,3},{3,5},{5,7},{7,1},{8,10},{10,12},{12... | collective-permute-start | bytes 344072 | tf_op jit(solution)/shard_map/dense_tokens/ppermute | solution.py:18
  56.4 11.2 %collective-permute-start.1 = (bf16[4,16,896]{2,1,0:T(8,128)(2,1)S(1)}, bf16[4,16,896]{2,1,0:T(8,128)(2,1)S(1)}, u32[]{:S(2)}, u32[]{:S(2)}) collective-permute-start(bf16[4,16,896]{2,1,0:T(8,128)(2,1)S(1)} %reshape.160), channel_id=1, source_target_pairs={{0,4},{2,6},{4,0},{6,2},{1,5},{3,7},{5,1},{7,3},{8,12},{10,14},{12... | collective-permute-start | bytes 344072 | tf_op jit(solution)/shard_map/dense_tokens/ppermute | solution.py:18
  59.0 17.1 %collective-permute-start.2 = (bf16[4,16,896]{2,1,0:T(8,128)(2,1)S(1)}, bf16[4,16,896]{2,1,0:T(8,128)(2,1)S(1)}, u32[]{:S(2)}, u32[]{:S(2)}) collective-permute-start(bf16[4,16,896]{2,1,0:T(8,128)(2,1)S(1)} %reshape.160), channel_id=1, source_target_pairs={{0,6},{2,0},{4,2},{6,4},{1,7},{3,1},{5,3},{7,5},{8,14},{10,8},{12,... | collective-permute-start | bytes 344072 | tf_op jit(solution)/shard_map/dense_tokens/ppermute | solution.py:18
  63.0 17.9 %collective-permute-start.11 = (bf16[72,3584]{1,0:T(8,128)(2,1)S(1)}, bf16[72,3584]{1,0:T(8,128)(2,1)S(1)}, u32[]{:S(2)}, u32[]{:S(2)}) collective-permute-start(bf16[72,3584]{1,0:T(8,128)(2,1)S(1)} %reshape.161.refs_0_), channel_id=1, source_target_pairs={{0,96},{32,0},{64,32},{96,64},{1,97},{33,1},{65,33},{97,65},{2,98}... | collective-permute-start | bytes 1548296 | tf_op jit(solution)/shard_map/rows_y/ppermute | solution.py:18
  67.6 14.2 %collective-permute-start.12 = (bf16[72,3584]{1,0:T(8,128)(2,1)S(1)}, bf16[72,3584]{1,0:T(8,128)(2,1)S(1)}, u32[]{:S(2)}, u32[]{:S(2)}) collective-permute-start(bf16[72,3584]{1,0:T(8,128)(2,1)S(1)} %reshape.162.refs_1_), channel_id=1, source_target_pairs={{0,32},{32,64},{64,96},{96,0},{1,33},{33,65},{65,97},{97,1},{2,34}... | collective-permute-start | bytes 1548296 | tf_op jit(solution)/shard_map/rows_y/ppermute | solution.py:18
  69.5 18.3 %collective-permute-start.10 = (bf16[72,3584]{1,0:T(8,128)(2,1)}, bf16[72,3584]{1,0:T(8,128)(2,1)S(1)}, u32[]{:S(2)}, u32[]{:S(2)}) collective-permute-start(bf16[72,3584]{1,0:T(8,128)(2,1)} %collective-permute-done.9.refs_8_), channel_id=1, source_target_pairs={{0,96},{32,0},{64,32},{96,64},{1,97},{33,1},{65,33},{97,65},{2,98}... | collective-permute-start | bytes 1548296 | tf_op jit(solution)/shard_map/rows_y/ppermute | solution.py:18
  74.1 18.7 %collective-permute-start.8 = (bf16[72,3584]{1,0:T(8,128)(2,1)}, bf16[72,3584]{1,0:T(8,128)(2,1)S(1)}, u32[]{:S(2)}, u32[]{:S(2)}) collective-permute-start(bf16[72,3584]{1,0:T(8,128)(2,1)} %collective-permute-done.7.refs_9_), channel_id=1, source_target_pairs={{0,32},{32,64},{64,96},{96,0},{1,33},{33,65},{65,97},{97,1},{2,34}... | collective-permute-start | bytes 1548296 | tf_op jit(solution)/shard_map/rows_y/ppermute | solution.py:18
  76.1 6.1 %collective-permute-start.3 = (bf16[4,4,16,896]{3,2,1,0:T(8,128)(2,1)S(1)}, bf16[4,4,16,896]{3,2,1,0:T(8,128)(2,1)S(1)}, u32[]{:S(2)}, u32[]{:S(2)}) collective-permute-start(bf16[4,4,16,896]{3,2,1,0:T(8,128)(2,1)S(1)} %pad_maximum_fusion.3.own), channel_id=1, source_target_pairs={{0,1},{1,0},{2,3},{3,2},{4,5},{5,4},{6,7},{7,6},{8,9},{9,8},{10,11... | collective-permute-start | bytes 1376264 | tf_op jit(solution)/shard_map/dense_tokens/ppermute | solution.py:18
  102.7 21.0 %all-to-all-start.1 = ((bf16[4,128,768]{2,1,0:T(8,128)(2,1)}), bf16[4,128,768]{2,1,0:T(8,128)(2,1)}, u32[]{:S(2)}, u32[]{:S(2)}) async-start(bf16[4,128,768]{2,1,0:T(8,128)(2,1)} %get-tuple-element.29), calls=%async_computation.1 | async-start | bytes 1572864 | tf_op jit(solution)/shard_map/dense_hidden/all_to_all | solution.py:22
  107.2 24.6 %collective-permute-start.18 = (bf16[72,3584]{1,0:T(8,128)(2,1)S(1)}, bf16[72,3584]{1,0:T(8,128)(2,1)}, u32[]{:S(2)}, u32[]{:S(2)}) collective-permute-start(bf16[72,3584]{1,0:T(8,128)(2,1)S(1)} %get-tuple-element.33), channel_id=1, source_target_pairs={{0,96},{32,0},{64,32},{96,64},{1,97},{33,1},{65,33},{97,65},{2,98}... | collective-permute-start | bytes 1548296 | tf_op jit(solution)/shard_map/partials_y/ppermute | solution.py:18
  109.1 26.0 %collective-permute-start.17 = (bf16[72,3584]{1,0:T(8,128)(2,1)}, bf16[72,3584]{1,0:T(8,128)(2,1)}, u32[]{:S(2)}, u32[]{:S(2)}) collective-permute-start(bf16[72,3584]{1,0:T(8,128)(2,1)} %get-tuple-element.31), channel_id=1, source_target_pairs={{0,32},{32,64},{64,96},{96,0},{1,33},{33,65},{65,97},{97,1},{2,34}... | collective-permute-start | bytes 1548296 | tf_op jit(solution)/shard_map/partials_y/ppermute | solution.py:18
  112.5 33.2 %collective-permute-start.20 = (bf16[72,3584]{1,0:T(8,128)(2,1)}, bf16[72,3584]{1,0:T(8,128)(2,1)S(1)}, u32[]{:S(2)}, u32[]{:S(2)}) collective-permute-start(bf16[72,3584]{1,0:T(8,128)(2,1)} %get-tuple-element.37), channel_id=1, source_target_pairs={{0,96},{32,0},{64,32},{96,64},{1,97},{33,1},{65,33},{97,65},{2,98}... | collective-permute-start | bytes 1548296 | tf_op jit(solution)/shard_map/partials_y/ppermute | solution.py:18
  115.6 30.8 %collective-permute-start.21 = (bf16[72,3584]{1,0:T(8,128)(2,1)}, bf16[72,3584]{1,0:T(8,128)(2,1)}, u32[]{:S(2)}, u32[]{:S(2)}) collective-permute-start(bf16[72,3584]{1,0:T(8,128)(2,1)} %get-tuple-element.38), channel_id=1, source_target_pairs={{0,32},{32,64},{64,96},{96,0},{1,33},{33,65},{65,97},{97,1},{2,34}... | collective-permute-start | bytes 1548296 | tf_op jit(solution)/shard_map/partials_y/ppermute | solution.py:18
  125.9 39.6 %all-to-all-start.2 = ((bf16[4,128,384]{2,1,0:T(8,128)(2,1)}), bf16[4,128,384]{2,1,0:T(8,128)(2,1)S(1)}, u32[]{:S(2)}, u32[]{:S(2)}) async-start(bf16[4,128,384]{2,1,0:T(8,128)(2,1)} %broadcast_in_dim.46), calls=%async_computation.2 | async-start | bytes 786432 | tf_op jit(solution)/shard_map/dense_out/all_to_all | solution.py:22
  133.2 13.2 %collective-permute-start.22 = (bf16[72,3584]{1,0:T(8,128)(2,1)S(1)}, bf16[72,3584]{1,0:T(8,128)(2,1)}, u32[]{:S(2)}, u32[]{:S(2)}) collective-permute-start(bf16[72,3584]{1,0:T(8,128)(2,1)S(1)} %partials_y.4), channel_id=1, source_target_pairs={{0,96},{32,0},{64,32},{96,64},{1,97},{33,1},{65,33},{97,65},{2,98}... | collective-permute-start | bytes 1548296 | tf_op jit(solution)/shard_map/partials_y/ppermute | solution.py:18
  137.4 14.2 %collective-permute-start.19 = (bf16[72,3584]{1,0:T(8,128)(2,1)}, bf16[72,3584]{1,0:T(8,128)(2,1)}, u32[]{:S(2)}, u32[]{:S(2)}) collective-permute-start(bf16[72,3584]{1,0:T(8,128)(2,1)} %partials_y.3), channel_id=1, source_target_pairs={{0,32},{32,64},{64,96},{96,0},{1,33},{33,65},{65,97},{97,1},{2,34}... | collective-permute-start | bytes 1548296 | tf_op jit(solution)/shard_map/partials_y/ppermute | solution.py:18
  156.3 22.8 %collective-permute-start.23 = (bf16[36,3584]{1,0:T(8,128)(2,1)}, bf16[36,3584]{1,0:T(8,128)(2,1)}, u32[]{:S(2)}, u32[]{:S(2)}) collective-permute-start(bf16[36,3584]{1,0:T(8,128)(2,1)} %get-tuple-element.40), channel_id=1, source_target_pairs={{0,24},{8,0},{16,8},{24,16},{1,25},{9,1},{17,9},{25,17},{2,26},{10... | collective-permute-start | bytes 774152 | tf_op jit(solution)/shard_map/partials_z/ppermute | solution.py:18
  158.5 22.9 %collective-permute-start.24 = (bf16[36,3584]{1,0:T(8,128)(2,1)}, bf16[36,3584]{1,0:T(8,128)(2,1)}, u32[]{:S(2)}, u32[]{:S(2)}) collective-permute-start(bf16[36,3584]{1,0:T(8,128)(2,1)} %get-tuple-element.41), channel_id=1, source_target_pairs={{0,16},{8,24},{16,0},{24,8},{1,17},{9,25},{17,1},{25,9},{2,18},{10... | collective-permute-start | bytes 774152 | tf_op jit(solution)/shard_map/partials_z/ppermute | solution.py:18
  160.7 20.7 %collective-permute-start.25 = (bf16[36,3584]{1,0:T(8,128)(2,1)S(1)}, bf16[36,3584]{1,0:T(8,128)(2,1)}, u32[]{:S(2)}, u32[]{:S(2)}) collective-permute-start(bf16[36,3584]{1,0:T(8,128)(2,1)S(1)} %get-tuple-element.42), channel_id=1, source_target_pairs={{0,8},{8,16},{16,24},{24,0},{1,9},{9,17},{17,25},{25,1},{2,10},{10... | collective-permute-start | bytes 774152 | tf_op jit(solution)/shard_map/partials_z/ppermute | solution.py:18
  170.7 21.1 %all-to-all-start.3 = ((bf16[8,256,224]{1,2,0:T(8,128)(2,1)}), bf16[8,256,224]{1,2,0:T(8,128)(2,1)S(1)}, u32[]{:S(2)}, u32[]{:S(2)}) async-start(bf16[8,256,224]{1,2,0:T(8,128)(2,1)} %copy.71), calls=%async_computation.3 | async-start | bytes 1835008 | tf_op jit(solution)/shard_map/dense_out/all_to_all | solution.py:22
  191.7 14.5 %all-to-all-start.4 = ((bf16[8,36,448]{2,1,0:T(8,128)(2,1)}), bf16[8,36,448]{2,1,0:T(8,128)(2,1)S(1)}, u32[]{:S(2)}, u32[]{:S(2)}) async-start(bf16[8,36,448]{2,1,0:T(8,128)(2,1)} %bitcast.47), calls=%async_computation.4 | async-start | bytes 655360 | tf_op jit(solution)/shard_map/combine/all_to_all | solution.py:22
  197.3 9.1 %collective-permute-start.13 = (bf16[64,224]{1,0:T(8,128)(2,1)S(1)}, bf16[64,224]{1,0:T(8,128)(2,1)S(1)}, u32[]{:S(2)}, u32[]{:S(2)}) collective-permute-start(bf16[64,224]{1,0:T(8,128)(2,1)S(1)} %get-tuple-element.52), channel_id=1, source_target_pairs={{0,8},{8,16},{16,24},{24,0},{1,9},{9,17},{17,25},{25,1},{2,10},{10... | collective-permute-start | bytes 86024 | tf_op jit(solution)/shard_map/dense_out/ppermute | solution.py:18
  200.1 6.3 %collective-permute-start.14 = (bf16[64,224]{1,0:T(8,128)(2,1)S(1)}, bf16[64,224]{1,0:T(8,128)(2,1)S(1)}, u32[]{:S(2)}, u32[]{:S(2)}) collective-permute-start(bf16[64,224]{1,0:T(8,128)(2,1)S(1)} %get-tuple-element.51), channel_id=1, source_target_pairs={{0,16},{8,24},{16,0},{24,8},{1,17},{9,25},{17,1},{25,9},{2,18},{10... | collective-permute-start | bytes 86024 | tf_op jit(solution)/shard_map/dense_out/ppermute | solution.py:18
  202.9 6.5 %collective-permute-start.15 = (bf16[64,224]{1,0:T(8,128)(2,1)S(1)}, bf16[64,224]{1,0:T(8,128)(2,1)S(1)}, u32[]{:S(2)}, u32[]{:S(2)}) collective-permute-start(bf16[64,224]{1,0:T(8,128)(2,1)S(1)} %get-tuple-element.50), channel_id=1, source_target_pairs={{0,24},{8,0},{16,8},{24,16},{1,25},{9,1},{17,9},{25,17},{2,26},{10... | collective-permute-start | bytes 86024 | tf_op jit(solution)/shard_map/dense_out/ppermute | solution.py:18
  210.0 4.6 %collective-permute-start.16 = (bf16[2,64,224]{2,1,0:T(8,128)(2,1)S(1)}, bf16[2,64,224]{2,1,0:T(8,128)(2,1)S(1)}, u32[]{:S(2)}, u32[]{:S(2)}) collective-permute-start(bf16[2,64,224]{2,1,0:T(8,128)(2,1)S(1)} %constant_dynamic-slice_fusion), channel_id=1, source_target_pairs={{0,1},{1,0},{2,3},{3,2},{4,5},{5,4},{6,7},{7,6},{8,9},{9,8},{10,11... | collective-permute-start | bytes 172040 | tf_op jit(solution)/shard_map/dense_out/ppermute | solution.py:18
  215.1 21.8 %collective-permute-start.26 = (bf16[128,448]{0,1:T(8,128)(2,1)S(1)}, bf16[128,448]{0,1:T(8,128)(2,1)S(1)}, u32[]{:S(2)}, u32[]{:S(2)}) collective-permute-start(bf16[128,448]{0,1:T(8,128)(2,1)S(1)} %fusion.1), channel_id=1, source_target_pairs={{0,128},{128,256},{256,384},{384,0},{1,129},{129,257},{257,385},{3... | collective-permute-start | bytes 344072 | tf_op jit(solution)/shard_map/next_section/ppermute | solution.py:18
  (23 other events, 250.9 us)

commit v7 on v6

--- a/solution.py
+++ b/solution.py
@@ -75,17 +75,12 @@
         out[...] = result[k * size : (k + 1) * size].astype(out.dtype)
 
 
-def rows_and_dense_kernel(columns, place, own, other, *refs):
-    weights, pre = refs[:4], refs[-1]
+def dense_in_kernel(columns, tokens, *refs):
+    weights, out = refs[:4], refs[4]
     joined = jnp.concatenate([part[:, :columns] for part in weights], axis=0)
     for z in range(4):
-        shares = [side[k, z] for side in (own, other) for k in range(4)]
-        size = shares[0].shape[0]
-        result = dot(jnp.concatenate(shares, axis=0), joined).astype(BF16)
-        for i in range(len(shares)):
-            start = pl.multiple_of(place[i] * size, size)
-            pre[z, pl.ds(start, size)] = result[i * size : (i + 1) * size]
-    rows_kernel(*refs[4:-1])
+        rows = jnp.concatenate([tokens[e, z] for e in range(tokens.shape[0])], axis=0)
+        out[z] = dot(rows, joined).astype(BF16)
 
 
 def late_kernel(part, relay, out):
@@ -197,30 +192,22 @@
         far_high = shifted(next_high, "y", -1)
 
     with jax.named_scope("dense_tokens"):
-        own_shares = jnp.stack([line_share] + [shifted(line_share, "x", by) for by in (1, 2, 3)])
-        other_shares = shifted(own_shares, "core", 1)
-        place_x = (lax.axis_index("x") - steps_back) % 4
-        place_share = jnp.concatenate([2 * place_x + core, 2 * place_x + 1 - core])
+        line_tokens = exchanged(repeated(line_share, n_expert), EXPERT_AXES)
+        line_tokens = after(line_tokens, prev_low, next_low, prev_high, next_high)
+        pre = local_call(
+            functools.partial(dense_in_kernel, 2 * hidden),
+            jax.ShapeDtypeStruct((4, tok_rows, 2 * hidden), BF16),
+        )(line_tokens, *slabs)
 
     half_bf16, half_f32 = (jax.ShapeDtypeStruct(low.shape, dtype) for dtype in (BF16, F32))
     in_smem, in_vmem = (pl.BlockSpec(memory_space=space) for space in (pltpu.SMEM, pltpu.VMEM))
     with jax.named_scope("experts"):
-        relay_next, relay_prev, early_next, early_prev, next_part, prev_part, pre = local_call(
-            functools.partial(rows_and_dense_kernel, 2 * hidden),
-            [half_bf16] * 4
-            + [half_f32] * 2
-            + [jax.ShapeDtypeStruct((4, tok_rows, 2 * hidden), BF16)],
-            in_specs=[in_smem] + [in_vmem] * 14,
-        )(
-            place_share,
-            own_shares,
-            other_shares,
-            *slabs,
-            gate_up,
-            down,
-            *(far_low, far_high, next_high, prev_low, next_low, prev_high),
-        )
-
+        relay_next, relay_prev, early_next, early_prev, next_part, prev_part = local_call(
+            rows_kernel, [half_bf16] * 4 + [half_f32] * 2
+        )(gate_up, down, far_low, far_high, next_high, prev_low, next_low, prev_high)
+
+    with jax.named_scope("partials_y"):
+        relay_next, relay_prev = shifted(relay_next, "y", 1), shifted(relay_prev, "y", -1)
     with jax.named_scope("dense_hidden"):
         pre = exchanged(pre, "z")
         pre = jnp.sum(pre.astype(F32), axis=0)
@@ -236,7 +223,6 @@
         )(place_y, every_act, *slabs)
 
     with jax.named_scope("partials_y"):
-        relay_next, relay_prev = shifted(relay_next, "y", 1), shifted(relay_prev, "y", -1)
         early_next, early_prev = shifted(early_next, "y", 1), shifted(early_prev, "y", -1)
         late_next = local_call(late_kernel, half_bf16)(next_part, relay_next)
         late_prev = local_call(late_kernel, half_bf16)(prev_part, relay_prev)

time: 239 us -> 246 us (1.029)
  waiting for transfers between devices: 57 us -> 66.1 us
  starting transfers between devices: 121 us -> 116 us
  Pallas kernels: 24 us -> 26.7 us
    ppermute x27 -> x23, waiting for transfers between devices: 43.2 us -> 56 us  [shifted(): return lax.ppermute(x, axis, [(i, (i + by) % peers) for i in range(peers)])]
    ppermute x27 -> x23, starting transfers between devices: 91.8 us -> 79.8 us  [shifted(): return lax.ppermute(x, axis, [(i, (i + by) % peers) for i in range(peers)])]
    all_to_all x5 -> x6, starting transfers between devices: 28.7 us -> 36.4 us  [exchanged(): return lax.all_to_all(x, axes, split_axis=0, concat_axis=0, tiled=True)]
    all_to_all x5 -> x6, waiting for transfers between devices: 13.8 us -> 10.1 us  [exchanged(): return lax.all_to_all(x, axes, split_axis=0, concat_axis=0, tiled=True)]
    pallas_call x1 -> x2, Pallas kernels: 9.05 us -> 10.9 us  [the longest x1 7.71 us: body(): local_call(rows_kernel, [half_bf16] * 4 + [half_f32] * 2)]
    unnamed x49 -> x43, local copies, waits for them, and re-layouts: 10.6 us -> 9.42 us
  transfers between devices with their start and end apart: 32 -> 29, of which waited for: 13 -> 12; matrix products, arithmetic and copies ran while one was open for 9% -> 9% of each run, Pallas kernels for 6% -> 10%
where the time goes in v7:
time: 246 us; the launch traced here: 244 us
  starting transfers between devices  116 us (47%)
  waiting for transfers between devices  66.1 us (27%)
  Pallas kernels  26.7 us (11%)
  local copies, waits for them, and re-layouts  21.6 us (9%)
  other arithmetic  12.1 us (5%)
    ppermute x23, starting transfers between devices, shifted(): return lax.ppermute(x, axis, [(i, (i + by) % peers) for i in range(peers)])  79.8 us
    ppermute x23, waiting for transfers between devices, shifted(): return lax.ppermute(x, axis, [(i, (i + by) % peers) for i in range(peers)])  56 us
    all_to_all x6, starting transfers between devices, exchanged(): return lax.all_to_all(x, axes, split_axis=0, concat_axis=0, tiled=True)  36.4 us
    all_to_all x6, waiting for transfers between devices, exchanged(): return lax.all_to_all(x, axes, split_axis=0, concat_axis=0, tiled=True)  10.1 us
    unnamed x43, local copies, waits for them, and re-layouts  9.42 us
    pallas_call x1, Pallas kernels, body(): local_call(rows_kernel, [half_bf16] * 4 + [half_f32] * 2)  7.71 us
    concatenate x1, other arithmetic, body(): jnp.concatenate([expert_gate[0, 0], blank, expert_up[0, 0], blank], axis=1)  5.03 us
  transfers between devices with their start and end apart: 29, of which 12 were waited for; matrix products, arithmetic and copies ran while one was open for 9% of the time, Pallas kernels for 10%

profile of v7, /device:TPU:99, one launch (start us, length us, event | category | flops | bytes accessed | tf_op | source)
XLA Modules:
  0.0 244.3 jit_solution(16646781658605515001)
XLA Ops:
  7.0 4.5 %all-to-all-start = ((bf16[4,40,3584]{2,1,0:T(8,128)(2,1)}), bf16[4,40,3584]{2,1,0:T(8,128)(2,1)}, u32[]{:S(2)}, u32[]{:S(2)}) async-start(bf16[4,40,3584]{2,1,0:T(8,128)(2,1)} %pad_maximum_fusion.1), calls=%async_computation | async-start | bytes 2293760 | tf_op jit(solution)/shard_map/rows_z/all_to_all | solution.py:22
  11.6 3.2 %collective-permute-start = (bf16[224,1152]{1,0:T(8,128)(2,1)S(1)}, bf16[224,1152]{1,0:T(8,128)(2,1)S(1)}, u32[]{:S(2)}, u32[]{:S(2)}) collective-permute-start(bf16[224,1152]{1,0:T(8,128)(2,1)S(1)} %pad_maximum_fusion.2.refs_0_), channel_id=1, source_target_pairs={{0,32},{32,64},{64,96},{96,0},{1,33},{33,65},{65,97},{97,1},{2,34}... | collective-permute-start | bytes 1548296 | tf_op jit(solution)/shard_map/dense_weights/ppermute | solution.py:18
  14.8 4.5 %collective-permute-start.1 = (bf16[224,1152]{1,0:T(8,128)(2,1)S(1)}, bf16[224,1152]{1,0:T(8,128)(2,1)S(1)}, u32[]{:S(2)}, u32[]{:S(2)}) collective-permute-start(bf16[224,1152]{1,0:T(8,128)(2,1)S(1)} %pad_maximum_fusion.2.refs_0_), channel_id=1, source_target_pairs={{0,64},{32,96},{64,0},{96,32},{1,65},{33,97},{65,1},{97,33},{2,66}... | collective-permute-start | bytes 1548296 | tf_op jit(solution)/shard_map/dense_weights/ppermute | solution.py:18
  19.3 3.0 %collective-permute-start.2 = (bf16[224,1152]{1,0:T(8,128)(2,1)S(1)}, bf16[224,1152]{1,0:T(8,128)(2,1)}, u32[]{:S(2)}, u32[]{:S(2)}) collective-permute-start(bf16[224,1152]{1,0:T(8,128)(2,1)S(1)} %pad_maximum_fusion.2.refs_0_), channel_id=1, source_target_pairs={{0,96},{32,0},{64,32},{96,64},{1,97},{33,1},{65,33},{97,65},{2,98}... | collective-permute-start | bytes 1548296 | tf_op jit(solution)/shard_map/dense_weights/ppermute | solution.py:18
  27.5 5.0 %pad_maximum_fusion.gate_up = bf16[3584,512]{1,0:T(8,128)(2,1)} fusion(bf16[3584,104]{1,0:T(8,128)(2,1)S(1)} %broadcast_in_dim.54, bf16[3584,152]{1,0:T(8,128)(2,1)} %bitcast.47, bf16[3584,152]{1,0:T(8,128)(2,1)} %bitcast.46), kind=kLoop, calls=%fused_computation.3 | loop fusion | flops 14680064 | bytes 6594560 | tf_op jit(solution)/shard_map/concatenate | solution.py:173
  32.6 6.4 %collective-permute-done.1.refs_2_ = bf16[224,1152]{1,0:T(8,128)(2,1)S(1)} collective-permute-done((bf16[224,1152]{1,0:T(8,128)(2,1)S(1)}, bf16[224,1152]{1,0:T(8,128)(2,1)S(1)}, u32[]{:S(2)}, u32[]{:S(2)}) %collective-permute-start.1) | collective-permute-done | bytes 516128 | tf_op jit(solution)/shard_map/dense_weights/ppermute | solution.py:18
  43.1 6.1 %all-to-all-start.1 = ((bf16[8,4,16,896]{3,2,1,0:T(8,128)(2,1)}), bf16[8,4,16,896]{3,2,1,0:T(8,128)(2,1)}, u32[]{:S(2)}, u32[]{:S(2)}) async-start(bf16[8,4,16,896]{3,2,1,0:T(8,128)(2,1)} %broadcast_in_dim.28), calls=%async_computation.1 | async-start | bytes 1835008 | tf_op jit(solution)/shard_map/dense_tokens/all_to_all | solution.py:22
  52.5 4.1 %collective-permute-start.3 = (bf16[72,3584]{1,0:T(8,128)(2,1)S(1)}, bf16[72,3584]{1,0:T(8,128)(2,1)}, u32[]{:S(2)}, u32[]{:S(2)}) collective-permute-start(bf16[72,3584]{1,0:T(8,128)(2,1)S(1)} %reshape.155.refs_0_), channel_id=1, source_target_pairs={{0,32},{32,64},{64,96},{96,0},{1,33},{33,65},{65,97},{97,1},{2,34}... | collective-permute-start | bytes 1548296 | tf_op jit(solution)/shard_map/rows_y/ppermute | solution.py:18
  59.1 3.0 %collective-permute-start.4 = (bf16[72,3584]{1,0:T(8,128)(2,1)S(1)}, bf16[72,3584]{1,0:T(8,128)(2,1)S(1)}, u32[]{:S(2)}, u32[]{:S(2)}) collective-permute-start(bf16[72,3584]{1,0:T(8,128)(2,1)S(1)} %reshape.155.refs_0_), channel_id=1, source_target_pairs={{0,96},{32,0},{64,32},{96,64},{1,97},{33,1},{65,33},{97,65},{2,98}... | collective-permute-start | bytes 1548296 | tf_op jit(solution)/shard_map/rows_y/ppermute | solution.py:18
  64.4 4.3 %collective-permute-done.3.refs_3_ = bf16[72,3584]{1,0:T(8,128)(2,1)} collective-permute-done((bf16[72,3584]{1,0:T(8,128)(2,1)S(1)}, bf16[72,3584]{1,0:T(8,128)(2,1)}, u32[]{:S(2)}, u32[]{:S(2)}) %collective-permute-start.3) | collective-permute-done | bytes 516128 | tf_op jit(solution)/shard_map/rows_y/ppermute | solution.py:18
  71.4 11.0 %collective-permute-done.4.refs_4_ = bf16[72,3584]{1,0:T(8,128)(2,1)S(1)} collective-permute-done((bf16[72,3584]{1,0:T(8,128)(2,1)S(1)}, bf16[72,3584]{1,0:T(8,128)(2,1)S(1)}, u32[]{:S(2)}, u32[]{:S(2)}) %collective-permute-start.4) | collective-permute-done | bytes 516128 | tf_op jit(solution)/shard_map/rows_y/ppermute | solution.py:18
  84.2 3.2 %dense_tokens.1 = bf16[4,128,768]{2,1,0:T(8,128)(2,1)} custom-call(bf16[8,4,16,896]{3,2,1,0:T(8,128)(2,1)} %all-to-all-done.1.tokens, bf16[224,1152]{1,0:T(8,128)(2,1)S(1)} %pad_maximum_fusion.2.refs_0_, bf16[224,1152]{1,0:T(8,128)(2,1)S(1)} %collective-permute-done.refs_1_, bf16[224,1152]{1,0:T(8,128)(2,1)S(1)} %copy-done.2, ...), custom_call_target="tpu_custom_call" | custom-call | flops 2147483648 | bytes 4194304 | tf_op jit(solution)/shard_map/dense_tokens/pallas_call | solution.py:197
  87.4 4.5 %all-to-all-start.2 = ((bf16[4,128,768]{2,1,0:T(8,128)(2,1)}), bf16[4,128,768]{2,1,0:T(8,128)(2,1)}, u32[]{:S(2)}, u32[]{:S(2)}) async-start(bf16[4,128,768]{2,1,0:T(8,128)(2,1)} %dense_tokens.1), calls=%async_computation.2 | async-start | bytes 1572864 | tf_op jit(solution)/shard_map/dense_hidden/all_to_all | solution.py:22
  94.2 4.3 %collective-permute-start.12 = (bf16[72,3584]{1,0:T(8,128)(2,1)S(1)}, bf16[72,3584]{1,0:T(8,128)(2,1)S(1)}, u32[]{:S(2)}, u32[]{:S(2)}) collective-permute-start(bf16[72,3584]{1,0:T(8,128)(2,1)S(1)} %collective-permute-done.6.refs_2_), channel_id=1, source_target_pairs={{0,96},{32,0},{64,32},{96,64},{1,97},{33,1},{65,33},{97,65},{2,98}... | collective-permute-start | bytes 1548296 | tf_op jit(solution)/shard_map/rows_y/ppermute | solution.py:18
  98.5 8.0 %collective-permute-done.11.refs_0_ = bf16[72,3584]{1,0:T(8,128)(2,1)S(1)} collective-permute-done((bf16[72,3584]{1,0:T(8,128)(2,1)}, bf16[72,3584]{1,0:T(8,128)(2,1)S(1)}, u32[]{:S(2)}, u32[]{:S(2)}) %collective-permute-start.11) | collective-permute-done | bytes 516128 | tf_op jit(solution)/shard_map/rows_y/ppermute | solution.py:18
  107.9 7.7 %experts.1 = (bf16[72,3584]{1,0:T(8,128)(2,1)}, bf16[72,3584]{1,0:T(8,128)(2,1)}, bf16[72,3584]{1,0:T(8,128)(2,1)}, bf16[72,3584]{1,0:T(8,128)(2,1)}, f32[72,3584]{1,0:T(8,128)}, /*index=5*/f32[72,3584]{1,0:T(8,128)}) custom-call(bf16[3584,512]{1,0:T(8,128)(2,1)} %pad_maximum_fusion.gate_up, bf16[152,3584]{1,0:T(8,128)(2,1)} %bitcast.61, ...), custom_call_target="tpu_custom_call" | custom-call | flops 2147483648 | bytes 4194304 | tf_op jit(solution)/shard_map/experts/pallas_call | solution.py:205
  115.6 5.3 %collective-permute-start.14 = (bf16[72,3584]{1,0:T(8,128)(2,1)}, bf16[72,3584]{1,0:T(8,128)(2,1)}, u32[]{:S(2)}, u32[]{:S(2)}) collective-permute-start(bf16[72,3584]{1,0:T(8,128)(2,1)} %get-tuple-element.33), channel_id=1, source_target_pairs={{0,96},{32,0},{64,32},{96,64},{1,97},{33,1},{65,33},{97,65},{2,98}... | collective-permute-start | bytes 1548296 | tf_op jit(solution)/shard_map/partials_y/ppermute | solution.py:18
  122.9 4.6 %collective-permute-start.16 = (bf16[72,3584]{1,0:T(8,128)(2,1)}, bf16[72,3584]{1,0:T(8,128)(2,1)}, u32[]{:S(2)}, u32[]{:S(2)}) collective-permute-start(bf16[72,3584]{1,0:T(8,128)(2,1)} %get-tuple-element.37), channel_id=1, source_target_pairs={{0,96},{32,0},{64,32},{96,64},{1,97},{33,1},{65,33},{97,65},{2,98}... | collective-permute-start | bytes 1548296 | tf_op jit(solution)/shard_map/partials_y/ppermute | solution.py:18
  131.6 4.5 %all-to-all-start.3 = ((bf16[4,128,384]{2,1,0:T(8,128)(2,1)}), bf16[4,128,384]{2,1,0:T(8,128)(2,1)S(1)}, u32[]{:S(2)}, u32[]{:S(2)}) async-start(bf16[4,128,384]{2,1,0:T(8,128)(2,1)} %broadcast_in_dim.55), calls=%async_computation.3 | async-start | bytes 786432 | tf_op jit(solution)/shard_map/dense_out/all_to_all | solution.py:22
  138.3 4.6 %collective-permute-start.18 = (bf16[72,3584]{1,0:T(8,128)(2,1)}, bf16[72,3584]{1,0:T(8,128)(2,1)}, u32[]{:S(2)}, u32[]{:S(2)}) collective-permute-start(bf16[72,3584]{1,0:T(8,128)(2,1)} %partials_y.4), channel_id=1, source_target_pairs={{0,96},{32,0},{64,32},{96,64},{1,97},{33,1},{65,33},{97,65},{2,98}... | collective-permute-start | bytes 1548296 | tf_op jit(solution)/shard_map/partials_y/ppermute | solution.py:18
  147.1 4.8 %partials_y.5 = (f32[72,3584]{1,0:T(8,128)}, f32[72,3584]{1,0:T(8,128)}) custom-call(bf16[3584,512]{1,0:T(8,128)(2,1)} %pad_maximum_fusion.gate_up, bf16[152,3584]{1,0:T(8,128)(2,1)} %bitcast.62, bf16[72,3584]{1,0:T(8,128)(2,1)S(1)} %reshape.155.refs_0_, bf16[72,3584]{1,0:T(8,128)(2,1)S(1)} %reshape.156.refs_1_), custom_call_target="tpu_custom_call" | custom-call | flops 2147483648 | bytes 4194304 | tf_op jit(solution)/shard_map/partials_y/pallas_call | solution.py:229
  151.9 4.6 %collective-permute-done.15.refs_0_ = bf16[72,3584]{1,0:T(8,128)(2,1)} collective-permute-done((bf16[72,3584]{1,0:T(8,128)(2,1)}, bf16[72,3584]{1,0:T(8,128)(2,1)}, u32[]{:S(2)}, u32[]{:S(2)}) %collective-permute-start.15) | collective-permute-done | bytes 516128 | tf_op jit(solution)/shard_map/partials_y/ppermute | solution.py:18
  156.5 3.7 %partials_z.1 = (f32[36,3584]{1,0:T(8,128)}, bf16[36,3584]{1,0:T(8,128)(2,1)}, bf16[36,3584]{1,0:T(8,128)(2,1)}, bf16[36,3584]{1,0:T(8,128)(2,1)S(1)}) custom-call(s32[4]{0:T(128)S(1)} %and_select_fusion.place, f32[72,3584]{1,0:T(8,128)} %get-tuple-element.35.low, f32[72,3584]{1,0:T(8,128)} %get-tuple-element.36.high, ...), custom_call_target="tpu_custom_call" | custom-call | flops 2147483648 | bytes 4194304 | tf_op jit(solution)/shard_map/partials_z/pallas_call | solution.py:236
  164.7 4.7 %collective-permute-start.21 = (bf16[36,3584]{1,0:T(8,128)(2,1)S(1)}, bf16[36,3584]{1,0:T(8,128)(2,1)}, u32[]{:S(2)}, u32[]{:S(2)}) collective-permute-start(bf16[36,3584]{1,0:T(8,128)(2,1)S(1)} %get-tuple-element.42), channel_id=1, source_target_pairs={{0,8},{8,16},{16,24},{24,0},{1,9},{9,17},{17,25},{25,1},{2,10},{10... | collective-permute-start | bytes 774152 | tf_op jit(solution)/shard_map/partials_z/ppermute | solution.py:18
  174.6 11.4 %all-to-all-start.4 = ((bf16[8,256,224]{1,2,0:T(8,128)(2,1)}), bf16[8,256,224]{1,2,0:T(8,128)(2,1)S(1)}, u32[]{:S(2)}, u32[]{:S(2)}) async-start(bf16[8,256,224]{1,2,0:T(8,128)(2,1)} %copy.71), calls=%async_computation.4 | async-start | bytes 1835008 | tf_op jit(solution)/shard_map/dense_out/all_to_all | solution.py:22
  188.5 10.1 %all-to-all-done.4 = bf16[8,256,224]{1,2,0:T(8,128)(2,1)S(1)} async-done(((bf16[8,256,224]{1,2,0:T(8,128)(2,1)}), bf16[8,256,224]{1,2,0:T(8,128)(2,1)S(1)}, u32[]{:S(2)}, u32[]{:S(2)}) %all-to-all-start.4) | async-done | bytes 917536 | tf_op jit(solution)/shard_map/dense_out/all_to_all | solution.py:22
  198.5 5.3 %all-to-all-start.5 = ((bf16[8,36,448]{2,1,0:T(8,128)(2,1)}), bf16[8,36,448]{2,1,0:T(8,128)(2,1)S(1)}, u32[]{:S(2)}, u32[]{:S(2)}) async-start(bf16[8,36,448]{2,1,0:T(8,128)(2,1)} %bitcast.44), calls=%async_computation.5 | async-start | bytes 655360 | tf_op jit(solution)/shard_map/combine/all_to_all | solution.py:22
  209.7 3.4 %collective-permute-start.9 = (bf16[64,224]{1,0:T(8,128)(2,1)S(1)}, bf16[64,224]{1,0:T(8,128)(2,1)S(1)}, u32[]{:S(2)}, u32[]{:S(2)}) collective-permute-start(bf16[64,224]{1,0:T(8,128)(2,1)S(1)} %get-tuple-element.50), channel_id=1, source_target_pairs={{0,24},{8,0},{16,8},{24,16},{1,25},{9,1},{17,9},{25,17},{2,26},{10... | collective-permute-start | bytes 86024 | tf_op jit(solution)/shard_map/dense_out/ppermute | solution.py:18
  213.2 2.9 %collective-permute-done.9 = bf16[64,224]{1,0:T(8,128)(2,1)S(1)} collective-permute-done((bf16[64,224]{1,0:T(8,128)(2,1)S(1)}, bf16[64,224]{1,0:T(8,128)(2,1)S(1)}, u32[]{:S(2)}, u32[]{:S(2)}) %collective-permute-start.9) | collective-permute-done | bytes 28704 | tf_op jit(solution)/shard_map/dense_out/ppermute | solution.py:18
  216.8 3.7 %collective-permute-start.10 = (bf16[2,64,224]{2,1,0:T(8,128)(2,1)S(1)}, bf16[2,64,224]{2,1,0:T(8,128)(2,1)S(1)}, u32[]{:S(2)}, u32[]{:S(2)}) collective-permute-start(bf16[2,64,224]{2,1,0:T(8,128)(2,1)S(1)} %constant_dynamic-slice_fusion), channel_id=1, source_target_pairs={{0,1},{1,0},{2,3},{3,2},{4,5},{5,4},{6,7},{7,6},{8,9},{9,8},{10,11... | collective-permute-start | bytes 172040 | tf_op jit(solution)/shard_map/dense_out/ppermute | solution.py:18
  221.9 8.8 %collective-permute-start.22 = (bf16[128,448]{0,1:T(8,128)(2,1)S(1)}, bf16[128,448]{0,1:T(8,128)(2,1)S(1)}, u32[]{:S(2)}, u32[]{:S(2)}) collective-permute-start(bf16[128,448]{0,1:T(8,128)(2,1)S(1)} %fusion.1), channel_id=1, source_target_pairs={{0,128},{128,256},{256,384},{384,0},{1,129},{129,257},{257,385},{3... | collective-permute-start | bytes 344072 | tf_op jit(solution)/shard_map/next_section/ppermute | solution.py:18
  230.7 12.9 %collective-permute-done.22 = bf16[128,448]{0,1:T(8,128)(2,1)S(1)} collective-permute-done((bf16[128,448]{0,1:T(8,128)(2,1)S(1)}, bf16[128,448]{0,1:T(8,128)(2,1)S(1)}, u32[]{:S(2)}, u32[]{:S(2)}) %collective-permute-start.22) | collective-permute-done | bytes 114720 | tf_op jit(solution)/shard_map/next_section/ppermute | solution.py:18
  (130 shorter events, 65.4 us)
Async XLA Ops:
  7.0 34.0 %all-to-all-start = ((bf16[4,40,3584]{2,1,0:T(8,128)(2,1)}), bf16[4,40,3584]{2,1,0:T(8,128)(2,1)}, u32[]{:S(2)}, u32[]{:S(2)}) async-start(bf16[4,40,3584]{2,1,0:T(8,128)(2,1)} %pad_maximum_fusion.1), calls=%async_computation | async-start | bytes 2293760 | tf_op jit(solution)/shard_map/rows_z/all_to_all | solution.py:22
  11.6 21.0 %collective-permute-start = (bf16[224,1152]{1,0:T(8,128)(2,1)S(1)}, bf16[224,1152]{1,0:T(8,128)(2,1)S(1)}, u32[]{:S(2)}, u32[]{:S(2)}) collective-permute-start(bf16[224,1152]{1,0:T(8,128)(2,1)S(1)} %pad_maximum_fusion.2.refs_0_), channel_id=1, source_target_pairs={{0,32},{32,64},{64,96},{96,0},{1,33},{33,65},{65,97},{97,1},{2,34}... | collective-permute-start | bytes 1548296 | tf_op jit(solution)/shard_map/dense_weights/ppermute | solution.py:18
  14.8 24.2 %collective-permute-start.1 = (bf16[224,1152]{1,0:T(8,128)(2,1)S(1)}, bf16[224,1152]{1,0:T(8,128)(2,1)S(1)}, u32[]{:S(2)}, u32[]{:S(2)}) collective-permute-start(bf16[224,1152]{1,0:T(8,128)(2,1)S(1)} %pad_maximum_fusion.2.refs_0_), channel_id=1, source_target_pairs={{0,64},{32,96},{64,0},{96,32},{1,65},{33,97},{65,1},{97,33},{2,66}... | collective-permute-start | bytes 1548296 | tf_op jit(solution)/shard_map/dense_weights/ppermute | solution.py:18
  19.3 21.6 %collective-permute-start.2 = (bf16[224,1152]{1,0:T(8,128)(2,1)S(1)}, bf16[224,1152]{1,0:T(8,128)(2,1)}, u32[]{:S(2)}, u32[]{:S(2)}) collective-permute-start(bf16[224,1152]{1,0:T(8,128)(2,1)S(1)} %pad_maximum_fusion.2.refs_0_), channel_id=1, source_target_pairs={{0,96},{32,0},{64,32},{96,64},{1,97},{33,1},{65,33},{97,65},{2,98}... | collective-permute-start | bytes 1548296 | tf_op jit(solution)/shard_map/dense_weights/ppermute | solution.py:18
  43.1 40.1 %all-to-all-start.1 = ((bf16[8,4,16,896]{3,2,1,0:T(8,128)(2,1)}), bf16[8,4,16,896]{3,2,1,0:T(8,128)(2,1)}, u32[]{:S(2)}, u32[]{:S(2)}) async-start(bf16[8,4,16,896]{3,2,1,0:T(8,128)(2,1)} %broadcast_in_dim.28), calls=%async_computation.1 | async-start | bytes 1835008 | tf_op jit(solution)/shard_map/dense_tokens/all_to_all | solution.py:22
  52.5 16.2 %collective-permute-start.3 = (bf16[72,3584]{1,0:T(8,128)(2,1)S(1)}, bf16[72,3584]{1,0:T(8,128)(2,1)}, u32[]{:S(2)}, u32[]{:S(2)}) collective-permute-start(bf16[72,3584]{1,0:T(8,128)(2,1)S(1)} %reshape.155.refs_0_), channel_id=1, source_target_pairs={{0,32},{32,64},{64,96},{96,0},{1,33},{33,65},{65,97},{97,1},{2,34}... | collective-permute-start | bytes 1548296 | tf_op jit(solution)/shard_map/rows_y/ppermute | solution.py:18
  56.7 14.7 %collective-permute-start.6 = (bf16[72,3584]{1,0:T(8,128)(2,1)S(1)}, bf16[72,3584]{1,0:T(8,128)(2,1)S(1)}, u32[]{:S(2)}, u32[]{:S(2)}) collective-permute-start(bf16[72,3584]{1,0:T(8,128)(2,1)S(1)} %reshape.156.refs_1_), channel_id=1, source_target_pairs={{0,96},{32,0},{64,32},{96,64},{1,97},{33,1},{65,33},{97,65},{2,98}... | collective-permute-start | bytes 1548296 | tf_op jit(solution)/shard_map/rows_y/ppermute | solution.py:18
  59.1 23.2 %collective-permute-start.4 = (bf16[72,3584]{1,0:T(8,128)(2,1)S(1)}, bf16[72,3584]{1,0:T(8,128)(2,1)S(1)}, u32[]{:S(2)}, u32[]{:S(2)}) collective-permute-start(bf16[72,3584]{1,0:T(8,128)(2,1)S(1)} %reshape.155.refs_0_), channel_id=1, source_target_pairs={{0,96},{32,0},{64,32},{96,64},{1,97},{33,1},{65,33},{97,65},{2,98}... | collective-permute-start | bytes 1548296 | tf_op jit(solution)/shard_map/rows_y/ppermute | solution.py:18
  62.2 21.0 %collective-permute-start.5 = (bf16[72,3584]{1,0:T(8,128)(2,1)S(1)}, bf16[72,3584]{1,0:T(8,128)(2,1)}, u32[]{:S(2)}, u32[]{:S(2)}) collective-permute-start(bf16[72,3584]{1,0:T(8,128)(2,1)S(1)} %reshape.156.refs_1_), channel_id=1, source_target_pairs={{0,32},{32,64},{64,96},{96,0},{1,33},{33,65},{65,97},{97,1},{2,34}... | collective-permute-start | bytes 1548296 | tf_op jit(solution)/shard_map/rows_y/ppermute | solution.py:18
  71.4 22.8 %copy-start.16 = (bf16[72,3584]{1,0:T(8,128)(2,1)}, bf16[72,3584]{1,0:T(8,128)(2,1)S(1)}, u32[]{:S(2)}) copy-start(bf16[72,3584]{1,0:T(8,128)(2,1)S(1)} %collective-permute-done.6.refs_2_) | copy-start | bytes 1548292
  87.4 42.0 %all-to-all-start.2 = ((bf16[4,128,768]{2,1,0:T(8,128)(2,1)}), bf16[4,128,768]{2,1,0:T(8,128)(2,1)}, u32[]{:S(2)}, u32[]{:S(2)}) async-start(bf16[4,128,768]{2,1,0:T(8,128)(2,1)} %dense_tokens.1), calls=%async_computation.2 | async-start | bytes 1572864 | tf_op jit(solution)/shard_map/dense_hidden/all_to_all | solution.py:22
  92.0 14.5 %collective-permute-start.11 = (bf16[72,3584]{1,0:T(8,128)(2,1)}, bf16[72,3584]{1,0:T(8,128)(2,1)S(1)}, u32[]{:S(2)}, u32[]{:S(2)}) collective-permute-start(bf16[72,3584]{1,0:T(8,128)(2,1)} %collective-permute-done.3.refs_3_), channel_id=1, source_target_pairs={{0,32},{32,64},{64,96},{96,0},{1,33},{33,65},{65,97},{97,1},{2,34}... | collective-permute-start | bytes 1548296 | tf_op jit(solution)/shard_map/rows_y/ppermute | solution.py:18
  94.2 12.9 %collective-permute-start.12 = (bf16[72,3584]{1,0:T(8,128)(2,1)S(1)}, bf16[72,3584]{1,0:T(8,128)(2,1)S(1)}, u32[]{:S(2)}, u32[]{:S(2)}) collective-permute-start(bf16[72,3584]{1,0:T(8,128)(2,1)S(1)} %collective-permute-done.6.refs_2_), channel_id=1, source_target_pairs={{0,96},{32,0},{64,32},{96,64},{1,97},{33,1},{65,33},{97,65},{2,98}... | collective-permute-start | bytes 1548296 | tf_op jit(solution)/shard_map/rows_y/ppermute | solution.py:18
  115.6 20.5 %collective-permute-start.14 = (bf16[72,3584]{1,0:T(8,128)(2,1)}, bf16[72,3584]{1,0:T(8,128)(2,1)}, u32[]{:S(2)}, u32[]{:S(2)}) collective-permute-start(bf16[72,3584]{1,0:T(8,128)(2,1)} %get-tuple-element.33), channel_id=1, source_target_pairs={{0,96},{32,0},{64,32},{96,64},{1,97},{33,1},{65,33},{97,65},{2,98}... | collective-permute-start | bytes 1548296 | tf_op jit(solution)/shard_map/partials_y/ppermute | solution.py:18
  121.0 21.9 %collective-permute-start.13 = (bf16[72,3584]{1,0:T(8,128)(2,1)}, bf16[72,3584]{1,0:T(8,128)(2,1)}, u32[]{:S(2)}, u32[]{:S(2)}) collective-permute-start(bf16[72,3584]{1,0:T(8,128)(2,1)} %get-tuple-element.31), channel_id=1, source_target_pairs={{0,32},{32,64},{64,96},{96,0},{1,33},{33,65},{65,97},{97,1},{2,34}... | collective-permute-start | bytes 1548296 | tf_op jit(solution)/shard_map/partials_y/ppermute | solution.py:18
  122.9 29.0 %collective-permute-start.16 = (bf16[72,3584]{1,0:T(8,128)(2,1)}, bf16[72,3584]{1,0:T(8,128)(2,1)}, u32[]{:S(2)}, u32[]{:S(2)}) collective-permute-start(bf16[72,3584]{1,0:T(8,128)(2,1)} %get-tuple-element.37), channel_id=1, source_target_pairs={{0,96},{32,0},{64,32},{96,64},{1,97},{33,1},{65,33},{97,65},{2,98}... | collective-permute-start | bytes 1548296 | tf_op jit(solution)/shard_map/partials_y/ppermute | solution.py:18
  127.5 24.4 %collective-permute-start.17 = (bf16[72,3584]{1,0:T(8,128)(2,1)}, bf16[72,3584]{1,0:T(8,128)(2,1)}, u32[]{:S(2)}, u32[]{:S(2)}) collective-permute-start(bf16[72,3584]{1,0:T(8,128)(2,1)} %get-tuple-element.38), channel_id=1, source_target_pairs={{0,32},{32,64},{64,96},{96,0},{1,33},{33,65},{65,97},{97,1},{2,34}... | collective-permute-start | bytes 1548296 | tf_op jit(solution)/shard_map/partials_y/ppermute | solution.py:18
  131.6 37.9 %all-to-all-start.3 = ((bf16[4,128,384]{2,1,0:T(8,128)(2,1)}), bf16[4,128,384]{2,1,0:T(8,128)(2,1)S(1)}, u32[]{:S(2)}, u32[]{:S(2)}) async-start(bf16[4,128,384]{2,1,0:T(8,128)(2,1)} %broadcast_in_dim.55), calls=%async_computation.3 | async-start | bytes 786432 | tf_op jit(solution)/shard_map/dense_out/all_to_all | solution.py:22
  138.3 13.6 %collective-permute-start.18 = (bf16[72,3584]{1,0:T(8,128)(2,1)}, bf16[72,3584]{1,0:T(8,128)(2,1)}, u32[]{:S(2)}, u32[]{:S(2)}) collective-permute-start(bf16[72,3584]{1,0:T(8,128)(2,1)} %partials_y.4), channel_id=1, source_target_pairs={{0,96},{32,0},{64,32},{96,64},{1,97},{33,1},{65,33},{97,65},{2,98}... | collective-permute-start | bytes 1548296 | tf_op jit(solution)/shard_map/partials_y/ppermute | solution.py:18
  145.1 11.4 %collective-permute-start.15 = (bf16[72,3584]{1,0:T(8,128)(2,1)}, bf16[72,3584]{1,0:T(8,128)(2,1)}, u32[]{:S(2)}, u32[]{:S(2)}) collective-permute-start(bf16[72,3584]{1,0:T(8,128)(2,1)} %partials_y.3), channel_id=1, source_target_pairs={{0,32},{32,64},{64,96},{96,0},{1,33},{33,65},{65,97},{97,1},{2,34}... | collective-permute-start | bytes 1548296 | tf_op jit(solution)/shard_map/partials_y/ppermute | solution.py:18
  160.2 25.7 %collective-permute-start.19 = (bf16[36,3584]{1,0:T(8,128)(2,1)}, bf16[36,3584]{1,0:T(8,128)(2,1)}, u32[]{:S(2)}, u32[]{:S(2)}) collective-permute-start(bf16[36,3584]{1,0:T(8,128)(2,1)} %get-tuple-element.40), channel_id=1, source_target_pairs={{0,24},{8,0},{16,8},{24,16},{1,25},{9,1},{17,9},{25,17},{2,26},{10... | collective-permute-start | bytes 774152 | tf_op jit(solution)/shard_map/partials_z/ppermute | solution.py:18
  162.4 23.5 %collective-permute-start.20 = (bf16[36,3584]{1,0:T(8,128)(2,1)}, bf16[36,3584]{1,0:T(8,128)(2,1)}, u32[]{:S(2)}, u32[]{:S(2)}) collective-permute-start(bf16[36,3584]{1,0:T(8,128)(2,1)} %get-tuple-element.41), channel_id=1, source_target_pairs={{0,16},{8,24},{16,0},{24,8},{1,17},{9,25},{17,1},{25,9},{2,18},{10... | collective-permute-start | bytes 774152 | tf_op jit(solution)/shard_map/partials_z/ppermute | solution.py:18
  164.7 21.3 %collective-permute-start.21 = (bf16[36,3584]{1,0:T(8,128)(2,1)S(1)}, bf16[36,3584]{1,0:T(8,128)(2,1)}, u32[]{:S(2)}, u32[]{:S(2)}) collective-permute-start(bf16[36,3584]{1,0:T(8,128)(2,1)S(1)} %get-tuple-element.42), channel_id=1, source_target_pairs={{0,8},{8,16},{16,24},{24,0},{1,9},{9,17},{17,25},{25,1},{2,10},{10... | collective-permute-start | bytes 774152 | tf_op jit(solution)/shard_map/partials_z/ppermute | solution.py:18
  174.6 24.0 %all-to-all-start.4 = ((bf16[8,256,224]{1,2,0:T(8,128)(2,1)}), bf16[8,256,224]{1,2,0:T(8,128)(2,1)S(1)}, u32[]{:S(2)}, u32[]{:S(2)}) async-start(bf16[8,256,224]{1,2,0:T(8,128)(2,1)} %copy.71), calls=%async_computation.4 | async-start | bytes 1835008 | tf_op jit(solution)/shard_map/dense_out/all_to_all | solution.py:22
  187.3 33.3 %copy-start.7 = (bf16[128,288]{0,1:T(8,128)(2,1)S(1)}, bf16[128,288]{0,1:T(8,128)(2,1)}, u32[]{:S(2)}) copy-start(bf16[128,288]{0,1:T(8,128)(2,1)} %get-tuple-element.24) | copy-start | bytes 221188
  198.5 14.6 %all-to-all-start.5 = ((bf16[8,36,448]{2,1,0:T(8,128)(2,1)}), bf16[8,36,448]{2,1,0:T(8,128)(2,1)S(1)}, u32[]{:S(2)}, u32[]{:S(2)}) async-start(bf16[8,36,448]{2,1,0:T(8,128)(2,1)} %bitcast.44), calls=%async_computation.5 | async-start | bytes 655360 | tf_op jit(solution)/shard_map/combine/all_to_all | solution.py:22
  203.9 17.7 %copy-start.11 = (bf16[1,128,448]{1,2,0:T(8,128)(2,1)S(1)}, bf16[1,128,448]{1,2,0:T(8,128)(2,1)}, u32[]{:S(2)}) copy-start(bf16[1,128,448]{1,2,0:T(8,128)(2,1)} %param.11) | copy-start | bytes 344068
  204.1 9.1 %collective-permute-start.7 = (bf16[64,224]{1,0:T(8,128)(2,1)S(1)}, bf16[64,224]{1,0:T(8,128)(2,1)S(1)}, u32[]{:S(2)}, u32[]{:S(2)}) collective-permute-start(bf16[64,224]{1,0:T(8,128)(2,1)S(1)} %get-tuple-element.52), channel_id=1, source_target_pairs={{0,8},{8,16},{16,24},{24,0},{1,9},{9,17},{17,25},{25,1},{2,10},{10... | collective-permute-start | bytes 86024 | tf_op jit(solution)/shard_map/dense_out/ppermute | solution.py:18
  206.9 6.3 %collective-permute-start.8 = (bf16[64,224]{1,0:T(8,128)(2,1)S(1)}, bf16[64,224]{1,0:T(8,128)(2,1)S(1)}, u32[]{:S(2)}, u32[]{:S(2)}) collective-permute-start(bf16[64,224]{1,0:T(8,128)(2,1)S(1)} %get-tuple-element.51), channel_id=1, source_target_pairs={{0,16},{8,24},{16,0},{24,8},{1,17},{9,25},{17,1},{25,9},{2,18},{10... | collective-permute-start | bytes 86024 | tf_op jit(solution)/shard_map/dense_out/ppermute | solution.py:18
  209.7 6.5 %collective-permute-start.9 = (bf16[64,224]{1,0:T(8,128)(2,1)S(1)}, bf16[64,224]{1,0:T(8,128)(2,1)S(1)}, u32[]{:S(2)}, u32[]{:S(2)}) collective-permute-start(bf16[64,224]{1,0:T(8,128)(2,1)S(1)} %get-tuple-element.50), channel_id=1, source_target_pairs={{0,24},{8,0},{16,8},{24,16},{1,25},{9,1},{17,9},{25,17},{2,26},{10... | collective-permute-start | bytes 86024 | tf_op jit(solution)/shard_map/dense_out/ppermute | solution.py:18
  216.8 4.6 %collective-permute-start.10 = (bf16[2,64,224]{2,1,0:T(8,128)(2,1)S(1)}, bf16[2,64,224]{2,1,0:T(8,128)(2,1)S(1)}, u32[]{:S(2)}, u32[]{:S(2)}) collective-permute-start(bf16[2,64,224]{2,1,0:T(8,128)(2,1)S(1)} %constant_dynamic-slice_fusion), channel_id=1, source_target_pairs={{0,1},{1,0},{2,3},{3,2},{4,5},{5,4},{6,7},{7,6},{8,9},{9,8},{10,11... | collective-permute-start | bytes 172040 | tf_op jit(solution)/shard_map/dense_out/ppermute | solution.py:18
  221.9 21.7 %collective-permute-start.22 = (bf16[128,448]{0,1:T(8,128)(2,1)S(1)}, bf16[128,448]{0,1:T(8,128)(2,1)S(1)}, u32[]{:S(2)}, u32[]{:S(2)}) collective-permute-start(bf16[128,448]{0,1:T(8,128)(2,1)S(1)} %fusion.1), channel_id=1, source_target_pairs={{0,128},{128,256},{256,384},{384,0},{1,129},{129,257},{257,385},{3... | collective-permute-start | bytes 344072 | tf_op jit(solution)/shard_map/next_section/ppermute | solution.py:18
  (17 other events, 103.5 us)

commit v8 on v7

--- a/solution.py
+++ b/solution.py
@@ -46,58 +46,52 @@
     return jnp.sum(named * earlier[:, None, :], axis=2, dtype=jnp.int32)
 
 
-def local_call(kernel, out_shape, **kwargs):
+def local_call(kernel, out_shape, flops=2 * 1024**3, **kwargs):
     return pl.pallas_call(
         kernel,
         out_shape=out_shape,
         compiler_params=pltpu.CompilerParams(vmem_limit_bytes=52 * 1024 * 1024),
         cost_estimate=pl.CostEstimate(
-            flops=2 * 1024**3, bytes_accessed=4 * 1024**2, transcendentals=0
+            flops=flops, bytes_accessed=4 * 1024**2, transcendentals=0
         ),
         **kwargs,
     )
 
 
-def expert_rows(parts, gate_up, down):
+def rows_kernel(count, gate_up, down, *refs):
+    parts, outs, whole = refs[:count], refs[count : 2 * count], refs[-1]
+    start, spans = 0, []
+    for part in parts:
+        spans.append(slice(start, start + part.shape[0]))
+        whole[spans[-1]] = part[...].astype(F32)
+        start += part.shape[0]
     inner = down.shape[0]
-    rows = jnp.concatenate([part[...].astype(F32) for part in parts], axis=0).astype(BF16)
-    both = dot(rows, gate_up[...])
-    start = both.shape[1] // 2
-    first, second = both[:, :inner], both[:, start : start + inner]
-    return dot((first / (1.0 + jnp.exp(-first)) * second).astype(BF16), down[...])
-
-
-def rows_kernel(gate_up, down, *refs):
-    parts, outs = refs[: len(refs) // 2], refs[len(refs) // 2 :]
-    result = expert_rows(parts, gate_up, down)
-    size = parts[0].shape[0]
-    for k, out in enumerate(outs):
-        out[...] = result[k * size : (k + 1) * size].astype(out.dtype)
-
-
-def dense_in_kernel(columns, tokens, *refs):
-    weights, out = refs[:4], refs[4]
+    both = dot(whole[...].astype(BF16), gate_up[...])
+    middle = both.shape[1] // 2
+    first, second = both[:, :inner], both[:, middle : middle + inner]
+    act = (first / (1.0 + jnp.exp(-first)) * second).astype(BF16)
+    whole[...] = dot(act, down[...])
+    for span, out in zip(spans, outs):
+        out[...] = whole[span].astype(out.dtype)
+
+
+def rows_and_dense_kernel(count, columns, tokens, *refs):
+    weights, rest, pre, whole = refs[:4], refs[4:-2], refs[-2], refs[-1]
     joined = jnp.concatenate([part[:, :columns] for part in weights], axis=0)
     for z in range(4):
         rows = jnp.concatenate([tokens[e, z] for e in range(tokens.shape[0])], axis=0)
-        out[z] = dot(rows, joined).astype(BF16)
-
-
-def late_kernel(part, relay, out):
-    out[...] = (part[...] + relay[...].astype(F32)).astype(BF16)
-
-
-def total_kernel(capacity, place, low, high, *refs):
-    sums, outs, whole = refs[:4], refs[4:8], refs[8]
-    half = 2 * capacity
-    whole[:half] = low[...] + sums[0][...].astype(F32) + sums[1][...].astype(F32)
-    whole[half:] = high[...] + sums[2][...].astype(F32) + sums[3][...].astype(F32)
+        pre[z] = dot(rows, joined).astype(BF16)
+    rows_kernel(count, *rest, whole)
+
+
+def total_kernel(own, one, two, three, *refs):
+    outs, whole = refs[:3], refs[3]
+    whole[...] = own[...] + (
+        one[...].astype(F32) + two[...].astype(F32) + three[...].astype(F32)
+    )
+    size = outs[0].shape[0]
     for k, out in enumerate(outs):
-        for j in range(4):
-
-            @pl.when(place[k] == j)
-            def _(out=out, j=j):
-                out[...] = whole[j * capacity : (j + 1) * capacity].astype(out.dtype)
+        out[...] = whole[k * size : (k + 1) * size].astype(out.dtype)
 
 
 def in_line_order(parts, axis):
@@ -182,32 +176,32 @@
         arrived = exchanged(jnp.concatenate(sent, axis=1), "z")
         line_share = arrived[:, capacity:].reshape(4, share, slab)
         coarse, fine, gate_up = after((coarse, fine, gate_up), routed)
-        group = after(arrived, coarse, fine, gate_up, *slabs[1:])[:, :capacity]
-        low, high = (block.reshape(half, width) for block in (group[:2], group[2:]))
-
+
+    around = (1, -1, 2)
     with jax.named_scope("rows_y"):
-        prev_low, next_low = shifted(low, "y", 1), shifted(low, "y", -1)
-        far_low = shifted(prev_low, "y", 1)
-        next_high, prev_high = shifted(high, "y", -1), shifted(high, "y", 1)
-        far_high = shifted(next_high, "y", -1)
+        own_rows = [shifted(routed, "y", by) for by in around]
+        line = after(arrived, coarse, fine, gate_up, slabs[1], slabs[3], *own_rows)[:, :capacity]
+        line = line.at[place_z[1:]].get(mode="promise_in_bounds").reshape(3 * capacity, width)
+        line_rows = [shifted(line, "y", by) for by in around]
 
     with jax.named_scope("dense_tokens"):
         line_tokens = exchanged(repeated(line_share, n_expert), EXPERT_AXES)
-        line_tokens = after(line_tokens, prev_low, next_low, prev_high, next_high)
-        pre = local_call(
-            functools.partial(dense_in_kernel, 2 * hidden),
-            jax.ShapeDtypeStruct((4, tok_rows, 2 * hidden), BF16),
-        )(line_tokens, *slabs)
-
-    half_bf16, half_f32 = (jax.ShapeDtypeStruct(low.shape, dtype) for dtype in (BF16, F32))
-    in_smem, in_vmem = (pl.BlockSpec(memory_space=space) for space in (pltpu.SMEM, pltpu.VMEM))
+
+    def held(like, dtype):
+        return jax.ShapeDtypeStruct(like.shape, dtype)
+
     with jax.named_scope("experts"):
-        relay_next, relay_prev, early_next, early_prev, next_part, prev_part = local_call(
-            rows_kernel, [half_bf16] * 4 + [half_f32] * 2
-        )(gate_up, down, far_low, far_high, next_high, prev_low, next_low, prev_high)
-
+        *parts, pre = local_call(
+            functools.partial(rows_and_dense_kernel, 6, 2 * hidden),
+            [held(line, BF16)] * 3
+            + [held(routed, BF16)] * 3
+            + [jax.ShapeDtypeStruct((4, tok_rows, 2 * hidden), BF16)],
+            scratch_shapes=[pltpu.VMEM((12 * capacity, width), F32)],
+        )(line_tokens, *slabs, gate_up, down, *line_rows, *own_rows)
     with jax.named_scope("partials_y"):
-        relay_next, relay_prev = shifted(relay_next, "y", 1), shifted(relay_prev, "y", -1)
+        line_back = [shifted(part, "y", -by) for part, by in zip(parts[:3], around)]
+        own_back = [shifted(part, "y", -by) for part, by in zip(parts[3:], around)]
+
     with jax.named_scope("dense_hidden"):
         pre = exchanged(pre, "z")
         pre = jnp.sum(pre.astype(F32), axis=0)
@@ -219,28 +213,25 @@
         by_block = local_call(
             functools.partial(dense_out_kernel, 2 * hidden),
             jax.ShapeDtypeStruct((n_expert, 4 * half_tokens, step), BF16),
-            in_specs=[in_smem] + [in_vmem] * 5,
+            in_specs=[pl.BlockSpec(memory_space=pltpu.SMEM)]
+            + [pl.BlockSpec(memory_space=pltpu.VMEM)] * 5,
         )(place_y, every_act, *slabs)
 
-    with jax.named_scope("partials_y"):
-        early_next, early_prev = shifted(early_next, "y", 1), shifted(early_prev, "y", -1)
-        late_next = local_call(late_kernel, half_bf16)(next_part, relay_next)
-        late_prev = local_call(late_kernel, half_bf16)(prev_part, relay_prev)
-        own_low, own_high = local_call(rows_kernel, [half_f32] * 2)(
-            after(gate_up, late_next, late_prev), down, low, high
-        )
-        late_next, late_prev = shifted(late_next, "y", 1), shifted(late_prev, "y", -1)
-
+    with jax.named_scope("experts"):
+        line_part, own_part = local_call(
+            functools.partial(rows_kernel, 2),
+            [held(line, F32), held(routed, F32)],
+            scratch_shapes=[pltpu.VMEM((4 * capacity, width), F32)],
+        )(after(gate_up, parts[0]), down, line, routed)
     with jax.named_scope("partials_z"):
-        rows_f32, rows_bf16 = (jax.ShapeDtypeStruct(routed.shape, dtype) for dtype in (F32, BF16))
-        kept_rows, *sent = local_call(
-            functools.partial(total_kernel, capacity),
-            [rows_f32] + [rows_bf16] * 3,
-            in_specs=[in_smem] + [in_vmem] * 6,
-            scratch_shapes=[pltpu.VMEM((4 * capacity, width), F32)],
-        )(place_z, own_low, own_high, late_next, early_prev, early_next, late_prev)
+        sent = local_call(
+            total_kernel,
+            [held(routed, BF16)] * 3,
+            flops=200 * 1024**3,
+            scratch_shapes=[pltpu.VMEM((3 * capacity, width), F32)],
+        )(line_part, *line_back)
         recv = [shifted(part, "z", by) for part, by in zip(sent, (-1, -2, -3))]
-        expert_out = (kept_rows + sum(part.astype(F32) for part in recv)).astype(BF16)
+        expert_out = (own_part + sum(part.astype(F32) for part in own_back + recv)).astype(BF16)
 
     with jax.named_scope("dense_out"):
         block_sum = jnp.sum(exchanged(by_block, EXPERT_AXES).astype(F32), axis=0).astype(BF16)

time: 246 us -> 253 us (1.028)
  waiting for transfers between devices: 66.1 us -> 74.7 us
  Pallas kernels: 26.7 us -> 20.6 us
  local copies, waits for them, and re-layouts: 21.6 us -> 26.3 us
    ppermute x23, waiting for transfers between devices: 56 us -> 65 us  [shifted(): return lax.ppermute(x, axis, [(i, (i + by) % peers) for i in range(peers)])]
    pallas_call x6 -> x3, Pallas kernels: 23.9 us -> 17.6 us  [the longest x1 9.27 us: body(): local_call(functools.partial(rows_and_dense_kernel, 6, 2 * hidden), [held...]
    all_to_all x6, starting transfers between devices: 36.4 us -> 40.7 us  [exchanged(): return lax.all_to_all(x, axes, split_axis=0, concat_axis=0, tiled=True)]
    unnamed x43 -> x49, local copies, waits for them, and re-layouts: 9.42 us -> 13.3 us
    ppermute x23, starting transfers between devices: 79.8 us -> 76 us  [shifted(): return lax.ppermute(x, axis, [(i, (i + by) % peers) for i in range(peers)])]
    gather x0 -> x1, local copies, waits for them, and re-layouts: none -> 3.08 us  [body(): line.at[place_z[1:]].get(mode='promise_in_bounds')]
  transfers between devices with their start and end apart: 29 -> 29, of which waited for: 12 -> 6; matrix products, arithmetic and copies ran while one was open for 9% -> 10% of each run, Pallas kernels for 10% -> 4%
where the time goes in v8:
time: 253 us; the launch traced here: 252 us
  starting transfers between devices  117 us (46%)
  waiting for transfers between devices  74.7 us (30%)
  local copies, waits for them, and re-layouts  26.3 us (10%)
  Pallas kernels  20.6 us (8%)
  other arithmetic  11.9 us (5%)
    ppermute x23, starting transfers between devices, shifted(): return lax.ppermute(x, axis, [(i, (i + by) % peers) for i in range(peers)])  76 us
    ppermute x23, waiting for transfers between devices, shifted(): return lax.ppermute(x, axis, [(i, (i + by) % peers) for i in range(peers)])  65 us
    all_to_all x6, starting transfers between devices, exchanged(): return lax.all_to_all(x, axes, split_axis=0, concat_axis=0, tiled=True)  40.7 us
    unnamed x49, local copies, waits for them, and re-layouts  13.3 us
    all_to_all x6, waiting for transfers between devices, exchanged(): return lax.all_to_all(x, axes, split_axis=0, concat_axis=0, tiled=True)  9.73 us
    pallas_call x1, Pallas kernels, body(): local_call(functools.partial(rows_and_dense_kernel, 6, 2 * hidden), [held...  9.27 us
  transfers between devices with their start and end apart: 29, of which 6 were waited for; matrix products, arithmetic and copies ran while one was open for 10% of the time, Pallas kernels for 4%

profile of v8, /device:TPU:99, one launch (start us, length us, event | category | flops | bytes accessed | tf_op | source)
XLA Modules:
  0.0 251.9 jit_solution(9166411753089957036)
XLA Ops:
  5.7 4.5 %all-to-all-start = ((bf16[4,40,3584]{2,1,0:T(8,128)(2,1)}), bf16[4,40,3584]{2,1,0:T(8,128)(2,1)}, u32[]{:S(2)}, u32[]{:S(2)}) async-start(bf16[4,40,3584]{2,1,0:T(8,128)(2,1)} %pad_maximum_fusion.1), calls=%async_computation | async-start | bytes 2293760 | tf_op jit(solution)/shard_map/rows_z/all_to_all | solution.py:22
  10.3 3.2 %collective-permute-start = (bf16[224,1152]{1,0:T(8,128)(2,1)S(1)}, bf16[224,1152]{1,0:T(8,128)(2,1)S(1)}, u32[]{:S(2)}, u32[]{:S(2)}) collective-permute-start(bf16[224,1152]{1,0:T(8,128)(2,1)S(1)} %pad_maximum_fusion.2.refs_0_), channel_id=1, source_target_pairs={{0,32},{32,64},{64,96},{96,0},{1,33},{33,65},{65,97},{97,1},{2,34}... | collective-permute-start | bytes 1548296 | tf_op jit(solution)/shard_map/dense_weights/ppermute | solution.py:18
  13.5 3.4 %collective-permute-start.2 = (bf16[224,1152]{1,0:T(8,128)(2,1)S(1)}, bf16[224,1152]{1,0:T(8,128)(2,1)}, u32[]{:S(2)}, u32[]{:S(2)}) collective-permute-start(bf16[224,1152]{1,0:T(8,128)(2,1)S(1)} %pad_maximum_fusion.2.refs_0_), channel_id=1, source_target_pairs={{0,96},{32,0},{64,32},{96,64},{1,97},{33,1},{65,33},{97,65},{2,98}... | collective-permute-start | bytes 1548296 | tf_op jit(solution)/shard_map/dense_weights/ppermute | solution.py:18
  18.8 4.6 %collective-permute-start.4 = (bf16[36,3584]{1,0:T(8,128)(2,1)S(1)}, bf16[36,3584]{1,0:T(8,128)(2,1)S(1)}, u32[]{:S(2)}, u32[]{:S(2)}) collective-permute-start(bf16[36,3584]{1,0:T(8,128)(2,1)S(1)} %convolution_convert_fusion.refs_1_), channel_id=1, source_target_pairs={{0,96},{32,0},{64,32},{96,64},{1,97},{33,1},{65,33},{97,65},{2,98}... | collective-permute-start | bytes 774152 | tf_op jit(solution)/shard_map/rows_y/ppermute | solution.py:18
  31.2 5.0 %pad_maximum_fusion.refs_4_.gate_up = bf16[3584,512]{1,0:T(8,128)(2,1)} fusion(bf16[3584,104]{1,0:T(8,128)(2,1)S(1)} %broadcast_in_dim.57, bf16[3584,152]{1,0:T(8,128)(2,1)} %bitcast.47, bf16[3584,152]{1,0:T(8,128)(2,1)} %bitcast.46), kind=kLoop, calls=%fused_computation.4 | loop fusion | flops 14680064 | bytes 6594560 | tf_op jit(solution)/shard_map/concatenate | solution.py:167
  39.2 9.9 %all-to-all-start.1 = ((bf16[8,4,16,896]{3,2,1,0:T(8,128)(2,1)}), bf16[8,4,16,896]{3,2,1,0:T(8,128)(2,1)}, u32[]{:S(2)}, u32[]{:S(2)}) async-start(bf16[8,4,16,896]{3,2,1,0:T(8,128)(2,1)} %broadcast_in_dim.30), calls=%async_computation.1 | async-start | bytes 1835008 | tf_op jit(solution)/shard_map/dense_tokens/all_to_all | solution.py:22
  50.5 3.1 %gather_fusion.1 = bf16[3,36,3584]{2,1,0:T(8,128)(2,1)} fusion(bf16[4,36,3584]{2,1,0:T(8,128)(2,1)} %bitcast.45, s32[1024]{0:T(1024)S(1)} %pad_clamp_fusion.1), kind=kCustom, calls=%fused_computation.1 | custom fusion | bytes 1548300 | tf_op jit(solution)/shard_map/rows_y/gather | solution.py:184
  57.4 4.0 %collective-permute-start.7 = (bf16[108,3584]{1,0:T(8,128)(2,1)S(1)}, bf16[108,3584]{1,0:T(8,128)(2,1)S(1)}, u32[]{:S(2)}, u32[]{:S(2)}) collective-permute-start(bf16[108,3584]{1,0:T(8,128)(2,1)S(1)} %reshape.152.refs_0_), channel_id=1, source_target_pairs={{0,96},{32,0},{64,32},{96,64},{1,97},{33,1},{65,33},{97,65},{2,98}... | collective-permute-start | bytes 2322440 | tf_op jit(solution)/shard_map/rows_y/ppermute | solution.py:18
  61.4 3.9 %collective-permute-start.8 = (bf16[108,3584]{1,0:T(8,128)(2,1)S(1)}, bf16[108,3584]{1,0:T(8,128)(2,1)}, u32[]{:S(2)}, u32[]{:S(2)}) collective-permute-start(bf16[108,3584]{1,0:T(8,128)(2,1)S(1)} %reshape.152.refs_0_), channel_id=1, source_target_pairs={{0,64},{32,96},{64,0},{96,32},{1,65},{33,97},{65,1},{97,33},{2,66}... | collective-permute-start | bytes 2322440 | tf_op jit(solution)/shard_map/rows_y/ppermute | solution.py:18
  65.3 2.9 %collective-permute-start.1 = (bf16[224,1152]{1,0:T(8,128)(2,1)S(1)}, bf16[224,1152]{1,0:T(8,128)(2,1)S(1)}, u32[]{:S(2)}, u32[]{:S(2)}) collective-permute-start(bf16[224,1152]{1,0:T(8,128)(2,1)S(1)} %pad_maximum_fusion.2.refs_0_), channel_id=1, source_target_pairs={{0,64},{32,96},{64,0},{96,32},{1,65},{33,97},{65,1},{97,33},{2,66}... | collective-permute-start | bytes 1548296 | tf_op jit(solution)/shard_map/dense_weights/ppermute | solution.py:18
  68.2 38.0 %collective-permute-done.1.refs_2_ = bf16[224,1152]{1,0:T(8,128)(2,1)S(1)} collective-permute-done((bf16[224,1152]{1,0:T(8,128)(2,1)S(1)}, bf16[224,1152]{1,0:T(8,128)(2,1)S(1)}, u32[]{:S(2)}, u32[]{:S(2)}) %collective-permute-start.1) | collective-permute-done | bytes 516128 | tf_op jit(solution)/shard_map/dense_weights/ppermute | solution.py:18
  111.0 9.3 %experts.2 = (bf16[108,3584]{1,0:T(8,128)(2,1)}, bf16[108,3584]{1,0:T(8,128)(2,1)}, bf16[108,3584]{1,0:T(8,128)(2,1)}, bf16[36,3584]{1,0:T(8,128)(2,1)}, bf16[36...) custom-call(bf16[8,4,16,896]{3,2,1,0:T(8,128)(2,1)} %all-to-all-done.1.tokens, ...), custom_call_target="tpu_custom_call" | custom-call | flops 2147483648 | bytes 4194304 | tf_op jit(solution)/shard_map/experts/pallas_call | solution.py:194
  120.3 4.5 %all-to-all-start.2 = ((bf16[4,128,768]{2,1,0:T(8,128)(2,1)}), bf16[4,128,768]{2,1,0:T(8,128)(2,1)}, u32[]{:S(2)}, u32[]{:S(2)}) async-start(bf16[4,128,768]{2,1,0:T(8,128)(2,1)} %get-tuple-element.28), calls=%async_computation.2 | async-start | bytes 1572864 | tf_op jit(solution)/shard_map/dense_hidden/all_to_all | solution.py:22
  124.8 5.6 %collective-permute-start.16 = (bf16[108,3584]{1,0:T(8,128)(2,1)}, bf16[108,3584]{1,0:T(8,128)(2,1)}, u32[]{:S(2)}, u32[]{:S(2)}) collective-permute-start(bf16[108,3584]{1,0:T(8,128)(2,1)} %get-tuple-element.29), channel_id=1, source_target_pairs={{0,96},{32,0},{64,32},{96,64},{1,97},{33,1},{65,33},{97,65},{2,98}... | collective-permute-start | bytes 2322440 | tf_op jit(solution)/shard_map/partials_y/ppermute | solution.py:18
  132.3 3.1 %collective-permute-start.18 = (bf16[108,3584]{1,0:T(8,128)(2,1)}, bf16[108,3584]{1,0:T(8,128)(2,1)}, u32[]{:S(2)}, u32[]{:S(2)}) collective-permute-start(bf16[108,3584]{1,0:T(8,128)(2,1)} %get-tuple-element.37), channel_id=1, source_target_pairs={{0,64},{32,96},{64,0},{96,32},{1,65},{33,97},{65,1},{97,33},{2,66}... | collective-permute-start | bytes 2322440 | tf_op jit(solution)/shard_map/partials_y/ppermute | solution.py:18
  135.4 3.4 %collective-permute-start.13 = (bf16[36,3584]{1,0:T(8,128)(2,1)}, bf16[36,3584]{1,0:T(8,128)(2,1)}, u32[]{:S(2)}, u32[]{:S(2)}) collective-permute-start(bf16[36,3584]{1,0:T(8,128)(2,1)} %get-tuple-element.32), channel_id=1, source_target_pairs={{0,96},{32,0},{64,32},{96,64},{1,97},{33,1},{65,33},{97,65},{2,98}... | collective-permute-start | bytes 774152 | tf_op jit(solution)/shard_map/partials_y/ppermute | solution.py:18
  141.4 4.6 %experts.3 = (f32[108,3584]{1,0:T(8,128)}, f32[36,3584]{1,0:T(8,128)S(1)}) custom-call(bf16[3584,512]{1,0:T(8,128)(2,1)} %pad_maximum_fusion.refs_4_.gate_up, bf16[152,3584]{1,0:T(8,128)(2,1)} %bitcast.49, bf16[108,3584]{1,0:T(8,128)(2,1)S(1)} %reshape.152.refs_0_, bf16[36,3584]{1,0:T(8,128)(2,1)S(1)} %convolution_convert_fusion.refs_1_), custom_call_target="tpu_custom_call" | custom-call | flops 2147483648 | bytes 4194304 | tf_op jit(solution)/shard_map/experts/pallas_call | solution.py:221
  148.1 4.5 %all-to-all-start.3 = ((bf16[4,128,384]{2,1,0:T(8,128)(2,1)}), bf16[4,128,384]{2,1,0:T(8,128)(2,1)}, u32[]{:S(2)}, u32[]{:S(2)}) async-start(bf16[4,128,384]{2,1,0:T(8,128)(2,1)} %broadcast_in_dim.59), calls=%async_computation.3 | async-start | bytes 786432 | tf_op jit(solution)/shard_map/dense_out/all_to_all | solution.py:22
  152.7 3.7 %collective-permute-start.15 = (bf16[36,3584]{1,0:T(8,128)(2,1)}, bf16[36,3584]{1,0:T(8,128)(2,1)}, u32[]{:S(2)}, u32[]{:S(2)}) collective-permute-start(bf16[36,3584]{1,0:T(8,128)(2,1)} %get-tuple-element.34), channel_id=1, source_target_pairs={{0,64},{32,96},{64,0},{96,32},{1,65},{33,97},{65,1},{97,33},{2,66}... | collective-permute-start | bytes 774152 | tf_op jit(solution)/shard_map/partials_y/ppermute | solution.py:18
  156.4 10.8 %collective-permute-done.18.three = bf16[108,3584]{1,0:T(8,128)(2,1)} collective-permute-done((bf16[108,3584]{1,0:T(8,128)(2,1)}, bf16[108,3584]{1,0:T(8,128)(2,1)}, u32[]{:S(2)}, u32[]{:S(2)}) %collective-permute-start.18) | collective-permute-done | bytes 774176 | tf_op jit(solution)/shard_map/partials_y/ppermute | solution.py:18
  167.1 3.7 %partials_z.1 = (bf16[36,3584]{1,0:T(8,128)(2,1)}, bf16[36,3584]{1,0:T(8,128)(2,1)}, bf16[36,3584]{1,0:T(8,128)(2,1)S(1)}) custom-call(f32[108,3584]{1,0:T(8,128)} %get-tuple-element.35.own, bf16[108,3584]{1,0:T(8,128)(2,1)} %collective-permute-done.16.one, bf16[108,3584]{1,0:T(8,128)(2,1)} %collective-permute-done.17.two, ...), custom_call_target="tpu_custom_call" | custom-call | flops 214748364800 | bytes 4194304 | tf_op jit(solution)/shard_map/partials_z/pallas_call | solution.py:227
  175.3 4.8 %collective-permute-start.21 = (bf16[36,3584]{1,0:T(8,128)(2,1)S(1)}, bf16[36,3584]{1,0:T(8,128)(2,1)}, u32[]{:S(2)}, u32[]{:S(2)}) collective-permute-start(bf16[36,3584]{1,0:T(8,128)(2,1)S(1)} %get-tuple-element.40), channel_id=1, source_target_pairs={{0,8},{8,16},{16,24},{24,0},{1,9},{9,17},{17,25},{25,1},{2,10},{10... | collective-permute-start | bytes 774152 | tf_op jit(solution)/shard_map/partials_z/ppermute | solution.py:18
  180.1 2.9 %dense_out.1 = bf16[8,256,224]{2,1,0:T(8,128)(2,1)} custom-call(s32[4]{0:T(128)S(1)} %and_select_fusion.3.place, bf16[512,384]{1,0:T(8,128)(2,1)} %bitcast.13.act, bf16[224,1152]{1,0:T(8,128)(2,1)S(1)} %copy-done.2, bf16[224,1152]{1,0:T(8,128)(2,1)S(1)} %copy-done.4, bf16[224,1152]{1,0:T(8,128)(2,1)S(1)} %copy-done.6, ...), custom_call_target="tpu_custom_call" | custom-call | flops 2147483648 | bytes 4194304 | tf_op jit(solution)/shard_map/dense_out/pallas_call | solution.py:213
  185.3 11.9 %all-to-all-start.4 = ((bf16[8,256,224]{1,2,0:T(8,128)(2,1)}), bf16[8,256,224]{1,2,0:T(8,128)(2,1)S(1)}, u32[]{:S(2)}, u32[]{:S(2)}) async-start(bf16[8,256,224]{1,2,0:T(8,128)(2,1)} %copy.71), calls=%async_computation.4 | async-start | bytes 1835008 | tf_op jit(solution)/shard_map/dense_out/all_to_all | solution.py:22
  200.1 9.7 %all-to-all-done.4 = bf16[8,256,224]{1,2,0:T(8,128)(2,1)S(1)} async-done(((bf16[8,256,224]{1,2,0:T(8,128)(2,1)}), bf16[8,256,224]{1,2,0:T(8,128)(2,1)S(1)}, u32[]{:S(2)}, u32[]{:S(2)}) %all-to-all-start.4) | async-done | bytes 917536 | tf_op jit(solution)/shard_map/dense_out/all_to_all | solution.py:22
  209.8 5.3 %all-to-all-start.5 = ((bf16[8,36,448]{2,1,0:T(8,128)(2,1)}), bf16[8,36,448]{2,1,0:T(8,128)(2,1)S(1)}, u32[]{:S(2)}, u32[]{:S(2)}) async-start(bf16[8,36,448]{2,1,0:T(8,128)(2,1)} %bitcast.44), calls=%async_computation.5 | async-start | bytes 655360 | tf_op jit(solution)/shard_map/combine/all_to_all | solution.py:22
  218.2 2.8 %collective-permute-start.10 = (bf16[64,224]{1,0:T(8,128)(2,1)S(1)}, bf16[64,224]{1,0:T(8,128)(2,1)S(1)}, u32[]{:S(2)}, u32[]{:S(2)}) collective-permute-start(bf16[64,224]{1,0:T(8,128)(2,1)S(1)} %get-tuple-element.47), channel_id=1, source_target_pairs={{0,16},{8,24},{16,0},{24,8},{1,17},{9,25},{17,1},{25,9},{2,18},{10... | collective-permute-start | bytes 86024 | tf_op jit(solution)/shard_map/dense_out/ppermute | solution.py:18
  221.0 3.4 %collective-permute-start.11 = (bf16[64,224]{1,0:T(8,128)(2,1)S(1)}, bf16[64,224]{1,0:T(8,128)(2,1)S(1)}, u32[]{:S(2)}, u32[]{:S(2)}) collective-permute-start(bf16[64,224]{1,0:T(8,128)(2,1)S(1)} %get-tuple-element.46), channel_id=1, source_target_pairs={{0,24},{8,0},{16,8},{24,16},{1,25},{9,1},{17,9},{25,17},{2,26},{10... | collective-permute-start | bytes 86024 | tf_op jit(solution)/shard_map/dense_out/ppermute | solution.py:18
  224.5 2.9 %collective-permute-done.11 = bf16[64,224]{1,0:T(8,128)(2,1)S(1)} collective-permute-done((bf16[64,224]{1,0:T(8,128)(2,1)S(1)}, bf16[64,224]{1,0:T(8,128)(2,1)S(1)}, u32[]{:S(2)}, u32[]{:S(2)}) %collective-permute-start.11) | collective-permute-done | bytes 28704 | tf_op jit(solution)/shard_map/dense_out/ppermute | solution.py:18
  228.1 3.7 %collective-permute-start.12 = (bf16[2,64,224]{2,1,0:T(8,128)(2,1)S(1)}, bf16[2,64,224]{2,1,0:T(8,128)(2,1)S(1)}, u32[]{:S(2)}, u32[]{:S(2)}) collective-permute-start(bf16[2,64,224]{2,1,0:T(8,128)(2,1)S(1)} %constant_dynamic-slice_fusion), channel_id=1, source_target_pairs={{0,1},{1,0},{2,3},{3,2},{4,5},{5,4},{6,7},{7,6},{8,9},{9,8},{10,11... | collective-permute-start | bytes 172040 | tf_op jit(solution)/shard_map/dense_out/ppermute | solution.py:18
  233.2 5.4 %collective-permute-start.22 = (bf16[128,448]{0,1:T(8,128)(2,1)S(1)}, bf16[128,448]{0,1:T(8,128)(2,1)S(1)}, u32[]{:S(2)}, u32[]{:S(2)}) collective-permute-start(bf16[128,448]{0,1:T(8,128)(2,1)S(1)} %fusion.1), channel_id=1, source_target_pairs={{0,128},{128,256},{256,384},{384,0},{1,129},{129,257},{257,385},{3... | collective-permute-start | bytes 344072 | tf_op jit(solution)/shard_map/next_section/ppermute | solution.py:18
  238.6 12.6 %collective-permute-done.22 = bf16[128,448]{0,1:T(8,128)(2,1)S(1)} collective-permute-done((bf16[128,448]{0,1:T(8,128)(2,1)S(1)}, bf16[128,448]{0,1:T(8,128)(2,1)S(1)}, u32[]{:S(2)}, u32[]{:S(2)}) %collective-permute-start.22) | collective-permute-done | bytes 114720 | tf_op jit(solution)/shard_map/next_section/ppermute | solution.py:18
  (134 shorter events, 49.9 us)
Async XLA Ops:
  5.7 31.3 %all-to-all-start = ((bf16[4,40,3584]{2,1,0:T(8,128)(2,1)}), bf16[4,40,3584]{2,1,0:T(8,128)(2,1)}, u32[]{:S(2)}, u32[]{:S(2)}) async-start(bf16[4,40,3584]{2,1,0:T(8,128)(2,1)} %pad_maximum_fusion.1), calls=%async_computation | async-start | bytes 2293760 | tf_op jit(solution)/shard_map/rows_z/all_to_all | solution.py:22
  10.3 55.0 %copy-start.1 = (bf16[224,1152]{1,0:T(8,128)(2,1)}, bf16[224,1152]{1,0:T(8,128)(2,1)S(1)}, u32[]{:S(2)}) copy-start(bf16[224,1152]{1,0:T(8,128)(2,1)S(1)} %pad_maximum_fusion.2.refs_0_) | copy-start | bytes 1548292
  10.3 40.2 %collective-permute-start = (bf16[224,1152]{1,0:T(8,128)(2,1)S(1)}, bf16[224,1152]{1,0:T(8,128)(2,1)S(1)}, u32[]{:S(2)}, u32[]{:S(2)}) collective-permute-start(bf16[224,1152]{1,0:T(8,128)(2,1)S(1)} %pad_maximum_fusion.2.refs_0_), channel_id=1, source_target_pairs={{0,32},{32,64},{64,96},{96,0},{1,33},{33,65},{65,97},{97,1},{2,34}... | collective-permute-start | bytes 1548296 | tf_op jit(solution)/shard_map/dense_weights/ppermute | solution.py:18
  13.5 37.0 %collective-permute-start.2 = (bf16[224,1152]{1,0:T(8,128)(2,1)S(1)}, bf16[224,1152]{1,0:T(8,128)(2,1)}, u32[]{:S(2)}, u32[]{:S(2)}) collective-permute-start(bf16[224,1152]{1,0:T(8,128)(2,1)S(1)} %pad_maximum_fusion.2.refs_0_), channel_id=1, source_target_pairs={{0,96},{32,0},{64,32},{96,64},{1,97},{33,1},{65,33},{97,65},{2,98}... | collective-permute-start | bytes 1548296 | tf_op jit(solution)/shard_map/dense_weights/ppermute | solution.py:18
  16.9 32.1 %collective-permute-start.3 = (bf16[36,3584]{1,0:T(8,128)(2,1)S(1)}, bf16[36,3584]{1,0:T(8,128)(2,1)S(1)}, u32[]{:S(2)}, u32[]{:S(2)}) collective-permute-start(bf16[36,3584]{1,0:T(8,128)(2,1)S(1)} %convolution_convert_fusion.refs_1_), channel_id=1, source_target_pairs={{0,32},{32,64},{64,96},{96,0},{1,33},{33,65},{65,97},{97,1},{2,34}... | collective-permute-start | bytes 774152 | tf_op jit(solution)/shard_map/rows_y/ppermute | solution.py:18
  18.8 30.9 %collective-permute-start.4 = (bf16[36,3584]{1,0:T(8,128)(2,1)S(1)}, bf16[36,3584]{1,0:T(8,128)(2,1)S(1)}, u32[]{:S(2)}, u32[]{:S(2)}) collective-permute-start(bf16[36,3584]{1,0:T(8,128)(2,1)S(1)} %convolution_convert_fusion.refs_1_), channel_id=1, source_target_pairs={{0,96},{32,0},{64,32},{96,64},{1,97},{33,1},{65,33},{97,65},{2,98}... | collective-permute-start | bytes 774152 | tf_op jit(solution)/shard_map/rows_y/ppermute | solution.py:18
  23.4 27.1 %collective-permute-start.5 = (bf16[36,3584]{1,0:T(8,128)(2,1)S(1)}, bf16[36,3584]{1,0:T(8,128)(2,1)S(1)}, u32[]{:S(2)}, u32[]{:S(2)}) collective-permute-start(bf16[36,3584]{1,0:T(8,128)(2,1)S(1)} %convolution_convert_fusion.refs_1_), channel_id=1, source_target_pairs={{0,64},{32,96},{64,0},{96,32},{1,65},{33,97},{65,1},{97,33},{2,66}... | collective-permute-start | bytes 774152 | tf_op jit(solution)/shard_map/rows_y/ppermute | solution.py:18
  39.2 68.9 %all-to-all-start.1 = ((bf16[8,4,16,896]{3,2,1,0:T(8,128)(2,1)}), bf16[8,4,16,896]{3,2,1,0:T(8,128)(2,1)}, u32[]{:S(2)}, u32[]{:S(2)}) async-start(bf16[8,4,16,896]{3,2,1,0:T(8,128)(2,1)} %broadcast_in_dim.30), calls=%async_computation.1 | async-start | bytes 1835008 | tf_op jit(solution)/shard_map/dense_tokens/all_to_all | solution.py:22
  50.5 57.6 %copy-start.3 = (bf16[224,1152]{1,0:T(8,128)(2,1)}, bf16[224,1152]{1,0:T(8,128)(2,1)S(1)}, u32[]{:S(2)}) copy-start(bf16[224,1152]{1,0:T(8,128)(2,1)S(1)} %collective-permute-done.refs_1_) | copy-start | bytes 1548292
  54.9 51.4 %collective-permute-start.6 = (bf16[108,3584]{1,0:T(8,128)(2,1)S(1)}, bf16[108,3584]{1,0:T(8,128)(2,1)S(1)}, u32[]{:S(2)}, u32[]{:S(2)}) collective-permute-start(bf16[108,3584]{1,0:T(8,128)(2,1)S(1)} %reshape.152.refs_0_), channel_id=1, source_target_pairs={{0,32},{32,64},{64,96},{96,0},{1,33},{33,65},{65,97},{97,1},{2,34}... | collective-permute-start | bytes 2322440 | tf_op jit(solution)/shard_map/rows_y/ppermute | solution.py:18
  57.4 48.9 %collective-permute-start.7 = (bf16[108,3584]{1,0:T(8,128)(2,1)S(1)}, bf16[108,3584]{1,0:T(8,128)(2,1)S(1)}, u32[]{:S(2)}, u32[]{:S(2)}) collective-permute-start(bf16[108,3584]{1,0:T(8,128)(2,1)S(1)} %reshape.152.refs_0_), channel_id=1, source_target_pairs={{0,96},{32,0},{64,32},{96,64},{1,97},{33,1},{65,33},{97,65},{2,98}... | collective-permute-start | bytes 2322440 | tf_op jit(solution)/shard_map/rows_y/ppermute | solution.py:18
  61.4 46.7 %collective-permute-start.8 = (bf16[108,3584]{1,0:T(8,128)(2,1)S(1)}, bf16[108,3584]{1,0:T(8,128)(2,1)}, u32[]{:S(2)}, u32[]{:S(2)}) collective-permute-start(bf16[108,3584]{1,0:T(8,128)(2,1)S(1)} %reshape.152.refs_0_), channel_id=1, source_target_pairs={{0,64},{32,96},{64,0},{96,32},{1,65},{33,97},{65,1},{97,33},{2,66}... | collective-permute-start | bytes 2322440 | tf_op jit(solution)/shard_map/rows_y/ppermute | solution.py:18
  65.3 40.9 %collective-permute-start.1 = (bf16[224,1152]{1,0:T(8,128)(2,1)S(1)}, bf16[224,1152]{1,0:T(8,128)(2,1)S(1)}, u32[]{:S(2)}, u32[]{:S(2)}) collective-permute-start(bf16[224,1152]{1,0:T(8,128)(2,1)S(1)} %pad_maximum_fusion.2.refs_0_), channel_id=1, source_target_pairs={{0,64},{32,96},{64,0},{96,32},{1,65},{33,97},{65,1},{97,33},{2,66}... | collective-permute-start | bytes 1548296 | tf_op jit(solution)/shard_map/dense_weights/ppermute | solution.py:18
  120.3 25.7 %all-to-all-start.2 = ((bf16[4,128,768]{2,1,0:T(8,128)(2,1)}), bf16[4,128,768]{2,1,0:T(8,128)(2,1)}, u32[]{:S(2)}, u32[]{:S(2)}) async-start(bf16[4,128,768]{2,1,0:T(8,128)(2,1)} %get-tuple-element.28), calls=%async_computation.2 | async-start | bytes 1572864 | tf_op jit(solution)/shard_map/dense_hidden/all_to_all | solution.py:22
  124.8 27.9 %collective-permute-start.16 = (bf16[108,3584]{1,0:T(8,128)(2,1)}, bf16[108,3584]{1,0:T(8,128)(2,1)}, u32[]{:S(2)}, u32[]{:S(2)}) collective-permute-start(bf16[108,3584]{1,0:T(8,128)(2,1)} %get-tuple-element.29), channel_id=1, source_target_pairs={{0,96},{32,0},{64,32},{96,64},{1,97},{33,1},{65,33},{97,65},{2,98}... | collective-permute-start | bytes 2322440 | tf_op jit(solution)/shard_map/partials_y/ppermute | solution.py:18
  130.4 26.0 %collective-permute-start.17 = (bf16[108,3584]{1,0:T(8,128)(2,1)}, bf16[108,3584]{1,0:T(8,128)(2,1)}, u32[]{:S(2)}, u32[]{:S(2)}) collective-permute-start(bf16[108,3584]{1,0:T(8,128)(2,1)} %get-tuple-element.36), channel_id=1, source_target_pairs={{0,32},{32,64},{64,96},{96,0},{1,33},{33,65},{65,97},{97,1},{2,34}... | collective-permute-start | bytes 2322440 | tf_op jit(solution)/shard_map/partials_y/ppermute | solution.py:18
  132.3 34.9 %collective-permute-start.18 = (bf16[108,3584]{1,0:T(8,128)(2,1)}, bf16[108,3584]{1,0:T(8,128)(2,1)}, u32[]{:S(2)}, u32[]{:S(2)}) collective-permute-start(bf16[108,3584]{1,0:T(8,128)(2,1)} %get-tuple-element.37), channel_id=1, source_target_pairs={{0,64},{32,96},{64,0},{96,32},{1,65},{33,97},{65,1},{97,33},{2,66}... | collective-permute-start | bytes 2322440 | tf_op jit(solution)/shard_map/partials_y/ppermute | solution.py:18
  135.4 39.8 %collective-permute-start.13 = (bf16[36,3584]{1,0:T(8,128)(2,1)}, bf16[36,3584]{1,0:T(8,128)(2,1)}, u32[]{:S(2)}, u32[]{:S(2)}) collective-permute-start(bf16[36,3584]{1,0:T(8,128)(2,1)} %get-tuple-element.32), channel_id=1, source_target_pairs={{0,96},{32,0},{64,32},{96,64},{1,97},{33,1},{65,33},{97,65},{2,98}... | collective-permute-start | bytes 774152 | tf_op jit(solution)/shard_map/partials_y/ppermute | solution.py:18
  138.9 58.4 %collective-permute-start.14 = (bf16[36,3584]{1,0:T(8,128)(2,1)}, bf16[36,3584]{1,0:T(8,128)(2,1)}, u32[]{:S(2)}, u32[]{:S(2)}) collective-permute-start(bf16[36,3584]{1,0:T(8,128)(2,1)} %get-tuple-element.33), channel_id=1, source_target_pairs={{0,32},{32,64},{64,96},{96,0},{1,33},{33,65},{65,97},{97,1},{2,34}... | collective-permute-start | bytes 774152 | tf_op jit(solution)/shard_map/partials_y/ppermute | solution.py:18
  148.1 32.0 %all-to-all-start.3 = ((bf16[4,128,384]{2,1,0:T(8,128)(2,1)}), bf16[4,128,384]{2,1,0:T(8,128)(2,1)}, u32[]{:S(2)}, u32[]{:S(2)}) async-start(bf16[4,128,384]{2,1,0:T(8,128)(2,1)} %broadcast_in_dim.59), calls=%async_computation.3 | async-start | bytes 786432 | tf_op jit(solution)/shard_map/dense_out/all_to_all | solution.py:22
  152.7 44.6 %collective-permute-start.15 = (bf16[36,3584]{1,0:T(8,128)(2,1)}, bf16[36,3584]{1,0:T(8,128)(2,1)}, u32[]{:S(2)}, u32[]{:S(2)}) collective-permute-start(bf16[36,3584]{1,0:T(8,128)(2,1)} %get-tuple-element.34), channel_id=1, source_target_pairs={{0,64},{32,96},{64,0},{96,32},{1,65},{33,97},{65,1},{97,33},{2,66}... | collective-permute-start | bytes 774152 | tf_op jit(solution)/shard_map/partials_y/ppermute | solution.py:18
  170.9 26.4 %collective-permute-start.19 = (bf16[36,3584]{1,0:T(8,128)(2,1)}, bf16[36,3584]{1,0:T(8,128)(2,1)}, u32[]{:S(2)}, u32[]{:S(2)}) collective-permute-start(bf16[36,3584]{1,0:T(8,128)(2,1)} %get-tuple-element.38), channel_id=1, source_target_pairs={{0,24},{8,0},{16,8},{24,16},{1,25},{9,1},{17,9},{25,17},{2,26},{10... | collective-permute-start | bytes 774152 | tf_op jit(solution)/shard_map/partials_z/ppermute | solution.py:18
  173.1 24.2 %collective-permute-start.20 = (bf16[36,3584]{1,0:T(8,128)(2,1)}, bf16[36,3584]{1,0:T(8,128)(2,1)}, u32[]{:S(2)}, u32[]{:S(2)}) collective-permute-start(bf16[36,3584]{1,0:T(8,128)(2,1)} %get-tuple-element.39), channel_id=1, source_target_pairs={{0,16},{8,24},{16,0},{24,8},{1,17},{9,25},{17,1},{25,9},{2,18},{10... | collective-permute-start | bytes 774152 | tf_op jit(solution)/shard_map/partials_z/ppermute | solution.py:18
  175.3 22.0 %collective-permute-start.21 = (bf16[36,3584]{1,0:T(8,128)(2,1)S(1)}, bf16[36,3584]{1,0:T(8,128)(2,1)}, u32[]{:S(2)}, u32[]{:S(2)}) collective-permute-start(bf16[36,3584]{1,0:T(8,128)(2,1)S(1)} %get-tuple-element.40), channel_id=1, source_target_pairs={{0,8},{8,16},{16,24},{24,0},{1,9},{9,17},{17,25},{25,1},{2,10},{10... | collective-permute-start | bytes 774152 | tf_op jit(solution)/shard_map/partials_z/ppermute | solution.py:18
  185.3 24.5 %all-to-all-start.4 = ((bf16[8,256,224]{1,2,0:T(8,128)(2,1)}), bf16[8,256,224]{1,2,0:T(8,128)(2,1)S(1)}, u32[]{:S(2)}, u32[]{:S(2)}) async-start(bf16[8,256,224]{1,2,0:T(8,128)(2,1)} %copy.71), calls=%async_computation.4 | async-start | bytes 1835008 | tf_op jit(solution)/shard_map/dense_out/all_to_all | solution.py:22
  200.1 31.7 %copy-start.16 = (bf16[128,288]{0,1:T(8,128)(2,1)S(1)}, bf16[128,288]{0,1:T(8,128)(2,1)}, u32[]{:S(2)}) copy-start(bf16[128,288]{0,1:T(8,128)(2,1)} %get-tuple-element.25) | copy-start | bytes 221188
  209.8 14.6 %all-to-all-start.5 = ((bf16[8,36,448]{2,1,0:T(8,128)(2,1)}), bf16[8,36,448]{2,1,0:T(8,128)(2,1)S(1)}, u32[]{:S(2)}, u32[]{:S(2)}) async-start(bf16[8,36,448]{2,1,0:T(8,128)(2,1)} %bitcast.44), calls=%async_computation.5 | async-start | bytes 655360 | tf_op jit(solution)/shard_map/combine/all_to_all | solution.py:22
  215.4 9.1 %collective-permute-start.9 = (bf16[64,224]{1,0:T(8,128)(2,1)S(1)}, bf16[64,224]{1,0:T(8,128)(2,1)S(1)}, u32[]{:S(2)}, u32[]{:S(2)}) collective-permute-start(bf16[64,224]{1,0:T(8,128)(2,1)S(1)} %get-tuple-element.48), channel_id=1, source_target_pairs={{0,8},{8,16},{16,24},{24,0},{1,9},{9,17},{17,25},{25,1},{2,10},{10... | collective-permute-start | bytes 86024 | tf_op jit(solution)/shard_map/dense_out/ppermute | solution.py:18
  218.2 6.3 %collective-permute-start.10 = (bf16[64,224]{1,0:T(8,128)(2,1)S(1)}, bf16[64,224]{1,0:T(8,128)(2,1)S(1)}, u32[]{:S(2)}, u32[]{:S(2)}) collective-permute-start(bf16[64,224]{1,0:T(8,128)(2,1)S(1)} %get-tuple-element.47), channel_id=1, source_target_pairs={{0,16},{8,24},{16,0},{24,8},{1,17},{9,25},{17,1},{25,9},{2,18},{10... | collective-permute-start | bytes 86024 | tf_op jit(solution)/shard_map/dense_out/ppermute | solution.py:18
  221.0 6.5 %collective-permute-start.11 = (bf16[64,224]{1,0:T(8,128)(2,1)S(1)}, bf16[64,224]{1,0:T(8,128)(2,1)S(1)}, u32[]{:S(2)}, u32[]{:S(2)}) collective-permute-start(bf16[64,224]{1,0:T(8,128)(2,1)S(1)} %get-tuple-element.46), channel_id=1, source_target_pairs={{0,24},{8,0},{16,8},{24,16},{1,25},{9,1},{17,9},{25,17},{2,26},{10... | collective-permute-start | bytes 86024 | tf_op jit(solution)/shard_map/dense_out/ppermute | solution.py:18
  228.1 4.6 %collective-permute-start.12 = (bf16[2,64,224]{2,1,0:T(8,128)(2,1)S(1)}, bf16[2,64,224]{2,1,0:T(8,128)(2,1)S(1)}, u32[]{:S(2)}, u32[]{:S(2)}) collective-permute-start(bf16[2,64,224]{2,1,0:T(8,128)(2,1)S(1)} %constant_dynamic-slice_fusion), channel_id=1, source_target_pairs={{0,1},{1,0},{2,3},{3,2},{4,5},{5,4},{6,7},{7,6},{8,9},{9,8},{10,11... | collective-permute-start | bytes 172040 | tf_op jit(solution)/shard_map/dense_out/ppermute | solution.py:18
  233.2 18.1 %collective-permute-start.22 = (bf16[128,448]{0,1:T(8,128)(2,1)S(1)}, bf16[128,448]{0,1:T(8,128)(2,1)S(1)}, u32[]{:S(2)}, u32[]{:S(2)}) collective-permute-start(bf16[128,448]{0,1:T(8,128)(2,1)S(1)} %fusion.1), channel_id=1, source_target_pairs={{0,128},{128,256},{256,384},{384,0},{1,129},{129,257},{257,385},{3... | collective-permute-start | bytes 344072 | tf_op jit(solution)/shard_map/next_section/ppermute | solution.py:18
  (20 other events, 118.0 us)

commit v9 on v7

--- a/solution.py
+++ b/solution.py
@@ -11,6 +11,7 @@
 GRID = (4, 4, 4, 4, 2)
 EXPERT_AXES = ("x", "core")
 BF16, F32 = jnp.bfloat16, jnp.float32
+LONG = 100 * 1024**3
 
 
 def shifted(x, axis, by):
@@ -46,13 +47,13 @@
     return jnp.sum(named * earlier[:, None, :], axis=2, dtype=jnp.int32)
 
 
-def local_call(kernel, out_shape, **kwargs):
+def local_call(kernel, out_shape, flops=2 * 1024**3, **kwargs):
     return pl.pallas_call(
         kernel,
         out_shape=out_shape,
         compiler_params=pltpu.CompilerParams(vmem_limit_bytes=52 * 1024 * 1024),
         cost_estimate=pl.CostEstimate(
-            flops=2 * 1024**3, bytes_accessed=4 * 1024**2, transcendentals=0
+            flops=flops, bytes_accessed=4 * 1024**2, transcendentals=0
         ),
         **kwargs,
     )
@@ -83,8 +84,9 @@
         out[z] = dot(rows, joined).astype(BF16)
 
 
-def late_kernel(part, relay, out):
-    out[...] = (part[...] + relay[...].astype(F32)).astype(BF16)
+def late_kernel(part_next, part_prev, relay_next, relay_prev, to_next, to_prev):
+    to_next[...] = (part_next[...] + relay_next[...].astype(F32)).astype(BF16)
+    to_prev[...] = (part_prev[...] + relay_prev[...].astype(F32)).astype(BF16)
 
 
 def total_kernel(capacity, place, low, high, *refs):
@@ -193,7 +195,6 @@
 
     with jax.named_scope("dense_tokens"):
         line_tokens = exchanged(repeated(line_share, n_expert), EXPERT_AXES)
-        line_tokens = after(line_tokens, prev_low, next_low, prev_high, next_high)
         pre = local_call(
             functools.partial(dense_in_kernel, 2 * hidden),
             jax.ShapeDtypeStruct((4, tok_rows, 2 * hidden), BF16),
@@ -203,7 +204,7 @@
     in_smem, in_vmem = (pl.BlockSpec(memory_space=space) for space in (pltpu.SMEM, pltpu.VMEM))
     with jax.named_scope("experts"):
         relay_next, relay_prev, early_next, early_prev, next_part, prev_part = local_call(
-            rows_kernel, [half_bf16] * 4 + [half_f32] * 2
+            rows_kernel, [half_bf16] * 4 + [half_f32] * 2, LONG
         )(gate_up, down, far_low, far_high, next_high, prev_low, next_low, prev_high)
 
     with jax.named_scope("partials_y"):
@@ -224,8 +225,9 @@
 
     with jax.named_scope("partials_y"):
         early_next, early_prev = shifted(early_next, "y", 1), shifted(early_prev, "y", -1)
-        late_next = local_call(late_kernel, half_bf16)(next_part, relay_next)
-        late_prev = local_call(late_kernel, half_bf16)(prev_part, relay_prev)
+        late_next, late_prev = local_call(late_kernel, [half_bf16] * 2, LONG)(
+            next_part, prev_part, relay_next, relay_prev
+        )
         own_low, own_high = local_call(rows_kernel, [half_f32] * 2)(
             after(gate_up, late_next, late_prev), down, low, high
         )

time: 246 us -> 230 us (0.935)
  the two profiles are of different devices: /device:TPU:99 before, /device:TPU:24 now
where the time goes in v9:
time: 230 us; the launch traced here: 228 us
  starting transfers between devices  109 us (47%)
  waiting for transfers between devices  57.1 us (25%)
  Pallas kernels  25.1 us (11%)
  local copies, waits for them, and re-layouts  22.5 us (10%)
  other arithmetic  12.2 us (5%)
    ppermute x23, starting transfers between devices, shifted(): return lax.ppermute(x, axis, [(i, (i + by) % peers) for i in range(peers)])  82.1 us
    ppermute x23, waiting for transfers between devices, shifted(): return lax.ppermute(x, axis, [(i, (i + by) % peers) for i in range(peers)])  52 us
    all_to_all x6, starting transfers between devices, exchanged(): return lax.all_to_all(x, axes, split_axis=0, concat_axis=0, tiled=True)  27.3 us
    pallas_call x1, Pallas kernels, body(): local_call(rows_kernel, [half_bf16] * 4 + [half_f32] * 2, LONG)  7.72 us
    unnamed x29, local copies, waits for them, and re-layouts  5.96 us
    all_to_all x6, waiting for transfers between devices, exchanged(): return lax.all_to_all(x, axes, split_axis=0, concat_axis=0, tiled=True)  5.15 us
    concatenate x1, other arithmetic, body(): jnp.concatenate([expert_gate[0, 0], blank, expert_up[0, 0], blank], axis=1)  5.02 us
    pallas_call x1, Pallas kernels, body(): local_call(rows_kernel, [half_f32] * 2)  4.75 us
  transfers between devices with their start and end apart: 29, of which 13 were waited for; matrix products, arithmetic and copies ran while one was open for 11% of the time, Pallas kernels for 11%

profile of v9, /device:TPU:24, one launch (start us, length us, event | category | flops | bytes accessed | tf_op | source)
XLA Modules:
  0.0 227.9 jit_solution(14374440252278027125)
XLA Ops:
  5.3 5.9 %all-to-all-start = ((bf16[4,40,3584]{2,1,0:T(8,128)(2,1)}), bf16[4,40,3584]{2,1,0:T(8,128)(2,1)}, u32[]{:S(2)}, u32[]{:S(2)}) async-start(bf16[4,40,3584]{2,1,0:T(8,128)(2,1)} %pad_maximum_fusion.1), calls=%async_computation | async-start | bytes 2293760 | tf_op jit(solution)/shard_map/rows_z/all_to_all | solution.py:23
  14.0 6.6 %collective-permute-start.1 = (bf16[224,1152]{1,0:T(8,128)(2,1)S(1)}, bf16[224,1152]{1,0:T(8,128)(2,1)S(1)}, u32[]{:S(2)}, u32[]{:S(2)}) collective-permute-start(bf16[224,1152]{1,0:T(8,128)(2,1)S(1)} %pad_maximum_fusion.2.refs_0_), channel_id=1, source_target_pairs={{0,64},{32,96},{64,0},{96,32},{1,65},{33,97},{65,1},{97,33},{2,66}... | collective-permute-start | bytes 1548296 | tf_op jit(solution)/shard_map/dense_weights/ppermute | solution.py:19
  28.6 5.0 %pad_maximum_fusion.gate_up = bf16[3584,512]{1,0:T(8,128)(2,1)} fusion(bf16[3584,104]{1,0:T(8,128)(2,1)S(1)} %broadcast_in_dim.55, bf16[3584,152]{1,0:T(8,128)(2,1)} %bitcast.47, bf16[3584,152]{1,0:T(8,128)(2,1)} %bitcast.46), kind=kLoop, calls=%fused_computation.3 | loop fusion | flops 14680064 | bytes 6594560 | tf_op jit(solution)/shard_map/concatenate | solution.py:175
  33.7 5.0 %collective-permute-done.2.refs_3_ = bf16[224,1152]{1,0:T(8,128)(2,1)S(1)} collective-permute-done((bf16[224,1152]{1,0:T(8,128)(2,1)S(1)}, bf16[224,1152]{1,0:T(8,128)(2,1)S(1)}, u32[]{:S(2)}, u32[]{:S(2)}) %collective-permute-start.2) | collective-permute-done | bytes 516128 | tf_op jit(solution)/shard_map/dense_weights/ppermute | solution.py:19
  44.7 4.5 %collective-permute-start.7 = (bf16[72,3584]{1,0:T(8,128)(2,1)S(1)}, bf16[72,3584]{1,0:T(8,128)(2,1)}, u32[]{:S(2)}, u32[]{:S(2)}) collective-permute-start(bf16[72,3584]{1,0:T(8,128)(2,1)S(1)} %reshape.157.refs_0_), channel_id=1, source_target_pairs={{0,32},{32,64},{64,96},{96,0},{1,33},{33,65},{65,97},{97,1},{2,34}... | collective-permute-start | bytes 1548296 | tf_op jit(solution)/shard_map/rows_y/ppermute | solution.py:19
  57.5 4.3 %all-to-all-start.1 = ((bf16[8,4,16,896]{3,2,1,0:T(8,128)(2,1)}), bf16[8,4,16,896]{3,2,1,0:T(8,128)(2,1)}, u32[]{:S(2)}, u32[]{:S(2)}) async-start(bf16[8,4,16,896]{3,2,1,0:T(8,128)(2,1)} %broadcast_in_dim.28), calls=%async_computation.1 | async-start | bytes 1835008 | tf_op jit(solution)/shard_map/dense_tokens/all_to_all | solution.py:23
  63.8 5.1 %collective-permute-start.12 = (bf16[72,3584]{1,0:T(8,128)(2,1)S(1)}, bf16[72,3584]{1,0:T(8,128)(2,1)}, u32[]{:S(2)}, u32[]{:S(2)}) collective-permute-start(bf16[72,3584]{1,0:T(8,128)(2,1)S(1)} %reshape.158.refs_1_), channel_id=1, source_target_pairs={{0,32},{32,64},{64,96},{96,0},{1,33},{33,65},{65,97},{97,1},{2,34}... | collective-permute-start | bytes 1548296 | tf_op jit(solution)/shard_map/rows_y/ppermute | solution.py:19
  68.9 3.9 %collective-permute-start.8 = (bf16[72,3584]{1,0:T(8,128)(2,1)}, bf16[72,3584]{1,0:T(8,128)(2,1)}, u32[]{:S(2)}, u32[]{:S(2)}) collective-permute-start(bf16[72,3584]{1,0:T(8,128)(2,1)} %collective-permute-done.7.refs_3_), channel_id=1, source_target_pairs={{0,32},{32,64},{64,96},{96,0},{1,33},{33,65},{65,97},{97,1},{2,34}... | collective-permute-start | bytes 1548296 | tf_op jit(solution)/shard_map/rows_y/ppermute | solution.py:19
  76.5 3.2 %dense_tokens.1 = bf16[4,128,768]{2,1,0:T(8,128)(2,1)} custom-call(bf16[8,4,16,896]{3,2,1,0:T(8,128)(2,1)} %all-to-all-done.1.tokens, bf16[224,1152]{1,0:T(8,128)(2,1)S(1)} %pad_maximum_fusion.2.refs_0_, bf16[224,1152]{1,0:T(8,128)(2,1)S(1)} %collective-permute-done.refs_1_, bf16[224,1152]{1,0:T(8,128)(2,1)S(1)} %collective-permute-done.1.refs_2_, ...), custom_call_target="tpu_custom_call" | custom-call | flops 2147483648 | bytes 4194304 | tf_op jit(solution)/shard_map/dense_tokens/pallas_call | solution.py:198
  79.7 4.8 %all-to-all-start.2 = ((bf16[4,128,768]{2,1,0:T(8,128)(2,1)}), bf16[4,128,768]{2,1,0:T(8,128)(2,1)}, u32[]{:S(2)}, u32[]{:S(2)}) async-start(bf16[4,128,768]{2,1,0:T(8,128)(2,1)} %dense_tokens.1), calls=%async_computation.2 | async-start | bytes 1572864 | tf_op jit(solution)/shard_map/dense_hidden/all_to_all | solution.py:23
  84.6 7.2 %collective-permute-done.8.refs_0_ = bf16[72,3584]{1,0:T(8,128)(2,1)} collective-permute-done((bf16[72,3584]{1,0:T(8,128)(2,1)}, bf16[72,3584]{1,0:T(8,128)(2,1)}, u32[]{:S(2)}, u32[]{:S(2)}) %collective-permute-start.8) | collective-permute-done | bytes 516128 | tf_op jit(solution)/shard_map/rows_y/ppermute | solution.py:19
  91.7 7.7 %experts.1 = (bf16[72,3584]{1,0:T(8,128)(2,1)}, bf16[72,3584]{1,0:T(8,128)(2,1)}, bf16[72,3584]{1,0:T(8,128)(2,1)}, bf16[72,3584]{1,0:T(8,128)(2,1)}, f32[72,3584]{1,0:T(8,128)}, /*index=5*/f32[72,3584]{1,0:T(8,128)}) custom-call(bf16[3584,512]{1,0:T(8,128)(2,1)} %pad_maximum_fusion.gate_up, bf16[152,3584]{1,0:T(8,128)(2,1)} %bitcast.61, ...), custom_call_target="tpu_custom_call" | custom-call | flops 107374182400 | bytes 4194304 | tf_op jit(solution)/shard_map/experts/pallas_call | solution.py:206
  99.4 5.6 %collective-permute-start.13 = (bf16[72,3584]{1,0:T(8,128)(2,1)}, bf16[72,3584]{1,0:T(8,128)(2,1)}, u32[]{:S(2)}, u32[]{:S(2)}) collective-permute-start(bf16[72,3584]{1,0:T(8,128)(2,1)} %get-tuple-element.32), channel_id=1, source_target_pairs={{0,32},{32,64},{64,96},{96,0},{1,33},{33,65},{65,97},{97,1},{2,34}... | collective-permute-start | bytes 1548296 | tf_op jit(solution)/shard_map/partials_y/ppermute | solution.py:19
  109.1 4.9 %collective-permute-start.17 = (bf16[72,3584]{1,0:T(8,128)(2,1)}, bf16[72,3584]{1,0:T(8,128)(2,1)}, u32[]{:S(2)}, u32[]{:S(2)}) collective-permute-start(bf16[72,3584]{1,0:T(8,128)(2,1)} %get-tuple-element.40), channel_id=1, source_target_pairs={{0,32},{32,64},{64,96},{96,0},{1,33},{33,65},{65,97},{97,1},{2,34}... | collective-permute-start | bytes 1548296 | tf_op jit(solution)/shard_map/partials_y/ppermute | solution.py:19
  116.2 4.8 %all-to-all-start.3 = ((bf16[4,128,384]{2,1,0:T(8,128)(2,1)}), bf16[4,128,384]{2,1,0:T(8,128)(2,1)S(1)}, u32[]{:S(2)}, u32[]{:S(2)}) async-start(bf16[4,128,384]{2,1,0:T(8,128)(2,1)} %broadcast_in_dim.29), calls=%async_computation.3 | async-start | bytes 786432 | tf_op jit(solution)/shard_map/dense_out/all_to_all | solution.py:23
  123.1 2.9 %partials_y.2 = (bf16[72,3584]{1,0:T(8,128)(2,1)}, bf16[72,3584]{1,0:T(8,128)(2,1)}) custom-call(f32[72,3584]{1,0:T(8,128)} %get-tuple-element.30.part_next, f32[72,3584]{1,0:T(8,128)} %get-tuple-element.31.part_prev, bf16[72,3584]{1,0:T(8,128)(2,1)} %collective-permute-done.13.relay_next, bf16[72,3584]{1,0:T(8,128)(2,1)} %collective-permute-done.14.relay_prev), custom_call_target="tpu_custom_call" | custom-call | flops 107374182400 | bytes 4194304 | tf_op jit(solution)/shard_map/partials_y/pallas_call | solution.py:228
  127.9 3.9 %collective-permute-start.18 = (bf16[72,3584]{1,0:T(8,128)(2,1)}, bf16[72,3584]{1,0:T(8,128)(2,1)}, u32[]{:S(2)}, u32[]{:S(2)}) collective-permute-start(bf16[72,3584]{1,0:T(8,128)(2,1)} %get-tuple-element.35), channel_id=1, source_target_pairs={{0,96},{32,0},{64,32},{96,64},{1,97},{33,1},{65,33},{97,65},{2,98}... | collective-permute-start | bytes 1548296 | tf_op jit(solution)/shard_map/partials_y/ppermute | solution.py:19
  132.0 4.8 %partials_y.3 = (f32[72,3584]{1,0:T(8,128)}, f32[72,3584]{1,0:T(8,128)}) custom-call(bf16[3584,512]{1,0:T(8,128)(2,1)} %pad_maximum_fusion.gate_up, bf16[152,3584]{1,0:T(8,128)(2,1)} %bitcast.62, bf16[72,3584]{1,0:T(8,128)(2,1)S(1)} %reshape.157.refs_0_, bf16[72,3584]{1,0:T(8,128)(2,1)S(1)} %reshape.158.refs_1_), custom_call_target="tpu_custom_call" | custom-call | flops 2147483648 | bytes 4194304 | tf_op jit(solution)/shard_map/partials_y/pallas_call | solution.py:231
  138.8 4.9 %collective-permute-done.18.refs_3_ = bf16[72,3584]{1,0:T(8,128)(2,1)} collective-permute-done((bf16[72,3584]{1,0:T(8,128)(2,1)}, bf16[72,3584]{1,0:T(8,128)(2,1)}, u32[]{:S(2)}, u32[]{:S(2)}) %collective-permute-start.18) | collective-permute-done | bytes 516128 | tf_op jit(solution)/shard_map/partials_y/ppermute | solution.py:19
  143.7 3.8 %partials_z.1 = (f32[36,3584]{1,0:T(8,128)}, bf16[36,3584]{1,0:T(8,128)(2,1)}, bf16[36,3584]{1,0:T(8,128)(2,1)}, bf16[36,3584]{1,0:T(8,128)(2,1)S(1)}) custom-call(s32[4]{0:T(128)S(1)} %and_select_fusion.place, f32[72,3584]{1,0:T(8,128)} %get-tuple-element.37.low, f32[72,3584]{1,0:T(8,128)} %get-tuple-element.38.high, ...), custom_call_target="tpu_custom_call" | custom-call | flops 2147483648 | bytes 4194304 | tf_op jit(solution)/shard_map/partials_z/pallas_call | solution.py:238
  147.4 5.4 %collective-permute-start.19 = (bf16[36,3584]{1,0:T(8,128)(2,1)}, bf16[36,3584]{1,0:T(8,128)(2,1)}, u32[]{:S(2)}, u32[]{:S(2)}) collective-permute-start(bf16[36,3584]{1,0:T(8,128)(2,1)} %get-tuple-element.42), channel_id=1, source_target_pairs={{0,24},{8,0},{16,8},{24,16},{1,25},{9,1},{17,9},{25,17},{2,26},{10... | collective-permute-start | bytes 774152 | tf_op jit(solution)/shard_map/partials_z/ppermute | solution.py:19
  154.8 3.2 %collective-permute-start.21 = (bf16[36,3584]{1,0:T(8,128)(2,1)S(1)}, bf16[36,3584]{1,0:T(8,128)(2,1)}, u32[]{:S(2)}, u32[]{:S(2)}) collective-permute-start(bf16[36,3584]{1,0:T(8,128)(2,1)S(1)} %get-tuple-element.44), channel_id=1, source_target_pairs={{0,8},{8,16},{16,24},{24,0},{1,9},{9,17},{17,25},{25,1},{2,10},{10... | collective-permute-start | bytes 774152 | tf_op jit(solution)/shard_map/partials_z/ppermute | solution.py:19
  158.1 2.8 %dense_out.1 = bf16[8,256,224]{2,1,0:T(8,128)(2,1)} custom-call(s32[4]{0:T(128)S(1)} %and_select_fusion.3.place, bf16[512,384]{1,0:T(8,128)(2,1)S(1)} %bitcast.45, bf16[224,1152]{1,0:T(8,128)(2,1)S(1)} %pad_maximum_fusion.2.refs_0_, bf16[224,1152]{1,0:T(8,128)(2,1)S(1)} %collective-permute-done.refs_1_, bf16[224,1152]{1,0:T(8,128)(2,1)S(1)} %copy-done.2, ...), custom_call_target="tpu_custom_call" | custom-call | flops 2147483648 | bytes 4194304 | tf_op jit(solution)/shard_map/dense_out/pallas_call | solution.py:220
  163.1 4.1 %all-to-all-start.4 = ((bf16[8,256,224]{1,2,0:T(8,128)(2,1)}), bf16[8,256,224]{1,2,0:T(8,128)(2,1)S(1)}, u32[]{:S(2)}, u32[]{:S(2)}) async-start(bf16[8,256,224]{1,2,0:T(8,128)(2,1)} %copy.69), calls=%async_computation.4 | async-start | bytes 1835008 | tf_op jit(solution)/shard_map/dense_out/all_to_all | solution.py:23
  167.2 8.7 %collective-permute-done.20 = bf16[36,3584]{1,0:T(8,128)(2,1)} collective-permute-done((bf16[36,3584]{1,0:T(8,128)(2,1)}, bf16[36,3584]{1,0:T(8,128)(2,1)}, u32[]{:S(2)}, u32[]{:S(2)}) %collective-permute-start.20) | collective-permute-done | bytes 258080 | tf_op jit(solution)/shard_map/partials_z/ppermute | solution.py:19
  178.4 3.4 %all-to-all-done.4 = bf16[8,256,224]{1,2,0:T(8,128)(2,1)S(1)} async-done(((bf16[8,256,224]{1,2,0:T(8,128)(2,1)}), bf16[8,256,224]{1,2,0:T(8,128)(2,1)S(1)}, u32[]{:S(2)}, u32[]{:S(2)}) %all-to-all-start.4) | async-done | bytes 917536 | tf_op jit(solution)/shard_map/dense_out/all_to_all | solution.py:23
  181.8 3.4 %all-to-all-start.5 = ((bf16[8,36,448]{2,1,0:T(8,128)(2,1)}), bf16[8,36,448]{2,1,0:T(8,128)(2,1)S(1)}, u32[]{:S(2)}, u32[]{:S(2)}) async-start(bf16[8,36,448]{2,1,0:T(8,128)(2,1)} %bitcast.44), calls=%async_computation.5 | async-start | bytes 655360 | tf_op jit(solution)/shard_map/combine/all_to_all | solution.py:23
  185.5 4.6 %collective-permute-start.5 = (bf16[64,224]{1,0:T(8,128)(2,1)S(1)}, bf16[64,224]{1,0:T(8,128)(2,1)S(1)}, u32[]{:S(2)}, u32[]{:S(2)}) collective-permute-start(bf16[64,224]{1,0:T(8,128)(2,1)S(1)} %get-tuple-element.52), channel_id=1, source_target_pairs={{0,24},{8,0},{16,8},{24,16},{1,25},{9,1},{17,9},{25,17},{2,26},{10... | collective-permute-start | bytes 86024 | tf_op jit(solution)/shard_map/dense_out/ppermute | solution.py:19
  190.1 3.0 %collective-permute-start.4 = (bf16[64,224]{1,0:T(8,128)(2,1)S(1)}, bf16[64,224]{1,0:T(8,128)(2,1)S(1)}, u32[]{:S(2)}, u32[]{:S(2)}) collective-permute-start(bf16[64,224]{1,0:T(8,128)(2,1)S(1)} %get-tuple-element.53), channel_id=1, source_target_pairs={{0,16},{8,24},{16,0},{24,8},{1,17},{9,25},{17,1},{25,9},{2,18},{10... | collective-permute-start | bytes 86024 | tf_op jit(solution)/shard_map/dense_out/ppermute | solution.py:19
  196.8 3.9 %collective-permute-done.3 = bf16[64,224]{1,0:T(8,128)(2,1)S(1)} collective-permute-done((bf16[64,224]{1,0:T(8,128)(2,1)S(1)}, bf16[64,224]{1,0:T(8,128)(2,1)S(1)}, u32[]{:S(2)}, u32[]{:S(2)}) %collective-permute-start.3) | collective-permute-done | bytes 28704 | tf_op jit(solution)/shard_map/dense_out/ppermute | solution.py:19
  205.1 9.1 %collective-permute-start.22 = (bf16[128,448]{0,1:T(8,128)(2,1)S(1)}, bf16[128,448]{0,1:T(8,128)(2,1)S(1)}, u32[]{:S(2)}, u32[]{:S(2)}) collective-permute-start(bf16[128,448]{0,1:T(8,128)(2,1)S(1)} %fusion.1), channel_id=1, source_target_pairs={{0,128},{128,256},{256,384},{384,0},{1,129},{129,257},{257,385},{3... | collective-permute-start | bytes 344072 | tf_op jit(solution)/shard_map/next_section/ppermute | solution.py:19
  214.2 13.1 %collective-permute-done.22 = bf16[128,448]{0,1:T(8,128)(2,1)S(1)} collective-permute-done((bf16[128,448]{0,1:T(8,128)(2,1)S(1)}, bf16[128,448]{0,1:T(8,128)(2,1)S(1)}, u32[]{:S(2)}, u32[]{:S(2)}) %collective-permute-start.22) | collective-permute-done | bytes 114720 | tf_op jit(solution)/shard_map/next_section/ppermute | solution.py:19
  (115 shorter events, 63.6 us)
Async XLA Ops:
  5.3 35.9 %all-to-all-start = ((bf16[4,40,3584]{2,1,0:T(8,128)(2,1)}), bf16[4,40,3584]{2,1,0:T(8,128)(2,1)}, u32[]{:S(2)}, u32[]{:S(2)}) async-start(bf16[4,40,3584]{2,1,0:T(8,128)(2,1)} %pad_maximum_fusion.1), calls=%async_computation | async-start | bytes 2293760 | tf_op jit(solution)/shard_map/rows_z/all_to_all | solution.py:23
  11.3 27.4 %collective-permute-start.2 = (bf16[224,1152]{1,0:T(8,128)(2,1)S(1)}, bf16[224,1152]{1,0:T(8,128)(2,1)S(1)}, u32[]{:S(2)}, u32[]{:S(2)}) collective-permute-start(bf16[224,1152]{1,0:T(8,128)(2,1)S(1)} %pad_maximum_fusion.2.refs_0_), channel_id=1, source_target_pairs={{0,96},{32,0},{64,32},{96,64},{1,97},{33,1},{65,33},{97,65},{2,98}... | collective-permute-start | bytes 1548296 | tf_op jit(solution)/shard_map/dense_weights/ppermute | solution.py:19
  14.0 24.7 %collective-permute-start.1 = (bf16[224,1152]{1,0:T(8,128)(2,1)S(1)}, bf16[224,1152]{1,0:T(8,128)(2,1)S(1)}, u32[]{:S(2)}, u32[]{:S(2)}) collective-permute-start(bf16[224,1152]{1,0:T(8,128)(2,1)S(1)} %pad_maximum_fusion.2.refs_0_), channel_id=1, source_target_pairs={{0,64},{32,96},{64,0},{96,32},{1,65},{33,97},{65,1},{97,33},{2,66}... | collective-permute-start | bytes 1548296 | tf_op jit(solution)/shard_map/dense_weights/ppermute | solution.py:19
  20.6 20.6 %collective-permute-start = (bf16[224,1152]{1,0:T(8,128)(2,1)S(1)}, bf16[224,1152]{1,0:T(8,128)(2,1)S(1)}, u32[]{:S(2)}, u32[]{:S(2)}) collective-permute-start(bf16[224,1152]{1,0:T(8,128)(2,1)S(1)} %pad_maximum_fusion.2.refs_0_), channel_id=1, source_target_pairs={{0,32},{32,64},{64,96},{96,0},{1,33},{33,65},{65,97},{97,1},{2,34}... | collective-permute-start | bytes 1548296 | tf_op jit(solution)/shard_map/dense_weights/ppermute | solution.py:19
  38.7 37.8 %copy-start.1 = (bf16[224,1152]{1,0:T(8,128)(2,1)}, bf16[224,1152]{1,0:T(8,128)(2,1)S(1)}, u32[]{:S(2)}) copy-start(bf16[224,1152]{1,0:T(8,128)(2,1)S(1)} %collective-permute-done.1.refs_2_) | copy-start | bytes 1548292
  44.7 24.2 %collective-permute-start.7 = (bf16[72,3584]{1,0:T(8,128)(2,1)S(1)}, bf16[72,3584]{1,0:T(8,128)(2,1)}, u32[]{:S(2)}, u32[]{:S(2)}) collective-permute-start(bf16[72,3584]{1,0:T(8,128)(2,1)S(1)} %reshape.157.refs_0_), channel_id=1, source_target_pairs={{0,32},{32,64},{64,96},{96,0},{1,33},{33,65},{65,97},{97,1},{2,34}... | collective-permute-start | bytes 1548296 | tf_op jit(solution)/shard_map/rows_y/ppermute | solution.py:19
  50.4 22.4 %collective-permute-start.9 = (bf16[72,3584]{1,0:T(8,128)(2,1)S(1)}, bf16[72,3584]{1,0:T(8,128)(2,1)}, u32[]{:S(2)}, u32[]{:S(2)}) collective-permute-start(bf16[72,3584]{1,0:T(8,128)(2,1)S(1)} %reshape.158.refs_1_), channel_id=1, source_target_pairs={{0,96},{32,0},{64,32},{96,64},{1,97},{33,1},{65,33},{97,65},{2,98}... | collective-permute-start | bytes 1548296 | tf_op jit(solution)/shard_map/rows_y/ppermute | solution.py:19
  57.5 19.0 %all-to-all-start.1 = ((bf16[8,4,16,896]{3,2,1,0:T(8,128)(2,1)}), bf16[8,4,16,896]{3,2,1,0:T(8,128)(2,1)}, u32[]{:S(2)}, u32[]{:S(2)}) async-start(bf16[8,4,16,896]{3,2,1,0:T(8,128)(2,1)} %broadcast_in_dim.28), calls=%async_computation.1 | async-start | bytes 1835008 | tf_op jit(solution)/shard_map/dense_tokens/all_to_all | solution.py:23
  61.8 22.7 %collective-permute-start.11 = (bf16[72,3584]{1,0:T(8,128)(2,1)S(1)}, bf16[72,3584]{1,0:T(8,128)(2,1)}, u32[]{:S(2)}, u32[]{:S(2)}) collective-permute-start(bf16[72,3584]{1,0:T(8,128)(2,1)S(1)} %reshape.157.refs_0_), channel_id=1, source_target_pairs={{0,96},{32,0},{64,32},{96,64},{1,97},{33,1},{65,33},{97,65},{2,98}... | collective-permute-start | bytes 1548296 | tf_op jit(solution)/shard_map/rows_y/ppermute | solution.py:19
  63.8 20.8 %collective-permute-start.12 = (bf16[72,3584]{1,0:T(8,128)(2,1)S(1)}, bf16[72,3584]{1,0:T(8,128)(2,1)}, u32[]{:S(2)}, u32[]{:S(2)}) collective-permute-start(bf16[72,3584]{1,0:T(8,128)(2,1)S(1)} %reshape.158.refs_1_), channel_id=1, source_target_pairs={{0,32},{32,64},{64,96},{96,0},{1,33},{33,65},{65,97},{97,1},{2,34}... | collective-permute-start | bytes 1548296 | tf_op jit(solution)/shard_map/rows_y/ppermute | solution.py:19
  68.9 22.8 %collective-permute-start.8 = (bf16[72,3584]{1,0:T(8,128)(2,1)}, bf16[72,3584]{1,0:T(8,128)(2,1)}, u32[]{:S(2)}, u32[]{:S(2)}) collective-permute-start(bf16[72,3584]{1,0:T(8,128)(2,1)} %collective-permute-done.7.refs_3_), channel_id=1, source_target_pairs={{0,32},{32,64},{64,96},{96,0},{1,33},{33,65},{65,97},{97,1},{2,34}... | collective-permute-start | bytes 1548296 | tf_op jit(solution)/shard_map/rows_y/ppermute | solution.py:19
  72.9 18.9 %collective-permute-start.10 = (bf16[72,3584]{1,0:T(8,128)(2,1)}, bf16[72,3584]{1,0:T(8,128)(2,1)}, u32[]{:S(2)}, u32[]{:S(2)}) collective-permute-start(bf16[72,3584]{1,0:T(8,128)(2,1)} %collective-permute-done.9.refs_2_), channel_id=1, source_target_pairs={{0,96},{32,0},{64,32},{96,64},{1,97},{33,1},{65,33},{97,65},{2,98}... | collective-permute-start | bytes 1548296 | tf_op jit(solution)/shard_map/rows_y/ppermute | solution.py:19
  79.7 34.3 %all-to-all-start.2 = ((bf16[4,128,768]{2,1,0:T(8,128)(2,1)}), bf16[4,128,768]{2,1,0:T(8,128)(2,1)}, u32[]{:S(2)}, u32[]{:S(2)}) async-start(bf16[4,128,768]{2,1,0:T(8,128)(2,1)} %dense_tokens.1), calls=%async_computation.2 | async-start | bytes 1572864 | tf_op jit(solution)/shard_map/dense_hidden/all_to_all | solution.py:23
  99.4 21.6 %collective-permute-start.13 = (bf16[72,3584]{1,0:T(8,128)(2,1)}, bf16[72,3584]{1,0:T(8,128)(2,1)}, u32[]{:S(2)}, u32[]{:S(2)}) collective-permute-start(bf16[72,3584]{1,0:T(8,128)(2,1)} %get-tuple-element.32), channel_id=1, source_target_pairs={{0,32},{32,64},{64,96},{96,0},{1,33},{33,65},{65,97},{97,1},{2,34}... | collective-permute-start | bytes 1548296 | tf_op jit(solution)/shard_map/partials_y/ppermute | solution.py:19
  105.0 18.1 %collective-permute-start.14 = (bf16[72,3584]{1,0:T(8,128)(2,1)}, bf16[72,3584]{1,0:T(8,128)(2,1)}, u32[]{:S(2)}, u32[]{:S(2)}) collective-permute-start(bf16[72,3584]{1,0:T(8,128)(2,1)} %get-tuple-element.33), channel_id=1, source_target_pairs={{0,96},{32,0},{64,32},{96,64},{1,97},{33,1},{65,33},{97,65},{2,98}... | collective-permute-start | bytes 1548296 | tf_op jit(solution)/shard_map/partials_y/ppermute | solution.py:19
  107.0 29.7 %collective-permute-start.16 = (bf16[72,3584]{1,0:T(8,128)(2,1)}, bf16[72,3584]{1,0:T(8,128)(2,1)}, u32[]{:S(2)}, u32[]{:S(2)}) collective-permute-start(bf16[72,3584]{1,0:T(8,128)(2,1)} %get-tuple-element.39), channel_id=1, source_target_pairs={{0,96},{32,0},{64,32},{96,64},{1,97},{33,1},{65,33},{97,65},{2,98}... | collective-permute-start | bytes 1548296 | tf_op jit(solution)/shard_map/partials_y/ppermute | solution.py:19
  109.1 27.6 %collective-permute-start.17 = (bf16[72,3584]{1,0:T(8,128)(2,1)}, bf16[72,3584]{1,0:T(8,128)(2,1)}, u32[]{:S(2)}, u32[]{:S(2)}) collective-permute-start(bf16[72,3584]{1,0:T(8,128)(2,1)} %get-tuple-element.40), channel_id=1, source_target_pairs={{0,32},{32,64},{64,96},{96,0},{1,33},{33,65},{65,97},{97,1},{2,34}... | collective-permute-start | bytes 1548296 | tf_op jit(solution)/shard_map/partials_y/ppermute | solution.py:19
  116.2 41.8 %all-to-all-start.3 = ((bf16[4,128,384]{2,1,0:T(8,128)(2,1)}), bf16[4,128,384]{2,1,0:T(8,128)(2,1)S(1)}, u32[]{:S(2)}, u32[]{:S(2)}) async-start(bf16[4,128,384]{2,1,0:T(8,128)(2,1)} %broadcast_in_dim.29), calls=%async_computation.3 | async-start | bytes 786432 | tf_op jit(solution)/shard_map/dense_out/all_to_all | solution.py:23
  126.0 12.8 %collective-permute-start.15 = (bf16[72,3584]{1,0:T(8,128)(2,1)}, bf16[72,3584]{1,0:T(8,128)(2,1)}, u32[]{:S(2)}, u32[]{:S(2)}) collective-permute-start(bf16[72,3584]{1,0:T(8,128)(2,1)} %get-tuple-element.34), channel_id=1, source_target_pairs={{0,32},{32,64},{64,96},{96,0},{1,33},{33,65},{65,97},{97,1},{2,34}... | collective-permute-start | bytes 1548296 | tf_op jit(solution)/shard_map/partials_y/ppermute | solution.py:19
  127.9 15.7 %collective-permute-start.18 = (bf16[72,3584]{1,0:T(8,128)(2,1)}, bf16[72,3584]{1,0:T(8,128)(2,1)}, u32[]{:S(2)}, u32[]{:S(2)}) collective-permute-start(bf16[72,3584]{1,0:T(8,128)(2,1)} %get-tuple-element.35), channel_id=1, source_target_pairs={{0,96},{32,0},{64,32},{96,64},{1,97},{33,1},{65,33},{97,65},{2,98}... | collective-permute-start | bytes 1548296 | tf_op jit(solution)/shard_map/partials_y/ppermute | solution.py:19
  147.4 19.8 %collective-permute-start.19 = (bf16[36,3584]{1,0:T(8,128)(2,1)}, bf16[36,3584]{1,0:T(8,128)(2,1)}, u32[]{:S(2)}, u32[]{:S(2)}) collective-permute-start(bf16[36,3584]{1,0:T(8,128)(2,1)} %get-tuple-element.42), channel_id=1, source_target_pairs={{0,24},{8,0},{16,8},{24,16},{1,25},{9,1},{17,9},{25,17},{2,26},{10... | collective-permute-start | bytes 774152 | tf_op jit(solution)/shard_map/partials_z/ppermute | solution.py:19
  152.9 23.0 %collective-permute-start.20 = (bf16[36,3584]{1,0:T(8,128)(2,1)}, bf16[36,3584]{1,0:T(8,128)(2,1)}, u32[]{:S(2)}, u32[]{:S(2)}) collective-permute-start(bf16[36,3584]{1,0:T(8,128)(2,1)} %get-tuple-element.43), channel_id=1, source_target_pairs={{0,16},{8,24},{16,0},{24,8},{1,17},{9,25},{17,1},{25,9},{2,18},{10... | collective-permute-start | bytes 774152 | tf_op jit(solution)/shard_map/partials_z/ppermute | solution.py:19
  154.8 21.1 %collective-permute-start.21 = (bf16[36,3584]{1,0:T(8,128)(2,1)S(1)}, bf16[36,3584]{1,0:T(8,128)(2,1)}, u32[]{:S(2)}, u32[]{:S(2)}) collective-permute-start(bf16[36,3584]{1,0:T(8,128)(2,1)S(1)} %get-tuple-element.44), channel_id=1, source_target_pairs={{0,8},{8,16},{16,24},{24,0},{1,9},{9,17},{17,25},{25,1},{2,10},{10... | collective-permute-start | bytes 774152 | tf_op jit(solution)/shard_map/partials_z/ppermute | solution.py:19
  163.1 18.6 %all-to-all-start.4 = ((bf16[8,256,224]{1,2,0:T(8,128)(2,1)}), bf16[8,256,224]{1,2,0:T(8,128)(2,1)S(1)}, u32[]{:S(2)}, u32[]{:S(2)}) async-start(bf16[8,256,224]{1,2,0:T(8,128)(2,1)} %copy.69), calls=%async_computation.4 | async-start | bytes 1835008 | tf_op jit(solution)/shard_map/dense_out/all_to_all | solution.py:23
  177.1 26.2 %copy-start.5 = (bf16[128,288]{0,1:T(8,128)(2,1)S(1)}, bf16[128,288]{0,1:T(8,128)(2,1)}, u32[]{:S(2)}) copy-start(bf16[128,288]{0,1:T(8,128)(2,1)} %get-tuple-element.26) | copy-start | bytes 221188
  181.8 13.4 %all-to-all-start.5 = ((bf16[8,36,448]{2,1,0:T(8,128)(2,1)}), bf16[8,36,448]{2,1,0:T(8,128)(2,1)S(1)}, u32[]{:S(2)}, u32[]{:S(2)}) async-start(bf16[8,36,448]{2,1,0:T(8,128)(2,1)} %bitcast.44), calls=%async_computation.5 | async-start | bytes 655360 | tf_op jit(solution)/shard_map/combine/all_to_all | solution.py:23
  185.2 19.5 %copy-start.4 = (bf16[128,288]{0,1:T(8,128)(2,1)S(1)}, bf16[128,288]{0,1:T(8,128)(2,1)}, u32[]{:S(2)}) copy-start(bf16[128,288]{0,1:T(8,128)(2,1)} %get-tuple-element.28) | copy-start | bytes 221188
  185.5 9.7 %collective-permute-start.5 = (bf16[64,224]{1,0:T(8,128)(2,1)S(1)}, bf16[64,224]{1,0:T(8,128)(2,1)S(1)}, u32[]{:S(2)}, u32[]{:S(2)}) collective-permute-start(bf16[64,224]{1,0:T(8,128)(2,1)S(1)} %get-tuple-element.52), channel_id=1, source_target_pairs={{0,24},{8,0},{16,8},{24,16},{1,25},{9,1},{17,9},{25,17},{2,26},{10... | collective-permute-start | bytes 86024 | tf_op jit(solution)/shard_map/dense_out/ppermute | solution.py:19
  190.1 6.7 %collective-permute-start.4 = (bf16[64,224]{1,0:T(8,128)(2,1)S(1)}, bf16[64,224]{1,0:T(8,128)(2,1)S(1)}, u32[]{:S(2)}, u32[]{:S(2)}) collective-permute-start(bf16[64,224]{1,0:T(8,128)(2,1)S(1)} %get-tuple-element.53), channel_id=1, source_target_pairs={{0,16},{8,24},{16,0},{24,8},{1,17},{9,25},{17,1},{25,9},{2,18},{10... | collective-permute-start | bytes 86024 | tf_op jit(solution)/shard_map/dense_out/ppermute | solution.py:19
  193.2 7.6 %collective-permute-start.3 = (bf16[64,224]{1,0:T(8,128)(2,1)S(1)}, bf16[64,224]{1,0:T(8,128)(2,1)S(1)}, u32[]{:S(2)}, u32[]{:S(2)}) collective-permute-start(bf16[64,224]{1,0:T(8,128)(2,1)S(1)} %get-tuple-element.54), channel_id=1, source_target_pairs={{0,8},{8,16},{16,24},{24,0},{1,9},{9,17},{17,25},{25,1},{2,10},{10... | collective-permute-start | bytes 86024 | tf_op jit(solution)/shard_map/dense_out/ppermute | solution.py:19
  201.4 3.1 %collective-permute-start.6 = (bf16[2,64,224]{2,1,0:T(8,128)(2,1)S(1)}, bf16[2,64,224]{2,1,0:T(8,128)(2,1)S(1)}, u32[]{:S(2)}, u32[]{:S(2)}) collective-permute-start(bf16[2,64,224]{2,1,0:T(8,128)(2,1)S(1)} %constant_dynamic-slice_fusion), channel_id=1, source_target_pairs={{0,1},{1,0},{2,3},{3,2},{4,5},{5,4},{6,7},{7,6},{8,9},{9,8},{10,11... | collective-permute-start | bytes 172040 | tf_op jit(solution)/shard_map/dense_out/ppermute | solution.py:19
  205.1 22.2 %collective-permute-start.22 = (bf16[128,448]{0,1:T(8,128)(2,1)S(1)}, bf16[128,448]{0,1:T(8,128)(2,1)S(1)}, u32[]{:S(2)}, u32[]{:S(2)}) collective-permute-start(bf16[128,448]{0,1:T(8,128)(2,1)S(1)} %fusion.1), channel_id=1, source_target_pairs={{0,128},{128,256},{256,384},{384,0},{1,129},{129,257},{257,385},{3... | collective-permute-start | bytes 344072 | tf_op jit(solution)/shard_map/next_section/ppermute | solution.py:19
  (10 other events, 110.5 us)

commit v10 on v9

--- a/solution.py
+++ b/solution.py
@@ -100,6 +100,26 @@
             @pl.when(place[k] == j)
             def _(out=out, j=j):
                 out[...] = whole[j * capacity : (j + 1) * capacity].astype(out.dtype)
+
+
+def unpack_kernel(capacity, arrived, low, high, tokens, rows, share):
+    half = low.shape[0] // capacity
+    for first, out in ((0, low), (half, high)):
+        for k in range(half):
+            block = arrived[first + k].astype(F32)
+            rows[k * capacity : (k + 1) * capacity] = block[:capacity]
+        out[...] = rows[...].astype(BF16)
+    width = tokens.shape[3]
+    for z in range(tokens.shape[1]):
+        block = arrived[z].astype(F32)
+        for r in range(tokens.shape[2] // 4):
+            for j in range(4):
+                share[4 * r + j : 4 * r + j + 1] = block[
+                    capacity + r : capacity + r + 1, j * width : (j + 1) * width
+                ]
+        value = share[...].astype(BF16)
+        for e in range(tokens.shape[0]):
+            tokens[e, z] = value
 
 
 def in_line_order(parts, axis):
@@ -182,10 +202,13 @@
         own_share = own_share.at[:, place_y].get(mode="promise_in_bounds").transpose(2, 0, 1, 3)
         sent = [repeated(routed, 4), own_share.reshape(4, share // 4, width)]
         arrived = exchanged(jnp.concatenate(sent, axis=1), "z")
-        line_share = arrived[:, capacity:].reshape(4, share, slab)
         coarse, fine, gate_up = after((coarse, fine, gate_up), routed)
-        group = after(arrived, coarse, fine, gate_up, *slabs[1:])[:, :capacity]
-        low, high = (block.reshape(half, width) for block in (group[:2], group[2:]))
+        low, high, line_tokens = local_call(
+            functools.partial(unpack_kernel, capacity),
+            [jax.ShapeDtypeStruct((half, width), BF16)] * 2
+            + [jax.ShapeDtypeStruct((n_expert, 4, share, slab), BF16)],
+            scratch_shapes=[pltpu.VMEM((half, width), F32), pltpu.VMEM((share, slab), F32)],
+        )(after(arrived, coarse, fine, gate_up, *slabs[1:]))
 
     with jax.named_scope("rows_y"):
         prev_low, next_low = shifted(low, "y", 1), shifted(low, "y", -1)
@@ -194,7 +217,7 @@
         far_high = shifted(next_high, "y", -1)
 
     with jax.named_scope("dense_tokens"):
-        line_tokens = exchanged(repeated(line_share, n_expert), EXPERT_AXES)
+        line_tokens = exchanged(line_tokens, EXPERT_AXES)
         pre = local_call(
             functools.partial(dense_in_kernel, 2 * hidden),
             jax.ShapeDtypeStruct((4, tok_rows, 2 * hidden), BF16),
@@ -240,7 +263,7 @@
             [rows_f32] + [rows_bf16] * 3,
             in_specs=[in_smem] + [in_vmem] * 6,
             scratch_shapes=[pltpu.VMEM((4 * capacity, width), F32)],
-        )(place_z, own_low, own_high, late_next, early_prev, early_next, late_prev)
+        )(place_z, after(own_low, by_block), own_high, late_next, early_prev, early_next, late_prev)
         recv = [shifted(part, "z", by) for part, by in zip(sent, (-1, -2, -3))]
         expert_out = (kept_rows + sum(part.astype(F32) for part in recv)).astype(BF16)
 

time: 230 us -> 218 us (0.948)
  local copies, waits for them, and re-layouts: 22.5 us -> 13.7 us
  waiting for transfers between devices: 57.1 us -> 52.1 us
    all_to_all x6, waiting for transfers between devices: 5.15 us -> 1.16 us  [exchanged(): return lax.all_to_all(x, axes, split_axis=0, concat_axis=0, tiled=True)]
    slice x2 -> x0, local copies, waits for them, and re-layouts: 3.94 us -> none  [the longest x1 2.3 us: body(): low, high = (block.reshape(half, width) for block in (group[:2], group[2:]))]
    broadcast_in_dim x3 -> x1, local copies, waits for them, and re-layouts: 3.62 us -> 0.08 us  [repeated(): return jnp.broadcast_to(x[None], (times,) + x.shape)]
    pallas_call x0 -> x1, Pallas kernels: none -> 2.79 us  [body(): local_call(functools.partial(unpack_kernel, capacity), [jax.ShapeDtypeStr...]
    reshape x2 -> x0, local copies, waits for them, and re-layouts: 2.34 us -> none  [body(): low, high = (block.reshape(half, width) for block in (group[:2], group[2:]))]
    unnamed x29 -> x51, local copies, waits for them, and re-layouts: 5.96 us -> 7.93 us
  transfers between devices with their start and end apart: 29 -> 29, of which waited for: 13 -> 13; matrix products, arithmetic and copies ran while one was open for 11% -> 8% of each run, Pallas kernels for 11% -> 10%
where the time goes in v10:
time: 218 us; the launch traced here: 216 us
  starting transfers between devices  109 us (50%)
  waiting for transfers between devices  52.1 us (24%)
  Pallas kernels  27.4 us (13%)
  local copies, waits for them, and re-layouts  13.7 us (6%)
  other arithmetic  12.3 us (6%)
    ppermute x23, starting transfers between devices, shifted(): return lax.ppermute(x, axis, [(i, (i + by) % peers) for i in range(peers)])  81.1 us
    ppermute x23, waiting for transfers between devices, shifted(): return lax.ppermute(x, axis, [(i, (i + by) % peers) for i in range(peers)])  50.9 us
    all_to_all x6, starting transfers between devices, exchanged(): return lax.all_to_all(x, axes, split_axis=0, concat_axis=0, tiled=True)  27.5 us
    unnamed x51, local copies, waits for them, and re-layouts  7.93 us
    pallas_call x1, Pallas kernels, body(): local_call(rows_kernel, [half_bf16] * 4 + [half_f32] * 2, LONG)  7.37 us
    concatenate x1, other arithmetic, body(): jnp.concatenate([expert_gate[0, 0], blank, expert_up[0, 0], blank], axis=1)  5.04 us
    pallas_call x1, Pallas kernels, body(): local_call(rows_kernel, [half_f32] * 2)  4.88 us
  transfers between devices with their start and end apart: 29, of which 13 were waited for; matrix products, arithmetic and copies ran while one was open for 8% of the time, Pallas kernels for 10%

profile of v10, /device:TPU:24, one launch (start us, length us, event | category | flops | bytes accessed | tf_op | source)
XLA Modules:
  0.0 215.5 jit_solution(10816570857077967481)
XLA Ops:
  5.4 5.9 %all-to-all-start = ((bf16[4,40,3584]{2,1,0:T(8,128)(2,1)}), bf16[4,40,3584]{2,1,0:T(8,128)(2,1)}, u32[]{:S(2)}, u32[]{:S(2)}) async-start(bf16[4,40,3584]{2,1,0:T(8,128)(2,1)} %pad_maximum_fusion.1), calls=%async_computation | async-start | bytes 2293760 | tf_op jit(solution)/shard_map/rows_z/all_to_all | solution.py:23
  14.0 6.6 %collective-permute-start.1 = (bf16[224,1152]{1,0:T(8,128)(2,1)S(1)}, bf16[224,1152]{1,0:T(8,128)(2,1)S(1)}, u32[]{:S(2)}, u32[]{:S(2)}) collective-permute-start(bf16[224,1152]{1,0:T(8,128)(2,1)S(1)} %pad_maximum_fusion.2.refs_0_), channel_id=1, source_target_pairs={{0,64},{32,96},{64,0},{96,32},{1,65},{33,97},{65,1},{97,33},{2,66}... | collective-permute-start | bytes 1548296 | tf_op jit(solution)/shard_map/dense_weights/ppermute | solution.py:19
  27.8 5.0 %pad_maximum_fusion.gate_up = bf16[3584,512]{1,0:T(8,128)(2,1)} fusion(bf16[3584,104]{1,0:T(8,128)(2,1)S(1)} %broadcast_in_dim.26, bf16[3584,152]{1,0:T(8,128)(2,1)} %bitcast.47, bf16[3584,152]{1,0:T(8,128)(2,1)} %bitcast.46), kind=kLoop, calls=%fused_computation.3 | loop fusion | flops 14680064 | bytes 6594560 | tf_op jit(solution)/shard_map/concatenate | solution.py:195
  32.8 6.0 %collective-permute-done.2.refs_3_ = bf16[224,1152]{1,0:T(8,128)(2,1)} collective-permute-done((bf16[224,1152]{1,0:T(8,128)(2,1)S(1)}, bf16[224,1152]{1,0:T(8,128)(2,1)}, u32[]{:S(2)}, u32[]{:S(2)}) %collective-permute-start.2) | collective-permute-done | bytes 516128 | tf_op jit(solution)/shard_map/dense_weights/ppermute | solution.py:19
  44.0 4.5 %collective-permute-start.7 = (bf16[72,3584]{1,0:T(8,128)(2,1)S(1)}, bf16[72,3584]{1,0:T(8,128)(2,1)}, u32[]{:S(2)}, u32[]{:S(2)}) collective-permute-start(bf16[72,3584]{1,0:T(8,128)(2,1)S(1)} %get-tuple-element.35.refs_0_), channel_id=1, source_target_pairs={{0,32},{32,64},{64,96},{96,0},{1,33},{33,65},{65,97},{97,1},{2,34}... | collective-permute-start | bytes 1548296 | tf_op jit(solution)/shard_map/rows_y/ppermute | solution.py:19
  50.5 4.3 %all-to-all-start.1 = ((bf16[8,4,16,896]{3,2,1,0:T(8,128)(2,1)}), bf16[8,4,16,896]{3,2,1,0:T(8,128)(2,1)}, u32[]{:S(2)}, u32[]{:S(2)}) async-start(bf16[8,4,16,896]{3,2,1,0:T(8,128)(2,1)} %get-tuple-element.34), calls=%async_computation.1 | async-start | bytes 1835008 | tf_op jit(solution)/shard_map/dense_tokens/all_to_all | solution.py:23
  56.7 5.1 %collective-permute-start.12 = (bf16[72,3584]{1,0:T(8,128)(2,1)S(1)}, bf16[72,3584]{1,0:T(8,128)(2,1)}, u32[]{:S(2)}, u32[]{:S(2)}) collective-permute-start(bf16[72,3584]{1,0:T(8,128)(2,1)S(1)} %get-tuple-element.36.refs_1_), channel_id=1, source_target_pairs={{0,32},{32,64},{64,96},{96,0},{1,33},{33,65},{65,97},{97,1},{2,34}... | collective-permute-start | bytes 1548296 | tf_op jit(solution)/shard_map/rows_y/ppermute | solution.py:19
  61.9 3.9 %collective-permute-start.8 = (bf16[72,3584]{1,0:T(8,128)(2,1)}, bf16[72,3584]{1,0:T(8,128)(2,1)}, u32[]{:S(2)}, u32[]{:S(2)}) collective-permute-start(bf16[72,3584]{1,0:T(8,128)(2,1)} %collective-permute-done.7.refs_3_), channel_id=1, source_target_pairs={{0,32},{32,64},{64,96},{96,0},{1,33},{33,65},{65,97},{97,1},{2,34}... | collective-permute-start | bytes 1548296 | tf_op jit(solution)/shard_map/rows_y/ppermute | solution.py:19
  69.5 3.2 %dense_tokens.1 = bf16[4,128,768]{2,1,0:T(8,128)(2,1)} custom-call(bf16[8,4,16,896]{3,2,1,0:T(8,128)(2,1)} %all-to-all-done.1.tokens, bf16[224,1152]{1,0:T(8,128)(2,1)S(1)} %pad_maximum_fusion.2.refs_0_, bf16[224,1152]{1,0:T(8,128)(2,1)S(1)} %collective-permute-done.refs_1_, bf16[224,1152]{1,0:T(8,128)(2,1)S(1)} %collective-permute-done.1.refs_2_, ...), custom_call_target="tpu_custom_call" | custom-call | flops 2147483648 | bytes 4194304 | tf_op jit(solution)/shard_map/dense_tokens/pallas_call | solution.py:221
  72.6 4.8 %all-to-all-start.2 = ((bf16[4,128,768]{2,1,0:T(8,128)(2,1)}), bf16[4,128,768]{2,1,0:T(8,128)(2,1)}, u32[]{:S(2)}, u32[]{:S(2)}) async-start(bf16[4,128,768]{2,1,0:T(8,128)(2,1)} %dense_tokens.1), calls=%async_computation.2 | async-start | bytes 1572864 | tf_op jit(solution)/shard_map/dense_hidden/all_to_all | solution.py:23
  77.5 7.2 %collective-permute-done.8.refs_0_ = bf16[72,3584]{1,0:T(8,128)(2,1)} collective-permute-done((bf16[72,3584]{1,0:T(8,128)(2,1)}, bf16[72,3584]{1,0:T(8,128)(2,1)}, u32[]{:S(2)}, u32[]{:S(2)}) %collective-permute-start.8) | collective-permute-done | bytes 516128 | tf_op jit(solution)/shard_map/rows_y/ppermute | solution.py:19
  87.3 7.4 %experts.1 = (bf16[72,3584]{1,0:T(8,128)(2,1)S(1)}, bf16[72,3584]{1,0:T(8,128)(2,1)S(1)}, bf16[72,3584]{1,0:T(8,128)(2,1)}, bf16[72,3584]{1,0:T(8,128)(2,1)}, f32[72,3584]{1,0:T(8,128)}, /*index=5*/f32[72,3584]{1,0:T(8,128)}) custom-call(bf16[3584,512]{1,0:T(8,128)(2,1)} %pad_maximum_fusion.gate_up, bf16[152,3584]{1,0:T(8,128)(2,1)} %bitcast.61, ...), custom_call_target="tpu_custom_call" | custom-call | flops 107374182400 | bytes 4194304 | tf_op jit(solution)/shard_map/experts/pallas_call | solution.py:229
  94.6 3.0 %collective-permute-start.13 = (bf16[72,3584]{1,0:T(8,128)(2,1)S(1)}, bf16[72,3584]{1,0:T(8,128)(2,1)S(1)}, u32[]{:S(2)}, u32[]{:S(2)}) collective-permute-start(bf16[72,3584]{1,0:T(8,128)(2,1)S(1)} %get-tuple-element.39), channel_id=1, source_target_pairs={{0,32},{32,64},{64,96},{96,0},{1,33},{33,65},{65,97},{97,1},{2,34}... | collective-permute-start | bytes 1548296 | tf_op jit(solution)/shard_map/partials_y/ppermute | solution.py:19
  97.6 2.8 %collective-permute-start.14 = (bf16[72,3584]{1,0:T(8,128)(2,1)S(1)}, bf16[72,3584]{1,0:T(8,128)(2,1)}, u32[]{:S(2)}, u32[]{:S(2)}) collective-permute-start(bf16[72,3584]{1,0:T(8,128)(2,1)S(1)} %get-tuple-element.40), channel_id=1, source_target_pairs={{0,96},{32,0},{64,32},{96,64},{1,97},{33,1},{65,33},{97,65},{2,98}... | collective-permute-start | bytes 1548296 | tf_op jit(solution)/shard_map/partials_y/ppermute | solution.py:19
  102.4 5.1 %collective-permute-start.17 = (bf16[72,3584]{1,0:T(8,128)(2,1)}, bf16[72,3584]{1,0:T(8,128)(2,1)}, u32[]{:S(2)}, u32[]{:S(2)}) collective-permute-start(bf16[72,3584]{1,0:T(8,128)(2,1)} %get-tuple-element.48), channel_id=1, source_target_pairs={{0,32},{32,64},{64,96},{96,0},{1,33},{33,65},{65,97},{97,1},{2,34}... | collective-permute-start | bytes 1548296 | tf_op jit(solution)/shard_map/partials_y/ppermute | solution.py:19
  109.7 4.8 %all-to-all-start.3 = ((bf16[4,128,384]{2,1,0:T(8,128)(2,1)}), bf16[4,128,384]{2,1,0:T(8,128)(2,1)S(1)}, u32[]{:S(2)}, u32[]{:S(2)}) async-start(bf16[4,128,384]{2,1,0:T(8,128)(2,1)} %broadcast_in_dim.46), calls=%async_computation.3 | async-start | bytes 786432 | tf_op jit(solution)/shard_map/dense_out/all_to_all | solution.py:23
  119.4 2.8 %collective-permute-start.15 = (bf16[72,3584]{1,0:T(8,128)(2,1)}, bf16[72,3584]{1,0:T(8,128)(2,1)}, u32[]{:S(2)}, u32[]{:S(2)}) collective-permute-start(bf16[72,3584]{1,0:T(8,128)(2,1)} %get-tuple-element.41), channel_id=1, source_target_pairs={{0,32},{32,64},{64,96},{96,0},{1,33},{33,65},{65,97},{97,1},{2,34}... | collective-permute-start | bytes 1548296 | tf_op jit(solution)/shard_map/partials_y/ppermute | solution.py:19
  122.2 3.0 %collective-permute-start.18 = (bf16[72,3584]{1,0:T(8,128)(2,1)}, bf16[72,3584]{1,0:T(8,128)(2,1)}, u32[]{:S(2)}, u32[]{:S(2)}) collective-permute-start(bf16[72,3584]{1,0:T(8,128)(2,1)} %get-tuple-element.42), channel_id=1, source_target_pairs={{0,96},{32,0},{64,32},{96,64},{1,97},{33,1},{65,33},{97,65},{2,98}... | collective-permute-start | bytes 1548296 | tf_op jit(solution)/shard_map/partials_y/ppermute | solution.py:19
  126.3 4.9 %partials_y.3 = (f32[72,3584]{1,0:T(8,128)}, f32[72,3584]{1,0:T(8,128)}) custom-call(bf16[3584,512]{1,0:T(8,128)(2,1)} %pad_maximum_fusion.gate_up, bf16[152,3584]{1,0:T(8,128)(2,1)} %bitcast.62, bf16[72,3584]{1,0:T(8,128)(2,1)S(1)} %copy-done.6, bf16[72,3584]{1,0:T(8,128)(2,1)S(1)} %copy-done.8), custom_call_target="tpu_custom_call" | custom-call | flops 2147483648 | bytes 4194304 | tf_op jit(solution)/shard_map/partials_y/pallas_call | solution.py:254
  131.2 2.8 %dense_out.1 = bf16[8,256,224]{2,1,0:T(8,128)(2,1)} custom-call(s32[4]{0:T(128)S(1)} %and_select_fusion.3.place, bf16[512,384]{1,0:T(8,128)(2,1)S(1)} %bitcast.45, bf16[224,1152]{1,0:T(8,128)(2,1)S(1)} %pad_maximum_fusion.2.refs_0_, bf16[224,1152]{1,0:T(8,128)(2,1)S(1)} %copy-done.4, bf16[224,1152]{1,0:T(8,128)(2,1)S(1)} %copy-done.2, ...), custom_call_target="tpu_custom_call" | custom-call | flops 2147483648 | bytes 4194304 | tf_op jit(solution)/shard_map/dense_out/pallas_call | solution.py:243
  134.0 3.3 %collective-permute-done.18.refs_3_ = bf16[72,3584]{1,0:T(8,128)(2,1)} collective-permute-done((bf16[72,3584]{1,0:T(8,128)(2,1)}, bf16[72,3584]{1,0:T(8,128)(2,1)}, u32[]{:S(2)}, u32[]{:S(2)}) %collective-permute-start.18) | collective-permute-done | bytes 516128 | tf_op jit(solution)/shard_map/partials_y/ppermute | solution.py:19
  137.3 3.6 %partials_z.1 = (f32[36,3584]{1,0:T(8,128)}, bf16[36,3584]{1,0:T(8,128)(2,1)S(1)}, bf16[36,3584]{1,0:T(8,128)(2,1)S(1)}, bf16[36,3584]{1,0:T(8,128)(2,1)S(1)}) custom-call(s32[4]{0:T(128)S(1)} %and_select_fusion.place, f32[72,3584]{1,0:T(8,128)} %get-tuple-element.45.low, f32[72,3584]{1,0:T(8,128)} %get-tuple-element.46.high, ...), custom_call_target="tpu_custom_call" | custom-call | flops 2147483648 | bytes 4194304 | tf_op jit(solution)/shard_map/partials_z/pallas_call | solution.py:261
  140.9 5.6 %collective-permute-start.19 = (bf16[36,3584]{1,0:T(8,128)(2,1)S(1)}, bf16[36,3584]{1,0:T(8,128)(2,1)}, u32[]{:S(2)}, u32[]{:S(2)}) collective-permute-start(bf16[36,3584]{1,0:T(8,128)(2,1)S(1)} %get-tuple-element.50), channel_id=1, source_target_pairs={{0,24},{8,0},{16,8},{24,16},{1,25},{9,1},{17,9},{25,17},{2,26},{10... | collective-permute-start | bytes 774152 | tf_op jit(solution)/shard_map/partials_z/ppermute | solution.py:19
  148.4 3.2 %collective-permute-start.21 = (bf16[36,3584]{1,0:T(8,128)(2,1)S(1)}, bf16[36,3584]{1,0:T(8,128)(2,1)}, u32[]{:S(2)}, u32[]{:S(2)}) collective-permute-start(bf16[36,3584]{1,0:T(8,128)(2,1)S(1)} %get-tuple-element.52), channel_id=1, source_target_pairs={{0,8},{8,16},{16,24},{24,0},{1,9},{9,17},{17,25},{25,1},{2,10},{10... | collective-permute-start | bytes 774152 | tf_op jit(solution)/shard_map/partials_z/ppermute | solution.py:19
  153.0 4.0 %all-to-all-start.4 = ((bf16[8,256,224]{1,2,0:T(8,128)(2,1)}), bf16[8,256,224]{1,2,0:T(8,128)(2,1)S(1)}, u32[]{:S(2)}, u32[]{:S(2)}) async-start(bf16[8,256,224]{1,2,0:T(8,128)(2,1)} %copy.72), calls=%async_computation.4 | async-start | bytes 1835008 | tf_op jit(solution)/shard_map/dense_out/all_to_all | solution.py:23
  157.0 12.0 %collective-permute-done.20 = bf16[36,3584]{1,0:T(8,128)(2,1)} collective-permute-done((bf16[36,3584]{1,0:T(8,128)(2,1)S(1)}, bf16[36,3584]{1,0:T(8,128)(2,1)}, u32[]{:S(2)}, u32[]{:S(2)}) %collective-permute-start.20) | collective-permute-done | bytes 258080 | tf_op jit(solution)/shard_map/partials_z/ppermute | solution.py:19
  171.6 3.6 %all-to-all-start.5 = ((bf16[8,36,448]{2,1,0:T(8,128)(2,1)}), bf16[8,36,448]{2,1,0:T(8,128)(2,1)S(1)}, u32[]{:S(2)}, u32[]{:S(2)}) async-start(bf16[8,36,448]{2,1,0:T(8,128)(2,1)} %bitcast.44), calls=%async_computation.5 | async-start | bytes 655360 | tf_op jit(solution)/shard_map/combine/all_to_all | solution.py:23
  175.5 4.4 %collective-permute-start.5 = (bf16[64,224]{1,0:T(8,128)(2,1)S(1)}, bf16[64,224]{1,0:T(8,128)(2,1)S(1)}, u32[]{:S(2)}, u32[]{:S(2)}) collective-permute-start(bf16[64,224]{1,0:T(8,128)(2,1)S(1)} %get-tuple-element.58), channel_id=1, source_target_pairs={{0,24},{8,0},{16,8},{24,16},{1,25},{9,1},{17,9},{25,17},{2,26},{10... | collective-permute-start | bytes 86024 | tf_op jit(solution)/shard_map/dense_out/ppermute | solution.py:19
  180.0 3.0 %collective-permute-start.4 = (bf16[64,224]{1,0:T(8,128)(2,1)S(1)}, bf16[64,224]{1,0:T(8,128)(2,1)S(1)}, u32[]{:S(2)}, u32[]{:S(2)}) collective-permute-start(bf16[64,224]{1,0:T(8,128)(2,1)S(1)} %get-tuple-element.59), channel_id=1, source_target_pairs={{0,16},{8,24},{16,0},{24,8},{1,17},{9,25},{17,1},{25,9},{2,18},{10... | collective-permute-start | bytes 86024 | tf_op jit(solution)/shard_map/dense_out/ppermute | solution.py:19
  186.7 3.9 %collective-permute-done.3 = bf16[64,224]{1,0:T(8,128)(2,1)S(1)} collective-permute-done((bf16[64,224]{1,0:T(8,128)(2,1)S(1)}, bf16[64,224]{1,0:T(8,128)(2,1)S(1)}, u32[]{:S(2)}, u32[]{:S(2)}) %collective-permute-start.3) | collective-permute-done | bytes 28704 | tf_op jit(solution)/shard_map/dense_out/ppermute | solution.py:19
  194.9 9.1 %collective-permute-start.22 = (bf16[128,448]{0,1:T(8,128)(2,1)S(1)}, bf16[128,448]{0,1:T(8,128)(2,1)S(1)}, u32[]{:S(2)}, u32[]{:S(2)}) collective-permute-start(bf16[128,448]{0,1:T(8,128)(2,1)S(1)} %fusion.1), channel_id=1, source_target_pairs={{0,128},{128,256},{256,384},{384,0},{1,129},{129,257},{257,385},{3... | collective-permute-start | bytes 344072 | tf_op jit(solution)/shard_map/next_section/ppermute | solution.py:19
  204.0 10.9 %collective-permute-done.22 = bf16[128,448]{0,1:T(8,128)(2,1)S(1)} collective-permute-done((bf16[128,448]{0,1:T(8,128)(2,1)S(1)}, bf16[128,448]{0,1:T(8,128)(2,1)S(1)}, u32[]{:S(2)}, u32[]{:S(2)}) %collective-permute-start.22) | collective-permute-done | bytes 114720 | tf_op jit(solution)/shard_map/next_section/ppermute | solution.py:19
  (132 shorter events, 54.8 us)
Async XLA Ops:
  5.4 35.9 %all-to-all-start = ((bf16[4,40,3584]{2,1,0:T(8,128)(2,1)}), bf16[4,40,3584]{2,1,0:T(8,128)(2,1)}, u32[]{:S(2)}, u32[]{:S(2)}) async-start(bf16[4,40,3584]{2,1,0:T(8,128)(2,1)} %pad_maximum_fusion.1), calls=%async_computation | async-start | bytes 2293760 | tf_op jit(solution)/shard_map/rows_z/all_to_all | solution.py:23
  11.3 27.5 %collective-permute-start.2 = (bf16[224,1152]{1,0:T(8,128)(2,1)S(1)}, bf16[224,1152]{1,0:T(8,128)(2,1)}, u32[]{:S(2)}, u32[]{:S(2)}) collective-permute-start(bf16[224,1152]{1,0:T(8,128)(2,1)S(1)} %pad_maximum_fusion.2.refs_0_), channel_id=1, source_target_pairs={{0,96},{32,0},{64,32},{96,64},{1,97},{33,1},{65,33},{97,65},{2,98}... | collective-permute-start | bytes 1548296 | tf_op jit(solution)/shard_map/dense_weights/ppermute | solution.py:19
  14.0 24.8 %collective-permute-start.1 = (bf16[224,1152]{1,0:T(8,128)(2,1)S(1)}, bf16[224,1152]{1,0:T(8,128)(2,1)S(1)}, u32[]{:S(2)}, u32[]{:S(2)}) collective-permute-start(bf16[224,1152]{1,0:T(8,128)(2,1)S(1)} %pad_maximum_fusion.2.refs_0_), channel_id=1, source_target_pairs={{0,64},{32,96},{64,0},{96,32},{1,65},{33,97},{65,1},{97,33},{2,66}... | collective-permute-start | bytes 1548296 | tf_op jit(solution)/shard_map/dense_weights/ppermute | solution.py:19
  20.6 20.6 %collective-permute-start = (bf16[224,1152]{1,0:T(8,128)(2,1)S(1)}, bf16[224,1152]{1,0:T(8,128)(2,1)S(1)}, u32[]{:S(2)}, u32[]{:S(2)}) collective-permute-start(bf16[224,1152]{1,0:T(8,128)(2,1)S(1)} %pad_maximum_fusion.2.refs_0_), channel_id=1, source_target_pairs={{0,32},{32,64},{64,96},{96,0},{1,33},{33,65},{65,97},{97,1},{2,34}... | collective-permute-start | bytes 1548296 | tf_op jit(solution)/shard_map/dense_weights/ppermute | solution.py:19
  38.8 30.7 %copy-start.1 = (bf16[224,1152]{1,0:T(8,128)(2,1)}, bf16[224,1152]{1,0:T(8,128)(2,1)S(1)}, u32[]{:S(2)}) copy-start(bf16[224,1152]{1,0:T(8,128)(2,1)S(1)} %collective-permute-done.1.refs_2_) | copy-start | bytes 1548292
  44.0 28.6 %copy-start.5 = (bf16[72,3584]{1,0:T(8,128)(2,1)}, bf16[72,3584]{1,0:T(8,128)(2,1)S(1)}, u32[]{:S(2)}) copy-start(bf16[72,3584]{1,0:T(8,128)(2,1)S(1)} %get-tuple-element.35.refs_0_) | copy-start | bytes 1548292
  44.0 28.6 %copy-start.7 = (bf16[72,3584]{1,0:T(8,128)(2,1)}, bf16[72,3584]{1,0:T(8,128)(2,1)S(1)}, u32[]{:S(2)}) copy-start(bf16[72,3584]{1,0:T(8,128)(2,1)S(1)} %get-tuple-element.36.refs_1_) | copy-start | bytes 1548292
  44.0 17.8 %collective-permute-start.7 = (bf16[72,3584]{1,0:T(8,128)(2,1)S(1)}, bf16[72,3584]{1,0:T(8,128)(2,1)}, u32[]{:S(2)}, u32[]{:S(2)}) collective-permute-start(bf16[72,3584]{1,0:T(8,128)(2,1)S(1)} %get-tuple-element.35.refs_0_), channel_id=1, source_target_pairs={{0,32},{32,64},{64,96},{96,0},{1,33},{33,65},{65,97},{97,1},{2,34}... | collective-permute-start | bytes 1548296 | tf_op jit(solution)/shard_map/rows_y/ppermute | solution.py:19
  48.6 17.9 %collective-permute-start.9 = (bf16[72,3584]{1,0:T(8,128)(2,1)S(1)}, bf16[72,3584]{1,0:T(8,128)(2,1)}, u32[]{:S(2)}, u32[]{:S(2)}) collective-permute-start(bf16[72,3584]{1,0:T(8,128)(2,1)S(1)} %get-tuple-element.36.refs_1_), channel_id=1, source_target_pairs={{0,96},{32,0},{64,32},{96,64},{1,97},{33,1},{65,33},{97,65},{2,98}... | collective-permute-start | bytes 1548296 | tf_op jit(solution)/shard_map/rows_y/ppermute | solution.py:19
  50.5 19.0 %all-to-all-start.1 = ((bf16[8,4,16,896]{3,2,1,0:T(8,128)(2,1)}), bf16[8,4,16,896]{3,2,1,0:T(8,128)(2,1)}, u32[]{:S(2)}, u32[]{:S(2)}) async-start(bf16[8,4,16,896]{3,2,1,0:T(8,128)(2,1)} %get-tuple-element.34), calls=%async_computation.1 | async-start | bytes 1835008 | tf_op jit(solution)/shard_map/dense_tokens/all_to_all | solution.py:23
  54.8 22.7 %collective-permute-start.11 = (bf16[72,3584]{1,0:T(8,128)(2,1)S(1)}, bf16[72,3584]{1,0:T(8,128)(2,1)}, u32[]{:S(2)}, u32[]{:S(2)}) collective-permute-start(bf16[72,3584]{1,0:T(8,128)(2,1)S(1)} %get-tuple-element.35.refs_0_), channel_id=1, source_target_pairs={{0,96},{32,0},{64,32},{96,64},{1,97},{33,1},{65,33},{97,65},{2,98}... | collective-permute-start | bytes 1548296 | tf_op jit(solution)/shard_map/rows_y/ppermute | solution.py:19
  56.7 20.8 %collective-permute-start.12 = (bf16[72,3584]{1,0:T(8,128)(2,1)S(1)}, bf16[72,3584]{1,0:T(8,128)(2,1)}, u32[]{:S(2)}, u32[]{:S(2)}) collective-permute-start(bf16[72,3584]{1,0:T(8,128)(2,1)S(1)} %get-tuple-element.36.refs_1_), channel_id=1, source_target_pairs={{0,32},{32,64},{64,96},{96,0},{1,33},{33,65},{65,97},{97,1},{2,34}... | collective-permute-start | bytes 1548296 | tf_op jit(solution)/shard_map/rows_y/ppermute | solution.py:19
  61.9 22.8 %collective-permute-start.8 = (bf16[72,3584]{1,0:T(8,128)(2,1)}, bf16[72,3584]{1,0:T(8,128)(2,1)}, u32[]{:S(2)}, u32[]{:S(2)}) collective-permute-start(bf16[72,3584]{1,0:T(8,128)(2,1)} %collective-permute-done.7.refs_3_), channel_id=1, source_target_pairs={{0,32},{32,64},{64,96},{96,0},{1,33},{33,65},{65,97},{97,1},{2,34}... | collective-permute-start | bytes 1548296 | tf_op jit(solution)/shard_map/rows_y/ppermute | solution.py:19
  66.4 20.9 %collective-permute-start.10 = (bf16[72,3584]{1,0:T(8,128)(2,1)}, bf16[72,3584]{1,0:T(8,128)(2,1)}, u32[]{:S(2)}, u32[]{:S(2)}) collective-permute-start(bf16[72,3584]{1,0:T(8,128)(2,1)} %collective-permute-done.9.refs_2_), channel_id=1, source_target_pairs={{0,96},{32,0},{64,32},{96,64},{1,97},{33,1},{65,33},{97,65},{2,98}... | collective-permute-start | bytes 1548296 | tf_op jit(solution)/shard_map/rows_y/ppermute | solution.py:19
  72.6 34.9 %all-to-all-start.2 = ((bf16[4,128,768]{2,1,0:T(8,128)(2,1)}), bf16[4,128,768]{2,1,0:T(8,128)(2,1)}, u32[]{:S(2)}, u32[]{:S(2)}) async-start(bf16[4,128,768]{2,1,0:T(8,128)(2,1)} %dense_tokens.1), calls=%async_computation.2 | async-start | bytes 1572864 | tf_op jit(solution)/shard_map/dense_hidden/all_to_all | solution.py:23
  94.6 19.9 %collective-permute-start.13 = (bf16[72,3584]{1,0:T(8,128)(2,1)S(1)}, bf16[72,3584]{1,0:T(8,128)(2,1)S(1)}, u32[]{:S(2)}, u32[]{:S(2)}) collective-permute-start(bf16[72,3584]{1,0:T(8,128)(2,1)S(1)} %get-tuple-element.39), channel_id=1, source_target_pairs={{0,32},{32,64},{64,96},{96,0},{1,33},{33,65},{65,97},{97,1},{2,34}... | collective-permute-start | bytes 1548296 | tf_op jit(solution)/shard_map/partials_y/ppermute | solution.py:19
  97.6 17.9 %collective-permute-start.14 = (bf16[72,3584]{1,0:T(8,128)(2,1)S(1)}, bf16[72,3584]{1,0:T(8,128)(2,1)}, u32[]{:S(2)}, u32[]{:S(2)}) collective-permute-start(bf16[72,3584]{1,0:T(8,128)(2,1)S(1)} %get-tuple-element.40), channel_id=1, source_target_pairs={{0,96},{32,0},{64,32},{96,64},{1,97},{33,1},{65,33},{97,65},{2,98}... | collective-permute-start | bytes 1548296 | tf_op jit(solution)/shard_map/partials_y/ppermute | solution.py:19
  100.5 33.5 %collective-permute-start.16 = (bf16[72,3584]{1,0:T(8,128)(2,1)}, bf16[72,3584]{1,0:T(8,128)(2,1)}, u32[]{:S(2)}, u32[]{:S(2)}) collective-permute-start(bf16[72,3584]{1,0:T(8,128)(2,1)} %get-tuple-element.47), channel_id=1, source_target_pairs={{0,96},{32,0},{64,32},{96,64},{1,97},{33,1},{65,33},{97,65},{2,98}... | collective-permute-start | bytes 1548296 | tf_op jit(solution)/shard_map/partials_y/ppermute | solution.py:19
  102.4 31.6 %collective-permute-start.17 = (bf16[72,3584]{1,0:T(8,128)(2,1)}, bf16[72,3584]{1,0:T(8,128)(2,1)}, u32[]{:S(2)}, u32[]{:S(2)}) collective-permute-start(bf16[72,3584]{1,0:T(8,128)(2,1)} %get-tuple-element.48), channel_id=1, source_target_pairs={{0,32},{32,64},{64,96},{96,0},{1,33},{33,65},{65,97},{97,1},{2,34}... | collective-permute-start | bytes 1548296 | tf_op jit(solution)/shard_map/partials_y/ppermute | solution.py:19
  109.7 21.4 %all-to-all-start.3 = ((bf16[4,128,384]{2,1,0:T(8,128)(2,1)}), bf16[4,128,384]{2,1,0:T(8,128)(2,1)S(1)}, u32[]{:S(2)}, u32[]{:S(2)}) async-start(bf16[4,128,384]{2,1,0:T(8,128)(2,1)} %broadcast_in_dim.46), calls=%async_computation.3 | async-start | bytes 786432 | tf_op jit(solution)/shard_map/dense_out/all_to_all | solution.py:23
  119.4 14.6 %collective-permute-start.15 = (bf16[72,3584]{1,0:T(8,128)(2,1)}, bf16[72,3584]{1,0:T(8,128)(2,1)}, u32[]{:S(2)}, u32[]{:S(2)}) collective-permute-start(bf16[72,3584]{1,0:T(8,128)(2,1)} %get-tuple-element.41), channel_id=1, source_target_pairs={{0,32},{32,64},{64,96},{96,0},{1,33},{33,65},{65,97},{97,1},{2,34}... | collective-permute-start | bytes 1548296 | tf_op jit(solution)/shard_map/partials_y/ppermute | solution.py:19
  122.2 15.1 %collective-permute-start.18 = (bf16[72,3584]{1,0:T(8,128)(2,1)}, bf16[72,3584]{1,0:T(8,128)(2,1)}, u32[]{:S(2)}, u32[]{:S(2)}) collective-permute-start(bf16[72,3584]{1,0:T(8,128)(2,1)} %get-tuple-element.42), channel_id=1, source_target_pairs={{0,96},{32,0},{64,32},{96,64},{1,97},{33,1},{65,33},{97,65},{2,98}... | collective-permute-start | bytes 1548296 | tf_op jit(solution)/shard_map/partials_y/ppermute | solution.py:19
  140.9 16.2 %collective-permute-start.19 = (bf16[36,3584]{1,0:T(8,128)(2,1)S(1)}, bf16[36,3584]{1,0:T(8,128)(2,1)}, u32[]{:S(2)}, u32[]{:S(2)}) collective-permute-start(bf16[36,3584]{1,0:T(8,128)(2,1)S(1)} %get-tuple-element.50), channel_id=1, source_target_pairs={{0,24},{8,0},{16,8},{24,16},{1,25},{9,1},{17,9},{25,17},{2,26},{10... | collective-permute-start | bytes 774152 | tf_op jit(solution)/shard_map/partials_z/ppermute | solution.py:19
  146.4 22.6 %collective-permute-start.20 = (bf16[36,3584]{1,0:T(8,128)(2,1)S(1)}, bf16[36,3584]{1,0:T(8,128)(2,1)}, u32[]{:S(2)}, u32[]{:S(2)}) collective-permute-start(bf16[36,3584]{1,0:T(8,128)(2,1)S(1)} %get-tuple-element.51), channel_id=1, source_target_pairs={{0,16},{8,24},{16,0},{24,8},{1,17},{9,25},{17,1},{25,9},{2,18},{10... | collective-permute-start | bytes 774152 | tf_op jit(solution)/shard_map/partials_z/ppermute | solution.py:19
  148.4 20.7 %collective-permute-start.21 = (bf16[36,3584]{1,0:T(8,128)(2,1)S(1)}, bf16[36,3584]{1,0:T(8,128)(2,1)}, u32[]{:S(2)}, u32[]{:S(2)}) collective-permute-start(bf16[36,3584]{1,0:T(8,128)(2,1)S(1)} %get-tuple-element.52), channel_id=1, source_target_pairs={{0,8},{8,16},{16,24},{24,0},{1,9},{9,17},{17,25},{25,1},{2,10},{10... | collective-permute-start | bytes 774152 | tf_op jit(solution)/shard_map/partials_z/ppermute | solution.py:19
  153.0 18.6 %all-to-all-start.4 = ((bf16[8,256,224]{1,2,0:T(8,128)(2,1)}), bf16[8,256,224]{1,2,0:T(8,128)(2,1)S(1)}, u32[]{:S(2)}, u32[]{:S(2)}) async-start(bf16[8,256,224]{1,2,0:T(8,128)(2,1)} %copy.72), calls=%async_computation.4 | async-start | bytes 1835008 | tf_op jit(solution)/shard_map/dense_out/all_to_all | solution.py:23
  171.6 14.2 %all-to-all-start.5 = ((bf16[8,36,448]{2,1,0:T(8,128)(2,1)}), bf16[8,36,448]{2,1,0:T(8,128)(2,1)S(1)}, u32[]{:S(2)}, u32[]{:S(2)}) async-start(bf16[8,36,448]{2,1,0:T(8,128)(2,1)} %bitcast.44), calls=%async_computation.5 | async-start | bytes 655360 | tf_op jit(solution)/shard_map/combine/all_to_all | solution.py:23
  175.5 10.3 %collective-permute-start.5 = (bf16[64,224]{1,0:T(8,128)(2,1)S(1)}, bf16[64,224]{1,0:T(8,128)(2,1)S(1)}, u32[]{:S(2)}, u32[]{:S(2)}) collective-permute-start(bf16[64,224]{1,0:T(8,128)(2,1)S(1)} %get-tuple-element.58), channel_id=1, source_target_pairs={{0,24},{8,0},{16,8},{24,16},{1,25},{9,1},{17,9},{25,17},{2,26},{10... | collective-permute-start | bytes 86024 | tf_op jit(solution)/shard_map/dense_out/ppermute | solution.py:19
  180.0 6.7 %collective-permute-start.4 = (bf16[64,224]{1,0:T(8,128)(2,1)S(1)}, bf16[64,224]{1,0:T(8,128)(2,1)S(1)}, u32[]{:S(2)}, u32[]{:S(2)}) collective-permute-start(bf16[64,224]{1,0:T(8,128)(2,1)S(1)} %get-tuple-element.59), channel_id=1, source_target_pairs={{0,16},{8,24},{16,0},{24,8},{1,17},{9,25},{17,1},{25,9},{2,18},{10... | collective-permute-start | bytes 86024 | tf_op jit(solution)/shard_map/dense_out/ppermute | solution.py:19
  183.0 7.6 %collective-permute-start.3 = (bf16[64,224]{1,0:T(8,128)(2,1)S(1)}, bf16[64,224]{1,0:T(8,128)(2,1)S(1)}, u32[]{:S(2)}, u32[]{:S(2)}) collective-permute-start(bf16[64,224]{1,0:T(8,128)(2,1)S(1)} %get-tuple-element.60), channel_id=1, source_target_pairs={{0,8},{8,16},{16,24},{24,0},{1,9},{9,17},{17,25},{25,1},{2,10},{10... | collective-permute-start | bytes 86024 | tf_op jit(solution)/shard_map/dense_out/ppermute | solution.py:19
  191.2 3.1 %collective-permute-start.6 = (bf16[2,64,224]{2,1,0:T(8,128)(2,1)S(1)}, bf16[2,64,224]{2,1,0:T(8,128)(2,1)S(1)}, u32[]{:S(2)}, u32[]{:S(2)}) collective-permute-start(bf16[2,64,224]{2,1,0:T(8,128)(2,1)S(1)} %constant_dynamic-slice_fusion), channel_id=1, source_target_pairs={{0,1},{1,0},{2,3},{3,2},{4,5},{5,4},{6,7},{7,6},{8,9},{9,8},{10,11... | collective-permute-start | bytes 172040 | tf_op jit(solution)/shard_map/dense_out/ppermute | solution.py:19
  194.9 20.0 %collective-permute-start.22 = (bf16[128,448]{0,1:T(8,128)(2,1)S(1)}, bf16[128,448]{0,1:T(8,128)(2,1)S(1)}, u32[]{:S(2)}, u32[]{:S(2)}) collective-permute-start(bf16[128,448]{0,1:T(8,128)(2,1)S(1)} %fusion.1), channel_id=1, source_target_pairs={{0,128},{128,256},{256,384},{384,0},{1,129},{129,257},{257,385},{3... | collective-permute-start | bytes 344072 | tf_op jit(solution)/shard_map/next_section/ppermute | solution.py:19
  (21 other events, 206.6 us)

commit v11 on v10

--- a/solution.py
+++ b/solution.py
@@ -82,11 +82,6 @@
     for z in range(4):
         rows = jnp.concatenate([tokens[e, z] for e in range(tokens.shape[0])], axis=0)
         out[z] = dot(rows, joined).astype(BF16)
-
-
-def late_kernel(part_next, part_prev, relay_next, relay_prev, to_next, to_prev):
-    to_next[...] = (part_next[...] + relay_next[...].astype(F32)).astype(BF16)
-    to_prev[...] = (part_prev[...] + relay_prev[...].astype(F32)).astype(BF16)
 
 
 def total_kernel(capacity, place, low, high, *refs):
@@ -248,9 +243,10 @@
 
     with jax.named_scope("partials_y"):
         early_next, early_prev = shifted(early_next, "y", 1), shifted(early_prev, "y", -1)
-        late_next, late_prev = local_call(late_kernel, [half_bf16] * 2, LONG)(
-            next_part, prev_part, relay_next, relay_prev
-        )
+        relay_next, relay_prev = after((relay_next, relay_prev), line_act)
+        late_next = (next_part + relay_next.astype(F32)).astype(BF16)
+        late_prev = (prev_part + relay_prev.astype(F32)).astype(BF16)
+        late_next, late_prev = after((late_next, late_prev))
         own_low, own_high = local_call(rows_kernel, [half_f32] * 2)(
             after(gate_up, late_next, late_prev), down, low, high
         )
@@ -264,7 +260,7 @@
             in_specs=[in_smem] + [in_vmem] * 6,
             scratch_shapes=[pltpu.VMEM((4 * capacity, width), F32)],
         )(place_z, after(own_low, by_block), own_high, late_next, early_prev, early_next, late_prev)
-        recv = [shifted(part, "z", by) for part, by in zip(sent, (-1, -2, -3))]
+        recv = [shifted(sent[k], "z", -1 - k) for k in (1, 2, 0)]
         expert_out = (kept_rows + sum(part.astype(F32) for part in recv)).astype(BF16)
 
     with jax.named_scope("dense_out"):

time: 218 us -> 215 us (0.986)
  the two profiles are of different devices: /device:TPU:24 before, /device:TPU:123 now
where the time goes in v11:
time: 215 us; the launch traced here: 214 us
  starting transfers between devices  108 us (50%)
  waiting for transfers between devices  52.8 us (25%)
  Pallas kernels  24.8 us (12%)
  other arithmetic  14.5 us (7%)
  local copies, waits for them, and re-layouts  11.7 us (5%)
    ppermute x23, starting transfers between devices, shifted(): return lax.ppermute(x, axis, [(i, (i + by) % peers) for i in range(peers)])  75.9 us
    ppermute x23, waiting for transfers between devices, shifted(): return lax.ppermute(x, axis, [(i, (i + by) % peers) for i in range(peers)])  43.1 us
    all_to_all x6, starting transfers between devices, exchanged(): return lax.all_to_all(x, axes, split_axis=0, concat_axis=0, tiled=True)  32.6 us
    all_to_all x6, waiting for transfers between devices, exchanged(): return lax.all_to_all(x, axes, split_axis=0, concat_axis=0, tiled=True)  9.63 us
    pallas_call x1, Pallas kernels, body(): local_call(rows_kernel, [half_bf16] * 4 + [half_f32] * 2, LONG)  7.71 us
    unnamed x25, local copies, waits for them, and re-layouts  5.07 us
    concatenate x1, other arithmetic, body(): jnp.concatenate([expert_gate[0, 0], blank, expert_up[0, 0], blank], axis=1)  5.04 us
    pallas_call x1, Pallas kernels, body(): local_call(rows_kernel, [half_f32] * 2)  4.94 us
  transfers between devices with their start and end apart: 29, of which 12 were waited for; matrix products, arithmetic and copies ran while one was open for 9% of the time, Pallas kernels for 9%

profile of v11, /device:TPU:123, one launch (start us, length us, event | category | flops | bytes accessed | tf_op | source)
XLA Modules:
  0.0 213.8 jit_solution(8353526189539538008)
XLA Ops:
  5.4 4.5 %all-to-all-start = ((bf16[4,40,3584]{2,1,0:T(8,128)(2,1)}), bf16[4,40,3584]{2,1,0:T(8,128)(2,1)}, u32[]{:S(2)}, u32[]{:S(2)}) async-start(bf16[4,40,3584]{2,1,0:T(8,128)(2,1)} %pad_maximum_fusion.1), calls=%async_computation | async-start | bytes 2293760 | tf_op jit(solution)/shard_map/rows_z/all_to_all | solution.py:23
  14.9 3.8 %collective-permute-start = (bf16[224,1152]{1,0:T(8,128)(2,1)S(1)}, bf16[224,1152]{1,0:T(8,128)(2,1)S(1)}, u32[]{:S(2)}, u32[]{:S(2)}) collective-permute-start(bf16[224,1152]{1,0:T(8,128)(2,1)S(1)} %pad_maximum_fusion.2.refs_0_), channel_id=1, source_target_pairs={{0,32},{32,64},{64,96},{96,0},{1,33},{33,65},{65,97},{97,1},{2,34}... | collective-permute-start | bytes 1548296 | tf_op jit(solution)/shard_map/dense_weights/ppermute | solution.py:19
  20.4 2.7 %copy.71 = bf16[1,1,3584,152]{3,2,1,0:T(8,128)(2,1)} copy(bf16[1,1,3584,152]{2,3,1,0:T(8,128)(2,1)} %param.18) | data formatting | bytes 2179072 | tf_op args[8]
  23.4 5.0 %pad_maximum_fusion.gate_up = bf16[3584,512]{1,0:T(8,128)(2,1)} fusion(bf16[3584,104]{1,0:T(8,128)(2,1)S(1)} %broadcast_in_dim.26, bf16[3584,152]{1,0:T(8,128)(2,1)} %bitcast.47, bf16[3584,152]{1,0:T(8,128)(2,1)} %bitcast.46), kind=kLoop, calls=%fused_computation.3 | loop fusion | flops 14680064 | bytes 6594560 | tf_op jit(solution)/shard_map/concatenate | solution.py:190
  28.4 6.2 %collective-permute-done.1.refs_2_ = bf16[224,1152]{1,0:T(8,128)(2,1)S(1)} collective-permute-done((bf16[224,1152]{1,0:T(8,128)(2,1)S(1)}, bf16[224,1152]{1,0:T(8,128)(2,1)S(1)}, u32[]{:S(2)}, u32[]{:S(2)}) %collective-permute-start.1) | collective-permute-done | bytes 516128 | tf_op jit(solution)/shard_map/dense_weights/ppermute | solution.py:19
  34.6 4.6 %collective-permute-done.refs_1_ = bf16[224,1152]{1,0:T(8,128)(2,1)S(1)} collective-permute-done((bf16[224,1152]{1,0:T(8,128)(2,1)S(1)}, bf16[224,1152]{1,0:T(8,128)(2,1)S(1)}, u32[]{:S(2)}, u32[]{:S(2)}) %collective-permute-start) | collective-permute-done | bytes 516128 | tf_op jit(solution)/shard_map/dense_weights/ppermute | solution.py:19
  41.9 5.3 %collective-permute-start.7 = (bf16[72,3584]{1,0:T(8,128)(2,1)S(1)}, bf16[72,3584]{1,0:T(8,128)(2,1)}, u32[]{:S(2)}, u32[]{:S(2)}) collective-permute-start(bf16[72,3584]{1,0:T(8,128)(2,1)S(1)} %get-tuple-element.37.refs_0_), channel_id=1, source_target_pairs={{0,32},{32,64},{64,96},{96,0},{1,33},{33,65},{65,97},{97,1},{2,34}... | collective-permute-start | bytes 1548296 | tf_op jit(solution)/shard_map/rows_y/ppermute | solution.py:19
  49.2 5.3 %all-to-all-start.1 = ((bf16[8,4,16,896]{3,2,1,0:T(8,128)(2,1)}), bf16[8,4,16,896]{3,2,1,0:T(8,128)(2,1)}, u32[]{:S(2)}, u32[]{:S(2)}) async-start(bf16[8,4,16,896]{3,2,1,0:T(8,128)(2,1)} %get-tuple-element.36), calls=%async_computation.1 | async-start | bytes 1835008 | tf_op jit(solution)/shard_map/dense_tokens/all_to_all | solution.py:23
  56.3 4.9 %collective-permute-start.12 = (bf16[72,3584]{1,0:T(8,128)(2,1)}, bf16[72,3584]{1,0:T(8,128)(2,1)}, u32[]{:S(2)}, u32[]{:S(2)}) collective-permute-start(bf16[72,3584]{1,0:T(8,128)(2,1)} %get-tuple-element.38.refs_1_), channel_id=1, source_target_pairs={{0,32},{32,64},{64,96},{96,0},{1,33},{33,65},{65,97},{97,1},{2,34}... | collective-permute-start | bytes 1548296 | tf_op jit(solution)/shard_map/rows_y/ppermute | solution.py:19
  61.2 3.4 %collective-permute-start.8 = (bf16[72,3584]{1,0:T(8,128)(2,1)}, bf16[72,3584]{1,0:T(8,128)(2,1)}, u32[]{:S(2)}, u32[]{:S(2)}) collective-permute-start(bf16[72,3584]{1,0:T(8,128)(2,1)} %collective-permute-done.7.refs_3_), channel_id=1, source_target_pairs={{0,32},{32,64},{64,96},{96,0},{1,33},{33,65},{65,97},{97,1},{2,34}... | collective-permute-start | bytes 1548296 | tf_op jit(solution)/shard_map/rows_y/ppermute | solution.py:19
  67.1 3.2 %dense_tokens.1 = bf16[4,128,768]{2,1,0:T(8,128)(2,1)} custom-call(bf16[8,4,16,896]{3,2,1,0:T(8,128)(2,1)} %all-to-all-done.1.tokens, bf16[224,1152]{1,0:T(8,128)(2,1)S(1)} %pad_maximum_fusion.2.refs_0_, bf16[224,1152]{1,0:T(8,128)(2,1)S(1)} %collective-permute-done.refs_1_, bf16[224,1152]{1,0:T(8,128)(2,1)S(1)} %collective-permute-done.1.refs_2_, ...), custom_call_target="tpu_custom_call" | custom-call | flops 2147483648 | bytes 4194304 | tf_op jit(solution)/shard_map/dense_tokens/pallas_call | solution.py:216
  70.3 4.5 %all-to-all-start.2 = ((bf16[4,128,768]{2,1,0:T(8,128)(2,1)}), bf16[4,128,768]{2,1,0:T(8,128)(2,1)}, u32[]{:S(2)}, u32[]{:S(2)}) async-start(bf16[4,128,768]{2,1,0:T(8,128)(2,1)} %dense_tokens.1), calls=%async_computation.2 | async-start | bytes 1572864 | tf_op jit(solution)/shard_map/dense_hidden/all_to_all | solution.py:23
  74.9 8.5 %collective-permute-done.8.refs_0_ = bf16[72,3584]{1,0:T(8,128)(2,1)} collective-permute-done((bf16[72,3584]{1,0:T(8,128)(2,1)}, bf16[72,3584]{1,0:T(8,128)(2,1)}, u32[]{:S(2)}, u32[]{:S(2)}) %collective-permute-start.8) | collective-permute-done | bytes 516128 | tf_op jit(solution)/shard_map/rows_y/ppermute | solution.py:19
  85.3 7.7 %experts.1 = (bf16[72,3584]{1,0:T(8,128)(2,1)}, bf16[72,3584]{1,0:T(8,128)(2,1)}, bf16[72,3584]{1,0:T(8,128)(2,1)}, bf16[72,3584]{1,0:T(8,128)(2,1)}, f32[72,3584]{1,0:T(8,128)}, /*index=5*/f32[72,3584]{1,0:T(8,128)}) custom-call(bf16[3584,512]{1,0:T(8,128)(2,1)} %pad_maximum_fusion.gate_up, bf16[152,3584]{1,0:T(8,128)(2,1)} %bitcast.61, ...), custom_call_target="tpu_custom_call" | custom-call | flops 107374182400 | bytes 4194304 | tf_op jit(solution)/shard_map/experts/pallas_call | solution.py:224
  93.0 3.4 %collective-permute-start.13 = (bf16[72,3584]{1,0:T(8,128)(2,1)}, bf16[72,3584]{1,0:T(8,128)(2,1)}, u32[]{:S(2)}, u32[]{:S(2)}) collective-permute-start(bf16[72,3584]{1,0:T(8,128)(2,1)} %get-tuple-element.40), channel_id=1, source_target_pairs={{0,32},{32,64},{64,96},{96,0},{1,33},{33,65},{65,97},{97,1},{2,34}... | collective-permute-start | bytes 1548296 | tf_op jit(solution)/shard_map/partials_y/ppermute | solution.py:19
  100.2 4.6 %collective-permute-start.17 = (bf16[72,3584]{1,0:T(8,128)(2,1)}, bf16[72,3584]{1,0:T(8,128)(2,1)}, u32[]{:S(2)}, u32[]{:S(2)}) collective-permute-start(bf16[72,3584]{1,0:T(8,128)(2,1)} %get-tuple-element.52), channel_id=1, source_target_pairs={{0,32},{32,64},{64,96},{96,0},{1,33},{33,65},{65,97},{97,1},{2,34}... | collective-permute-start | bytes 1548296 | tf_op jit(solution)/shard_map/partials_y/ppermute | solution.py:19
  107.0 4.5 %all-to-all-start.3 = ((bf16[4,128,384]{2,1,0:T(8,128)(2,1)}), bf16[4,128,384]{2,1,0:T(8,128)(2,1)S(1)}, u32[]{:S(2)}, u32[]{:S(2)}) async-start(bf16[4,128,384]{2,1,0:T(8,128)(2,1)} %broadcast_in_dim.46), calls=%async_computation.3 | async-start | bytes 786432 | tf_op jit(solution)/shard_map/dense_out/all_to_all | solution.py:23
  111.5 2.9 %add_convert_fusion = (bf16[72,3584]{1,0:T(8,128)(2,1)}, bf16[72,3584]{1,0:T(8,128)(2,1)}) fusion(f32[72,3584]{1,0:T(8,128)} %get-tuple-element.43, bf16[72,3584]{1,0:T(8,128)(2,1)} %collective-permute-done.14, f32[72,3584]{1,0:T(8,128)} %get-tuple-element.39, bf16[72,3584]{1,0:T(8,128)(2,1)} %collective-permute-done.13), kind=kLoop, calls=%fused_computation.9 | loop fusion | flops 1548288 | bytes 4128768 | tf_op jit(solution)/shard_map/partials_y/convert_element_type | solution.py:248
  114.5 3.3 %collective-permute-start.15 = (bf16[72,3584]{1,0:T(8,128)(2,1)}, bf16[72,3584]{1,0:T(8,128)(2,1)}, u32[]{:S(2)}, u32[]{:S(2)}) collective-permute-start(bf16[72,3584]{1,0:T(8,128)(2,1)} %get-tuple-element.45), channel_id=1, source_target_pairs={{0,32},{32,64},{64,96},{96,0},{1,33},{33,65},{65,97},{97,1},{2,34}... | collective-permute-start | bytes 1548296 | tf_op jit(solution)/shard_map/partials_y/ppermute | solution.py:19
  119.8 4.9 %partials_y.1 = (f32[72,3584]{1,0:T(8,128)}, f32[72,3584]{1,0:T(8,128)}) custom-call(bf16[3584,512]{1,0:T(8,128)(2,1)} %pad_maximum_fusion.gate_up, bf16[152,3584]{1,0:T(8,128)(2,1)} %bitcast.62, bf16[72,3584]{1,0:T(8,128)(2,1)S(1)} %get-tuple-element.37.refs_0_, bf16[72,3584]{1,0:T(8,128)(2,1)} %get-tuple-element.38.refs_1_), custom_call_target="tpu_custom_call" | custom-call | flops 2147483648 | bytes 4194304 | tf_op jit(solution)/shard_map/partials_y/pallas_call | solution.py:250
  124.8 2.8 %dense_out.1 = bf16[8,256,224]{2,1,0:T(8,128)(2,1)} custom-call(s32[4]{0:T(128)S(1)} %and_select_fusion.3.place, bf16[512,384]{1,0:T(8,128)(2,1)S(1)} %bitcast.45, bf16[224,1152]{1,0:T(8,128)(2,1)S(1)} %pad_maximum_fusion.2.refs_0_, bf16[224,1152]{1,0:T(8,128)(2,1)S(1)} %collective-permute-done.refs_1_, ...), custom_call_target="tpu_custom_call" | custom-call | flops 2147483648 | bytes 4194304 | tf_op jit(solution)/shard_map/dense_out/pallas_call | solution.py:238
  127.6 5.0 %collective-permute-done.18.refs_3_ = bf16[72,3584]{1,0:T(8,128)(2,1)} collective-permute-done((bf16[72,3584]{1,0:T(8,128)(2,1)}, bf16[72,3584]{1,0:T(8,128)(2,1)}, u32[]{:S(2)}, u32[]{:S(2)}) %collective-permute-start.18) | collective-permute-done | bytes 516128 | tf_op jit(solution)/shard_map/partials_y/ppermute | solution.py:19
  132.7 3.5 %partials_z.1 = (f32[36,3584]{1,0:T(8,128)}, bf16[36,3584]{1,0:T(8,128)(2,1)S(1)}, bf16[36,3584]{1,0:T(8,128)(2,1)S(1)}, bf16[36,3584]{1,0:T(8,128)(2,1)S(1)}) custom-call(s32[4]{0:T(128)S(1)} %and_select_fusion.place, f32[72,3584]{1,0:T(8,128)} %get-tuple-element.49.low, f32[72,3584]{1,0:T(8,128)} %get-tuple-element.50.high, ...), custom_call_target="tpu_custom_call" | custom-call | flops 2147483648 | bytes 4194304 | tf_op jit(solution)/shard_map/partials_z/pallas_call | solution.py:257
  138.4 4.0 %collective-permute-start.20 = (bf16[36,3584]{1,0:T(8,128)(2,1)S(1)}, bf16[36,3584]{1,0:T(8,128)(2,1)}, u32[]{:S(2)}, u32[]{:S(2)}) collective-permute-start(bf16[36,3584]{1,0:T(8,128)(2,1)S(1)} %get-tuple-element.55), channel_id=1, source_target_pairs={{0,8},{8,16},{16,24},{24,0},{1,9},{9,17},{17,25},{25,1},{2,10},{10... | collective-permute-start | bytes 774152 | tf_op jit(solution)/shard_map/partials_z/ppermute | solution.py:19
  146.7 8.4 %all-to-all-start.4 = ((bf16[8,256,224]{1,2,0:T(8,128)(2,1)}), bf16[8,256,224]{1,2,0:T(8,128)(2,1)S(1)}, u32[]{:S(2)}, u32[]{:S(2)}) async-start(bf16[8,256,224]{1,2,0:T(8,128)(2,1)} %copy.72), calls=%async_computation.4 | async-start | bytes 1835008 | tf_op jit(solution)/shard_map/dense_out/all_to_all | solution.py:23
  158.7 9.0 %all-to-all-done.4 = bf16[8,256,224]{1,2,0:T(8,128)(2,1)S(1)} async-done(((bf16[8,256,224]{1,2,0:T(8,128)(2,1)}), bf16[8,256,224]{1,2,0:T(8,128)(2,1)S(1)}, u32[]{:S(2)}, u32[]{:S(2)}) %all-to-all-start.4) | async-done | bytes 917536 | tf_op jit(solution)/shard_map/dense_out/all_to_all | solution.py:23
  167.7 5.3 %all-to-all-start.5 = ((bf16[8,36,448]{2,1,0:T(8,128)(2,1)}), bf16[8,36,448]{2,1,0:T(8,128)(2,1)S(1)}, u32[]{:S(2)}, u32[]{:S(2)}) async-start(bf16[8,36,448]{2,1,0:T(8,128)(2,1)} %bitcast.44), calls=%async_computation.5 | async-start | bytes 655360 | tf_op jit(solution)/shard_map/combine/all_to_all | solution.py:23
  173.3 2.9 %collective-permute-start.5 = (bf16[64,224]{1,0:T(8,128)(2,1)S(1)}, bf16[64,224]{1,0:T(8,128)(2,1)S(1)}, u32[]{:S(2)}, u32[]{:S(2)}) collective-permute-start(bf16[64,224]{1,0:T(8,128)(2,1)S(1)} %get-tuple-element.62), channel_id=1, source_target_pairs={{0,24},{8,0},{16,8},{24,16},{1,25},{9,1},{17,9},{25,17},{2,26},{10... | collective-permute-start | bytes 86024 | tf_op jit(solution)/shard_map/dense_out/ppermute | solution.py:19
  176.2 4.7 %collective-permute-start.4 = (bf16[64,224]{1,0:T(8,128)(2,1)S(1)}, bf16[64,224]{1,0:T(8,128)(2,1)S(1)}, u32[]{:S(2)}, u32[]{:S(2)}) collective-permute-start(bf16[64,224]{1,0:T(8,128)(2,1)S(1)} %get-tuple-element.63), channel_id=1, source_target_pairs={{0,16},{8,24},{16,0},{24,8},{1,17},{9,25},{17,1},{25,9},{2,18},{10... | collective-permute-start | bytes 86024 | tf_op jit(solution)/shard_map/dense_out/ppermute | solution.py:19
  186.2 4.0 %collective-permute-start.6 = (bf16[2,64,224]{2,1,0:T(8,128)(2,1)S(1)}, bf16[2,64,224]{2,1,0:T(8,128)(2,1)S(1)}, u32[]{:S(2)}, u32[]{:S(2)}) collective-permute-start(bf16[2,64,224]{2,1,0:T(8,128)(2,1)S(1)} %constant_dynamic-slice_fusion), channel_id=1, source_target_pairs={{0,1},{1,0},{2,3},{3,2},{4,5},{5,4},{6,7},{7,6},{8,9},{9,8},{10,11... | collective-permute-start | bytes 172040 | tf_op jit(solution)/shard_map/dense_out/ppermute | solution.py:19
  191.6 8.8 %collective-permute-start.22 = (bf16[128,448]{0,1:T(8,128)(2,1)S(1)}, bf16[128,448]{0,1:T(8,128)(2,1)S(1)}, u32[]{:S(2)}, u32[]{:S(2)}) collective-permute-start(bf16[128,448]{0,1:T(8,128)(2,1)S(1)} %fusion.1), channel_id=1, source_target_pairs={{0,128},{128,256},{256,384},{384,0},{1,129},{129,257},{257,385},{3... | collective-permute-start | bytes 344072 | tf_op jit(solution)/shard_map/next_section/ppermute | solution.py:19
  200.4 12.7 %collective-permute-done.22 = bf16[128,448]{0,1:T(8,128)(2,1)S(1)} collective-permute-done((bf16[128,448]{0,1:T(8,128)(2,1)S(1)}, bf16[128,448]{0,1:T(8,128)(2,1)S(1)}, u32[]{:S(2)}, u32[]{:S(2)}) %collective-permute-start.22) | collective-permute-done | bytes 114720 | tf_op jit(solution)/shard_map/next_section/ppermute | solution.py:19
  (106 shorter events, 48.6 us)
Async XLA Ops:
  4.2 14.6 %copy-start.1 = (bf16[1,1,3584,152]{2,3,1,0:T(8,128)(2,1)S(1)}, bf16[1,1,3584,152]{2,3,1,0:T(8,128)(2,1)}, u32[]{:S(2)}) copy-start(bf16[1,1,3584,152]{2,3,1,0:T(8,128)(2,1)} %param.17) | copy-start | bytes 3268612
  5.4 33.9 %all-to-all-start = ((bf16[4,40,3584]{2,1,0:T(8,128)(2,1)}), bf16[4,40,3584]{2,1,0:T(8,128)(2,1)}, u32[]{:S(2)}, u32[]{:S(2)}) async-start(bf16[4,40,3584]{2,1,0:T(8,128)(2,1)} %pad_maximum_fusion.1), calls=%async_computation | async-start | bytes 2293760 | tf_op jit(solution)/shard_map/rows_z/all_to_all | solution.py:23
  10.0 18.4 %collective-permute-start.2 = (bf16[224,1152]{1,0:T(8,128)(2,1)S(1)}, bf16[224,1152]{1,0:T(8,128)(2,1)}, u32[]{:S(2)}, u32[]{:S(2)}) collective-permute-start(bf16[224,1152]{1,0:T(8,128)(2,1)S(1)} %pad_maximum_fusion.2.refs_0_), channel_id=1, source_target_pairs={{0,96},{32,0},{64,32},{96,64},{1,97},{33,1},{65,33},{97,65},{2,98}... | collective-permute-start | bytes 1548296 | tf_op jit(solution)/shard_map/dense_weights/ppermute | solution.py:19
  12.4 22.3 %collective-permute-start.1 = (bf16[224,1152]{1,0:T(8,128)(2,1)S(1)}, bf16[224,1152]{1,0:T(8,128)(2,1)S(1)}, u32[]{:S(2)}, u32[]{:S(2)}) collective-permute-start(bf16[224,1152]{1,0:T(8,128)(2,1)S(1)} %pad_maximum_fusion.2.refs_0_), channel_id=1, source_target_pairs={{0,64},{32,96},{64,0},{96,32},{1,65},{33,97},{65,1},{97,33},{2,66}... | collective-permute-start | bytes 1548296 | tf_op jit(solution)/shard_map/dense_weights/ppermute | solution.py:19
  14.9 24.4 %collective-permute-start = (bf16[224,1152]{1,0:T(8,128)(2,1)S(1)}, bf16[224,1152]{1,0:T(8,128)(2,1)S(1)}, u32[]{:S(2)}, u32[]{:S(2)}) collective-permute-start(bf16[224,1152]{1,0:T(8,128)(2,1)S(1)} %pad_maximum_fusion.2.refs_0_), channel_id=1, source_target_pairs={{0,32},{32,64},{64,96},{96,0},{1,33},{33,65},{65,97},{97,1},{2,34}... | collective-permute-start | bytes 1548296 | tf_op jit(solution)/shard_map/dense_weights/ppermute | solution.py:19
  41.9 19.3 %collective-permute-start.7 = (bf16[72,3584]{1,0:T(8,128)(2,1)S(1)}, bf16[72,3584]{1,0:T(8,128)(2,1)}, u32[]{:S(2)}, u32[]{:S(2)}) collective-permute-start(bf16[72,3584]{1,0:T(8,128)(2,1)S(1)} %get-tuple-element.37.refs_0_), channel_id=1, source_target_pairs={{0,32},{32,64},{64,96},{96,0},{1,33},{33,65},{65,97},{97,1},{2,34}... | collective-permute-start | bytes 1548296 | tf_op jit(solution)/shard_map/rows_y/ppermute | solution.py:19
  47.2 17.3 %collective-permute-start.9 = (bf16[72,3584]{1,0:T(8,128)(2,1)}, bf16[72,3584]{1,0:T(8,128)(2,1)}, u32[]{:S(2)}, u32[]{:S(2)}) collective-permute-start(bf16[72,3584]{1,0:T(8,128)(2,1)} %get-tuple-element.38.refs_1_), channel_id=1, source_target_pairs={{0,96},{32,0},{64,32},{96,64},{1,97},{33,1},{65,33},{97,65},{2,98}... | collective-permute-start | bytes 1548296 | tf_op jit(solution)/shard_map/rows_y/ppermute | solution.py:19
  49.2 18.0 %all-to-all-start.1 = ((bf16[8,4,16,896]{3,2,1,0:T(8,128)(2,1)}), bf16[8,4,16,896]{3,2,1,0:T(8,128)(2,1)}, u32[]{:S(2)}, u32[]{:S(2)}) async-start(bf16[8,4,16,896]{3,2,1,0:T(8,128)(2,1)} %get-tuple-element.36), calls=%async_computation.1 | async-start | bytes 1835008 | tf_op jit(solution)/shard_map/dense_tokens/all_to_all | solution.py:23
  54.4 20.4 %collective-permute-start.11 = (bf16[72,3584]{1,0:T(8,128)(2,1)S(1)}, bf16[72,3584]{1,0:T(8,128)(2,1)}, u32[]{:S(2)}, u32[]{:S(2)}) collective-permute-start(bf16[72,3584]{1,0:T(8,128)(2,1)S(1)} %get-tuple-element.37.refs_0_), channel_id=1, source_target_pairs={{0,96},{32,0},{64,32},{96,64},{1,97},{33,1},{65,33},{97,65},{2,98}... | collective-permute-start | bytes 1548296 | tf_op jit(solution)/shard_map/rows_y/ppermute | solution.py:19
  56.3 18.5 %collective-permute-start.12 = (bf16[72,3584]{1,0:T(8,128)(2,1)}, bf16[72,3584]{1,0:T(8,128)(2,1)}, u32[]{:S(2)}, u32[]{:S(2)}) collective-permute-start(bf16[72,3584]{1,0:T(8,128)(2,1)} %get-tuple-element.38.refs_1_), channel_id=1, source_target_pairs={{0,32},{32,64},{64,96},{96,0},{1,33},{33,65},{65,97},{97,1},{2,34}... | collective-permute-start | bytes 1548296 | tf_op jit(solution)/shard_map/rows_y/ppermute | solution.py:19
  61.2 22.1 %collective-permute-start.8 = (bf16[72,3584]{1,0:T(8,128)(2,1)}, bf16[72,3584]{1,0:T(8,128)(2,1)}, u32[]{:S(2)}, u32[]{:S(2)}) collective-permute-start(bf16[72,3584]{1,0:T(8,128)(2,1)} %collective-permute-done.7.refs_3_), channel_id=1, source_target_pairs={{0,32},{32,64},{64,96},{96,0},{1,33},{33,65},{65,97},{97,1},{2,34}... | collective-permute-start | bytes 1548296 | tf_op jit(solution)/shard_map/rows_y/ppermute | solution.py:19
  64.6 20.7 %collective-permute-start.10 = (bf16[72,3584]{1,0:T(8,128)(2,1)}, bf16[72,3584]{1,0:T(8,128)(2,1)}, u32[]{:S(2)}, u32[]{:S(2)}) collective-permute-start(bf16[72,3584]{1,0:T(8,128)(2,1)} %collective-permute-done.9.refs_2_), channel_id=1, source_target_pairs={{0,96},{32,0},{64,32},{96,64},{1,97},{33,1},{65,33},{97,65},{2,98}... | collective-permute-start | bytes 1548296 | tf_op jit(solution)/shard_map/rows_y/ppermute | solution.py:19
  70.3 34.5 %all-to-all-start.2 = ((bf16[4,128,768]{2,1,0:T(8,128)(2,1)}), bf16[4,128,768]{2,1,0:T(8,128)(2,1)}, u32[]{:S(2)}, u32[]{:S(2)}) async-start(bf16[4,128,768]{2,1,0:T(8,128)(2,1)} %dense_tokens.1), calls=%async_computation.2 | async-start | bytes 1572864 | tf_op jit(solution)/shard_map/dense_hidden/all_to_all | solution.py:23
  93.0 18.5 %collective-permute-start.13 = (bf16[72,3584]{1,0:T(8,128)(2,1)}, bf16[72,3584]{1,0:T(8,128)(2,1)}, u32[]{:S(2)}, u32[]{:S(2)}) collective-permute-start(bf16[72,3584]{1,0:T(8,128)(2,1)} %get-tuple-element.40), channel_id=1, source_target_pairs={{0,32},{32,64},{64,96},{96,0},{1,33},{33,65},{65,97},{97,1},{2,34}... | collective-permute-start | bytes 1548296 | tf_op jit(solution)/shard_map/partials_y/ppermute | solution.py:19
  96.4 15.2 %collective-permute-start.14 = (bf16[72,3584]{1,0:T(8,128)(2,1)}, bf16[72,3584]{1,0:T(8,128)(2,1)}, u32[]{:S(2)}, u32[]{:S(2)}) collective-permute-start(bf16[72,3584]{1,0:T(8,128)(2,1)} %get-tuple-element.41), channel_id=1, source_target_pairs={{0,96},{32,0},{64,32},{96,64},{1,97},{33,1},{65,33},{97,65},{2,98}... | collective-permute-start | bytes 1548296 | tf_op jit(solution)/shard_map/partials_y/ppermute | solution.py:19
  98.3 29.3 %collective-permute-start.16 = (bf16[72,3584]{1,0:T(8,128)(2,1)}, bf16[72,3584]{1,0:T(8,128)(2,1)}, u32[]{:S(2)}, u32[]{:S(2)}) collective-permute-start(bf16[72,3584]{1,0:T(8,128)(2,1)} %get-tuple-element.51), channel_id=1, source_target_pairs={{0,96},{32,0},{64,32},{96,64},{1,97},{33,1},{65,33},{97,65},{2,98}... | collective-permute-start | bytes 1548296 | tf_op jit(solution)/shard_map/partials_y/ppermute | solution.py:19
  100.2 27.4 %collective-permute-start.17 = (bf16[72,3584]{1,0:T(8,128)(2,1)}, bf16[72,3584]{1,0:T(8,128)(2,1)}, u32[]{:S(2)}, u32[]{:S(2)}) collective-permute-start(bf16[72,3584]{1,0:T(8,128)(2,1)} %get-tuple-element.52), channel_id=1, source_target_pairs={{0,32},{32,64},{64,96},{96,0},{1,33},{33,65},{65,97},{97,1},{2,34}... | collective-permute-start | bytes 1548296 | tf_op jit(solution)/shard_map/partials_y/ppermute | solution.py:19
  107.0 17.8 %all-to-all-start.3 = ((bf16[4,128,384]{2,1,0:T(8,128)(2,1)}), bf16[4,128,384]{2,1,0:T(8,128)(2,1)S(1)}, u32[]{:S(2)}, u32[]{:S(2)}) async-start(bf16[4,128,384]{2,1,0:T(8,128)(2,1)} %broadcast_in_dim.46), calls=%async_computation.3 | async-start | bytes 786432 | tf_op jit(solution)/shard_map/dense_out/all_to_all | solution.py:23
  114.5 13.1 %collective-permute-start.15 = (bf16[72,3584]{1,0:T(8,128)(2,1)}, bf16[72,3584]{1,0:T(8,128)(2,1)}, u32[]{:S(2)}, u32[]{:S(2)}) collective-permute-start(bf16[72,3584]{1,0:T(8,128)(2,1)} %get-tuple-element.45), channel_id=1, source_target_pairs={{0,32},{32,64},{64,96},{96,0},{1,33},{33,65},{65,97},{97,1},{2,34}... | collective-permute-start | bytes 1548296 | tf_op jit(solution)/shard_map/partials_y/ppermute | solution.py:19
  117.8 14.9 %collective-permute-start.18 = (bf16[72,3584]{1,0:T(8,128)(2,1)}, bf16[72,3584]{1,0:T(8,128)(2,1)}, u32[]{:S(2)}, u32[]{:S(2)}) collective-permute-start(bf16[72,3584]{1,0:T(8,128)(2,1)} %get-tuple-element.46), channel_id=1, source_target_pairs={{0,96},{32,0},{64,32},{96,64},{1,97},{33,1},{65,33},{97,65},{2,98}... | collective-permute-start | bytes 1548296 | tf_op jit(solution)/shard_map/partials_y/ppermute | solution.py:19
  136.1 20.1 %copy-start.2 = (f32[36,3584]{1,0:T(8,128)S(1)}, f32[36,3584]{1,0:T(8,128)}, u32[]{:S(2)}) copy-start(f32[36,3584]{1,0:T(8,128)} %get-tuple-element.53) | copy-start | bytes 1548292
  136.1 20.0 %collective-permute-start.19 = (bf16[36,3584]{1,0:T(8,128)(2,1)S(1)}, bf16[36,3584]{1,0:T(8,128)(2,1)}, u32[]{:S(2)}, u32[]{:S(2)}) collective-permute-start(bf16[36,3584]{1,0:T(8,128)(2,1)S(1)} %get-tuple-element.54), channel_id=1, source_target_pairs={{0,16},{8,24},{16,0},{24,8},{1,17},{9,25},{17,1},{25,9},{2,18},{10... | collective-permute-start | bytes 774152 | tf_op jit(solution)/shard_map/partials_z/ppermute | solution.py:19
  138.4 17.7 %collective-permute-start.20 = (bf16[36,3584]{1,0:T(8,128)(2,1)S(1)}, bf16[36,3584]{1,0:T(8,128)(2,1)}, u32[]{:S(2)}, u32[]{:S(2)}) collective-permute-start(bf16[36,3584]{1,0:T(8,128)(2,1)S(1)} %get-tuple-element.55), channel_id=1, source_target_pairs={{0,8},{8,16},{16,24},{24,0},{1,9},{9,17},{17,25},{25,1},{2,10},{10... | collective-permute-start | bytes 774152 | tf_op jit(solution)/shard_map/partials_z/ppermute | solution.py:19
  142.5 13.8 %collective-permute-start.21 = (bf16[36,3584]{1,0:T(8,128)(2,1)S(1)}, bf16[36,3584]{1,0:T(8,128)(2,1)}, u32[]{:S(2)}, u32[]{:S(2)}) collective-permute-start(bf16[36,3584]{1,0:T(8,128)(2,1)S(1)} %get-tuple-element.56), channel_id=1, source_target_pairs={{0,24},{8,0},{16,8},{24,16},{1,25},{9,1},{17,9},{25,17},{2,26},{10... | collective-permute-start | bytes 774152 | tf_op jit(solution)/shard_map/partials_z/ppermute | solution.py:19
  146.7 21.0 %all-to-all-start.4 = ((bf16[8,256,224]{1,2,0:T(8,128)(2,1)}), bf16[8,256,224]{1,2,0:T(8,128)(2,1)S(1)}, u32[]{:S(2)}, u32[]{:S(2)}) async-start(bf16[8,256,224]{1,2,0:T(8,128)(2,1)} %copy.72), calls=%async_computation.4 | async-start | bytes 1835008 | tf_op jit(solution)/shard_map/dense_out/all_to_all | solution.py:23
  167.7 15.4 %all-to-all-start.5 = ((bf16[8,36,448]{2,1,0:T(8,128)(2,1)}), bf16[8,36,448]{2,1,0:T(8,128)(2,1)S(1)}, u32[]{:S(2)}, u32[]{:S(2)}) async-start(bf16[8,36,448]{2,1,0:T(8,128)(2,1)} %bitcast.44), calls=%async_computation.5 | async-start | bytes 655360 | tf_op jit(solution)/shard_map/combine/all_to_all | solution.py:23
  173.0 18.2 %copy-start.6 = (bf16[1,128,448]{1,2,0:T(8,128)(2,1)S(1)}, bf16[1,128,448]{1,2,0:T(8,128)(2,1)}, u32[]{:S(2)}) copy-start(bf16[1,128,448]{1,2,0:T(8,128)(2,1)} %param.11) | copy-start | bytes 344068
  173.3 10.0 %collective-permute-start.5 = (bf16[64,224]{1,0:T(8,128)(2,1)S(1)}, bf16[64,224]{1,0:T(8,128)(2,1)S(1)}, u32[]{:S(2)}, u32[]{:S(2)}) collective-permute-start(bf16[64,224]{1,0:T(8,128)(2,1)S(1)} %get-tuple-element.62), channel_id=1, source_target_pairs={{0,24},{8,0},{16,8},{24,16},{1,25},{9,1},{17,9},{25,17},{2,26},{10... | collective-permute-start | bytes 86024 | tf_op jit(solution)/shard_map/dense_out/ppermute | solution.py:19
  176.2 7.1 %collective-permute-start.4 = (bf16[64,224]{1,0:T(8,128)(2,1)S(1)}, bf16[64,224]{1,0:T(8,128)(2,1)S(1)}, u32[]{:S(2)}, u32[]{:S(2)}) collective-permute-start(bf16[64,224]{1,0:T(8,128)(2,1)S(1)} %get-tuple-element.63), channel_id=1, source_target_pairs={{0,16},{8,24},{16,0},{24,8},{1,17},{9,25},{17,1},{25,9},{2,18},{10... | collective-permute-start | bytes 86024 | tf_op jit(solution)/shard_map/dense_out/ppermute | solution.py:19
  180.9 4.7 %collective-permute-start.3 = (bf16[64,224]{1,0:T(8,128)(2,1)S(1)}, bf16[64,224]{1,0:T(8,128)(2,1)S(1)}, u32[]{:S(2)}, u32[]{:S(2)}) collective-permute-start(bf16[64,224]{1,0:T(8,128)(2,1)S(1)} %get-tuple-element.64), channel_id=1, source_target_pairs={{0,8},{8,16},{16,24},{24,0},{1,9},{9,17},{17,25},{25,1},{2,10},{10... | collective-permute-start | bytes 86024 | tf_op jit(solution)/shard_map/dense_out/ppermute | solution.py:19
  186.2 4.9 %collective-permute-start.6 = (bf16[2,64,224]{2,1,0:T(8,128)(2,1)S(1)}, bf16[2,64,224]{2,1,0:T(8,128)(2,1)S(1)}, u32[]{:S(2)}, u32[]{:S(2)}) collective-permute-start(bf16[2,64,224]{2,1,0:T(8,128)(2,1)S(1)} %constant_dynamic-slice_fusion), channel_id=1, source_target_pairs={{0,1},{1,0},{2,3},{3,2},{4,5},{5,4},{6,7},{7,6},{8,9},{9,8},{10,11... | collective-permute-start | bytes 172040 | tf_op jit(solution)/shard_map/dense_out/ppermute | solution.py:19
  191.6 21.5 %collective-permute-start.22 = (bf16[128,448]{0,1:T(8,128)(2,1)S(1)}, bf16[128,448]{0,1:T(8,128)(2,1)S(1)}, u32[]{:S(2)}, u32[]{:S(2)}) collective-permute-start(bf16[128,448]{0,1:T(8,128)(2,1)S(1)} %fusion.1), channel_id=1, source_target_pairs={{0,128},{128,256},{256,384},{384,0},{1,129},{129,257},{257,385},{3... | collective-permute-start | bytes 344072 | tf_op jit(solution)/shard_map/next_section/ppermute | solution.py:19
  (8 other events, 30.8 us)

commit v12 on v11

--- a/solution.py
+++ b/solution.py
@@ -124,15 +124,16 @@
 
 def dense_out_kernel(columns, place, act, *refs):
     weights, out = refs[:4], refs[4]
+    size = out.shape[2] // 4
+    starts = [(2 * j + side) * size for side in range(2) for j in range(4)]
+    tokens = jnp.concatenate([act[start : start + size] for start in starts], axis=0)
     contract = (((1,), (1,)), ((), ()))
     for k in range(4):
         part = lax.dot_general(
-            act[...], weights[k][:, columns:], contract, preferred_element_type=F32
+            weights[k][:, columns:], tokens, contract, preferred_element_type=F32
         ).astype(BF16)
-        half = part.shape[0] // 8
         for side in range(2):
-            pieces = [part[(2 * j + side) * half : (2 * j + side + 1) * half] for j in range(4)]
-            out[2 * place[k] + side] = jnp.concatenate(pieces, axis=0)
+            out[2 * place[k] + side] = part[:, side * 4 * size : (side + 1) * 4 * size]
 
 
 def body(
@@ -222,7 +223,7 @@
     in_smem, in_vmem = (pl.BlockSpec(memory_space=space) for space in (pltpu.SMEM, pltpu.VMEM))
     with jax.named_scope("experts"):
         relay_next, relay_prev, early_next, early_prev, next_part, prev_part = local_call(
-            rows_kernel, [half_bf16] * 4 + [half_f32] * 2, LONG
+            rows_kernel, [half_bf16] * 6, LONG
         )(gate_up, down, far_low, far_high, next_high, prev_low, next_low, prev_high)
 
     with jax.named_scope("partials_y"):
@@ -237,15 +238,15 @@
         every_act = exchanged(line_act, "z").reshape(4 * tok_rows, hidden)
         by_block = local_call(
             functools.partial(dense_out_kernel, 2 * hidden),
-            jax.ShapeDtypeStruct((n_expert, 4 * half_tokens, step), BF16),
+            jax.ShapeDtypeStruct((n_expert, step, 4 * half_tokens), BF16),
             in_specs=[in_smem] + [in_vmem] * 5,
         )(place_y, every_act, *slabs)
 
     with jax.named_scope("partials_y"):
         early_next, early_prev = shifted(early_next, "y", 1), shifted(early_prev, "y", -1)
         relay_next, relay_prev = after((relay_next, relay_prev), line_act)
-        late_next = (next_part + relay_next.astype(F32)).astype(BF16)
-        late_prev = (prev_part + relay_prev.astype(F32)).astype(BF16)
+        late_next = (next_part.astype(F32) + relay_next.astype(F32)).astype(BF16)
+        late_prev = (prev_part.astype(F32) + relay_prev.astype(F32)).astype(BF16)
         late_next, late_prev = after((late_next, late_prev))
         own_low, own_high = local_call(rows_kernel, [half_f32] * 2)(
             after(gate_up, late_next, late_prev), down, low, high
@@ -265,7 +266,7 @@
 
     with jax.named_scope("dense_out"):
         block_sum = jnp.sum(exchanged(by_block, EXPERT_AXES).astype(F32), axis=0).astype(BF16)
-        block_sum = block_sum.reshape(4, half_tokens, step)
+        block_sum = block_sum.T.reshape(4, half_tokens, step)
         blocks = []
         for by in range(4):
             there = (lax.axis_index("z") + by) % 4

time: 215 us -> 216 us (level)
  the two profiles are of different devices: /device:TPU:123 before, /device:TPU:26 now
where the time goes in v12:
time: 216 us; the launch traced here: 215 us
  starting transfers between devices  111 us (51%)
  waiting for transfers between devices  54.2 us (25%)
  Pallas kernels  24.4 us (11%)
  other arithmetic  14.4 us (7%)
  local copies, waits for them, and re-layouts  9.46 us (4%)
    ppermute x23, starting transfers between devices, shifted(): return lax.ppermute(x, axis, [(i, (i + by) % peers) for i in range(peers)])  81 us
    ppermute x23, waiting for transfers between devices, shifted(): return lax.ppermute(x, axis, [(i, (i + by) % peers) for i in range(peers)])  51.8 us
    all_to_all x6, starting transfers between devices, exchanged(): return lax.all_to_all(x, axes, split_axis=0, concat_axis=0, tiled=True)  30 us
    pallas_call x1, Pallas kernels, body(): local_call(rows_kernel, [half_bf16] * 6, LONG)  7.35 us
    unnamed x25, local copies, waits for them, and re-layouts  5.07 us
    concatenate x1, other arithmetic, body(): jnp.concatenate([expert_gate[0, 0], blank, expert_up[0, 0], blank], axis=1)  5.04 us
    pallas_call x1, Pallas kernels, body(): local_call(rows_kernel, [half_f32] * 2)  4.87 us
  transfers between devices with their start and end apart: 29, of which 14 were waited for; matrix products, arithmetic and copies ran while one was open for 8% of the time, Pallas kernels for 8%

profile of v12, /device:TPU:26, one launch (start us, length us, event | category | flops | bytes accessed | tf_op | source)
XLA Modules:
  0.0 214.9 jit_solution(7425570860381268041)
XLA Ops:
  5.4 5.9 %all-to-all-start = ((bf16[4,40,3584]{2,1,0:T(8,128)(2,1)}), bf16[4,40,3584]{2,1,0:T(8,128)(2,1)}, u32[]{:S(2)}, u32[]{:S(2)}) async-start(bf16[4,40,3584]{2,1,0:T(8,128)(2,1)} %pad_maximum_fusion.1), calls=%async_computation | async-start | bytes 2293760 | tf_op jit(solution)/shard_map/rows_z/all_to_all | solution.py:23
  14.0 2.8 %collective-permute-start.1 = (bf16[224,1152]{1,0:T(8,128)(2,1)S(1)}, bf16[224,1152]{1,0:T(8,128)(2,1)S(1)}, u32[]{:S(2)}, u32[]{:S(2)}) collective-permute-start(bf16[224,1152]{1,0:T(8,128)(2,1)S(1)} %pad_maximum_fusion.2.refs_0_), channel_id=1, source_target_pairs={{0,64},{32,96},{64,0},{96,32},{1,65},{33,97},{65,1},{97,33},{2,66}... | collective-permute-start | bytes 1548296 | tf_op jit(solution)/shard_map/dense_weights/ppermute | solution.py:19
  16.9 4.1 %collective-permute-start = (bf16[224,1152]{1,0:T(8,128)(2,1)S(1)}, bf16[224,1152]{1,0:T(8,128)(2,1)S(1)}, u32[]{:S(2)}, u32[]{:S(2)}) collective-permute-start(bf16[224,1152]{1,0:T(8,128)(2,1)S(1)} %pad_maximum_fusion.2.refs_0_), channel_id=1, source_target_pairs={{0,32},{32,64},{64,96},{96,0},{1,33},{33,65},{65,97},{97,1},{2,34}... | collective-permute-start | bytes 1548296 | tf_op jit(solution)/shard_map/dense_weights/ppermute | solution.py:19
  25.6 5.0 %pad_maximum_fusion.gate_up = bf16[3584,512]{1,0:T(8,128)(2,1)} fusion(bf16[3584,104]{1,0:T(8,128)(2,1)S(1)} %broadcast_in_dim.26, bf16[3584,152]{1,0:T(8,128)(2,1)} %bitcast.48, bf16[3584,152]{1,0:T(8,128)(2,1)} %bitcast.47), kind=kLoop, calls=%fused_computation.3 | loop fusion | flops 14680064 | bytes 6594560 | tf_op jit(solution)/shard_map/concatenate | solution.py:191
  30.6 8.2 %collective-permute-done.2.refs_3_ = bf16[224,1152]{1,0:T(8,128)(2,1)} collective-permute-done((bf16[224,1152]{1,0:T(8,128)(2,1)S(1)}, bf16[224,1152]{1,0:T(8,128)(2,1)}, u32[]{:S(2)}, u32[]{:S(2)}) %collective-permute-start.2) | collective-permute-done | bytes 516128 | tf_op jit(solution)/shard_map/dense_weights/ppermute | solution.py:19
  43.9 4.5 %collective-permute-start.7 = (bf16[72,3584]{1,0:T(8,128)(2,1)S(1)}, bf16[72,3584]{1,0:T(8,128)(2,1)}, u32[]{:S(2)}, u32[]{:S(2)}) collective-permute-start(bf16[72,3584]{1,0:T(8,128)(2,1)S(1)} %get-tuple-element.37.refs_0_), channel_id=1, source_target_pairs={{0,32},{32,64},{64,96},{96,0},{1,33},{33,65},{65,97},{97,1},{2,34}... | collective-permute-start | bytes 1548296 | tf_op jit(solution)/shard_map/rows_y/ppermute | solution.py:19
  50.4 4.8 %all-to-all-start.1 = ((bf16[8,4,16,896]{3,2,1,0:T(8,128)(2,1)}), bf16[8,4,16,896]{3,2,1,0:T(8,128)(2,1)}, u32[]{:S(2)}, u32[]{:S(2)}) async-start(bf16[8,4,16,896]{3,2,1,0:T(8,128)(2,1)} %get-tuple-element.36), calls=%async_computation.1 | async-start | bytes 1835008 | tf_op jit(solution)/shard_map/dense_tokens/all_to_all | solution.py:23
  57.1 5.1 %collective-permute-start.12 = (bf16[72,3584]{1,0:T(8,128)(2,1)}, bf16[72,3584]{1,0:T(8,128)(2,1)}, u32[]{:S(2)}, u32[]{:S(2)}) collective-permute-start(bf16[72,3584]{1,0:T(8,128)(2,1)} %get-tuple-element.38.refs_1_), channel_id=1, source_target_pairs={{0,32},{32,64},{64,96},{96,0},{1,33},{33,65},{65,97},{97,1},{2,34}... | collective-permute-start | bytes 1548296 | tf_op jit(solution)/shard_map/rows_y/ppermute | solution.py:19
  62.3 3.9 %collective-permute-start.8 = (bf16[72,3584]{1,0:T(8,128)(2,1)}, bf16[72,3584]{1,0:T(8,128)(2,1)}, u32[]{:S(2)}, u32[]{:S(2)}) collective-permute-start(bf16[72,3584]{1,0:T(8,128)(2,1)} %collective-permute-done.7.refs_3_), channel_id=1, source_target_pairs={{0,32},{32,64},{64,96},{96,0},{1,33},{33,65},{65,97},{97,1},{2,34}... | collective-permute-start | bytes 1548296 | tf_op jit(solution)/shard_map/rows_y/ppermute | solution.py:19
  68.4 3.2 %dense_tokens.1 = bf16[4,128,768]{2,1,0:T(8,128)(2,1)} custom-call(bf16[8,4,16,896]{3,2,1,0:T(8,128)(2,1)} %all-to-all-done.1.tokens, bf16[224,1152]{1,0:T(8,128)(2,1)S(1)} %pad_maximum_fusion.2.refs_0_, bf16[224,1152]{1,0:T(8,128)(2,1)S(1)} %collective-permute-done.refs_1_, bf16[224,1152]{1,0:T(8,128)(2,1)S(1)} %collective-permute-done.1.refs_2_, ...), custom_call_target="tpu_custom_call" | custom-call | flops 2147483648 | bytes 4194304 | tf_op jit(solution)/shard_map/dense_tokens/pallas_call | solution.py:217
  71.7 4.8 %all-to-all-start.2 = ((bf16[4,128,768]{2,1,0:T(8,128)(2,1)}), bf16[4,128,768]{2,1,0:T(8,128)(2,1)}, u32[]{:S(2)}, u32[]{:S(2)}) async-start(bf16[4,128,768]{2,1,0:T(8,128)(2,1)} %dense_tokens.1), calls=%async_computation.2 | async-start | bytes 1572864 | tf_op jit(solution)/shard_map/dense_hidden/all_to_all | solution.py:23
  77.6 7.4 %collective-permute-done.8.refs_0_ = bf16[72,3584]{1,0:T(8,128)(2,1)} collective-permute-done((bf16[72,3584]{1,0:T(8,128)(2,1)}, bf16[72,3584]{1,0:T(8,128)(2,1)}, u32[]{:S(2)}, u32[]{:S(2)}) %collective-permute-start.8) | collective-permute-done | bytes 516128 | tf_op jit(solution)/shard_map/rows_y/ppermute | solution.py:19
  87.4 7.4 %experts.1 = (bf16[72,3584]{1,0:T(8,128)(2,1)}, bf16[72,3584]{1,0:T(8,128)(2,1)}, bf16[72,3584]{1,0:T(8,128)(2,1)}, bf16[72,3584]{1,0:T(8,128)(2,1)}, bf16[72,35...) custom-call(bf16[3584,512]{1,0:T(8,128)(2,1)} %pad_maximum_fusion.gate_up, bf16[152,3584]{1,0:T(8,128)(2,1)} %bitcast.63, ...), custom_call_target="tpu_custom_call" | custom-call | flops 107374182400 | bytes 4194304 | tf_op jit(solution)/shard_map/experts/pallas_call | solution.py:225
  94.7 3.2 %collective-permute-start.13 = (bf16[72,3584]{1,0:T(8,128)(2,1)}, bf16[72,3584]{1,0:T(8,128)(2,1)}, u32[]{:S(2)}, u32[]{:S(2)}) collective-permute-start(bf16[72,3584]{1,0:T(8,128)(2,1)} %get-tuple-element.40), channel_id=1, source_target_pairs={{0,32},{32,64},{64,96},{96,0},{1,33},{33,65},{65,97},{97,1},{2,34}... | collective-permute-start | bytes 1548296 | tf_op jit(solution)/shard_map/partials_y/ppermute | solution.py:19
  102.5 5.1 %collective-permute-start.17 = (bf16[72,3584]{1,0:T(8,128)(2,1)}, bf16[72,3584]{1,0:T(8,128)(2,1)}, u32[]{:S(2)}, u32[]{:S(2)}) collective-permute-start(bf16[72,3584]{1,0:T(8,128)(2,1)} %get-tuple-element.52), channel_id=1, source_target_pairs={{0,32},{32,64},{64,96},{96,0},{1,33},{33,65},{65,97},{97,1},{2,34}... | collective-permute-start | bytes 1548296 | tf_op jit(solution)/shard_map/partials_y/ppermute | solution.py:19
  109.8 4.8 %all-to-all-start.3 = ((bf16[4,128,384]{2,1,0:T(8,128)(2,1)}), bf16[4,128,384]{2,1,0:T(8,128)(2,1)S(1)}, u32[]{:S(2)}, u32[]{:S(2)}) async-start(bf16[4,128,384]{2,1,0:T(8,128)(2,1)} %broadcast_in_dim.46), calls=%async_computation.3 | async-start | bytes 786432 | tf_op jit(solution)/shard_map/dense_out/all_to_all | solution.py:23
  120.7 3.9 %collective-permute-start.18 = (bf16[72,3584]{1,0:T(8,128)(2,1)}, bf16[72,3584]{1,0:T(8,128)(2,1)}, u32[]{:S(2)}, u32[]{:S(2)}) collective-permute-start(bf16[72,3584]{1,0:T(8,128)(2,1)} %get-tuple-element.46), channel_id=1, source_target_pairs={{0,96},{32,0},{64,32},{96,64},{1,97},{33,1},{65,33},{97,65},{2,98}... | collective-permute-start | bytes 1548296 | tf_op jit(solution)/shard_map/partials_y/ppermute | solution.py:19
  124.7 4.9 %partials_y.1 = (f32[72,3584]{1,0:T(8,128)}, f32[72,3584]{1,0:T(8,128)}) custom-call(bf16[3584,512]{1,0:T(8,128)(2,1)} %pad_maximum_fusion.gate_up, bf16[152,3584]{1,0:T(8,128)(2,1)} %bitcast.64, bf16[72,3584]{1,0:T(8,128)(2,1)S(1)} %get-tuple-element.37.refs_0_, bf16[72,3584]{1,0:T(8,128)(2,1)} %get-tuple-element.38.refs_1_), custom_call_target="tpu_custom_call" | custom-call | flops 2147483648 | bytes 4194304 | tf_op jit(solution)/shard_map/partials_y/pallas_call | solution.py:251
  132.3 3.9 %collective-permute-done.18.refs_3_ = bf16[72,3584]{1,0:T(8,128)(2,1)} collective-permute-done((bf16[72,3584]{1,0:T(8,128)(2,1)}, bf16[72,3584]{1,0:T(8,128)(2,1)}, u32[]{:S(2)}, u32[]{:S(2)}) %collective-permute-start.18) | collective-permute-done | bytes 516128 | tf_op jit(solution)/shard_map/partials_y/ppermute | solution.py:19
  136.1 3.5 %partials_z.1 = (f32[36,3584]{1,0:T(8,128)}, bf16[36,3584]{1,0:T(8,128)(2,1)S(1)}, bf16[36,3584]{1,0:T(8,128)(2,1)S(1)}, bf16[36,3584]{1,0:T(8,128)(2,1)S(1)}) custom-call(s32[4]{0:T(128)S(1)} %and_select_fusion.place, f32[72,3584]{1,0:T(8,128)} %get-tuple-element.49.low, f32[72,3584]{1,0:T(8,128)} %get-tuple-element.50.high, ...), custom_call_target="tpu_custom_call" | custom-call | flops 2147483648 | bytes 4194304 | tf_op jit(solution)/shard_map/partials_z/pallas_call | solution.py:258
  139.7 4.7 %collective-permute-start.19 = (bf16[36,3584]{1,0:T(8,128)(2,1)S(1)}, bf16[36,3584]{1,0:T(8,128)(2,1)}, u32[]{:S(2)}, u32[]{:S(2)}) collective-permute-start(bf16[36,3584]{1,0:T(8,128)(2,1)S(1)} %get-tuple-element.54), channel_id=1, source_target_pairs={{0,16},{8,24},{16,0},{24,8},{1,17},{9,25},{17,1},{25,9},{2,18},{10... | collective-permute-start | bytes 774152 | tf_op jit(solution)/shard_map/partials_z/ppermute | solution.py:19
  144.3 3.4 %collective-permute-start.20 = (bf16[36,3584]{1,0:T(8,128)(2,1)S(1)}, bf16[36,3584]{1,0:T(8,128)(2,1)}, u32[]{:S(2)}, u32[]{:S(2)}) collective-permute-start(bf16[36,3584]{1,0:T(8,128)(2,1)S(1)} %get-tuple-element.55), channel_id=1, source_target_pairs={{0,8},{8,16},{16,24},{24,0},{1,9},{9,17},{17,25},{25,1},{2,10},{10... | collective-permute-start | bytes 774152 | tf_op jit(solution)/shard_map/partials_z/ppermute | solution.py:19
  147.7 4.3 %collective-permute-start.21 = (bf16[36,3584]{1,0:T(8,128)(2,1)S(1)}, bf16[36,3584]{1,0:T(8,128)(2,1)}, u32[]{:S(2)}, u32[]{:S(2)}) collective-permute-start(bf16[36,3584]{1,0:T(8,128)(2,1)S(1)} %get-tuple-element.56), channel_id=1, source_target_pairs={{0,24},{8,0},{16,8},{24,16},{1,25},{9,1},{17,9},{25,17},{2,26},{10... | collective-permute-start | bytes 774152 | tf_op jit(solution)/shard_map/partials_z/ppermute | solution.py:19
  152.1 4.8 %all-to-all-start.4 = ((bf16[8,224,256]{2,1,0:T(8,128)(2,1)}), bf16[8,224,256]{2,1,0:T(8,128)(2,1)S(1)}, u32[]{:S(2)}, u32[]{:S(2)}) async-start(bf16[8,224,256]{2,1,0:T(8,128)(2,1)} %dense_out.1), calls=%async_computation.4 | async-start | bytes 1835008 | tf_op jit(solution)/shard_map/dense_out/all_to_all | solution.py:23
  156.9 5.5 %collective-permute-done.19 = bf16[36,3584]{1,0:T(8,128)(2,1)} collective-permute-done((bf16[36,3584]{1,0:T(8,128)(2,1)S(1)}, bf16[36,3584]{1,0:T(8,128)(2,1)}, u32[]{:S(2)}, u32[]{:S(2)}) %collective-permute-start.19) | collective-permute-done | bytes 258080 | tf_op jit(solution)/shard_map/partials_z/ppermute | solution.py:19
  162.4 2.8 %collective-permute-done.21 = bf16[36,3584]{1,0:T(8,128)(2,1)} collective-permute-done((bf16[36,3584]{1,0:T(8,128)(2,1)S(1)}, bf16[36,3584]{1,0:T(8,128)(2,1)}, u32[]{:S(2)}, u32[]{:S(2)}) %collective-permute-start.21) | collective-permute-done | bytes 258080 | tf_op jit(solution)/shard_map/partials_z/ppermute | solution.py:19
  170.0 4.8 %all-to-all-start.5 = ((bf16[8,36,448]{2,1,0:T(8,128)(2,1)}), bf16[8,36,448]{2,1,0:T(8,128)(2,1)S(1)}, u32[]{:S(2)}, u32[]{:S(2)}) async-start(bf16[8,36,448]{2,1,0:T(8,128)(2,1)} %bitcast.45), calls=%async_computation.5 | async-start | bytes 655360 | tf_op jit(solution)/shard_map/combine/all_to_all | solution.py:23
  177.0 4.1 %collective-permute-start.4 = (bf16[64,224]{1,0:T(8,128)(2,1)S(1)}, bf16[64,224]{1,0:T(8,128)(2,1)S(1)}, u32[]{:S(2)}, u32[]{:S(2)}) collective-permute-start(bf16[64,224]{1,0:T(8,128)(2,1)S(1)} %get-tuple-element.63), channel_id=1, source_target_pairs={{0,16},{8,24},{16,0},{24,8},{1,17},{9,25},{17,1},{25,9},{2,18},{10... | collective-permute-start | bytes 86024 | tf_op jit(solution)/shard_map/dense_out/ppermute | solution.py:19
  181.1 3.9 %collective-permute-start.3 = (bf16[64,224]{1,0:T(8,128)(2,1)S(1)}, bf16[64,224]{1,0:T(8,128)(2,1)S(1)}, u32[]{:S(2)}, u32[]{:S(2)}) collective-permute-start(bf16[64,224]{1,0:T(8,128)(2,1)S(1)} %get-tuple-element.64), channel_id=1, source_target_pairs={{0,8},{8,16},{16,24},{24,0},{1,9},{9,17},{17,25},{25,1},{2,10},{10... | collective-permute-start | bytes 86024 | tf_op jit(solution)/shard_map/dense_out/ppermute | solution.py:19
  185.2 3.5 %collective-permute-done.3 = bf16[64,224]{1,0:T(8,128)(2,1)S(1)} collective-permute-done((bf16[64,224]{1,0:T(8,128)(2,1)S(1)}, bf16[64,224]{1,0:T(8,128)(2,1)S(1)}, u32[]{:S(2)}, u32[]{:S(2)}) %collective-permute-start.3) | collective-permute-done | bytes 28704 | tf_op jit(solution)/shard_map/dense_out/ppermute | solution.py:19
  193.0 9.1 %collective-permute-start.22 = (bf16[128,448]{0,1:T(8,128)(2,1)S(1)}, bf16[128,448]{0,1:T(8,128)(2,1)S(1)}, u32[]{:S(2)}, u32[]{:S(2)}) collective-permute-start(bf16[128,448]{0,1:T(8,128)(2,1)S(1)} %fusion.1), channel_id=1, source_target_pairs={{0,128},{128,256},{256,384},{384,0},{1,129},{129,257},{257,385},{3... | collective-permute-start | bytes 344072 | tf_op jit(solution)/shard_map/next_section/ppermute | solution.py:19
  202.1 12.1 %collective-permute-done.22 = bf16[128,448]{0,1:T(8,128)(2,1)S(1)} collective-permute-done((bf16[128,448]{0,1:T(8,128)(2,1)S(1)}, bf16[128,448]{0,1:T(8,128)(2,1)S(1)}, u32[]{:S(2)}, u32[]{:S(2)}) %collective-permute-start.22) | collective-permute-done | bytes 114720 | tf_op jit(solution)/shard_map/next_section/ppermute | solution.py:19
  (105 shorter events, 54.7 us)
Async XLA Ops:
  4.2 16.8 %copy-start.1 = (bf16[1,1,3584,152]{2,3,1,0:T(8,128)(2,1)S(1)}, bf16[1,1,3584,152]{2,3,1,0:T(8,128)(2,1)}, u32[]{:S(2)}) copy-start(bf16[1,1,3584,152]{2,3,1,0:T(8,128)(2,1)} %param.17) | copy-start | bytes 3268612
  5.4 35.9 %all-to-all-start = ((bf16[4,40,3584]{2,1,0:T(8,128)(2,1)}), bf16[4,40,3584]{2,1,0:T(8,128)(2,1)}, u32[]{:S(2)}, u32[]{:S(2)}) async-start(bf16[4,40,3584]{2,1,0:T(8,128)(2,1)} %pad_maximum_fusion.1), calls=%async_computation | async-start | bytes 2293760 | tf_op jit(solution)/shard_map/rows_z/all_to_all | solution.py:23
  11.3 27.5 %collective-permute-start.2 = (bf16[224,1152]{1,0:T(8,128)(2,1)S(1)}, bf16[224,1152]{1,0:T(8,128)(2,1)}, u32[]{:S(2)}, u32[]{:S(2)}) collective-permute-start(bf16[224,1152]{1,0:T(8,128)(2,1)S(1)} %pad_maximum_fusion.2.refs_0_), channel_id=1, source_target_pairs={{0,96},{32,0},{64,32},{96,64},{1,97},{33,1},{65,33},{97,65},{2,98}... | collective-permute-start | bytes 1548296 | tf_op jit(solution)/shard_map/dense_weights/ppermute | solution.py:19
  14.0 24.8 %collective-permute-start.1 = (bf16[224,1152]{1,0:T(8,128)(2,1)S(1)}, bf16[224,1152]{1,0:T(8,128)(2,1)S(1)}, u32[]{:S(2)}, u32[]{:S(2)}) collective-permute-start(bf16[224,1152]{1,0:T(8,128)(2,1)S(1)} %pad_maximum_fusion.2.refs_0_), channel_id=1, source_target_pairs={{0,64},{32,96},{64,0},{96,32},{1,65},{33,97},{65,1},{97,33},{2,66}... | collective-permute-start | bytes 1548296 | tf_op jit(solution)/shard_map/dense_weights/ppermute | solution.py:19
  16.9 24.4 %collective-permute-start = (bf16[224,1152]{1,0:T(8,128)(2,1)S(1)}, bf16[224,1152]{1,0:T(8,128)(2,1)S(1)}, u32[]{:S(2)}, u32[]{:S(2)}) collective-permute-start(bf16[224,1152]{1,0:T(8,128)(2,1)S(1)} %pad_maximum_fusion.2.refs_0_), channel_id=1, source_target_pairs={{0,32},{32,64},{64,96},{96,0},{1,33},{33,65},{65,97},{97,1},{2,34}... | collective-permute-start | bytes 1548296 | tf_op jit(solution)/shard_map/dense_weights/ppermute | solution.py:19
  43.9 18.4 %collective-permute-start.7 = (bf16[72,3584]{1,0:T(8,128)(2,1)S(1)}, bf16[72,3584]{1,0:T(8,128)(2,1)}, u32[]{:S(2)}, u32[]{:S(2)}) collective-permute-start(bf16[72,3584]{1,0:T(8,128)(2,1)S(1)} %get-tuple-element.37.refs_0_), channel_id=1, source_target_pairs={{0,32},{32,64},{64,96},{96,0},{1,33},{33,65},{65,97},{97,1},{2,34}... | collective-permute-start | bytes 1548296 | tf_op jit(solution)/shard_map/rows_y/ppermute | solution.py:19
  48.4 18.1 %collective-permute-start.9 = (bf16[72,3584]{1,0:T(8,128)(2,1)}, bf16[72,3584]{1,0:T(8,128)(2,1)}, u32[]{:S(2)}, u32[]{:S(2)}) collective-permute-start(bf16[72,3584]{1,0:T(8,128)(2,1)} %get-tuple-element.38.refs_1_), channel_id=1, source_target_pairs={{0,96},{32,0},{64,32},{96,64},{1,97},{33,1},{65,33},{97,65},{2,98}... | collective-permute-start | bytes 1548296 | tf_op jit(solution)/shard_map/rows_y/ppermute | solution.py:19
  50.4 18.1 %all-to-all-start.1 = ((bf16[8,4,16,896]{3,2,1,0:T(8,128)(2,1)}), bf16[8,4,16,896]{3,2,1,0:T(8,128)(2,1)}, u32[]{:S(2)}, u32[]{:S(2)}) async-start(bf16[8,4,16,896]{3,2,1,0:T(8,128)(2,1)} %get-tuple-element.36), calls=%async_computation.1 | async-start | bytes 1835008 | tf_op jit(solution)/shard_map/dense_tokens/all_to_all | solution.py:23
  55.2 22.4 %collective-permute-start.11 = (bf16[72,3584]{1,0:T(8,128)(2,1)S(1)}, bf16[72,3584]{1,0:T(8,128)(2,1)}, u32[]{:S(2)}, u32[]{:S(2)}) collective-permute-start(bf16[72,3584]{1,0:T(8,128)(2,1)S(1)} %get-tuple-element.37.refs_0_), channel_id=1, source_target_pairs={{0,96},{32,0},{64,32},{96,64},{1,97},{33,1},{65,33},{97,65},{2,98}... | collective-permute-start | bytes 1548296 | tf_op jit(solution)/shard_map/rows_y/ppermute | solution.py:19
  57.1 20.4 %collective-permute-start.12 = (bf16[72,3584]{1,0:T(8,128)(2,1)}, bf16[72,3584]{1,0:T(8,128)(2,1)}, u32[]{:S(2)}, u32[]{:S(2)}) collective-permute-start(bf16[72,3584]{1,0:T(8,128)(2,1)} %get-tuple-element.38.refs_1_), channel_id=1, source_target_pairs={{0,32},{32,64},{64,96},{96,0},{1,33},{33,65},{65,97},{97,1},{2,34}... | collective-permute-start | bytes 1548296 | tf_op jit(solution)/shard_map/rows_y/ppermute | solution.py:19
  62.3 22.7 %collective-permute-start.8 = (bf16[72,3584]{1,0:T(8,128)(2,1)}, bf16[72,3584]{1,0:T(8,128)(2,1)}, u32[]{:S(2)}, u32[]{:S(2)}) collective-permute-start(bf16[72,3584]{1,0:T(8,128)(2,1)} %collective-permute-done.7.refs_3_), channel_id=1, source_target_pairs={{0,32},{32,64},{64,96},{96,0},{1,33},{33,65},{65,97},{97,1},{2,34}... | collective-permute-start | bytes 1548296 | tf_op jit(solution)/shard_map/rows_y/ppermute | solution.py:19
  66.5 20.9 %collective-permute-start.10 = (bf16[72,3584]{1,0:T(8,128)(2,1)}, bf16[72,3584]{1,0:T(8,128)(2,1)}, u32[]{:S(2)}, u32[]{:S(2)}) collective-permute-start(bf16[72,3584]{1,0:T(8,128)(2,1)} %collective-permute-done.9.refs_2_), channel_id=1, source_target_pairs={{0,96},{32,0},{64,32},{96,64},{1,97},{33,1},{65,33},{97,65},{2,98}... | collective-permute-start | bytes 1548296 | tf_op jit(solution)/shard_map/rows_y/ppermute | solution.py:19
  71.7 36.0 %all-to-all-start.2 = ((bf16[4,128,768]{2,1,0:T(8,128)(2,1)}), bf16[4,128,768]{2,1,0:T(8,128)(2,1)}, u32[]{:S(2)}, u32[]{:S(2)}) async-start(bf16[4,128,768]{2,1,0:T(8,128)(2,1)} %dense_tokens.1), calls=%async_computation.2 | async-start | bytes 1572864 | tf_op jit(solution)/shard_map/dense_hidden/all_to_all | solution.py:23
  94.7 19.9 %collective-permute-start.13 = (bf16[72,3584]{1,0:T(8,128)(2,1)}, bf16[72,3584]{1,0:T(8,128)(2,1)}, u32[]{:S(2)}, u32[]{:S(2)}) collective-permute-start(bf16[72,3584]{1,0:T(8,128)(2,1)} %get-tuple-element.40), channel_id=1, source_target_pairs={{0,32},{32,64},{64,96},{96,0},{1,33},{33,65},{65,97},{97,1},{2,34}... | collective-permute-start | bytes 1548296 | tf_op jit(solution)/shard_map/partials_y/ppermute | solution.py:19
  97.9 18.1 %collective-permute-start.14 = (bf16[72,3584]{1,0:T(8,128)(2,1)}, bf16[72,3584]{1,0:T(8,128)(2,1)}, u32[]{:S(2)}, u32[]{:S(2)}) collective-permute-start(bf16[72,3584]{1,0:T(8,128)(2,1)} %get-tuple-element.41), channel_id=1, source_target_pairs={{0,96},{32,0},{64,32},{96,64},{1,97},{33,1},{65,33},{97,65},{2,98}... | collective-permute-start | bytes 1548296 | tf_op jit(solution)/shard_map/partials_y/ppermute | solution.py:19
  100.6 31.7 %collective-permute-start.16 = (bf16[72,3584]{1,0:T(8,128)(2,1)}, bf16[72,3584]{1,0:T(8,128)(2,1)}, u32[]{:S(2)}, u32[]{:S(2)}) collective-permute-start(bf16[72,3584]{1,0:T(8,128)(2,1)} %get-tuple-element.51), channel_id=1, source_target_pairs={{0,96},{32,0},{64,32},{96,64},{1,97},{33,1},{65,33},{97,65},{2,98}... | collective-permute-start | bytes 1548296 | tf_op jit(solution)/shard_map/partials_y/ppermute | solution.py:19
  102.5 29.8 %collective-permute-start.17 = (bf16[72,3584]{1,0:T(8,128)(2,1)}, bf16[72,3584]{1,0:T(8,128)(2,1)}, u32[]{:S(2)}, u32[]{:S(2)}) collective-permute-start(bf16[72,3584]{1,0:T(8,128)(2,1)} %get-tuple-element.52), channel_id=1, source_target_pairs={{0,32},{32,64},{64,96},{96,0},{1,33},{33,65},{65,97},{97,1},{2,34}... | collective-permute-start | bytes 1548296 | tf_op jit(solution)/shard_map/partials_y/ppermute | solution.py:19
  109.8 19.7 %all-to-all-start.3 = ((bf16[4,128,384]{2,1,0:T(8,128)(2,1)}), bf16[4,128,384]{2,1,0:T(8,128)(2,1)S(1)}, u32[]{:S(2)}, u32[]{:S(2)}) async-start(bf16[4,128,384]{2,1,0:T(8,128)(2,1)} %broadcast_in_dim.46), calls=%async_computation.3 | async-start | bytes 786432 | tf_op jit(solution)/shard_map/dense_out/all_to_all | solution.py:23
  118.8 13.5 %collective-permute-start.15 = (bf16[72,3584]{1,0:T(8,128)(2,1)}, bf16[72,3584]{1,0:T(8,128)(2,1)}, u32[]{:S(2)}, u32[]{:S(2)}) collective-permute-start(bf16[72,3584]{1,0:T(8,128)(2,1)} %get-tuple-element.45), channel_id=1, source_target_pairs={{0,32},{32,64},{64,96},{96,0},{1,33},{33,65},{65,97},{97,1},{2,34}... | collective-permute-start | bytes 1548296 | tf_op jit(solution)/shard_map/partials_y/ppermute | solution.py:19
  120.7 15.4 %collective-permute-start.18 = (bf16[72,3584]{1,0:T(8,128)(2,1)}, bf16[72,3584]{1,0:T(8,128)(2,1)}, u32[]{:S(2)}, u32[]{:S(2)}) collective-permute-start(bf16[72,3584]{1,0:T(8,128)(2,1)} %get-tuple-element.46), channel_id=1, source_target_pairs={{0,96},{32,0},{64,32},{96,64},{1,97},{33,1},{65,33},{97,65},{2,98}... | collective-permute-start | bytes 1548296 | tf_op jit(solution)/shard_map/partials_y/ppermute | solution.py:19
  139.7 25.5 %copy-start.2 = (f32[36,3584]{1,0:T(8,128)S(1)}, f32[36,3584]{1,0:T(8,128)}, u32[]{:S(2)}) copy-start(f32[36,3584]{1,0:T(8,128)} %get-tuple-element.53) | copy-start | bytes 1548292
  139.7 22.7 %collective-permute-start.19 = (bf16[36,3584]{1,0:T(8,128)(2,1)S(1)}, bf16[36,3584]{1,0:T(8,128)(2,1)}, u32[]{:S(2)}, u32[]{:S(2)}) collective-permute-start(bf16[36,3584]{1,0:T(8,128)(2,1)S(1)} %get-tuple-element.54), channel_id=1, source_target_pairs={{0,16},{8,24},{16,0},{24,8},{1,17},{9,25},{17,1},{25,9},{2,18},{10... | collective-permute-start | bytes 774152 | tf_op jit(solution)/shard_map/partials_z/ppermute | solution.py:19
  144.3 18.0 %collective-permute-start.20 = (bf16[36,3584]{1,0:T(8,128)(2,1)S(1)}, bf16[36,3584]{1,0:T(8,128)(2,1)}, u32[]{:S(2)}, u32[]{:S(2)}) collective-permute-start(bf16[36,3584]{1,0:T(8,128)(2,1)S(1)} %get-tuple-element.55), channel_id=1, source_target_pairs={{0,8},{8,16},{16,24},{24,0},{1,9},{9,17},{17,25},{25,1},{2,10},{10... | collective-permute-start | bytes 774152 | tf_op jit(solution)/shard_map/partials_z/ppermute | solution.py:19
  147.7 17.4 %collective-permute-start.21 = (bf16[36,3584]{1,0:T(8,128)(2,1)S(1)}, bf16[36,3584]{1,0:T(8,128)(2,1)}, u32[]{:S(2)}, u32[]{:S(2)}) collective-permute-start(bf16[36,3584]{1,0:T(8,128)(2,1)S(1)} %get-tuple-element.56), channel_id=1, source_target_pairs={{0,24},{8,0},{16,8},{24,16},{1,25},{9,1},{17,9},{25,17},{2,26},{10... | collective-permute-start | bytes 774152 | tf_op jit(solution)/shard_map/partials_z/ppermute | solution.py:19
  152.1 17.9 %all-to-all-start.4 = ((bf16[8,224,256]{2,1,0:T(8,128)(2,1)}), bf16[8,224,256]{2,1,0:T(8,128)(2,1)S(1)}, u32[]{:S(2)}, u32[]{:S(2)}) async-start(bf16[8,224,256]{2,1,0:T(8,128)(2,1)} %dense_out.1), calls=%async_computation.4 | async-start | bytes 1835008 | tf_op jit(solution)/shard_map/dense_out/all_to_all | solution.py:23
  170.0 15.1 %all-to-all-start.5 = ((bf16[8,36,448]{2,1,0:T(8,128)(2,1)}), bf16[8,36,448]{2,1,0:T(8,128)(2,1)S(1)}, u32[]{:S(2)}, u32[]{:S(2)}) async-start(bf16[8,36,448]{2,1,0:T(8,128)(2,1)} %bitcast.45), calls=%async_computation.5 | async-start | bytes 655360 | tf_op jit(solution)/shard_map/combine/all_to_all | solution.py:23
  174.8 17.9 %copy-start.6 = (bf16[1,128,448]{1,2,0:T(8,128)(2,1)S(1)}, bf16[1,128,448]{1,2,0:T(8,128)(2,1)}, u32[]{:S(2)}) copy-start(bf16[1,128,448]{1,2,0:T(8,128)(2,1)} %param.11) | copy-start | bytes 344068
  175.1 10.1 %collective-permute-start.5 = (bf16[64,224]{1,0:T(8,128)(2,1)S(1)}, bf16[64,224]{1,0:T(8,128)(2,1)S(1)}, u32[]{:S(2)}, u32[]{:S(2)}) collective-permute-start(bf16[64,224]{1,0:T(8,128)(2,1)S(1)} %get-tuple-element.62), channel_id=1, source_target_pairs={{0,24},{8,0},{16,8},{24,16},{1,25},{9,1},{17,9},{25,17},{2,26},{10... | collective-permute-start | bytes 86024 | tf_op jit(solution)/shard_map/dense_out/ppermute | solution.py:19
  177.0 8.2 %collective-permute-start.4 = (bf16[64,224]{1,0:T(8,128)(2,1)S(1)}, bf16[64,224]{1,0:T(8,128)(2,1)S(1)}, u32[]{:S(2)}, u32[]{:S(2)}) collective-permute-start(bf16[64,224]{1,0:T(8,128)(2,1)S(1)} %get-tuple-element.63), channel_id=1, source_target_pairs={{0,16},{8,24},{16,0},{24,8},{1,17},{9,25},{17,1},{25,9},{2,18},{10... | collective-permute-start | bytes 86024 | tf_op jit(solution)/shard_map/dense_out/ppermute | solution.py:19
  181.1 7.6 %collective-permute-start.3 = (bf16[64,224]{1,0:T(8,128)(2,1)S(1)}, bf16[64,224]{1,0:T(8,128)(2,1)S(1)}, u32[]{:S(2)}, u32[]{:S(2)}) collective-permute-start(bf16[64,224]{1,0:T(8,128)(2,1)S(1)} %get-tuple-element.64), channel_id=1, source_target_pairs={{0,8},{8,16},{16,24},{24,0},{1,9},{9,17},{17,25},{25,1},{2,10},{10... | collective-permute-start | bytes 86024 | tf_op jit(solution)/shard_map/dense_out/ppermute | solution.py:19
  189.4 3.1 %collective-permute-start.6 = (bf16[2,64,224]{2,1,0:T(8,128)(2,1)S(1)}, bf16[2,64,224]{2,1,0:T(8,128)(2,1)S(1)}, u32[]{:S(2)}, u32[]{:S(2)}) collective-permute-start(bf16[2,64,224]{2,1,0:T(8,128)(2,1)S(1)} %constant_dynamic-slice_fusion), channel_id=1, source_target_pairs={{0,1},{1,0},{2,3},{3,2},{4,5},{5,4},{6,7},{7,6},{8,9},{9,8},{10,11... | collective-permute-start | bytes 172040 | tf_op jit(solution)/shard_map/dense_out/ppermute | solution.py:19
  193.0 21.2 %collective-permute-start.22 = (bf16[128,448]{0,1:T(8,128)(2,1)S(1)}, bf16[128,448]{0,1:T(8,128)(2,1)S(1)}, u32[]{:S(2)}, u32[]{:S(2)}) collective-permute-start(bf16[128,448]{0,1:T(8,128)(2,1)S(1)} %fusion.1), channel_id=1, source_target_pairs={{0,128},{128,256},{256,384},{384,0},{1,129},{129,257},{257,385},{3... | collective-permute-start | bytes 344072 | tf_op jit(solution)/shard_map/next_section/ppermute | solution.py:19
  (8 other events, 34.9 us)
